TPU v7x, 32 devices: a whole 2x2x4 slice. The times are simulated.
32 devices in a mesh: rep: 2 (over x), shard: 16 (over z, y, core).
Axes of the slice: x: 2, y: 2, z: 4, core: 2. Of those that a mesh axis runs over, the one named last changes fastest.
Arguments:
- hidden_in: bfloat16 [2, 4096, 2048], P(None, ('rep', 'shard')), may hold values from -6 to 6
- segment_ids: int32 [2, 4096], P(None, ('rep', 'shard')), may hold values from 0 to 1, as said below
- out_grad: bfloat16 [2, 4096, 2048], P(None, ('rep', 'shard')), may hold values from -6 to 6
- norm_gain: bfloat16 [2048], P('shard'), may hold values from 0.5 to 1.5
- in_proj: bfloat16 [2048, 8192], P('shard'), may hold values from -0.125 to 0.125
- conv_weight: bfloat16 [4, 4096], P(None, 'shard'), may hold values from -2.5 to 2.5
- conv_bias: bfloat16 [4096], P('shard'), may hold values from -2.5 to 2.5
- x_proj: bfloat16 [4096, 160], P('shard'), may hold values from -0.09375 to 0.09375
- dt_weight: bfloat16 [128, 4096], P(None, 'shard'), may hold values from -0.5 to 0.5
- dt_bias: bfloat16 [4096], P('shard'), may hold values from -5 to -2
- a_log: bfloat16 [16, 4096], P(None, 'shard'), may hold values from -9 to 2.77
- d_skip: bfloat16 [4096], P('shard'), may hold values from -3 to 3
- out_proj: bfloat16 [4096, 2048], P('shard'), may hold values from -0.09375 to 0.09375
Outputs:
- layer_out: bfloat16 [2, 4096, 2048], P(None, ('rep', 'shard'))
- in_grad: float32 [2, 4096, 2048], P(None, ('rep', 'shard'))
- grad_gain: float32 [2048], P('shard')
- grad_in_proj: float32 [2048, 8192], P('shard')
- grad_conv_weight: float32 [4, 4096], P(None, 'shard')
- grad_conv_bias: float32 [4096], P('shard')
- grad_x_proj: float32 [4096, 160], P('shard')
- grad_dt_weight: float32 [128, 4096], P(None, 'shard')
- grad_dt_bias: float32 [4096], P('shard')
- grad_a_log: float32 [16, 4096], P(None, 'shard')
- grad_d_skip: float32 [4096], P('shard')
- grad_out_proj: float32 [4096, 2048], P('shard')
Inputs may be any that keep to these rules, and one draw needn't show every extreme that they name: `segment_ids`: ids never fall along a row, start at 0 and rise by exactly one at each document start. In one row drawn from the seed the whole row is a single document of 4096 tokens; every other row holds exactly max(2, 2) documents.
All inputs are finite; a program needn't handle non-finite values.
Results may differ from a plain program's by a relative error of at most 0.0084.
Values may be sent and summed in bfloat16 or wider, within the bound.
A program may use at most 768 MiB of HBM per device.

v0:
```python
import jax
import jax.numpy as jnp
from jax import lax
from jax.sharding import PartitionSpec as P


def from_behind(value, axis, steps):
    count = lax.axis_size(axis)
    leading, last = (max(0, -steps), min(count, count - steps))
    return lax.ppermute(value, axis, [(source, source + steps) for source in range(leading, last)])


def prefix(value, axis, combine, identity, reverse):
    peers, position = (lax.axis_size(axis), lax.axis_index(axis))
    everything = jax.tree.map(lambda part: lax.all_gather(part, axis), value)
    start = jax.tree.map(
        lambda part, zero: jnp.broadcast_to(jnp.asarray(zero, part.dtype), part.shape),
        value,
        identity,
    )

    def lap(k, before):
        at = peers - 1 - k if reverse else k
        reached = at > position if reverse else at < position
        new = combine(before, jax.tree.map(lambda part: part[at], everything))
        return jax.tree.map(lambda a, b: jnp.where(reached, a, b), new, before)

    return lax.fori_loop(0, peers, lap, start)


def shortened(value):
    return jax.tree.map(lambda a: a.astype(jnp.bfloat16) if a.dtype == jnp.float32 else a, value)


def cross(left_op, right_op):
    return lax.dot_general(
        left_op, right_op, (((0,), (0,)), ((), ())), preferred_element_type=jnp.float32
    )


def back_dot(left_op, right_op):
    return lax.dot_general(
        left_op, right_op, (((1,), (1,)), ((), ())), preferred_element_type=jnp.float32
    )


def dsilu(values):
    sigmoid_val = jax.nn.sigmoid(values)
    return sigmoid_val * (1.0 + values * (1.0 - sigmoid_val))


def chain_link(first_part, second_part):
    return (second_part[0] * first_part[0], second_part[0] * first_part[1] + second_part[1])


def make_advance(a_mat):

    def advance(running, pieces):
        step_t, x_t, b_t, keep_t = pieces
        decay_now = jnp.exp(step_t[None, :] * a_mat) * keep_t
        return decay_now * running + b_t[:, None] * (step_t * x_t)[None, :]

    return advance


def make_retreat(a_mat):

    def retreat(carried, pieces):
        flow_in, a_grad = carried
        prev_t, step_t, x_t, b_t, c_t, keep_t, dy_t = pieces
        decay_now = jnp.exp(step_t[None, :] * a_mat) * keep_t
        g_total = c_t[:, None] * dy_t[None, :] + flow_in
        through = g_total * prev_t * decay_now
        b_weighted = jnp.sum(g_total * b_t[:, None], axis=0)
        d_step = jnp.sum(through * a_mat, axis=0) + x_t * b_weighted
        d_b = jnp.sum(g_total * (step_t * x_t)[None, :], axis=1)
        d_x = step_t * b_weighted
        return ((decay_now * g_total, a_grad + through * step_t[None, :]), (d_step, d_b, d_x))

    return retreat


def on_device(
    hidden_in,
    segment_ids,
    out_grad,
    norm_gain,
    in_proj,
    conv_weight,
    conv_bias,
    x_proj,
    dt_weight,
    dt_bias,
    a_log,
    d_skip,
    out_proj,
):
    micro_count = hidden_in.shape[0]
    held_weights = None
    held_weights = (
        lax.all_gather(norm_gain, "shard", axis=0, tiled=True),
        lax.all_gather(in_proj, "shard", axis=0, tiled=True),
        lax.all_gather(conv_weight, "shard", axis=1, tiled=True),
        lax.all_gather(conv_bias, "shard", axis=0, tiled=True),
        lax.all_gather(x_proj, "shard", axis=0, tiled=True),
        lax.all_gather(dt_weight, "shard", axis=1, tiled=True),
        lax.all_gather(dt_bias, "shard", axis=0, tiled=True),
        lax.all_gather(a_log, "shard", axis=1, tiled=True),
        lax.all_gather(d_skip, "shard", axis=0, tiled=True),
        lax.all_gather(out_proj, "shard", axis=0, tiled=True),
    )
    accumulated = None
    row_outs = []
    row_grads = []
    for row_idx in range(micro_count):
        gain_full, w_in, conv_w, conv_b, w_x, w_dt, dt_b, alog_full, skip_full, w_out = held_weights
        inputs = hidden_in[row_idx].astype(jnp.float32)
        doc_ids = segment_ids[row_idx]
        length = inputs.shape[0]
        inner_dim = w_x.shape[0]
        rank_dim = w_dt.shape[0]
        state_dim = alog_full.shape[0]
        kernel = conv_w.shape[0]
        gain_wide = gain_full.astype(jnp.float32)
        conv_wide = conv_w.astype(jnp.float32)
        skip_wide = skip_full.astype(jnp.float32)
        a_mat = -jnp.exp(alog_full.astype(jnp.float32))
        scale_row = lax.rsqrt(jnp.mean(inputs * inputs, axis=1, keepdims=True) + 1e-05)
        normed = (inputs * scale_row * gain_wide[None, :]).astype(jnp.bfloat16)
        projected = jnp.dot(normed, w_in, preferred_element_type=jnp.float32).astype(jnp.bfloat16)
        x_wide = projected[:, :inner_dim].astype(jnp.float32)
        z_wide = projected[:, inner_dim:].astype(jnp.float32)
        tail_mask = (doc_ids[length - kernel + 1 :] == doc_ids[length - 1]).astype(jnp.float32)
        tail_send = x_wide[length - kernel + 1 :] * tail_mask[:, None]
        last_send = (doc_ids[length - 1 :] + 1).astype(jnp.float32)
        tail_recv, last_recv = (
            from_behind(tail_send.astype(jnp.bfloat16), ("rep", "shard"), 1).astype(
                tail_send.dtype
            ),
            from_behind(last_send.astype(jnp.bfloat16), ("rep", "shard"), 1).astype(
                last_send.dtype
            ),
        )
        joined = last_recv[0] == (doc_ids[0] + 1).astype(jnp.float32)
        lead_id = jnp.where(joined, doc_ids[0], -1)
        ext_ids = jnp.concatenate([jnp.ones((kernel - 1,), jnp.int32) * lead_id, doc_ids])
        ext_x = jnp.concatenate([tail_recv, x_wide], axis=0)
        convolved = conv_b.astype(jnp.float32)[None, :] + conv_wide[kernel - 1][None, :] * x_wide
        same_masks = []
        for offset in range(1, kernel):
            start_row = kernel - 1 - offset
            same_doc = (ext_ids[start_row : start_row + length] == doc_ids).astype(jnp.float32)[
                :, None
            ]
            same_masks.append(same_doc)
            convolved = (
                convolved
                + conv_wide[start_row][None, :] * ext_x[start_row : start_row + length] * same_doc
            )
        x_conv = jax.nn.silu(convolved).astype(jnp.bfloat16)
        x_conv_wide = x_conv.astype(jnp.float32)
        dbc_out = jnp.dot(x_conv, w_x, preferred_element_type=jnp.float32)
        step_low = dbc_out[:, :rank_dim].astype(jnp.bfloat16)
        b_mat = dbc_out[:, rank_dim : rank_dim + state_dim]
        c_mat = dbc_out[:, rank_dim + state_dim :]
        step_pre = (
            jnp.dot(step_low, w_dt, preferred_element_type=jnp.float32)
            + dt_b.astype(jnp.float32)[None, :]
        )
        step_size = jax.nn.softplus(step_pre)
        prior_ids = jnp.concatenate([jnp.ones((1,), jnp.int32) * lead_id, doc_ids[: length - 1]])
        keep_mask = (prior_ids == doc_ids).astype(jnp.float32)
        advance = make_advance(a_mat)

        def end_only(running, pieces):
            return (advance(running, pieces), None)

        def keep_every(running, pieces):
            updated = advance(running, pieces)
            return (updated, updated)

        series = (step_size, x_conv_wide, b_mat, keep_mask)
        zero_state = jnp.zeros(a_mat.shape, jnp.float32)
        unit_state = jnp.ones(a_mat.shape, jnp.float32)
        s_local, unused_local = lax.scan(end_only, zero_state, series, unroll=16)
        p_total = jnp.exp(a_mat * jnp.sum(step_size, axis=0)[None, :]) * jnp.prod(keep_mask)
        p_prefix, h_in = prefix(
            (p_total, s_local), ("rep", "shard"), chain_link, (unit_state, zero_state), False
        )
        s_final, states = lax.scan(keep_every, h_in, series, unroll=16)
        y_scan = jnp.einsum("ln,lne->le", c_mat, states, precision=lax.Precision.HIGHEST)
        y_full = y_scan + skip_wide[None, :] * x_conv_wide
        z_gate = jax.nn.silu(z_wide)
        gated_out = (y_full * z_gate).astype(jnp.bfloat16)
        layer_row = inputs + jnp.dot(gated_out, w_out, preferred_element_type=jnp.float32)
        row_outs.append(layer_row.astype(jnp.bfloat16))
        (
            gain_back,
            w_in_back,
            conv_back,
            conv_b_back,
            w_x_back,
            w_dt_back,
            dt_b_back,
            alog_back,
            skip_back,
            w_out_back,
        ) = held_weights
        cotangent = out_grad[row_idx]
        cotangent_wide = cotangent.astype(jnp.float32)
        grad_out_proj = cross(gated_out, cotangent)
        d_gated = back_dot(cotangent, w_out_back)
        d_y = d_gated * z_gate
        d_z = d_gated * y_full * dsilu(z_wide)
        grad_d_skip = jnp.sum(d_y * x_conv_wide, axis=0)
        prev_states = jnp.concatenate([h_in[None], states[: length - 1]], axis=0)

        def flow_only(flow_in, pieces):
            step_t, keep_t, c_t, dy_t = pieces
            decay_now = jnp.exp(step_t[None, :] * a_mat) * keep_t
            return (decay_now * (c_t[:, None] * dy_t[None, :] + flow_in), None)

        s_back, unused_back = lax.scan(
            flow_only, zero_state, (step_size, keep_mask, c_mat, d_y), reverse=True, unroll=16
        )
        q_prefix, q_in = prefix(
            (p_total, s_back), ("rep", "shard"), chain_link, (unit_state, zero_state), True
        )
        carried_out, per_token = lax.scan(
            make_retreat(a_mat),
            (q_in, zero_state),
            (prev_states, step_size, x_conv_wide, b_mat, c_mat, keep_mask, d_y),
            reverse=True,
            unroll=16,
        )
        grad_a_log = carried_out[1] * a_mat
        d_step, d_b, d_xs = per_token
        d_c = jnp.einsum("le,lne->ln", d_y, states, precision=lax.Precision.HIGHEST)
        d_pre = d_step * jax.nn.sigmoid(step_pre)
        grad_dt_bias = jnp.sum(d_pre, axis=0)
        d_pre_low = d_pre.astype(jnp.bfloat16)
        grad_dt_weight = cross(step_low, d_pre_low)
        d_step_low = back_dot(d_pre_low, w_dt_back)
        d_dbc = jnp.concatenate([d_step_low, d_b, d_c], axis=1).astype(jnp.bfloat16)
        grad_x_proj = cross(x_conv, d_dbc)
        d_xconv = d_y * skip_wide[None, :] + d_xs + back_dot(d_dbc, w_x_back)
        d_conv = d_xconv * dsilu(convolved)
        grad_conv_bias = jnp.sum(d_conv, axis=0)
        conv_rows = [None] * kernel
        conv_rows[kernel - 1] = jnp.sum(d_conv * x_wide, axis=0)
        d_ext = jnp.pad(d_conv * conv_wide[kernel - 1][None, :], ((kernel - 1, 0), (0, 0)))
        for offset in range(1, kernel):
            start_row = kernel - 1 - offset
            masked_grad = d_conv * same_masks[offset - 1]
            conv_rows[start_row] = jnp.sum(
                masked_grad * ext_x[start_row : start_row + length], axis=0
            )
            d_ext = d_ext + jnp.pad(
                masked_grad * conv_wide[start_row][None, :], ((start_row, offset), (0, 0))
            )
        grad_conv_weight = jnp.stack(conv_rows)
        tail_grad = from_behind(shortened(d_ext[: kernel - 1]), ("rep", "shard"), -1)
        d_x_local = d_ext[kernel - 1 :] + jnp.pad(
            tail_grad * tail_mask[:, None], ((length - kernel + 1, 0), (0, 0))
        )
        d_proj = jnp.concatenate([d_x_local, d_z], axis=1).astype(jnp.bfloat16)
        grad_in_proj = cross(normed, d_proj)
        d_normed = back_dot(d_proj, w_in_back)
        grad_gain = jnp.sum(d_normed * inputs * scale_row, axis=0)
        d_scaled = d_normed * gain_back.astype(jnp.float32)[None, :]
        cubed = scale_row * scale_row * scale_row
        in_row = (
            cotangent_wide
            + scale_row * d_scaled
            - inputs * cubed * jnp.mean(d_scaled * inputs, axis=1, keepdims=True)
        )
        row_grads.append(in_row)
        grad_terms = (
            grad_gain,
            grad_in_proj,
            grad_conv_weight,
            grad_conv_bias,
            grad_x_proj,
            grad_dt_weight,
            grad_dt_bias,
            grad_a_log,
            grad_d_skip,
            grad_out_proj,
        )
        accumulated = (
            grad_terms
            if accumulated is None
            else tuple((a + b for a, b in zip(accumulated, grad_terms)))
        )
    accumulated = (
        lax.psum_scatter(accumulated[0], "shard", scatter_dimension=0, tiled=True),
        lax.psum_scatter(accumulated[1], "shard", scatter_dimension=0, tiled=True),
        lax.psum_scatter(accumulated[2], "shard", scatter_dimension=1, tiled=True),
        lax.psum_scatter(accumulated[3], "shard", scatter_dimension=0, tiled=True),
        lax.psum_scatter(accumulated[4], "shard", scatter_dimension=0, tiled=True),
        lax.psum_scatter(accumulated[5], "shard", scatter_dimension=1, tiled=True),
        lax.psum_scatter(accumulated[6], "shard", scatter_dimension=0, tiled=True),
        lax.psum_scatter(accumulated[7], "shard", scatter_dimension=1, tiled=True),
        lax.psum_scatter(accumulated[8], "shard", scatter_dimension=0, tiled=True),
        lax.psum_scatter(accumulated[9], "shard", scatter_dimension=0, tiled=True),
    )
    replicated = lax.psum(
        (
            accumulated[0],
            accumulated[1],
            accumulated[2],
            accumulated[3],
            accumulated[4],
            accumulated[5],
            accumulated[6],
            accumulated[7],
            accumulated[8],
            accumulated[9],
        ),
        "rep",
    )
    return (
        jnp.stack(row_outs),
        jnp.stack(row_grads),
        replicated[0],
        replicated[1],
        replicated[2],
        replicated[3],
        replicated[4],
        replicated[5],
        replicated[6],
        replicated[7],
        replicated[8],
        replicated[9],
    )


def solution(mesh):
    return jax.shard_map(
        on_device,
        mesh=mesh,
        in_specs=(
            P(None, ("rep", "shard"), None),
            P(None, ("rep", "shard")),
            P(None, ("rep", "shard"), None),
            P("shard"),
            P("shard", None),
            P(None, "shard"),
            P("shard"),
            P("shard", None),
            P(None, "shard"),
            P("shard"),
            P(None, "shard"),
            P("shard"),
            P("shard", None),
        ),
        out_specs=(
            P(None, ("rep", "shard"), None),
            P(None, ("rep", "shard"), None),
            P("shard"),
            P("shard", None),
            P(None, "shard"),
            P("shard"),
            P("shard", None),
            P(None, "shard"),
            P("shard"),
            P(None, "shard"),
            P("shard"),
            P("shard", None),
        ),
        check_vma=False,
    )
```

profile of v0, /device:TPU:0, one launch (start us, length us, event | category | flops | bytes accessed | tf_op | source)
XLA Modules:
  0.0 4608.5 jit_solution(9581356293313594328)
XLA Ops:
  21.7 21.2 all-gather.7
  42.9 17.4 all-gather.8
  60.4 18.9 all-gather.6
  79.3 17.8 all_gather.71
  97.2 19.8 all_gather.75
  122.2 59.9 %all-gather.21.cloned.1.call-done = bf16[2048,8192]{1,0:T(8,128)(2,1)} async-done(((bf16[128,8192]{1,0:T(8,128)(2,1)}), bf16[2048,8192]{1,0:T(8,128)(2,1)}) %all-gather.21.cloned.1.call-update) | async-done | bytes 33554448 | tf_op jit(solution)/shard_map/all_gather | solution.py:102
  182.1 15.5 convolution_convert_fusion.1
  200.3 15.3 convolution_convert_fusion
  220.9 91.2 %all-gather.27.cloned.1.call-done = bf16[4096,2048]{1,0:T(8,128)(2,1)} async-done(((bf16[256,2048]{1,0:T(8,128)(2,1)}), bf16[4096,2048]{1,0:T(8,128)(2,1)}) %all-gather.27.cloned.1.call-update) | async-done | bytes 16777232 | tf_op jit(solution)/shard_map/all_gather | solution.py:110
  312.2 14.8 multiply_reduce_fusion.96
  327.0 23.3 all-gather.23.cloned.1.call-done
  352.6 14.8 multiply_reduce_fusion.97
  369.6 18.9 all-gather.25.cloned.1.call-done
  403.9 140.6 %while.184 = (s32[]{:T(128)}, f32[16,4096]{1,0:T(8,128)S(1)}, f32[8,16,4096]{2,1,0:T(8,128)}, f32[16,4096]{1,0:T(8,128)S(1)}, f32[8,16]{1,0:T(8,128)}, /*index=5...) while((s32[]{:T(128)}, f32[16,4096]{1,0:T(8,128)S(1)}, ...), condition=%wide.region_4.5_spmd.clone, body=%wide.region_3.4_spmd.clone.sunk | while | flops 5373970 | bytes 3149663 | solution.py:185
  546.0 139.4 %while.188 = (s32[]{:T(128)}, f32[16,4096]{1,0:T(8,128)S(1)}, f32[8,16,4096]{2,1,0:T(8,128)}, f32[16,4096]{1,0:T(8,128)S(1)}, f32[8,16]{1,0:T(8,128)}, /*index=5...) while((s32[]{:T(128)}, f32[16,4096]{1,0:T(8,128)S(1)}, ...), condition=%wide.region_19.20_spmd.clone, body=%wide.region_18.19_spmd.clone.sunk | while | flops 5308435 | bytes 2363251 | solution.py:223
  691.2 140.6 %while.186 = (s32[]{:T(128)}, f32[16,4096]{1,0:T(8,128)S(1)}, f32[8,16,4096]{2,1,0:T(8,128)}, f32[16,4096]{1,0:T(8,128)S(1)}, f32[8,16]{1,0:T(8,128)}, /*index=5...) while((s32[]{:T(128)}, f32[16,4096]{1,0:T(8,128)S(1)}, ...), condition=%wide.region_13.14_spmd.clone, body=%wide.region_12.13_spmd.clone.sunk | while | flops 5373970 | bytes 3149663 | solution.py:185
  832.7 19.9 all-gather.9
  854.7 141.4 %while.191 = (s32[]{:T(128)}, f32[16,4096]{1,0:T(8,128)}, f32[8,16,4096]{2,1,0:T(8,128)}, f32[16,4096]{1,0:T(8,128)S(1)}, f32[8,16]{1,0:T(8,128)}, /*index=5*/f3...) while((s32[]{:T(128)}, f32[16,4096]{1,0:T(8,128)}, ...), condition=%wide.region_74.75_spmd.clone, body=%wide.region_73.74_spmd.clone.sunk | while | flops 5308435 | bytes 2363251 | solution.py:223
  996.3 41.2 while.185
  1037.5 41.2 while.189
  1078.8 40.7 while.187
  1119.5 40.9 while.192
  1172.5 285.0 %while.182 = (s32[]{:T(128)}, f32[16,4096]{1,0:T(8,128)S(1)}, f32[8,16,16,4096]{3,2,1,0:T(8,128)}, f32[8,16,4096]{2,1,0:T(8,128)}, f32[16,4096]{1,0:T(8,128)S(1)...) while((s32[]{:T(128)}, f32[16,4096]{1,0:T(8,128)S(1)}, ...), condition=%wide.region_8.9_spmd, body=%wide.region_7.8_spmd.sunk | while | flops 13172752 | bytes 25188864 | solution.py:190
  1457.6 23.7 slice.5288
  1481.2 46.4 %fusion.416 = bf16[128,1,16]{2,1,0:T(2,128)(2,1)S(1)} fusion(f32[128,16,4096]{2,1,0:T(8,128)} %bitcast.2942, f32[128,4096,1]{1,0,2:T(8,128)S(1)} %bitcast.2953), kind=kOutput, calls=%fused_computation.1273 | convolution fusion | flops 100663296 | bytes 35655680 | tf_op jit(solution)/shard_map/le,lne->ln/dot_general | solution.py:238
  1528.3 23.1 fusion.495
  1551.3 23.4 pad_maximum_fusion
  1578.5 604.7 %while.190 = (s32[]{:T(128)}, f32[16,4096]{1,0:T(8,128)S(1)}, f32[16,4096]{1,0:T(8,128)}, f32[8,16,4096]{2,1,0:T(8,128)}, bf16[8,16,16]{2,1,0:T(8,128)(2,1)}, /*...) while((s32[]{:T(128)}, f32[16,4096]{1,0:T(8,128)S(1)}, ...), condition=%wide.region_71.72_spmd.clone, body=%wide.region_22.71_spmd.clone.sunk | while | flops 25558804 | bytes 27900400 | solution.py:229
  1707.4 14.2 fusion.580
  1783.1 14.2 fusion.580
  1858.8 14.2 fusion.580
  1934.2 14.2 fusion.580
  2085.2 14.2 fusion.580
  2201.0 294.7 %while.183 = (s32[]{:T(128)}, f32[16,4096]{1,0:T(8,128)S(1)}, f32[8,16,16,4096]{3,2,1,0:T(8,128)}, f32[8,16,4096]{2,1,0:T(8,128)}, f32[16,4096]{1,0:T(8,128)S(1)...) while((s32[]{:T(128)}, f32[16,4096]{1,0:T(8,128)S(1)}, ...), condition=%wide.region_17.18_spmd, body=%wide.region_16.17_spmd.sunk | while | flops 13172752 | bytes 25188864 | solution.py:190
  2495.8 23.7 slice.5291
  2519.5 46.2 %fusion.414 = bf16[128,1,16]{2,1,0:T(2,128)(2,1)S(1)} fusion(f32[128,16,4096]{2,1,0:T(8,128)} %bitcast.2945, f32[128,4096,1]{1,0,2:T(8,128)S(1)} %bitcast.2950), kind=kOutput, calls=%fused_computation.1271 | convolution fusion | flops 100663296 | bytes 35655680 | tf_op jit(solution)/shard_map/le,lne->ln/dot_general | solution.py:238
  2566.4 23.4 pad_maximum_fusion.1
  2593.6 604.0 %while.193 = (s32[]{:T(128)}, f32[16,4096]{1,0:T(8,128)S(1)}, f32[16,4096]{1,0:T(8,128)}, f32[8,16,4096]{2,1,0:T(8,128)}, bf16[8,16,16]{2,1,0:T(8,128)(2,1)}, /*...) while((s32[]{:T(128)}, f32[16,4096]{1,0:T(8,128)S(1)}, ...), condition=%wide.region_126.127_spmd.clone, body=%wide.region_77.126_spmd.clone.sunk | while | flops 25558804 | bytes 27900400 | solution.py:229
  3212.2 23.0 fusion.497
  3259.8 25.0 convolution_add_fusion.1
  3306.6 24.9 fusion.419
  3331.5 53.7 %convolution_add_fusion = f32[2048,8192]{1,0:T(8,128)} fusion(f32[2048,8192]{1,0:T(8,128)} %fusion.419, bf16[128,4096]{1,0:T(8,128)(2,1)S(1)} %copy-done.18, bf16[128,4096]{1,0:T(8,128)(2,1)S(1)} %fusion.412, f32[128]{0:T(128)S(1)} %copy-done.67, f32[2048]{0:T(1024)S(1)} %bitcast.3499, bf16[2,128,2048]{2,1,0:T(8,128)(2,1)S(1)} %copy-done.4), kind=kOutput, calls=%fused_computation.1192 | convolution fusion | flops 4316987392 | bytes 136847872 | tf_op jit(solution)/shard_map/dot_general | solution.py:36
  3391.6 276.7 %reduce-scatter.17.cloned.1.call-done = f32[256,2048]{1,0:T(8,128)} async-done(((f32[4096,2048]{1,0:T(8,128)}), f32[256,2048]{1,0:T(8,128)}) %reduce-scatter.17.cloned.1.call-update) | async-done | bytes 2097168 | tf_op jit(solution)/shard_map/reduce_scatter | solution.py:305
  3668.2 640.6 %reduce-scatter.9.cloned.1.call-done = f32[128,8192]{1,0:T(8,128)} async-done(((f32[2048,8192]{1,0:T(8,128)}), f32[128,8192]{1,0:T(8,128)}) %reduce-scatter.9.cloned.1.call-update) | async-done | bytes 4194320 | tf_op jit(solution)/shard_map/reduce_scatter | solution.py:297
  4328.6 17.3 fusion.418
  4345.9 19.6 fusion.429
  4365.5 59.5 %all-reduce.16 = (f32[2048]{0:T(1024)S(1)}, f32[4096]{0:T(1024)S(1)}, f32[4096]{0:T(1024)S(1)}, f32[4096]{0:T(1024)S(1)}) all-reduce(f32[2048]{0:T(1024)S(1)} %add.2111, f32[4096]{0:T(1024)S(1)} %add.2114, f32[4096]{0:T(1024)S(1)} %add.2117, f32[4096]{0:T(1024)S(1)} %add.2119), channel_id=8, replica_groups=mesh['rep'=2,'shard'=16] {'shard'}, use_global_device_ids=true, to_apply=%region_130.131.clone | all-reduce | flops 14336 | bytes 114688
  4441.3 152.8 %all-reduce.21.cloned.1.call-done = (f32[128,8192]{1,0:T(8,128)}, f32[256,160]{0,1:T(8,128)}, f32[128,256]{1,0:T(8,128)}, f32[256,2048]{1,0:T(8,128)}) async-done(((f32[128,8192]{1,0:T(8,128)}, f32[256,160]{0,1:T(8,128)}, f32[128,256]{1,0:T(8,128)}, f32[256,2048]{1,0:T(8,128)}), (f32[128,8192]{1,0:T(8,128)}, f32[256,160]{0,1:T(8,128)}, f32[128,256]{1,0:T(8,128)}, ...) | async-done | bytes 6586384 | tf_op jit(solution)/shard_map/psum | solution.py:307
  (2436 shorter events, 2630.7 us)
Async XLA Ops:
  7.2 89.9 %copy-start.81 = (bf16[16,256]{1,0:T(8,128)(2,1)S(1)}, bf16[16,256]{1,0:T(8,128)(2,1)}, u32[]{:S(2)}) copy-start(bf16[16,256]{1,0:T(8,128)(2,1)} %param.47) | copy-start | bytes 24580
  7.3 174.8 %all-gather.21.cloned.1.call-start = ((), (), s32[]{:S(2)}) async-start(), calls=%async_computation.6 | async-start | bytes 35651584 | tf_op jit(solution)/shard_map/all_gather | solution.py:102
  8.0 304.2 %all-gather.27.cloned.1.call-start = ((), (), s32[]{:S(2)}) async-start(), calls=%async_computation.9 | async-start | bytes 17825792 | tf_op jit(solution)/shard_map/all_gather | solution.py:110
  8.7 341.6 %all-gather.23.cloned.1.call-start = ((), (), s32[]{:S(2)}) async-start(), calls=%async_computation.7 | async-start | bytes 1392640 | tf_op jit(solution)/shard_map/all_gather | solution.py:105
  9.5 379.0 %all-gather.25.cloned.1.call-start = ((), (), s32[]{:S(2)}) async-start(), calls=%async_computation.8 | async-start | bytes 1114112 | tf_op jit(solution)/shard_map/all_gather | solution.py:106
  10.8 108.1 %collective-permute-start.3 = (bf16[1]{0:T(256)(128)(2,1)}, bf16[1]{0:T(256)(128)(2,1)}, u32[]{:S(2)}, u32[]{:S(2)}) collective-permute-start(bf16[1]{0:T(256)(128)(2,1)} %bitcast.194), channel_id=1, source_target_pairs={{0,1},{1,2},{2,3},{3,4},{4,5},{5,6},{6,7},{7,8},{8,9},{9,10},{10,1... | collective-permute-start | bytes 14 | tf_op jit(solution)/shard_map/ppermute | solution.py:10
  14.7 105.4 %collective-permute-start.1 = (bf16[1]{0:T(256)(128)(2,1)}, bf16[1]{0:T(256)(128)(2,1)}, u32[]{:S(2)}, u32[]{:S(2)}) collective-permute-start(bf16[1]{0:T(256)(128)(2,1)} %bitcast.172), channel_id=1, source_target_pairs={{0,1},{1,2},{2,3},{3,4},{4,5},{5,6},{6,7},{7,8},{8,9},{9,10},{10,1... | collective-permute-start | bytes 14 | tf_op jit(solution)/shard_map/ppermute | solution.py:10
  20.0 976.3 %all-gather.29.cloned.1.call-start = ((), (), s32[]{:S(2)}) async-start(), calls=%async_computation.15 | async-start | bytes 8650752 | tf_op jit(solution)/shard_map/all_gather | solution.py:15
  42.9 157.4 %copy-start.42 = (f32[16,1,128]{2,1,0:T(1,128)}, f32[16,1,128]{2,1,0:T(1,128)S(1)}, u32[]{:S(2)}) copy-start(f32[16,1,128]{2,1,0:T(1,128)S(1)} %convert_element_type.280) | copy-start | bytes 24580
  97.2 255.3 %copy-start.73 = (f32[1,4096]{1,0:T(1,128)}, f32[1,4096]{1,0:T(1,128)S(1)}, u32[]{:S(2)}) copy-start(f32[1,4096]{1,0:T(1,128)S(1)} %get-tuple-element.3013) | copy-start | bytes 49156
  97.2 255.3 %copy-start.75 = (f32[1,4096]{1,0:T(1,128)}, f32[1,4096]{1,0:T(1,128)S(1)}, u32[]{:S(2)}) copy-start(f32[1,4096]{1,0:T(1,128)S(1)} %get-tuple-element.3014) | copy-start | bytes 49156
  97.2 255.3 %copy-start.77 = (f32[1,4096]{1,0:T(1,128)}, f32[1,4096]{1,0:T(1,128)S(1)}, u32[]{:S(2)}) copy-start(f32[1,4096]{1,0:T(1,128)S(1)} %get-tuple-element.3015) | copy-start | bytes 49156
  97.2 255.3 %copy-start.79 = (f32[1,4096]{1,0:T(1,128)}, f32[1,4096]{1,0:T(1,128)S(1)}, u32[]{:S(2)}) copy-start(f32[1,4096]{1,0:T(1,128)S(1)} %get-tuple-element.3016) | copy-start | bytes 49156
  117.0 279.9 %copy-start.44 = (bf16[16,4096]{1,0:T(8,128)(2,1)}, bf16[16,4096]{1,0:T(8,128)(2,1)S(1)}, u32[]{:S(2)}) copy-start(bf16[16,4096]{1,0:T(8,128)(2,1)S(1)} %all_gather.75) | copy-start | bytes 393220
  117.5 80.1 %copy-start.64 = (f32[128]{0:T(128)}, f32[128]{0:T(128)S(1)}, u32[]{:S(2)}) copy-start(f32[128]{0:T(128)S(1)} %get-tuple-element.3046) | copy-start | bytes 1540
  117.5 82.8 %copy-start.66 = (f32[128]{0:T(128)}, f32[128]{0:T(128)S(1)}, u32[]{:S(2)}) copy-start(f32[128]{0:T(128)S(1)} %get-tuple-element.3034) | copy-start | bytes 1540
  118.9 97.0 %copy-start.84 = (f32[3]{0:T(128)}, f32[3]{0:T(128)S(1)}, u32[]{:S(2)}) copy-start(f32[3]{0:T(128)S(1)} %get-tuple-element.3022) | copy-start | bytes 40
  122.1 190.1 %copy-start.96 = (f32[128]{0:T(128)}, f32[128]{0:T(128)S(1)}, u32[]{:S(2)}) copy-start(f32[128]{0:T(128)S(1)} %get-tuple-element.3038) | copy-start | bytes 1540
  122.1 230.4 %copy-start.90 = (f32[128]{0:T(128)}, f32[128]{0:T(128)S(1)}, u32[]{:S(2)}) copy-start(f32[128]{0:T(128)S(1)} %get-tuple-element.3035) | copy-start | bytes 1540
  122.1 230.4 %copy-start.92 = (f32[128]{0:T(128)}, f32[128]{0:T(128)S(1)}, u32[]{:S(2)}) copy-start(f32[128]{0:T(128)S(1)} %get-tuple-element.3036) | copy-start | bytes 1540
  122.1 230.4 %copy-start.94 = (f32[128]{0:T(128)}, f32[128]{0:T(128)S(1)}, u32[]{:S(2)}) copy-start(f32[128]{0:T(128)S(1)} %get-tuple-element.3037) | copy-start | bytes 1540
  197.9 22.9 collective-permute-start
  215.7 96.5 %copy-start.27 = (bf16[128,8192]{1,0:T(8,128)(2,1)}, bf16[128,8192]{1,0:T(8,128)(2,1)S(1)}, u32[]{:S(2)}) copy-start(bf16[128,8192]{1,0:T(8,128)(2,1)S(1)} %convolution_convert_fusion) | copy-start | bytes 6291460
  215.7 96.5 %copy-start.98 = (f32[128]{0:T(128)S(1)}, f32[128]{0:T(128)}, u32[]{:S(2)}) copy-start(f32[128]{0:T(128)} %get-tuple-element.3039) | copy-start | bytes 1540
  217.8 3.1 collective-permute-start.2
  220.9 131.7 %copy-start.59 = (f32[3,4096]{1,0:T(4,128)}, f32[3,4096]{1,0:T(4,128)S(1)}, u32[]{:S(2)}) copy-start(f32[3,4096]{1,0:T(4,128)S(1)} %convert_element_type.228) | copy-start | bytes 147460
  220.9 106.1 %copy-start.61 = (f32[3,4096]{1,0:T(4,128)}, f32[3,4096]{1,0:T(4,128)S(1)}, u32[]{:S(2)}) copy-start(f32[3,4096]{1,0:T(4,128)S(1)} %convert_element_type.254) | copy-start | bytes 147460
  352.5 335.2 %copy-start.49 = (f32[128,160]{0,1:T(8,128)}, f32[128,160]{0,1:T(8,128)S(1)}, u32[]{:S(2)}) copy-start(f32[128,160]{0,1:T(8,128)S(1)} %fusion.496) | copy-start | bytes 245764
  399.1 597.2 %all-gather.31.cloned.1.call-start = ((), (), s32[]{:S(2)}) async-start(), calls=%async_computation.16 | async-start | bytes 8650752 | tf_op jit(solution)/shard_map/all_gather | solution.py:15
  545.2 492.3 %all-gather.37.cloned.1.call-start = ((), (), s32[]{:S(2)}) async-start(), calls=%async_computation.19 | async-start | bytes 8650752 | tf_op jit(solution)/shard_map/all_gather | solution.py:15
  686.1 392.7 %all-gather.33.cloned.1.call-start = ((), (), s32[]{:S(2)}) async-start(), calls=%async_computation.17 | async-start | bytes 8650752 | tf_op jit(solution)/shard_map/all_gather | solution.py:15
  686.9 391.9 %all-gather.35.cloned.1.call-start = ((), (), s32[]{:S(2)}) async-start(), calls=%async_computation.18 | async-start | bytes 8650752 | tf_op jit(solution)/shard_map/all_gather | solution.py:15
  691.2 141.5 %copy-start.103 = (bf16[256]{0:T(256)(128)(2,1)S(1)}, bf16[256]{0:T(256)(128)(2,1)}, u32[]{:S(2)}) copy-start(bf16[256]{0:T(256)(128)(2,1)} %param.48) | copy-start | bytes 1540
  832.5 287.0 %all-gather.39.cloned.1.call-start = ((), (), s32[]{:S(2)}) async-start(), calls=%async_computation.20 | async-start | bytes 8650752 | tf_op jit(solution)/shard_map/all_gather | solution.py:15
  996.0 82.8 %copy-start.5 = (f32[8,16,4096]{2,1,0:T(8,128)}, f32[8,16,4096]{2,1,0:T(8,128)S(1)}, u32[]{:S(2)}) copy-start(f32[8,16,4096]{2,1,0:T(8,128)S(1)} %get-tuple-element.5935) | copy-start | bytes 6291460
  996.0 2395.5 %reduce-scatter.13.cloned.1.call-start = ((), (), s32[]{:S(2)}) async-start(), calls=%async_computation.12 | async-start | bytes 2228224 | tf_op jit(solution)/shard_map/reduce_scatter | solution.py:301
  1037.5 123.8 %copy-start.14 = (f32[16,4096]{1,0:T(8,128)}, f32[16,4096]{1,0:T(8,128)S(1)}, u32[]{:S(2)}) copy-start(f32[16,4096]{1,0:T(8,128)S(1)} %get-tuple-element.5250) | copy-start | bytes 786436
  3204.8 186.8 %reduce-scatter.11.cloned.1.call-start = ((), (), s32[]{:S(2)}) async-start(), calls=%async_computation.11 | async-start | bytes 2785280 | tf_op jit(solution)/shard_map/reduce_scatter | solution.py:300
  3235.3 432.9 %reduce-scatter.17.cloned.1.call-start = ((), (), s32[]{:S(2)}) async-start(), calls=%async_computation.14 | async-start | bytes 35651584 | tf_op jit(solution)/shard_map/reduce_scatter | solution.py:305
  3284.8 1024.0 %reduce-scatter.9.cloned.1.call-start = ((), (), s32[]{:S(2)}) async-start(), calls=%async_computation.10 | async-start | bytes 71303168 | tf_op jit(solution)/shard_map/reduce_scatter | solution.py:297
  3293.6 8.5 collective-permute-start.5
  3300.8 3.1 collective-permute-start.4
  3385.2 1043.4 %reduce-scatter.19.cloned.1.call-start = ((), (), s32[]{:S(2)}) async-start(), calls=%async_computation.21 | async-start | bytes 2228224
  3387.4 1044.5 %reduce-scatter.15.cloned.1.call-start = ((), (), s32[]{:S(2)}) async-start(), calls=%async_computation.13 | async-start | bytes 278528 | tf_op jit(solution)/shard_map/reduce_scatter | solution.py:303
  3389.3 1204.8 %all-reduce.21.cloned.1.call-start = ((), (), s32[]{:S(2)}) async-start(), calls=%async_computation.22 | async-start | bytes 13172736 | tf_op jit(solution)/shard_map/psum | solution.py:307
  4345.9 79.3 %copy-start.33 = (f32[128,2048]{1,0:T(8,128)S(1)}, f32[128,2048]{1,0:T(8,128)}, u32[]{:S(2)}) copy-start(f32[128,2048]{1,0:T(8,128)} %fusion.418) | copy-start | bytes 3145732
  4345.9 79.3 %copy-start.86 = (f32[128]{0:T(128)S(1)}, f32[128]{0:T(128)}, u32[]{:S(2)}) copy-start(f32[128]{0:T(128)} %get-tuple-element.3033) | copy-start | bytes 1540
  4345.9 79.4 %copy-start.87 = (f32[128]{0:T(128)S(1)}, f32[128]{0:T(128)}, u32[]{:S(2)}) copy-start(f32[128]{0:T(128)} %get-tuple-element.3047) | copy-start | bytes 1540
  (95 other events, 1058.3 us)
Sparse Core Ops, SparseCore 0:
  9.7 172.3 all-gather.20
  184.2 127.9 all-gather.26
  314.3 35.9 all-gather.22
  352.3 36.0 all-gather.24
  399.3 77.0 all-gather.28
  545.4 76.9 all-gather.30
  686.2 76.8 all-gather.36
  766.0 76.1 all-gather.32
  845.1 75.9 all-gather.34
  996.2 74.8 all-gather.38
  3204.8 58.9 reduce-scatter.12
  3268.5 63.1 reduce-scatter.10
  3336.6 331.6 reduce-scatter.16
  3672.9 635.8 reduce-scatter.8
  4313.4 60.6 reduce-scatter.18
  4377.5 54.2 reduce-scatter.14
  4434.4 159.6 all-reduce.20
where the time goes:
time: 4650 us; the launch traced here: 4610 us
  other arithmetic  2020 us (43%)
  waiting for transfers between devices  1270 us (27%)
  local copies, waits for them, and re-layouts  674 us (14%)
  matrix products  401 us (9%)
  blocking collectives  184 us (4%)
    reduce_scatter x1, waiting for transfers between devices, on_device(): lax.psum_scatter(accumulated[1], 'shard', scatter_dimension=0, tiled=True)  641 us
    reduce_sum x112, other arithmetic, retreat(): d_step = jnp.sum(through * a_mat, axis=0) + x_t * b_weighted  521 us
    while x240, other arithmetic  398 us
    reduce_scatter x1, waiting for transfers between devices, on_device(): lax.psum_scatter(accumulated[9], 'shard', scatter_dimension=0, tiled=True)  277 us
    add x16, other arithmetic, retreat(): a_grad + through * step_t[None, :]  226 us
    mul x16, other arithmetic, flow_only(): return (decay_now * (c_t[:, None] * dy_t[None, :] + flow_in), None)  189 us
    add x16, other arithmetic, advance(): return decay_now * running + b_t[:, None] * (step_t * x_t)[None, :]  181 us
    select_n x128, other arithmetic, lap(): return jax.tree.map(lambda a, b: jnp.where(reached, a, b), new, before)  161 us
  transfers between devices with their start and end apart: 23, of which 9 were waited for; matrix products, arithmetic and copies ran while one was open for 22% of the time, Pallas kernels for 0%

commit v1 on v0

v1 whole, which is shorter than its diff:
```python
import functools
import jax, jax.numpy as jnp
from jax import lax
from jax.sharding import PartitionSpec as P
from jax.experimental import pallas as pl
from jax.experimental.pallas import tpu as pltpu

TB = 128
UN = 32
FG = 128

def wide(v, e):
    return jnp.concatenate([v] * (e // 128), axis=1) if e > 128 else v

def split3(v):
    def parts(v):
        hi = lax.reduce_precision(v, 8, 7)
        mid = lax.reduce_precision(v - hi, 8, 7)
        lo = lax.reduce_precision(v - hi - mid, 8, 7)
        return [hi, mid, lo]
    n = v.shape[1] // 2
    return jnp.concatenate(parts(v[:, :n]) + parts(v[:, n:]) + [jnp.zeros((v.shape[0], 128 - 6 * n), jnp.float32)], axis=1)

def fill(bcs_ref, bc_scr, n):
    lane = lax.broadcasted_iota(jnp.int32, (n, 128), 1)
    sub = lax.broadcasted_iota(jnp.int32, (n, 128), 0)
    mask = (lane % n) == sub
    r = lax.broadcasted_iota(jnp.int32, (128, 256), 0)
    c = lax.broadcasted_iota(jnp.int32, (128, 256), 1)
    ones = jnp.where((r >= 3 * n) == (c >= 128), 1.0, 0.0).astype(jnp.bfloat16)
    def body(g, _):
        rows = [jnp.where(mask, bcs_ref[pl.ds(g * FG + j, 1), :], 0.0).astype(jnp.bfloat16) for j in range(FG)]
        bc_scr[pl.ds(pl.multiple_of(g * (FG * n), FG * n), FG * n), :] = jnp.dot(jnp.concatenate(rows, axis=0), ones, preferred_element_type=jnp.float32)
        return 0
    lax.fori_loop(0, TB // FG, body, 0)

def fold_rows(vals, sub):
    for k in (1, 2, 4):
        m = (sub & k) == 0
        vals = [jnp.where(m, a, b) + pltpu.roll(jnp.where(m, b, a), 8 - k, 0) for a, b in zip(vals[::2], vals[1::2])]
    return vals[0]

def pass1(sd_ref, dx_ref, dy_ref, bcs_ref, a2_ref, cks_ref, ckp_ref, f_ref, s_scr, p_scr, f_scr, bc_scr, *, n):
    b = pl.program_id(0)
    e = a2_ref.shape[1]
    @pl.when(b == 0)
    def _():
        s_scr[...] = jnp.zeros_like(s_scr)
        p_scr[...] = jnp.ones_like(p_scr)
        f_scr[...] = jnp.zeros_like(f_scr)
    cks_ref[0] = s_scr[...]
    ckp_ref[0] = p_scr[...]
    fill(bcs_ref, bc_scr, n)
    a2 = a2_ref[...]
    def group(g, carry):
        s, p, f = carry
        for j in range(UN):
            t = g * UN + j
            bc = bc_scr[pl.ds(pl.multiple_of(t * n, n), n), :]
            bb, cc = wide(bc[:, :128], e), wide(bc[:, 128:], e)
            a = jnp.exp2(sd_ref[pl.ds(t, 1), :] * a2)
            s = a * s + bb * dx_ref[pl.ds(t, 1), :]
            p = p * a
            f = f + p * (cc * dy_ref[pl.ds(t, 1), :])
        return s, p, f
    s, p, f = lax.fori_loop(0, TB // UN, group, (s_scr[...], p_scr[...], f_scr[...]))
    s_scr[...] = s
    p_scr[...] = p
    f_scr[...] = f
    @pl.when(b == pl.num_programs(0) - 1)
    def _():
        f_ref[0] = s
        f_ref[1] = p
        f_ref[2] = f

def run_pass1(sd, dx, dy, bcs, a2):
    t, e = sd.shape
    n = a2.shape[0]
    nb = t // TB
    row = pl.BlockSpec((TB, e), lambda i: (i, 0))
    return pl.pallas_call(
        functools.partial(pass1, n=n),
        grid=(nb,),
        in_specs=[row, row, row, pl.BlockSpec((TB, 128), lambda i: (i, 0)), pl.BlockSpec((n, e), lambda i: (0, 0))],
        out_specs=[pl.BlockSpec((1, n, e), lambda i: (i, 0, 0)), pl.BlockSpec((1, n, e), lambda i: (i, 0, 0)), pl.BlockSpec((3, n, e), lambda i: (0, 0, 0))],
        out_shape=[jax.ShapeDtypeStruct((nb, n, e), jnp.float32)] * 2 + [jax.ShapeDtypeStruct((3, n, e), jnp.float32)],
        scratch_shapes=[pltpu.VMEM((n, e), jnp.float32)] * 3 + [pltpu.VMEM((TB * n, 256), jnp.float32)],
        compiler_params=pltpu.CompilerParams(vmem_limit_bytes=48 << 20),
    )(sd, dx, dy, bcs, a2)

def pass2(sd_ref, dx_ref, dy_ref, st_ref, bcs_ref, a2_ref, cks_ref, ckp_ref, hin_ref, qin_ref,
          y_ref, da_ref, gb_ref, dbc_ref, ga_ref,
          h_scr, a_scr, q_scr, bc_scr, *, n):
    b = pl.program_id(0)
    e = a2_ref.shape[1]
    @pl.when(b == 0)
    def _():
        q_scr[...] = qin_ref[...]
        ga_ref[...] = jnp.zeros_like(ga_ref)
    fill(bcs_ref, bc_scr, n)
    a2 = a2_ref[...]
    sub = lax.broadcasted_iota(jnp.int32, (8, e), 0)
    h0 = cks_ref[0] + ckp_ref[0] * hin_ref[...]
    h_scr[pl.ds(0, n), :] = h0
    def fwd(g, h):
        ys = []
        for j in range(UN):
            t = g * UN + j
            bc = bc_scr[pl.ds(pl.multiple_of(t * n, n), n), :]
            bb, cc = wide(bc[:, :128], e), wide(bc[:, 128:], e)
            a = jnp.exp2(sd_ref[pl.ds(t, 1), :] * a2)
            h = a * h + bb * dx_ref[pl.ds(t, 1), :]
            a_scr[pl.ds(pl.multiple_of(t * n, n), n), :] = a
            h_scr[pl.ds(pl.multiple_of(t * n + n, n), n), :] = h
            cy = cc * h
            ys.append(cy[:8] + cy[8:])
            if len(ys) == 8:
                y_ref[pl.ds(pl.multiple_of(t - 7, 8), 8), :] = fold_rows(ys, sub)
                ys = []
        return h
    lax.fori_loop(0, TB // UN, fwd, h0)
    lanes = lax.broadcasted_iota(jnp.int32, (n, TB), 1)
    def bwd(g, carry):
        q, ga, hn, db, dc = carry
        das, gbs = [], []
        for j in range(UN):
            t = TB - 1 - (g * UN + j)
            bc = bc_scr[pl.ds(pl.multiple_of(t * n, n), n), :]
            bb, cc = wide(bc[:, :128], e), wide(bc[:, 128:], e)
            a = a_scr[pl.ds(pl.multiple_of(t * n, n), n), :]
            hp = h_scr[pl.ds(pl.multiple_of(t * n, n), n), :]
            dyr = dy_ref[pl.ds(t, 1), :]
            gt = cc * dyr + q
            q = a * gt
            da = q * hp
            ga = ga + da * st_ref[pl.ds(t, 1), :]
            dA = da * a2
            gB = gt * bb
            das.append(dA[:8] + dA[8:])
            gbs.append(gB[:8] + gB[8:])
            pb = gt * dx_ref[pl.ds(t, 1), :]
            pc = dyr * hn
            pb = sum(pb[:, k:k + 128] for k in range(0, e, 128))
            pc = sum(pc[:, k:k + 128] for k in range(0, e, 128))
            db = jnp.where(lanes == t, jnp.sum(pb, axis=1, keepdims=True), db)
            dc = jnp.where(lanes == t, jnp.sum(pc, axis=1, keepdims=True), dc)
            hn = hp
            if len(das) == 8:
                da_ref[pl.ds(pl.multiple_of(t, 8), 8), :] = fold_rows(das[::-1], sub)
                gb_ref[pl.ds(pl.multiple_of(t, 8), 8), :] = fold_rows(gbs[::-1], sub)
                das, gbs = [], []
        return q, ga, hn, db, dc
    z = jnp.zeros((n, TB), jnp.float32)
    q, ga, _, db, dc = lax.fori_loop(0, TB // UN, bwd, (q_scr[...], ga_ref[...], h_scr[pl.ds(TB * n, n), :], z, z))
    q_scr[...] = q
    ga_ref[...] = ga
    dbc_ref[pl.ds(0, n), :] = db
    dbc_ref[pl.ds(n, n), :] = dc

def run_pass2(sd, dx, dy, st, bcs, a2, cks, ckp, hin, qin):
    t, e = sd.shape
    n = a2.shape[0]
    nb = t // TB
    row = pl.BlockSpec((TB, e), lambda i: (nb - 1 - i, 0))
    full = pl.BlockSpec((n, e), lambda i: (0, 0))
    ck = pl.BlockSpec((1, n, e), lambda i: (nb - 1 - i, 0, 0))
    dbcs = pl.BlockSpec((2 * n, TB), lambda i: (0, nb - 1 - i))
    bci = pl.BlockSpec((TB, 128), lambda i: (nb - 1 - i, 0))
    return pl.pallas_call(
        functools.partial(pass2, n=n),
        grid=(nb,),
        in_specs=[row] * 4 + [bci, full, ck, ck, full, full],
        out_specs=[row] * 3 + [dbcs, full],
        out_shape=[jax.ShapeDtypeStruct((t, e), jnp.float32)] * 3 + [jax.ShapeDtypeStruct((2 * n, t), jnp.float32), jax.ShapeDtypeStruct((n, e), jnp.float32)],
        scratch_shapes=[pltpu.VMEM((TB * n + n, e), jnp.float32), pltpu.VMEM((TB * n, e), jnp.float32),
                        pltpu.VMEM((n, e), jnp.float32), pltpu.VMEM((TB * n, 256), jnp.float32)],
        compiler_params=pltpu.CompilerParams(vmem_limit_bytes=48 << 20),
    )(sd, dx, dy, st, bcs, a2, cks, ckp, hin, qin)


def shift_rep(value, steps):
    count = lax.axis_size("rep")
    first, last = max(0, -steps), min(count, count - steps)
    return lax.ppermute(value, "rep", [(i, i + steps) for i in range(first, last)])

def sum_rep(value):
    if lax.axis_size("rep") != 2:
        return lax.psum(value, "rep")
    low = value.astype(jnp.bfloat16)
    other = lax.ppermute(low, "rep", [(0, 1), (1, 0)])
    return low.astype(jnp.float32) + other.astype(jnp.float32)

def nt(a, b):
    return lax.dot_general(a, b, (((1,), (1,)), ((), ())), preferred_element_type=jnp.float32)

def tn(a, b):
    return lax.dot_general(a, b, (((0,), (0,)), ((), ())), preferred_element_type=jnp.float32)

def mm(a, b):
    return jnp.dot(a, b, preferred_element_type=jnp.float32)

def dsilu(v):
    s = jax.nn.sigmoid(v)
    return s * (1.0 + v * (1.0 - s))

def on_device(hidden_in, segment_ids, out_grad, norm_gain, in_proj, conv_weight, conv_bias, x_proj,
              dt_weight, dt_bias, a_log, d_skip, out_proj):
    f32, bf16 = jnp.float32, jnp.bfloat16
    peers, reps = lax.axis_size("shard"), lax.axis_size("rep")
    rep = lax.axis_index("rep")
    m, tl, d = hidden_in.shape
    t = tl * peers
    dl = in_proj.shape[0]
    e = x_proj.shape[0]
    n = a_log.shape[0]
    rank = dt_weight.shape[0]
    taps = conv_weight.shape[0]
    back = taps - 1
    wide32 = lambda v: v.astype(f32)

    u = wide32(hidden_in)
    r = lax.rsqrt(jnp.mean(u * u, axis=2, keepdims=True) + 1e-5)
    nu = (u * r).astype(bf16)
    nu_all = lax.all_gather(nu, "shard", axis=1, tiled=True).reshape(m * t, d)
    dy_all = lax.all_gather(out_grad, "shard", axis=1, tiled=True).reshape(m * t, d)
    ids = lax.all_gather(segment_ids, "shard", axis=1, tiled=True)
    gain = wide32(norm_gain)[:, None]
    w_own = (wide32(in_proj) * gain).astype(bf16)
    w_split = w_own.reshape(dl, 2, peers, e).transpose(2, 0, 1, 3).reshape(peers * dl, 2 * e)
    w_cols = lax.all_to_all(w_split, "shard", 0, 0, tiled=True)

    ids_before = jnp.where(rep > 0, shift_rep(ids[:, t - back:], 1), -1)
    ext_ids = jnp.concatenate([ids_before, ids], axis=1)
    same = [None] + [wide32(ext_ids[:, back - k:back - k + t] == ids)[:, :, None] for k in range(1, taps)]

    xz = mm(nu_all, w_cols).astype(bf16).reshape(m, t, 2 * e)
    x_low = xz[:, :, :e]
    z = wide32(xz[:, :, e:])
    ext_x = jnp.concatenate([shift_rep(x_low[:, t - back:], 1), x_low], axis=1)
    x = wide32(x_low)
    cw = wide32(conv_weight)
    lagged = [x] + [wide32(ext_x[:, back - k:back - k + t]) * same[k] for k in range(1, taps)]
    conv = wide32(conv_bias) + sum(cw[back - k] * lagged[k] for k in range(taps))
    xc_low = jax.nn.silu(conv).astype(bf16)
    xc = wide32(xc_low)
    dbc = lax.psum(mm(xc_low.reshape(m * t, e), x_proj), "shard")
    dt_low = dbc[:, :rank].astype(bf16)
    bcs = split3(dbc[:, rank:]).reshape(m, t, 128)
    pre = (mm(dt_low, dt_weight) + wide32(dt_bias)).reshape(m, t, e)
    step = jax.nn.softplus(pre)
    a_mat = -jnp.exp(wide32(a_log))
    a2 = a_mat * 1.4426950408889634
    sd = jnp.where(same[1] > 0, step, 1e30)
    dx_in = step * xc

    d_gated = nt(dy_all, out_proj).reshape(m, t, e)
    sz = jax.nn.sigmoid(z)
    z_gate = z * sz
    dy_y = d_gated * z_gate

    firsts = [run_pass1(sd[i], dx_in[i], dy_y[i], bcs[i], a2) for i in range(m)]
    ends = lax.all_gather(jnp.stack([f[2] for f in firsts]), "rep")
    h_in = jnp.zeros((m, n, e), f32)
    q_in = jnp.zeros((m, n, e), f32)
    for k in range(reps - 1):
        h_in = jnp.where(k < rep, ends[k, :, 1] * h_in + ends[k, :, 0], h_in)
        o = reps - 1 - k
        q_in = jnp.where(o > rep, ends[o, :, 1] * q_in + ends[o, :, 2], q_in)
    seconds = [run_pass2(sd[i], dx_in[i], dy_y[i], step[i], bcs[i], a2, firsts[i][0], firsts[i][1], h_in[i], q_in[i])
               for i in range(m)]
    y_scan, d_a, gb = (jnp.stack([s[k] for s in seconds]) for k in range(3))
    d_bc = jnp.concatenate([s[3] for s in seconds], axis=1).T
    ga = sum(s[4] for s in seconds)

    skip = wide32(d_skip)
    y = y_scan + skip * xc
    gated = (y * z_gate).astype(bf16).reshape(m * t, e)
    part_out = mm(gated, out_proj).astype(bf16).reshape(m, t, d)
    out_sum = lax.psum_scatter(part_out, "shard", scatter_dimension=1, tiled=True)
    layer_out = (u + wide32(out_sum)).astype(bf16)
    grad_out_proj = tn(gated, dy_all)

    d_z = d_gated * y * (sz * (1.0 + z * (1.0 - sz)))
    d_step = d_a * 0.6931471805599453 + xc * gb
    d_pre = d_step * jax.nn.sigmoid(pre)
    d_pre_low = d_pre.astype(bf16).reshape(m * t, e)
    grad_dt_weight = tn(dt_low, d_pre_low)
    d_dbc = lax.psum(jnp.concatenate([nt(d_pre_low, dt_weight), d_bc], axis=1), "shard").astype(bf16)
    grad_x_proj = tn(xc_low.reshape(m * t, e), d_dbc)
    d_xc = dy_y * skip + step * gb + nt(d_dbc, x_proj).reshape(m, t, e)
    d_conv = d_xc * dsilu(conv)
    grad_conv = jnp.stack([jnp.sum(d_conv * lagged[back - j], axis=(0, 1)) for j in range(taps)])
    d_ext = jnp.pad(cw[back] * d_conv, ((0, 0), (back, 0), (0, 0)))
    for k in range(1, taps):
        d_ext = d_ext + jnp.pad(cw[back - k] * d_conv * same[k], ((0, 0), (back - k, k), (0, 0)))
    tail = shift_rep(d_ext[:, :back].astype(bf16), -1).astype(f32)
    d_x = d_ext[:, back:] + jnp.pad(tail, ((0, 0), (t - back, 0), (0, 0)))
    d_xz = jnp.concatenate([d_x, d_z], axis=2).astype(bf16).reshape(m * t, 2 * e)

    v_part = nt(d_xz, w_cols).astype(bf16).reshape(m, t, d)
    v = wide32(lax.psum_scatter(v_part, "shard", scatter_dimension=1, tiled=True))
    in_grad = wide32(out_grad) + r * v - u * (r * r * r) * jnp.mean(v * u, axis=2, keepdims=True)

    g_cols = sum_rep(tn(nu_all, d_xz)).astype(bf16)
    g_own = wide32(lax.all_to_all(g_cols, "shard", 0, 0, tiled=True))
    g_own = g_own.reshape(peers, dl, 2, e).transpose(1, 2, 0, 3).reshape(dl, 2 * e * peers)
    grad_in_proj = g_own * gain
    grad_gain = jnp.sum(g_own * wide32(in_proj), axis=1)

    grad_out_proj = sum_rep(grad_out_proj)
    small = jnp.concatenate([
        grad_conv, jnp.sum(d_conv, axis=(0, 1))[None], jnp.sum(d_pre, axis=(0, 1))[None],
        jnp.sum(dy_y * xc, axis=(0, 1))[None], ga * a_mat, grad_dt_weight, grad_x_proj.T], axis=0)
    small = sum_rep(small)
    cut, at = [], 0
    for size in (taps, 1, 1, 1, n, rank):
        cut.append(small[at:at + size])
        at += size
    return (layer_out, in_grad, grad_gain, grad_in_proj, cut[0], cut[1][0], small[at:].T, cut[5], cut[2][0],
            cut[4], cut[3][0], grad_out_proj)

def solution(mesh):
    tok, ids = P(None, ("rep", "shard"), None), P(None, ("rep", "shard"))
    row, col, one = P("shard", None), P(None, "shard"), P("shard")
    return jax.shard_map(
        on_device,
        mesh=mesh,
        in_specs=(tok, ids, tok, one, row, col, one, row, col, one, col, one, row),
        out_specs=(tok, tok, one, row, col, one, row, col, one, col, one, row),
        check_vma=False,
    )
```

time: 4650 us -> 1120 us (0.24)
  other arithmetic: 2020 us -> 67.5 us
  waiting for transfers between devices: 1270 us -> 415 us
  local copies, waits for them, and re-layouts: 674 us -> 175 us
  matrix products: 401 us -> 91.3 us
  Pallas kernels: 0 us -> 131 us
    reduce_scatter x5 -> x0, waiting for transfers between devices: 920 us -> none  [the longest x1 641 us: on_device(): lax.psum_scatter(accumulated[1], 'shard', scatter_dimension=0, tiled=True)]
    reduce_sum x147 -> x4, other arithmetic: 596 us -> 21 us  [the longest x1 10.9 us: on_device(): jnp.sum(d_pre, axis=(0, 1))[None]]
    add x56 -> x3, other arithmetic: 412 us -> 9.27 us  [the longest x1 6.01 us: on_device(): d_ext + jnp.pad(cw[back - k] * d_conv * same[k], ((0, 0), (back - k, k),...]
    while x240 -> x0, other arithmetic: 398 us -> none
    slice x172 -> x10, local copies, waits for them, and re-layouts: 342 us -> 5.82 us  [the longest x4 2.44 us: on_device(): cut.append(small[at:at + size])]
    mul x1060 -> x4, other arithmetic: 339 us -> 11.7 us  [the longest x1 5.85 us: on_device(): grad_in_proj = g_own * gain]
    dot_general x28 -> x12, matrix products: 401 us -> 91.3 us  [the longest x4 38.6 us: nt(): lax.dot_general(a, b, (((1,), (1,)), ((), ())), preferred_element_type=jn...]
    select_n x128 -> x3, other arithmetic: 161 us -> 4.5 us  [the longest x1 4.49 us: on_device(): step = jax.nn.softplus(pre)]
  transfers between devices with their start and end apart: 23 -> 13, of which waited for: 9 -> 9; matrix products, arithmetic and copies ran while one was open for 22% -> 18% of each run, Pallas kernels for 0% -> 0%
where the time goes in v1:
time: 1120 us; the launch traced here: 1110 us
  waiting for transfers between devices  415 us (37%)
  local copies, waits for them, and re-layouts  175 us (16%)
  blocking collectives  171 us (15%)
  Pallas kernels  131 us (12%)
  matrix products  91.3 us (8%)
  other arithmetic  67.5 us (6%)
  starting transfers between devices  44 us (4%)
  between operations  14.9 us (1%)
    unnamed x138, local copies, waits for them, and re-layouts  106 us
    pallas_call x2, Pallas kernels, run_pass2(): pl.pallas_call(functools.partial(pass2, n=n), grid=(nb,), in_specs=[row]...  93.3 us
    psum x1, blocking collectives, on_device(): lax.psum(jnp.concatenate([nt(d_pre_low, dt_weight), d_bc], axis=1), 'shard')  91.9 us
    psum x1, waiting for transfers between devices, on_device(): dbc = lax.psum(mm(xc_low.reshape(m * t, e), x_proj), 'shard')  91.9 us
    all_gather x1, waiting for transfers between devices, on_device(): lax.all_gather(out_grad, 'shard', axis=1, tiled=True).reshape(m * t, d)  87.8 us
    all_gather x1, waiting for transfers between devices, on_device(): nu_all = lax.all_gather(nu, 'shard', axis=1, tiled=True).reshape(m * t, d)  74.2 us
    all_gather x1, blocking collectives, on_device(): ids = lax.all_gather(segment_ids, 'shard', axis=1, tiled=True)  73.7 us
    ppermute x3, waiting for transfers between devices, sum_rep(): other = lax.ppermute(low, 'rep', [(0, 1), (1, 0)])  70.4 us
  transfers between devices with their start and end apart: 13, of which 9 were waited for; matrix products, arithmetic and copies ran while one was open for 18% of the time, Pallas kernels for 0%

profile of v1, /device:TPU:0, one launch (start us, length us, event | category | flops | bytes accessed | tf_op | source)
XLA Modules:
  0.0 1108.7 jit_solution(16740771783795890391)
XLA Ops:
  12.4 4.1 copy.74
  20.0 7.4 all-to-all-start
  27.5 73.7 %all_gather.15 = s32[2,2048]{1,0:T(2,128)S(1)} all-gather(s32[2,128]{1,0:T(2,128)S(1)} %copy-done.55), channel_id=1, replica_groups=mesh['rep'=2,'shard'=16] {'shard'}, dimensions={1}, use_global_device_ids=true | all-gather | bytes 17408 | tf_op jit(solution)/shard_map/all_gather | solution.py:226
  101.2 3.6 collective-permute-start
  108.7 74.2 %all-gather.4.cloned.1.call-done = bf16[2,2048,2048]{1,2,0:T(8,128)(2,1)} async-done(((bf16[2,128,2048]{1,2,0:T(8,128)(2,1)}), bf16[2,2048,2048]{1,2,0:T(8,128)(2,1)}) %all-gather.4.cloned.1.call-update) | async-done | bytes 16777232 | tf_op jit(solution)/shard_map/all_gather | solution.py:224
  182.9 22.7 %copy.73 = bf16[2,2048,2048]{2,1,0:T(8,128)(2,1)} copy(bf16[2,2048,2048]{1,2,0:T(8,128)(2,1)} %all-gather.4.cloned.1.call-done) | data formatting | bytes 33554432 | tf_op jit(solution)/shard_map/all_gather | solution.py:224
  205.6 12.5 %convolution_convert_fusion.2 = bf16[4096,512]{1,0:T(8,128)(2,1)S(1)} fusion(bf16[4096,2048]{1,0:T(8,128)(2,1)} %bitcast.127, bf16[2048,512]{1,0:T(8,128)(2,1)S(1)} %bitcast.143), kind=kOutput, calls=%fused_computation.10 | convolution fusion | flops 8592031744 | bytes 23068672 | tf_op jit(solution)/shard_map/dot_general | solution.py:200
  218.1 3.3 collective-permute-start.1
  223.0 87.8 %all-gather.6.cloned.1.call-done = bf16[2,2048,2048]{2,1,0:T(8,128)(2,1)} async-done(((bf16[2,128,2048]{2,1,0:T(8,128)(2,1)}), bf16[2,2048,2048]{2,1,0:T(8,128)(2,1)}) %all-gather.6.cloned.1.call-update) | async-done | bytes 16777232 | tf_op jit(solution)/shard_map/all_gather | solution.py:225
  310.9 19.6 %fusion.17 = (bf16[256]{0:T(256)(128)(2,1)}, f32[2,2048,256]{2,1,0:T(8,128)}, bf16[2,2048,256]{2,1,0:T(8,128)(2,1)S(1)}, f32[2,2048,256]{2,1,0:T(8,128)}, f32[2,2048,256]{2,1,0:T(8,128)}) fusion(bf16[2,2048,512]{2,1,0:T(8,128)(2,1)} %bitcast.130, f32[2,2048]{1,0:T(2,128)S(1)} %get-tuple-element.162, bf16[2,2048,256]{2,1,0:T(8,128)(2,1)} %slice.204, ...), kind=kOutput, calls=%fused_computation.34 | convolution fusion | flops 4334813184 | bytes 36758016 | tf_op jit(solution)/shard_map/dot_general | solution.py:194
  333.2 12.7 %reduce-scatter.7.cloned.1.call-start = ((), (), s32[]{:S(2)}) async-start(), calls=%async_computation.7 | async-start | bytes 17825792
  346.6 4.6 slice_bitcast_fusion.5
  351.1 91.9 %all-reduce.8.cloned.1.call-done = f32[4096,160]{1,0:T(8,128)} async-done(((f32[4096,160]{1,0:T(8,128)}), f32[4096,160]{1,0:T(8,128)}) %all-reduce.8.cloned.1.call-update) | async-done | bytes 2621456 | tf_op jit(solution)/shard_map/psum | solution.py:246
  443.0 7.5 subtract_reduce-precision_fusion
  451.9 9.7 concatenate.33
  465.1 4.5 compare_select_fusion
  469.9 6.3 slice_bitcast_fusion.4
  476.2 18.7 %shard_map.220 = (f32[16,16,256]{2,1,0:T(8,128)S(1)}, f32[16,16,256]{2,1,0:T(8,128)S(1)}, f32[3,16,256]{2,1,0:T(8,128)S(1)}) custom-call(f32[2048,256]{1,0:T(8,128)S(1)} %get-tuple-element.135.sd_ref, f32[2048,256]{1,0:T(8,128)S(1)} %get-tuple-element.171.dx_ref, f32[2048,256]{1,0:T(8,128)} %get-tuple-element.131.dy_ref, ...), custom_call_target="tpu_custom_call" | custom-call | tf_op jit(solution)/shard_map/pallas_call | solution.py:81
  494.9 18.7 %shard_map.221 = (f32[16,16,256]{2,1,0:T(8,128)S(1)}, f32[16,16,256]{2,1,0:T(8,128)S(1)}, f32[3,16,256]{2,1,0:T(8,128)S(1)}) custom-call(f32[2048,256]{1,0:T(8,128)S(1)} %get-tuple-element.136.sd_ref, f32[2048,256]{1,0:T(8,128)S(1)} %get-tuple-element.170.dx_ref, f32[2048,256]{1,0:T(8,128)} %get-tuple-element.132.dy_ref, ...), custom_call_target="tpu_custom_call" | custom-call | tf_op jit(solution)/shard_map/pallas_call | solution.py:81
  513.6 5.3 all-gather
  519.0 46.7 %shard_map.222 = (f32[2048,256]{1,0:T(8,128)S(1)}, f32[2048,256]{1,0:T(8,128)S(1)}, f32[2048,256]{1,0:T(8,128)}, f32[32,2048]{1,0:T(8,128)S(1)}, f32[16,256]{1,0:T(8,128)S(1)}) custom-call(f32[2048,256]{1,0:T(8,128)} %copy-done.3, f32[2048,256]{1,0:T(8,128)} %copy-done.5, f32[2048,256]{1,0:T(8,128)} %get-tuple-element.131.dy_ref, ...), custom_call_target="tpu_custom_call" | custom-call | tf_op jit(solution)/shard_map/pallas_call | solution.py:169
  565.7 46.6 %shard_map.223 = (f32[2048,256]{1,0:T(8,128)S(1)}, f32[2048,256]{1,0:T(8,128)S(1)}, f32[2048,256]{1,0:T(8,128)}, f32[32,2048]{1,0:T(8,128)S(1)}, f32[16,256]{1,0:T(8,128)S(1)}) custom-call(f32[2048,256]{1,0:T(8,128)} %copy-done.2, f32[2048,256]{1,0:T(8,128)} %copy-done.4, f32[2048,256]{1,0:T(8,128)} %get-tuple-element.132.dy_ref, ...), custom_call_target="tpu_custom_call" | custom-call | tf_op jit(solution)/shard_map/pallas_call | solution.py:169
  612.3 10.9 fusion.56
  623.2 9.7 convolution_convert_fusion.1
  632.9 27.9 %copy.88 = bf16[2,2048,2048]{2,0,1:T(2,128)(2,1)S(1)} copy(bf16[2,2048,2048]{2,1,0:T(8,128)(2,1)} %bitcast.116) | data formatting | bytes 33554432
  660.8 10.3 copy.94
  676.2 91.9 %all-reduce.9 = bf16[4096,160]{0,1:T(8,128)(2,1)} all-reduce(f32[4096,160]{0,1:T(8,128)} %pad_maximum_fusion.1), channel_id=1, replica_groups=mesh['rep'=2,'shard'=16] {'shard'}, use_global_device_ids=true, to_apply=%region_3.4 | all-reduce | flops 655360 | bytes 3932160 | tf_op jit(solution)/shard_map/psum | solution.py:288
  772.1 9.6 fusion.53
  781.7 5.2 broadcast_multiply_fusion
  787.0 6.0 pad_add_fusion
  795.0 3.8 collective-permute-done.2
  800.5 14.4 %convolution_convert_fusion = bf16[4096,2048]{1,0:T(8,128)(2,1)} fusion(bf16[2048,512]{1,0:T(8,128)(2,1)S(1)} %bitcast.144, bf16[4096,256]{1,0:T(8,128)(2,1)S(1)} %bitcast.142, bf16[4096,256]{1,0:T(8,128)(2,1)} %bitcast.145), kind=kOutput, calls=%fused_computation | convolution fusion | flops 8606711808 | bytes 23068672 | tf_op jit(solution)/shard_map/dot_general | solution.py:194
  814.9 27.9 %copy.90 = bf16[2,2048,2048]{2,0,1:T(2,128)(2,1)S(1)} copy(bf16[2,2048,2048]{2,1,0:T(8,128)(2,1)} %bitcast.126) | data formatting | bytes 33554432
  842.9 10.3 copy.95
  853.2 13.7 %bitcast_convert_fusion = bf16[2048,512]{1,0:T(8,128)(2,1)S(1)} fusion(bf16[2,2048,2048]{1,2,0:T(8,128)(2,1)} %all-gather.4.cloned.1.call-done, bf16[2,2048,256]{2,1,0:T(8,128)(2,1)} %get-tuple-element.147, bf16[2,2048,256]{2,1,0:T(8,128)(2,1)} %fusion.18), kind=kOutput, calls=%fused_computation.47 | convolution fusion | flops 8599371776 | bytes 23068672 | tf_op jit(solution)/shard_map/dot_general | solution.py:197
  867.0 46.5 %collective-permute-done.3 = bf16[2048,512]{1,0:T(8,128)(2,1)S(1)} collective-permute-done((bf16[2048,512]{1,0:T(8,128)(2,1)S(1)}, bf16[2048,512]{1,0:T(8,128)(2,1)S(1)}, u32[]{:S(2)}, u32[]{:S(2)}) %collective-permute-start.3) | collective-permute-done | bytes 2097184 | tf_op jit(solution)/shard_map/ppermute | solution.py:190
  915.5 13.7 %all-to-all-start.1 = ((bf16[16,128,512]{2,1,0:T(8,128)(2,1)}), bf16[16,128,512]{2,1,0:T(8,128)(2,1)}, u32[]{:S(2)}, u32[]{:S(2)}) async-start(bf16[16,128,512]{2,1,0:T(8,128)(2,1)} %bitcast.133), calls=%async_computation.1 | async-start | bytes 4194304 | tf_op jit(solution)/shard_map/all_to_all | solution.py:305
  929.3 12.4 %fusion.28 = bf16[256,2048]{1,0:T(8,128)(2,1)} fusion(bf16[2,2048,256]{2,1,0:T(8,128)(2,1)} %get-tuple-element.146, bf16[2,2048,2048]{2,1,0:T(8,128)(2,1)} %all-gather.6.cloned.1.call-done), kind=kOutput, calls=%fused_computation.72 | convolution fusion | flops 4295491584 | bytes 19922944 | tf_op jit(solution)/shard_map/dot_general | solution.py:197
  946.9 24.0 %collective-permute-done.4 = bf16[311,256]{1,0:T(8,128)(2,1)S(1)} collective-permute-done((bf16[311,256]{1,0:T(8,128)(2,1)S(1)}, bf16[311,256]{1,0:T(8,128)(2,1)S(1)}, u32[]{:S(2)}, u32[]{:S(2)}) %collective-permute-start.4) | collective-permute-done | bytes 159264 | tf_op jit(solution)/shard_map/ppermute | solution.py:190
  974.0 3.2 convert_add_fusion.1
  977.3 25.6 %all-to-all-done.1 = bf16[16,128,512]{2,1,0:T(8,128)(2,1)} async-done(((bf16[16,128,512]{2,1,0:T(8,128)(2,1)}), bf16[16,128,512]{2,1,0:T(8,128)(2,1)}, u32[]{:S(2)}, u32[]{:S(2)}) %all-to-all-start.1) | async-done | bytes 2097184 | tf_op jit(solution)/shard_map/all_to_all | solution.py:305
  1002.9 5.4 reshape.152
  1008.3 7.4 copy.81
  1015.7 5.8 bitcast_multiply_fusion
  1021.6 5.6 copy.85
  1031.3 59.2 %reduce-scatter.9.cloned.1.call-done = bf16[128,4096]{1,0:T(8,128)(2,1)} async-done(((bf16[2048,4096]{1,0:T(8,128)(2,1)}), bf16[128,4096]{1,0:T(8,128)(2,1)}) %reduce-scatter.9.cloned.1.call-update) | async-done | bytes 1048592
  1093.7 4.1 fusion.30
  1097.7 3.0 copy.84
  (201 shorter events, 54.5 us)
Async XLA Ops:
  7.2 303.7 %copy-start = (bf16[256,2048]{1,0:T(8,128)(2,1)S(1)}, bf16[256,2048]{1,0:T(8,128)(2,1)}, u32[]{:S(2)}) copy-start(bf16[256,2048]{1,0:T(8,128)(2,1)} %param.25) | copy-start | bytes 3145732
  7.2 175.7 %all-gather.4.cloned.1.call-start = ((), (), s32[]{:S(2)}) async-start(), calls=%async_computation.4 | async-start | bytes 17825792 | tf_op jit(solution)/shard_map/all_gather | solution.py:224
  11.7 299.2 %all-gather.6.cloned.1.call-start = ((), (), s32[]{:S(2)}) async-start(), calls=%async_computation.6 | async-start | bytes 17825792 | tf_op jit(solution)/shard_map/all_gather | solution.py:225
  18.5 86.3 %copy-start.58 = (bf16[256]{0:T(256)(128)(2,1)S(1)}, bf16[256]{0:T(256)(128)(2,1)}, u32[]{:S(2)}) copy-start(bf16[256]{0:T(256)(128)(2,1)} %param.19) | copy-start | bytes 1540
  18.5 86.3 %copy-start.39 = (bf16[4,256]{1,0:T(4,128)(2,1)S(1)}, bf16[4,256]{1,0:T(4,128)(2,1)}, u32[]{:S(2)}) copy-start(bf16[4,256]{1,0:T(4,128)(2,1)} %param.18) | copy-start | bytes 6148
  20.0 86.1 %all-to-all-start = ((bf16[16,128,512]{1,2,0:T(8,128)(2,1)}), bf16[16,128,512]{1,2,0:T(8,128)(2,1)S(1)}, u32[]{:S(2)}, u32[]{:S(2)}) async-start(bf16[16,128,512]{1,2,0:T(8,128)(2,1)} %bitcast.134), calls=%async_computation | async-start | bytes 4194304 | tf_op jit(solution)/shard_map/all_to_all | solution.py:230
  27.4 415.6 %all-reduce.8.cloned.1.call-start = ((), (), s32[]{:S(2)}) async-start(), calls=%async_computation.5 | async-start | bytes 8388608 | tf_op jit(solution)/shard_map/psum | solution.py:246
  101.2 4.9 collective-permute-start
  104.9 205.9 %copy-start.45 = (f32[1,256]{1,0:T(1,128)}, f32[1,256]{1,0:T(1,128)S(1)}, u32[]{:S(2)}) copy-start(f32[1,256]{1,0:T(1,128)S(1)} %get-tuple-element.163) | copy-start | bytes 3076
  104.9 205.9 %copy-start.47 = (f32[1,256]{1,0:T(1,128)}, f32[1,256]{1,0:T(1,128)S(1)}, u32[]{:S(2)}) copy-start(f32[1,256]{1,0:T(1,128)S(1)} %get-tuple-element.164) | copy-start | bytes 3076
  104.9 205.9 %copy-start.49 = (f32[1,256]{1,0:T(1,128)}, f32[1,256]{1,0:T(1,128)S(1)}, u32[]{:S(2)}) copy-start(f32[1,256]{1,0:T(1,128)S(1)} %get-tuple-element.165) | copy-start | bytes 3076
  104.9 205.9 %copy-start.51 = (f32[1,256]{1,0:T(1,128)}, f32[1,256]{1,0:T(1,128)S(1)}, u32[]{:S(2)}) copy-start(f32[1,256]{1,0:T(1,128)S(1)} %get-tuple-element.166) | copy-start | bytes 3076
  108.7 96.9 %copy-start.26 = (bf16[16,128,512]{2,1,0:T(8,128)(2,1)S(1)}, bf16[16,128,512]{2,1,0:T(8,128)(2,1)}, u32[]{:S(2)}) copy-start(bf16[16,128,512]{2,1,0:T(8,128)(2,1)} %copy.76) | copy-start | bytes 6291460
  218.1 92.7 %collective-permute-start.1 = (bf16[2,3,256]{2,1,0:T(4,128)(2,1)S(1)}, bf16[2,3,256]{2,1,0:T(4,128)(2,1)S(1)}, u32[]{:S(2)}, u32[]{:S(2)}) collective-permute-start(bf16[2,3,256]{2,1,0:T(4,128)(2,1)S(1)} %slice.206), channel_id=1, source_target_pairs={{0,16},{1,17},{2,18},{3,19},{4,20},{5,21},{6,22},{7,23},{8,24},{9,... | collective-permute-start | bytes 9224 | tf_op jit(solution)/shard_map/ppermute | solution.py:184
  221.5 108.9 %copy-start.31 = (f32[2,2048]{1,0:T(2,128)}, f32[2,2048]{1,0:T(2,128)S(1)}, u32[]{:S(2)}) copy-start(f32[2,2048]{1,0:T(2,128)S(1)} %get-tuple-element.161) | copy-start | bytes 49156
  221.5 108.9 %copy-start.33 = (f32[2,2048]{1,0:T(2,128)}, f32[2,2048]{1,0:T(2,128)S(1)}, u32[]{:S(2)}) copy-start(f32[2,2048]{1,0:T(2,128)S(1)} %get-tuple-element.162) | copy-start | bytes 49156
  310.8 19.6 %copy-start.42 = (bf16[2,3,256]{2,1,0:T(4,128)(2,1)}, bf16[2,3,256]{2,1,0:T(4,128)(2,1)S(1)}, u32[]{:S(2)}) copy-start(bf16[2,3,256]{2,1,0:T(4,128)(2,1)S(1)} %collective-permute-done.1) | copy-start | bytes 9220
  310.9 19.6 %copy-start.28 = (bf16[256,160]{0,1:T(8,128)(2,1)S(1)}, bf16[256,160]{0,1:T(8,128)(2,1)}, u32[]{:S(2)}) copy-start(bf16[256,160]{0,1:T(8,128)(2,1)} %param.20) | copy-start | bytes 245764
  333.2 12.8 %copy-start.59 = (bf16[256]{0:T(256)(128)(2,1)S(1)}, bf16[256]{0:T(256)(128)(2,1)}, u32[]{:S(2)}) copy-start(bf16[256]{0:T(256)(128)(2,1)} %param.22) | copy-start | bytes 1540
  333.2 12.8 %copy-start.60 = (bf16[256]{0:T(256)(128)(2,1)S(1)}, bf16[256]{0:T(256)(128)(2,1)}, u32[]{:S(2)}) copy-start(bf16[256]{0:T(256)(128)(2,1)} %param.24) | copy-start | bytes 1540
  333.2 13.4 %copy-start.35 = (bf16[16,256]{1,0:T(8,128)(2,1)S(1)}, bf16[16,256]{1,0:T(8,128)(2,1)}, u32[]{:S(2)}) copy-start(bf16[16,256]{1,0:T(8,128)(2,1)} %param.23) | copy-start | bytes 24580
  333.2 694.0 %reduce-scatter.7.cloned.1.call-start = ((), (), s32[]{:S(2)}) async-start(), calls=%async_computation.7 | async-start | bytes 17825792
  451.9 11.5 %copy-start.29 = (bf16[128,256]{1,0:T(8,128)(2,1)S(1)}, bf16[128,256]{1,0:T(8,128)(2,1)}, u32[]{:S(2)}) copy-start(bf16[128,256]{1,0:T(8,128)(2,1)} %param.21) | copy-start | bytes 196612
  464.4 11.8 %copy-start.8 = (f32[2048,128]{1,0:T(8,128)}, f32[2048,128]{1,0:T(8,128)S(1)}, u32[]{:S(2)}) copy-start(f32[2048,128]{1,0:T(8,128)S(1)} %get-tuple-element.148.bcs_ref) | copy-start | bytes 3145732
  464.4 30.5 %copy-start.6 = (f32[2048,128]{1,0:T(8,128)}, f32[2048,128]{1,0:T(8,128)S(1)}, u32[]{:S(2)}) copy-start(f32[2048,128]{1,0:T(8,128)S(1)} %get-tuple-element.149.bcs_ref) | copy-start | bytes 3145732
  469.9 25.0 %copy-start.2 = (f32[2048,256]{1,0:T(8,128)}, f32[2048,256]{1,0:T(8,128)S(1)}, u32[]{:S(2)}) copy-start(f32[2048,256]{1,0:T(8,128)S(1)} %get-tuple-element.136.sd_ref) | copy-start | bytes 6291460
  476.2 37.4 %copy-start.4 = (f32[2048,256]{1,0:T(8,128)}, f32[2048,256]{1,0:T(8,128)S(1)}, u32[]{:S(2)}) copy-start(f32[2048,256]{1,0:T(8,128)S(1)} %get-tuple-element.170.dx_ref) | copy-start | bytes 6291460
  476.2 37.5 %copy-start.5 = (f32[2048,256]{1,0:T(8,128)}, f32[2048,256]{1,0:T(8,128)S(1)}, u32[]{:S(2)}) copy-start(f32[2048,256]{1,0:T(8,128)S(1)} %get-tuple-element.171.dx_ref) | copy-start | bytes 6291460
  494.9 24.1 %copy-start.9 = (f32[2048,128]{1,0:T(8,128)S(1)}, f32[2048,128]{1,0:T(8,128)}, u32[]{:S(2)}) copy-start(f32[2048,128]{1,0:T(8,128)} %copy-done.8) | copy-start | bytes 3145732
  519.0 46.7 %copy-start.7 = (f32[2048,128]{1,0:T(8,128)S(1)}, f32[2048,128]{1,0:T(8,128)}, u32[]{:S(2)}) copy-start(f32[2048,128]{1,0:T(8,128)} %copy-done.6) | copy-start | bytes 3145732
  565.7 46.6 %copy-start.40 = (f32[256]{0:T(256)S(1)}, f32[256]{0:T(256)}, u32[]{:S(2)}) copy-start(f32[256]{0:T(256)} %convert_element_type.159) | copy-start | bytes 3076
  612.3 10.9 copy-start.10
  671.2 419.2 %reduce-scatter.9.cloned.1.call-start = ((), (), s32[]{:S(2)}) async-start(), calls=%async_computation.8 | async-start | bytes 17825792
  772.1 9.6 copy-start.46
  772.1 9.6 copy-start.48
  772.1 9.6 copy-start.50
  793.0 5.8 collective-permute-start.2
  866.9 62.3 %copy-start.61 = (bf16[256]{0:T(256)(128)(2,1)S(1)}, bf16[256]{0:T(256)(128)(2,1)}, u32[]{:S(2)}) copy-start(bf16[256]{0:T(256)(128)(2,1)} %get-tuple-element.112) | copy-start | bytes 1540
  866.9 62.4 %copy-start.56 = (bf16[256]{0:T(256)(128)(2,1)S(1)}, bf16[256]{0:T(256)(128)(2,1)}, u32[]{:S(2)}) copy-start(bf16[256]{0:T(256)(128)(2,1)} %get-tuple-element.116) | copy-start | bytes 1540
  866.9 46.5 %collective-permute-start.3 = (bf16[2048,512]{1,0:T(8,128)(2,1)S(1)}, bf16[2048,512]{1,0:T(8,128)(2,1)S(1)}, u32[]{:S(2)}, u32[]{:S(2)}) collective-permute-start(bf16[2048,512]{1,0:T(8,128)(2,1)S(1)} %bitcast_convert_fusion), channel_id=1, source_target_pairs={{0,16},{16,0},{1,17},{17,1},{2,18},{18,2},{3,19},{19,3},{4,20},{20... | collective-permute-start | bytes 6291464 | tf_op jit(solution)/shard_map/ppermute | solution.py:190
  915.5 87.4 %all-to-all-start.1 = ((bf16[16,128,512]{2,1,0:T(8,128)(2,1)}), bf16[16,128,512]{2,1,0:T(8,128)(2,1)}, u32[]{:S(2)}, u32[]{:S(2)}) async-start(bf16[16,128,512]{2,1,0:T(8,128)(2,1)} %bitcast.133), calls=%async_computation.1 | async-start | bytes 4194304 | tf_op jit(solution)/shard_map/all_to_all | solution.py:305
  929.3 12.4 %copy-start.18 = (bf16[4096,160]{0,1:T(8,128)(2,1)S(1)}, bf16[4096,160]{0,1:T(8,128)(2,1)}, u32[]{:S(2)}) copy-start(bf16[4096,160]{0,1:T(8,128)(2,1)} %all-reduce.9) | copy-start | bytes 3932164
  929.3 12.9 %copy-start.20 = (f32[4096,160]{1,0:T(8,128)S(1)}, f32[4096,160]{1,0:T(8,128)}, u32[]{:S(2)}) copy-start(f32[4096,160]{1,0:T(8,128)} %all-reduce.8.cloned.1.call-done) | copy-start | bytes 7864324
  941.7 32.4 %collective-permute-start.5 = (bf16[256,2048]{1,0:T(8,128)(2,1)}, bf16[256,2048]{1,0:T(8,128)(2,1)}, u32[]{:S(2)}, u32[]{:S(2)}) collective-permute-start(bf16[256,2048]{1,0:T(8,128)(2,1)} %fusion.28), channel_id=1, source_target_pairs={{0,16},{16,0},{1,17},{17,1},{2,18},{18,2},{3,19},{19,3},{4,20},{20... | collective-permute-start | bytes 3145736 | tf_op jit(solution)/shard_map/ppermute | solution.py:190
  944.5 26.4 %collective-permute-start.4 = (bf16[311,256]{1,0:T(8,128)(2,1)S(1)}, bf16[311,256]{1,0:T(8,128)(2,1)S(1)}, u32[]{:S(2)}, u32[]{:S(2)}) collective-permute-start(bf16[311,256]{1,0:T(8,128)(2,1)S(1)} %concatenate.40), channel_id=1, source_target_pairs={{0,16},{16,0},{1,17},{17,1},{2,18},{18,2},{3,19},{19,3},{4,20},{20... | collective-permute-start | bytes 477704 | tf_op jit(solution)/shard_map/ppermute | solution.py:190
  1027.2 66.1 %copy-start.16 = (bf16[2,128,2048]{1,2,0:T(8,128)(2,1)S(1)}, bf16[2,128,2048]{1,2,0:T(8,128)(2,1)}, u32[]{:S(2)}) copy-start(bf16[2,128,2048]{1,2,0:T(8,128)(2,1)} %copy-done.15) | copy-start | bytes 3145732
  1029.1 64.5 %copy-start.38 = (f32[2,128]{1,0:T(2,128)S(1)}, f32[2,128]{1,0:T(2,128)}, u32[]{:S(2)}) copy-start(f32[2,128]{1,0:T(2,128)} %copy-done.37) | copy-start | bytes 3076
  1029.2 64.5 %copy-start.44 = (f32[2,128]{1,0:T(2,128)S(1)}, f32[2,128]{1,0:T(2,128)}, u32[]{:S(2)}) copy-start(f32[2,128]{1,0:T(2,128)} %get-tuple-element.167) | copy-start | bytes 3076
  (27 other events, 128.3 us)
Sparse Core Ops, SparseCore 0:
  11.8 171.0 all-gather.3
  185.1 125.6 all-gather.5
  333.3 109.6 all-reduce.7
  671.3 192.7 reduce-scatter.6
  868.6 221.7 reduce-scatter.8

commit v2 on v1

v2 whole, which is shorter than its diff:
```python
import functools
import jax
import jax.numpy as jnp
from jax import lax
from jax.sharding import PartitionSpec as P
from jax.experimental import pallas as pl
from jax.experimental.pallas import tpu as pltpu

F32, BF16 = jnp.float32, jnp.bfloat16
LOG2E, LN2 = 1.4426950408889634, 0.6931471805599453
EDGE = 8
VMEM = 56 << 20


def nt(a, b):
    return lax.dot_general(a, b, (((1,), (1,)), ((), ())), preferred_element_type=F32)


def tn(a, b):
    return lax.dot_general(a, b, (((0,), (0,)), ((), ())), preferred_element_type=F32)


def mm(a, b):
    return jnp.dot(a, b, preferred_element_type=F32)


def softplus(v):
    return jnp.maximum(v, 0.0) + jnp.log1p(jnp.exp(-jnp.abs(v)))


def wide(v, e):
    return jnp.concatenate([v] * (e // 128), axis=1) if e > 128 else v


def at(start, size, unit=8):
    return pl.ds(pl.multiple_of(start, unit), size)


def call(kernel, grid, in_specs, out_specs, out_shape, scratch, args, flops=0):
    size = sum(a.size * a.dtype.itemsize for a in args) + sum(s.size * s.dtype.itemsize for s in out_shape)
    return pl.pallas_call(
        kernel, grid=grid, in_specs=in_specs, out_specs=out_specs, out_shape=out_shape,
        scratch_shapes=scratch, compiler_params=pltpu.CompilerParams(vmem_limit_bytes=VMEM),
        cost_estimate=pl.CostEstimate(flops=flops, bytes_accessed=size, transcendentals=0))(*args)


def whole(a):
    return pl.BlockSpec(a.shape, lambda i, r=len(a.shape): (0,) * r)


def block(a, order):
    return pl.BlockSpec((1,) + a.shape[1:], lambda i, r=len(a.shape): (order(i),) + (0,) * (r - 1))


def lags(x_ext, rows):
    return [x_ext[EDGE - k:EDGE - k + rows] for k in range(4)]


def convolve(lag, same, cw, cb):
    out = cb + cw[3:4] * lag[0]
    for k in range(1, 4):
        out = out + cw[3 - k:4 - k] * lag[k] * same[:, k - 1:k]
    return out


def front(nu_ref, w_ref, halo_ref, mask_ref, cw_ref, cb_ref, xp_ref, xz_ref, xc_ref, part_ref, edge_ref, carry, *, m, e):
    @pl.when(pl.program_id(0) == 0)
    def _():
        edge = mm(halo_ref[...], w_ref[:, :e]).astype(BF16)
        edge_ref[...] = edge
        carry[...] = edge.astype(F32)
    xz = mm(nu_ref[0], w_ref[...]).astype(BF16)
    xz_ref[0] = xz
    rows = xz.shape[0] // m
    cw, cb = cw_ref[...], cb_ref[...]
    for i in range(m):
        x = xz[i * rows:(i + 1) * rows, :e].astype(F32)
        ext = jnp.concatenate([carry[i * EDGE:(i + 1) * EDGE], x], axis=0)
        carry[i * EDGE:(i + 1) * EDGE] = x[rows - EDGE:]
        conv = convolve(lags(ext, rows), mask_ref[0, i * rows:(i + 1) * rows], cw, cb)
        xc_ref[0, i * rows:(i + 1) * rows] = (conv * jax.nn.sigmoid(conv)).astype(BF16)
    part_ref[0] = nt(xp_ref[...], xc_ref[0])


def lattice(peers):
    y = 2 if peers <= 16 else 4
    return peers // (2 * y), y, 2


def greet(targets):
    barrier = pltpu.get_barrier_semaphore()
    for target in targets:
        pl.semaphore_signal(barrier, inc=1, device_id={"shard": target}, device_id_type=pl.DeviceIdType.MESH)
    pl.semaphore_wait(barrier, len(targets))


def remote(src, dst, send, recv, target):
    return pltpu.make_async_remote_copy(src_ref=src, dst_ref=dst, send_sem=send, recv_sem=recv,
                                        device_id={"shard": target}, device_id_type=pl.DeviceIdType.MESH)


def spread_low(total, n):
    rows = jnp.concatenate([total, jnp.zeros((256 - total.shape[0], total.shape[1]), F32)], axis=0).T
    rank = total.shape[0] - 2 * n
    out = [rows[:, :rank].astype(BF16)]
    rest = rows[:, rank:]
    hi = rest.astype(BF16)
    mid = (rest - hi.astype(F32)).astype(BF16)
    lo = (rest - hi.astype(F32) - mid.astype(F32)).astype(BF16)
    for k in range(2):
        out += [p[:, k * n:(k + 1) * n] for p in (hi, mid, lo)]
    out.append(jnp.zeros((rows.shape[0], 128 - 6 * n), BF16))
    return jnp.concatenate(out, axis=1)


def spread_plain(total, n):
    return jnp.concatenate([total, jnp.zeros((256 - total.shape[0], total.shape[1]), F32)], axis=0).T.astype(BF16)


def allsum_kernel(part, out, rc, ac, ry, ay, rz, send, recv, *, dims, chunks, finish):
    nz, ny, _ = dims
    me = lax.axis_index("shard")
    c, y, z = me % 2, (me // 2) % ny, me // (2 * ny)
    where = lambda a, b, d: (a * ny + b) * 2 + d
    across = where(z, y, 1 - c)
    ys = [lax.rem(y + k, ny) for k in range(1, ny)]
    zs = [lax.rem(z + k, nz) for k in range(1, nz)]
    greet([across] + [where(z, b, c) for b in ys] + [where(a, y, c) for a in zs])
    width = part.shape[-1] // chunks
    lanes = [pl.ds(q * width, width) for q in range(chunks)]
    rows = [pl.ds(q * width, width) for q in range(chunks)]

    def start(copies):
        for copy in copies:
            copy.start()
        return copies

    def finish_all(copies):
        for copy in copies:
            copy.wait()
    base = [0]

    def sems(count):
        base[0] += count
        return [(send.at[base[0] - count + k], recv.at[base[0] - count + k]) for k in range(count)]

    first = []
    for q in range(chunks):
        (s, r), = sems(1)
        first.append(start([remote(part.at[:, :, 1 - c, :, lanes[q]], rc.at[q], s, r, across)]))
    second = []
    for q in range(chunks):
        finish_all(first[q])
        for a in range(nz):
            for b in range(ny):
                ac[q, a, b] = part[a, b, c, :, q * width:(q + 1) * width] + rc[q, a, b]
        second.append(start([remote(ac.at[q, :, b], ry.at[q, k], *sem, where(z, b, c))
                             for k, (b, sem) in enumerate(zip(ys, sems(ny - 1)))]))
    third = []
    for q in range(chunks):
        finish_all(second[q])
        for a in range(nz):
            got = ac[q, a, y]
            for k in range(ny - 1):
                got = got + ry[q, k, a]
            ay[q, a] = got
        third.append(start([remote(ay.at[q, a], rz.at[q, k], *sem, where(a, y, c))
                            for k, (a, sem) in enumerate(zip(zs, sems(nz - 1)))]))
    fourth = []
    for q in range(chunks):
        finish_all(third[q])
        got = ay[q, z]
        for k in range(nz - 1):
            got = got + rz[q, k]
        out[z, y, c, q * width:(q + 1) * width] = finish(got)
        mine = out.at[z, y, c, rows[q]]
        fourth.append(start([remote(mine, mine, *sem, where(a, y, c)) for a, sem in zip(zs, sems(nz - 1))]))
    fifth = []
    for q in range(chunks):
        finish_all(fourth[q])
        mine = out.at[:, y, c, rows[q]]
        fifth.append(start([remote(mine, mine, *sem, where(z, b, c)) for b, sem in zip(ys, sems(ny - 1))]))
    last = []
    for q in range(chunks):
        finish_all(fifth[q])
        mine = out.at[:, :, c, rows[q]]
        (s, r), = sems(1)
        last.append(start([remote(mine, mine, s, r, across)]))
    for q in range(chunks):
        finish_all(last[q])


def allsum(part, finish, collective_id):
    peers, cols, w = part.shape
    dims = lattice(peers)
    nz, ny, nc = dims
    chunks = w // 128
    copies = 2 * chunks * (1 + ny - 1 + nz - 1)
    out = pl.pallas_call(
        functools.partial(allsum_kernel, dims=dims, chunks=chunks, finish=finish),
        out_shape=jax.ShapeDtypeStruct((nz, ny, nc, w, 256), BF16),
        in_specs=[pl.BlockSpec(memory_space=pltpu.VMEM)],
        out_specs=pl.BlockSpec(memory_space=pltpu.VMEM),
        scratch_shapes=[pltpu.VMEM((chunks, nz, ny, cols, 128), F32), pltpu.VMEM((chunks, nz, ny, cols, 128), F32),
                        pltpu.VMEM((chunks, ny - 1, nz, cols, 128), F32), pltpu.VMEM((chunks, nz, cols, 128), F32),
                        pltpu.VMEM((chunks, nz - 1, cols, 128), F32),
                        pltpu.SemaphoreType.DMA((copies,)), pltpu.SemaphoreType.DMA((copies,))],
        compiler_params=pltpu.CompilerParams(collective_id=collective_id, has_side_effects=True, vmem_limit_bytes=VMEM),
    )(part.reshape(nz, ny, nc, cols, w))
    return out.reshape(peers, w, 256)


def fill(low_ref, bcs_scr, bc_scr, n):
    bcs_scr[...] = low_ref[0, :, 128:].astype(F32)
    lane = lax.broadcasted_iota(jnp.int32, (n, 128), 1)
    sub = lax.broadcasted_iota(jnp.int32, (n, 128), 0)
    mask = (lane % n) == sub
    r = lax.broadcasted_iota(jnp.int32, (128, 256), 0)
    c = lax.broadcasted_iota(jnp.int32, (128, 256), 1)
    ones = jnp.where((r >= 3 * n) == (c >= 128), 1.0, 0.0).astype(BF16)
    group = 128

    def body(g, _):
        rows = [jnp.where(mask, bcs_scr[pl.ds(g * group + j, 1), :], 0.0).astype(BF16) for j in range(group)]
        bc_scr[at(g * (group * n), group * n, 128), :] = mm(jnp.concatenate(rows, axis=0), ones)
        return 0
    lax.fori_loop(0, bcs_scr.shape[0] // group, body, 0)


def fold_rows(vals, sub):
    for k in (1, 2, 4):
        mask = (sub & k) == 0
        vals = [jnp.where(mask, a, b) + pltpu.roll(jnp.where(mask, b, a), 8 - k, 0)
                for a, b in zip(vals[::2], vals[1::2])]
    return vals[0]


def ahead(low_ref, xz_ref, xc_ref, mask_ref, dy_ref, wo_ref, wdt_ref, dtb_ref, a2_ref,
          cks_ref, ckp_ref, end_ref, dg_ref, s_scr, p_scr, f_scr, sd_scr, dx_scr, dy_scr, bcs_scr, bc_scr, *, m, n, e):
    b = pl.program_id(0)
    @pl.when(b == 0)
    def _():
        s_scr[...] = jnp.zeros_like(s_scr)
        p_scr[...] = jnp.ones_like(p_scr)
        f_scr[...] = jnp.zeros_like(f_scr)
    cks_ref[0] = s_scr[...]
    ckp_ref[0] = p_scr[...]
    fill(low_ref, bcs_scr, bc_scr, n)
    step = softplus(mm(low_ref[0, :, :128], wdt_ref[...]) + dtb_ref[...])
    sd_scr[...] = jnp.where(mask_ref[0, :, 0:1] > 0.0, step, 1e30)
    dx_scr[...] = step * xc_ref[0].astype(F32)
    dg = nt(dy_ref[0], wo_ref[...])
    dg_ref[0] = dg
    z = xz_ref[0, :, e:].astype(F32)
    dy_scr[...] = dg * (z * jax.nn.sigmoid(z))
    a2 = a2_ref[...]
    rows = sd_scr.shape[0] // m
    un = 16

    def group(g, carry):
        s, p, f = [list(c) for c in carry]
        for j in range(un):
            for i in range(m):
                t = i * rows + g * un + j
                bc = bc_scr[at(t * n, n, n), :]
                bb, cc = wide(bc[:, :128], e), wide(bc[:, 128:], e)
                a = jnp.exp2(sd_scr[pl.ds(t, 1), :] * a2)
                s[i] = a * s[i] + bb * dx_scr[pl.ds(t, 1), :]
                p[i] = p[i] * a
                f[i] = f[i] + p[i] * (cc * dy_scr[pl.ds(t, 1), :])
        return tuple(s), tuple(p), tuple(f)
    done = lax.fori_loop(0, rows // un, group,
                         tuple(tuple(scr[i] for i in range(m)) for scr in (s_scr, p_scr, f_scr)))
    for scr, vals in zip((s_scr, p_scr, f_scr), done):
        for i in range(m):
            scr[i] = vals[i]

    @pl.when(b == pl.num_programs(0) - 1)
    def _():
        end_ref[0] = s_scr[...]
        end_ref[1] = p_scr[...]
        end_ref[2] = f_scr[...]


def behind(low_ref, xz_ref, xc_ref, mask_ref, dy_ref, dg_ref, nu_ref, cks_ref, ckp_ref,
           wo_ref, wdt_ref, dtb_ref, a2_ref, skip_ref, hin_ref, qin_ref,
           out_ref, dz_ref, dxc_ref, part_ref, go_ref, gdt_ref, ga_ref, vec_ref, gz_ref,
           h_scr, a_scr, q_scr, bcs_scr, bc_scr, pre_scr, st_scr, sd_scr, dx_scr, dy_scr, y_scr, da_scr, gb_scr, *, m, n, e):
    b = pl.program_id(0)
    @pl.when(b == 0)
    def _():
        q_scr[...] = qin_ref[...]
        for ref in (go_ref, gdt_ref, ga_ref, vec_ref, gz_ref):
            ref[...] = jnp.zeros_like(ref)
    fill(low_ref, bcs_scr, bc_scr, n)
    pre = mm(low_ref[0, :, :128], wdt_ref[...]) + dtb_ref[...]
    pre_scr[...] = pre
    step = softplus(pre)
    st_scr[...] = step
    sd_scr[...] = jnp.where(mask_ref[0, :, 0:1] > 0.0, step, 1e30)
    dx_scr[...] = step * xc_ref[0].astype(F32)
    z = xz_ref[0, :, e:].astype(F32)
    dy_scr[...] = dg_ref[0] * (z * jax.nn.sigmoid(z))
    a2 = a2_ref[...]
    sub = lax.broadcasted_iota(jnp.int32, (8, e), 0)
    rows = sd_scr.shape[0] // m
    lanes = lax.broadcasted_iota(jnp.int32, (n, rows), 1)
    un = 32
    for i in range(m):
        r0 = i * rows
        h0 = cks_ref[0, i] + ckp_ref[0, i] * hin_ref[i]
        h_scr[pl.ds(0, n), :] = h0

        def fwd(g, h, r0=r0):
            ys = []
            for j in range(un):
                t = g * un + j
                bc = bc_scr[at((r0 + t) * n, n, n), :]
                bb, cc = wide(bc[:, :128], e), wide(bc[:, 128:], e)
                a = jnp.exp2(sd_scr[pl.ds(r0 + t, 1), :] * a2)
                h = a * h + bb * dx_scr[pl.ds(r0 + t, 1), :]
                a_scr[at(t * n, n, n), :] = a
                h_scr[at(t * n + n, n, n), :] = h
                cy = cc * h
                ys.append(cy[:8] + cy[8:])
                if len(ys) == 8:
                    y_scr[at(r0 + t - 7, 8), :] = fold_rows(ys, sub)
                    ys = []
            return h
        lax.fori_loop(0, rows // un, fwd, h0)

        def bwd(g, carry, r0=r0):
            q, ga, hn, db, dc = carry
            das, gbs = [], []
            for j in range(un):
                t = rows - 1 - (g * un + j)
                bc = bc_scr[at((r0 + t) * n, n, n), :]
                bb, cc = wide(bc[:, :128], e), wide(bc[:, 128:], e)
                a = a_scr[at(t * n, n, n), :]
                hp = h_scr[at(t * n, n, n), :]
                dyr = dy_scr[pl.ds(r0 + t, 1), :]
                gt = cc * dyr + q
                q = a * gt
                da = q * hp
                ga = ga + da * st_scr[pl.ds(r0 + t, 1), :]
                d_a = da * a2
                g_b = gt * bb
                das.append(d_a[:8] + d_a[8:])
                gbs.append(g_b[:8] + g_b[8:])
                pb = gt * dx_scr[pl.ds(r0 + t, 1), :]
                pc = dyr * hn
                pb = sum(pb[:, k:k + 128] for k in range(0, e, 128))
                pc = sum(pc[:, k:k + 128] for k in range(0, e, 128))
                db = jnp.where(lanes == t, jnp.sum(pb, axis=1, keepdims=True), db)
                dc = jnp.where(lanes == t, jnp.sum(pc, axis=1, keepdims=True), dc)
                hn = hp
                if len(das) == 8:
                    da_scr[at(r0 + t, 8), :] = fold_rows(das[::-1], sub)
                    gb_scr[at(r0 + t, 8), :] = fold_rows(gbs[::-1], sub)
                    das, gbs = [], []
            return q, ga, hn, db, dc
        zero = jnp.zeros((n, rows), F32)
        q, ga, _, db, dc = lax.fori_loop(
            0, rows // un, bwd, (q_scr[i], ga_ref[...], h_scr[pl.ds(rows * n, n), :], zero, zero))
        q_scr[i] = q
        ga_ref[...] = ga
        part_ref[0, 128:128 + n, r0:r0 + rows] = db
        part_ref[0, 128 + n:128 + 2 * n, r0:r0 + rows] = dc

    z = xz_ref[0, :, e:].astype(F32)
    sz = jax.nn.sigmoid(z)
    xc = xc_ref[0].astype(F32)
    skip = skip_ref[...]
    y = y_scr[...] + skip * xc
    gated = (y * (z * sz)).astype(BF16)
    out_ref[0] = mm(gated, wo_ref[...]).astype(BF16)
    go_ref[...] += tn(gated, dy_ref[0])
    dz = (dg_ref[0] * y * (sz * (1.0 + z * (1.0 - sz)))).astype(BF16)
    dz_ref[0] = dz
    gz_ref[...] += tn(nu_ref[0], dz)
    gb = gb_scr[...]
    dy_y = dy_scr[...]
    dxc_ref[0] = dy_y * skip + st_scr[...] * gb
    d_pre = (da_scr[...] * LN2 + xc * gb) * jax.nn.sigmoid(pre_scr[...])
    d_low = d_pre.astype(BF16)
    gdt_ref[...] += tn(low_ref[0, :, :128], d_low)
    part_ref[0, :128, :] = nt(wdt_ref[...], d_low)
    vec_ref[0:1] += jnp.sum(d_pre, axis=0, keepdims=True)
    vec_ref[1:2] += jnp.sum(dy_y * xc, axis=0, keepdims=True)


def dsilu(v):
    s = jax.nn.sigmoid(v)
    return s * (1.0 + v * (1.0 - s))


def back(xz_ref, prev_ref, edge_ref, mask_ref, dxc_ref, ddbc_ref, dz_ref, nu_ref, next_ref, w_ref, xpt_ref, cw_ref, cb_ref,
         v_ref, gx_ref, vec_ref, carry, dx_scr, *, m, e):
    b = pl.program_id(0)
    @pl.when(b == 0)
    def _():
        carry[...] = next_ref[...]
        gx_ref[...] = jnp.zeros_like(gx_ref)
        vec_ref[...] = jnp.zeros_like(vec_ref)
    first = b == pl.num_programs(0) - 1
    rows = xz_ref.shape[1] // m
    cw, cb = cw_ref[...], cb_ref[...]
    dxc_all = dxc_ref[0] + mm(ddbc_ref[0], xpt_ref[...])
    for i in range(m):
        part = slice(i * rows, (i + 1) * rows)
        x = xz_ref[0, part, :e].astype(F32)
        before = prev_ref[0, (i + 1) * rows - 2 * EDGE:(i + 1) * rows, :e].astype(F32)[EDGE:]
        before = jnp.where(first, edge_ref[i * EDGE:(i + 1) * EDGE], before)
        lag = lags(jnp.concatenate([before, x], axis=0), rows)
        same = mask_ref[0, part]
        dconv = dxc_all[part] * dsilu(convolve(lag, same, cw, cb))
        vec_ref[4:5] += jnp.sum(dconv, axis=0, keepdims=True)
        vec_ref[3:4] += jnp.sum(dconv * x, axis=0, keepdims=True)
        dx = cw[3:4] * dconv
        for k in range(1, 4):
            masked = dconv * same[:, k - 1:k]
            vec_ref[3 - k:4 - k] += jnp.sum(masked * lag[k], axis=0, keepdims=True)
            sent = cw[3 - k:4 - k] * masked
            ext = jnp.concatenate([sent, carry[k - 1, i]], axis=0)
            dx = dx + ext[k:k + rows]
            carry[k - 1, i] = sent[:EDGE]
        dx_scr[part] = dx
    dx = dx_scr[...].astype(BF16)
    v_ref[0] = nt(jnp.concatenate([dx, dz_ref[0]], axis=1), w_ref[...]).astype(BF16)
    gx_ref[...] += tn(nu_ref[0], dx)


def shift_rep(value, steps):
    count = lax.axis_size("rep")
    first, last = max(0, -steps), min(count, count - steps)
    return lax.ppermute(value, "rep", [(i, i + steps) for i in range(first, last)])


def sum_rep(value):
    if lax.axis_size("rep") != 2:
        return lax.psum(value.astype(F32), "rep")
    low = value.astype(BF16)
    other = lax.ppermute(low, "rep", [(0, 1), (1, 0)])
    return low.astype(F32) + other.astype(F32)


def on_device(hidden_in, segment_ids, out_grad, norm_gain, in_proj, conv_weight, conv_bias, x_proj,
              dt_weight, dt_bias, a_log, d_skip, out_proj):
    peers, reps = lax.axis_size("shard"), lax.axis_size("rep")
    rep = lax.axis_index("rep")
    m, tl, d = hidden_in.shape
    t, w = tl * peers, m * tl
    dl = in_proj.shape[0]
    e = x_proj.shape[0]
    n, rank, taps = a_log.shape[0], dt_weight.shape[0], conv_weight.shape[0]
    w32 = lambda v: v.astype(F32)
    shp = jax.ShapeDtypeStruct
    rising = lambda i: i
    falling = lambda i: peers - 1 - i

    gain = w32(lax.all_gather(norm_gain, "shard", axis=0, tiled=True))
    u = w32(hidden_in)
    r = lax.rsqrt(jnp.mean(u * u, axis=2, keepdims=True) + 1e-5)
    nu = (u * r * gain).astype(BF16).reshape(w, d)
    nu_all = lax.all_gather(nu, "shard")
    dy_all = lax.all_gather(out_grad.reshape(w, d), "shard")
    w_split = in_proj.reshape(dl, 2, peers, e).transpose(2, 0, 1, 3).reshape(peers * dl, 2 * e)
    w_cols = lax.all_to_all(w_split, "shard", 0, 0, tiled=True)

    ids = lax.all_gather(segment_ids, "shard")
    row_ids = ids.transpose(1, 0, 2).reshape(m, t)
    before = jnp.where(rep > 0, shift_rep(row_ids[:, t - taps + 1:], 1), -1)
    ext = jnp.concatenate([before, row_ids], axis=1)
    same = jnp.stack([w32(ext[:, taps - 1 - k:taps - 1 - k + t] == row_ids) for k in range(1, taps)], axis=-1)
    mask = jnp.pad(same, ((0, 0), (0, 0), (0, 8 - same.shape[-1])))
    mask = mask.reshape(m, peers, tl, 8).transpose(1, 0, 2, 3).reshape(peers, w, 8)
    halo = shift_rep(nu_all[peers - 1].reshape(m, tl, d)[:, tl - EDGE:].reshape(m * EDGE, d), 1)

    cw, cb = w32(conv_weight), w32(conv_bias)[None]
    ins = [nu_all, w_cols, halo, mask, cw, cb, x_proj.T]
    outs = [shp((peers, w, 2 * e), BF16), shp((peers, w, e), BF16), shp((peers, rank + 2 * n, w), F32),
            shp((m * EDGE, e), BF16)]
    xz, xc, part, edge = call(
        functools.partial(front, m=m, e=e), (peers,),
        [block(nu_all, rising)] + [whole(a) for a in ins[1:3]] + [block(mask, rising)] + [whole(a) for a in ins[4:]],
        [block(a, rising) for a in outs[:3]] + [whole(outs[3])], outs,
        [pltpu.VMEM((m * EDGE, e), F32)], ins, flops=2 * peers * w * d * 2 * e)

    low = allsum(part, functools.partial(spread_low, n=n), 0)
    a_mat = -jnp.exp(w32(a_log))
    a2 = a_mat * LOG2E
    dtb, skip = w32(dt_bias)[None], w32(d_skip)[None]

    ins = [low, xz, xc, mask, dy_all, out_proj, dt_weight, dtb, a2]
    outs = [shp((peers, m, n, e), F32)] * 2 + [shp((3, m, n, e), F32), shp((peers, w, e), F32)]
    cks, ckp, end, dg = call(
        functools.partial(ahead, m=m, n=n, e=e), (peers,),
        [block(a, rising) for a in ins[:5]] + [whole(a) for a in ins[5:]],
        [block(outs[0], rising), block(outs[1], rising), whole(outs[2]), block(outs[3], rising)], outs,
        [pltpu.VMEM((m, n, e), F32)] * 3 + [pltpu.VMEM((w, e), F32)] * 3 + [pltpu.VMEM((w, 128), F32), pltpu.VMEM((w * n, 256), F32)],
        ins, flops=40 * 10 ** 9)

    ends = lax.all_gather(end, "rep")
    h_in = jnp.zeros((m, n, e), F32)
    q_in = jnp.zeros((m, n, e), F32)
    for k in range(reps - 1):
        o = reps - 1 - k
        h_in = jnp.where(k < rep, ends[k, 1] * h_in + ends[k, 0], h_in)
        q_in = jnp.where(o > rep, ends[o, 1] * q_in + ends[o, 2], q_in)

    ins = [low, xz, xc, mask, dy_all, dg, nu_all, cks, ckp, out_proj, dt_weight, dtb, a2, skip, h_in, q_in]
    outs = [shp((peers, w, d), BF16), shp((peers, w, e), BF16), shp((peers, w, e), F32),
            shp((peers, rank + 2 * n, w), F32), shp((e, d), F32), shp((rank, e), F32), shp((n, e), F32), shp((8, e), F32),
            shp((d, e), F32)]
    part_out, dz, dxc, part, g_out, g_dt, g_a, vec, g_z = call(
        functools.partial(behind, m=m, n=n, e=e), (peers,),
        [block(a, falling) for a in ins[:9]] + [whole(a) for a in ins[9:]],
        [block(a, falling) for a in outs[:4]] + [whole(a) for a in outs[4:]], outs,
        [pltpu.VMEM((tl * n + n, e), F32), pltpu.VMEM((tl * n, e), F32), pltpu.VMEM((m, n, e), F32),
         pltpu.VMEM((w, 128), F32), pltpu.VMEM((w * n, 256), F32)] + [pltpu.VMEM((w, e), F32)] * 8, ins, flops=100 * 10 ** 9)

    out_sum = lax.psum_scatter(part_out, "shard", scatter_dimension=0, tiled=True).reshape(m, tl, d)
    layer_out = (u + w32(out_sum)).astype(BF16)

    ddbc = allsum(part, functools.partial(spread_plain, n=n), 1)
    xpt = jnp.pad(x_proj.T, ((0, 256 - x_proj.shape[1]), (0, 0)))

    x8 = w32(xz[0].reshape(m, tl, 2 * e)[:, :EDGE, :e])
    ext8 = jnp.concatenate([w32(edge).reshape(m, EDGE, e), x8], axis=1)
    same8 = mask[0].reshape(m, tl, 8)[:, :EDGE]
    conv8 = cb + cw[3] * x8
    for k in range(1, taps):
        conv8 = conv8 + cw[3 - k] * ext8[:, EDGE - k:2 * EDGE - k] * same8[:, :, k - 1:k]
    d8 = dxc[0].reshape(m, tl, e)[:, :EDGE] + mm(ddbc[0].reshape(m, tl, -1)[:, :EDGE].reshape(m * EDGE, -1), xpt).reshape(m, EDGE, e)
    d8 = d8 * dsilu(conv8)
    sent = jnp.stack([cw[3 - k] * d8 * same8[:, :, k - 1:k] for k in range(1, taps)])
    follow = shift_rep(sent, -1)

    ins = [xz, xz, w32(edge), mask, dxc, ddbc, dz, nu_all, follow, w_cols, xpt, cw, cb]
    outs = [shp((peers, w, d), BF16), shp((d, e), F32), shp((8, e), F32)]
    earlier = lambda i: jnp.maximum(peers - 2 - i, 0)
    specs = [block(a, falling) for a in ins[:8]] + [whole(a) for a in ins[8:]]
    specs[1], specs[2] = block(xz, earlier), whole(ins[2])
    v_part, g_x, vec2 = call(
        functools.partial(back, m=m, e=e), (peers,), specs,
        [block(outs[0], falling), whole(outs[1]), whole(outs[2])], outs,
        [pltpu.VMEM((taps - 1, m, EDGE, e), F32), pltpu.VMEM((w, e), F32)], ins, flops=2 * peers * w * d * 3 * e)

    v = w32(lax.psum_scatter(v_part, "shard", scatter_dimension=0, tiled=True)).reshape(m, tl, d) * gain
    in_grad = w32(out_grad) + r * v - u * (r * r * r) * jnp.mean(v * u, axis=2, keepdims=True)

    def to_owner(g):
        own = lax.all_to_all(g.astype(BF16), "shard", 0, 0, tiled=True)
        own = own.reshape(peers, dl, e).transpose(1, 0, 2).reshape(dl, peers * e)
        return sum_rep(own)
    grad_in_proj = jnp.concatenate([to_owner(g_x), to_owner(g_z)], axis=1)
    grad_gain = jnp.sum(grad_in_proj * w32(in_proj), axis=1) / w32(norm_gain)

    small = jnp.concatenate([vec, vec2, g_a * a_mat, g_dt, tn(xc.reshape(peers * w, e), ddbc.reshape(peers * w, -1)).T], axis=0)
    small = sum_rep(small)
    vec, vec2, g_a, g_dt, g_xp = (small[:8], small[8:16], small[16:16 + n], small[16 + n:16 + n + rank], small[16 + n + rank:])
    return (layer_out, in_grad, grad_gain, grad_in_proj, vec2[:taps], vec2[taps], g_xp[:rank + 2 * n].T, g_dt, vec[0],
            g_a, vec[1], sum_rep(g_out))


def solution(mesh):
    tok, ids = P(None, ("rep", "shard"), None), P(None, ("rep", "shard"))
    row, col, one = P("shard", None), P(None, "shard"), P("shard")
    return jax.shard_map(
        on_device,
        mesh=mesh,
        in_specs=(tok, ids, tok, one, row, col, one, row, col, one, col, one, row),
        out_specs=(tok, tok, one, row, col, one, row, col, one, col, one, row),
        check_vma=False,
    )
```

time: 1120 us -> 999 us (0.89)
  Pallas kernels: 131 us -> 347 us
  local copies, waits for them, and re-layouts: 175 us -> 21.8 us
  matrix products: 91.3 us -> 3.2 us
  blocking collectives: 171 us -> 109 us
  other arithmetic: 67.5 us -> 27.8 us
  waiting for transfers between devices: 415 us -> 448 us
  starting transfers between devices: 44 us -> 26.5 us
    reduce_scatter x0 -> x2, waiting for transfers between devices: none -> 273 us  [the longest x1 180 us: on_device(): lax.psum_scatter(part_out, 'shard', scatter_dimension=0, tiled=True)]
    pallas_call x4 -> x6, Pallas kernels: 131 us -> 347 us  [the longest x4 218 us: call(): pl.pallas_call(kernel, grid=grid, in_specs=in_specs, out_specs=out_specs,...]
    unnamed x138 -> x79, local copies, waits for them, and re-layouts: 106 us -> 4.87 us
    psum x1 -> x0, blocking collectives: 91.9 us -> none  [on_device(): lax.psum(jnp.concatenate([nt(d_pre_low, dt_weight), d_bc], axis=1), 'shard')]
    psum x1 -> x0, waiting for transfers between devices: 91.9 us -> none  [on_device(): dbc = lax.psum(mm(xc_low.reshape(m * t, e), x_proj), 'shard')]
    dot_general x12 -> x2, matrix products: 91.3 us -> 3.2 us  [the longest x1 3.06 us: tn(): lax.dot_general(a, b, (((0,), (0,)), ((), ())), preferred_element_type=F32)]
    all_gather x2, waiting for transfers between devices: 162 us -> 99.5 us  [the longest x1 64.9 us: on_device(): nu_all = lax.all_gather(nu, 'shard')]
    unnamed x7 -> x4, waiting for transfers between devices: 59.9 us -> 1.25 us
  transfers between devices with their start and end apart: 13 -> 14, of which waited for: 9 -> 9; matrix products, arithmetic and copies ran while one was open for 18% -> 3% of each run, Pallas kernels for 0% -> 10%
where the time goes in v2:
time: 999 us; the launch traced here: 998 us
  waiting for transfers between devices  448 us (45%)
  Pallas kernels  347 us (35%)
  blocking collectives  109 us (11%)
  other arithmetic  27.8 us (3%)
  starting transfers between devices  26.5 us (3%)
  local copies, waits for them, and re-layouts  21.8 us (2%)
  between operations  14.4 us (1%)
    pallas_call x4, Pallas kernels, call(): pl.pallas_call(kernel, grid=grid, in_specs=in_specs, out_specs=out_specs,...  218 us
    reduce_scatter x1, waiting for transfers between devices, on_device(): lax.psum_scatter(part_out, 'shard', scatter_dimension=0, tiled=True)  180 us
    pallas_call x2, Pallas kernels, allsum(): pl.pallas_call(functools.partial(allsum_kernel, dims=dims, chunks=chunks,...  129 us
    reduce_scatter x1, waiting for transfers between devices, on_device(): lax.psum_scatter(v_part, 'shard', scatter_dimension=0, tiled=True)  93.5 us
    all_gather x1, blocking collectives, on_device(): ids = lax.all_gather(segment_ids, 'shard')  79.7 us
    all_gather x1, waiting for transfers between devices, on_device(): nu_all = lax.all_gather(nu, 'shard')  64.9 us
    all_to_all x2, waiting for transfers between devices, to_owner(): own = lax.all_to_all(g.astype(BF16), 'shard', 0, 0, tiled=True)  44.9 us
    all_gather x1, waiting for transfers between devices, on_device(): dy_all = lax.all_gather(out_grad.reshape(w, d), 'shard')  34.7 us
  transfers between devices with their start and end apart: 14, of which 9 were waited for; matrix products, arithmetic and copies ran while one was open for 3% of the time, Pallas kernels for 10%

profile of v2, /device:TPU:0, one launch (start us, length us, event | category | flops | bytes accessed | tf_op | source)
XLA Modules:
  0.0 997.8 jit_solution(2784924502916525936)
XLA Ops:
  7.2 23.2 %all-gather.2 = bf16[16,1,128]{2,1,0:T(2,128)(2,1)S(1)} all-gather(bf16[1,1,128]{2,1,0:T(2,128)(2,1)} %bitcast.135), channel_id=1, replica_groups=mesh['rep'=2,'shard'=16] {'shard'}, dimensions={0}, use_global_device_ids=true | all-gather | bytes 4352 | tf_op jit(solution)/shard_map/all_gather | solution.py:461
  30.4 1.5 fusion
  32.5 2.7 fusion.2
  35.3 0.7 all-gather.9.cloned.1.call-update
  36.6 2.0 copy.57
  38.6 2.6 all_to_all.19
  41.3 3.9 all-to-all-start
  45.2 79.7 %all-gather.3 = s32[16,2,128]{2,1,0:T(2,128)S(1)} all-gather(s32[1,2,128]{2,1,0:T(2,128)S(1)} %bitcast.124), channel_id=2, replica_groups=mesh['rep'=2,'shard'=16] {'shard'}, dimensions={0}, use_global_device_ids=true | all-gather | bytes 17408 | tf_op jit(solution)/shard_map/all_gather | solution.py:470
  125.0 3.6 collective-permute-start.1
  132.4 64.9 %all-gather.7.cloned.1.call-done.nu_ref = bf16[16,256,2048]{2,1,0:T(8,128)(2,1)} async-done(((bf16[1,256,2048]{2,1,0:T(8,128)(2,1)}), bf16[16,256,2048]{2,1,0:T(8,128)(2,1)}) %all-gather.7.cloned.1.call-update) | async-done | bytes 16777232 | tf_op jit(solution)/shard_map/all_gather | solution.py:465
  197.3 1.2 slice-done
  198.5 3.4 collective-permute-start
  202.4 1.9 copy.61
  204.4 1.3 copy-done.9
  205.7 22.0 %shard_map.220 = (bf16[16,256,512]{2,1,0:T(8,128)(2,1)}, bf16[16,256,256]{2,1,0:T(8,128)(2,1)}, f32[16,160,256]{2,1,0:T(8,128)}, bf16[16,256]{1,0:T(8,128)(2,1)}) custom-call(bf16[16,256,2048]{2,1,0:T(8,128)(2,1)} %all-gather.7.cloned.1.call-done.nu_ref, bf16[2048,512]{1,0:T(8,128)(2,1)} %bitcast.102, bf16[16,2048]{1,0:T(8,128)(2,1)} %copy-done.33, ...), custom_call_target="tpu_custom_call" | custom-call | flops 8589934592 | bytes 28079104 | tf_op jit(solution)/shard_map/pallas_call | solution.py:41
  227.7 76.4 %shard_map.221 = bf16[4,2,2,256,256]{4,3,2,1,0:T(8,128)(2,1)} custom-call(f32[4,2,2,160,256]{4,3,2,1,0:T(8,128)} %bitcast.98), custom_call_target="tpu_custom_call" | custom-call | tf_op jit(solution)/shard_map/pallas_call | solution.py:199
  304.1 1.0 slice.137
  305.1 34.7 %all-gather.9.cloned.1.call-done.dy_ref = bf16[16,256,2048]{2,1,0:T(8,128)(2,1)} async-done(((bf16[1,256,2048]{2,1,0:T(8,128)(2,1)}), bf16[16,256,2048]{2,1,0:T(8,128)(2,1)}) %all-gather.9.cloned.1.call-update) | async-done | bytes 16777232 | tf_op jit(solution)/shard_map/all_gather | solution.py:466
  339.7 47.4 %shard_map.222 = (f32[16,2,16,256]{3,2,1,0:T(8,128)}, f32[16,2,16,256]{3,2,1,0:T(8,128)}, f32[3,2,16,256]{3,2,1,0:T(8,128)}, f32[16,256,256]{2,1,0:T(8,128)}) custom-call(bf16[16,256,256]{2,1,0:T(8,128)(2,1)} %bitcast.108, bf16[16,256,512]{2,1,0:T(8,128)(2,1)} %get-tuple-element.33.xz_ref.prev_ref, bf16[16,256,256]{2,1,0:T(8,128)(2,1)} %get-tuple-element.34.xc_ref, ...), custom_call_target="tpu_custom_call" | custom-call | flops 40000000000 | bytes 31769600 | tf_op jit(solution)/shard_map/pallas_call | solution.py:41
  387.1 6.0 all-gather.1
  393.8 118.3 %shard_map.223 = (bf16[16,256,2048]{2,1,0:T(8,128)(2,1)}, bf16[16,256,256]{2,1,0:T(8,128)(2,1)}, f32[16,256,256]{2,1,0:T(8,128)}, f32[16,160,256]{2,1,0:T(8,128)...) custom-call(bf16[16,256,256]{2,1,0:T(8,128)(2,1)} %bitcast.109, ...), custom_call_target="tpu_custom_call" | custom-call | flops 99999997952 | bytes 78555136 | tf_op jit(solution)/shard_map/pallas_call | solution.py:41
  512.2 52.6 %shard_map.224 = bf16[4,2,2,256,256]{4,3,2,1,0:T(8,128)(2,1)} custom-call(f32[4,2,2,160,256]{4,3,2,1,0:T(8,128)} %bitcast.97), custom_call_target="tpu_custom_call" | custom-call | tf_op jit(solution)/shard_map/pallas_call | solution.py:199
  564.8 0.9 slice.168
  565.8 1.0 slice.132
  567.6 1.3 collective-permute-start.2
  569.6 4.0 collective-permute-done.2.next_ref
  574.2 30.5 %shard_map.225 = (bf16[16,256,2048]{2,1,0:T(8,128)(2,1)}, f32[2048,256]{1,0:T(8,128)}, f32[8,256]{1,0:T(8,128)}) custom-call(bf16[16,256,512]{2,1,0:T(8,128)(2,1)} %get-tuple-element.33.xz_ref.prev_ref, bf16[16,256,512]{2,1,0:T(8,128)(2,1)} %get-tuple-element.33.xz_ref.prev_ref, f32[16,256]{1,0:T(8,128)} %get-tuple-element.71.edge_ref, ...), custom_call_target="tpu_custom_call" | custom-call | flops 12884901888 | bytes 54866944 | tf_op jit(solution)/shard_map/pallas_call | solution.py:41
  605.3 2.8 convert_element_type.102
  608.1 5.3 all-to-all-start.2
  613.4 1.1 convert_element_type.109
  614.5 1.2 copy-done.8
  615.8 1.1 convert_element_type.99
  616.9 19.5 %all-to-all-done.2 = bf16[16,128,256]{2,1,0:T(8,128)(2,1)S(1)} async-done(((bf16[16,128,256]{2,1,0:T(8,128)(2,1)}), bf16[16,128,256]{2,1,0:T(8,128)(2,1)S(1)}, u32[]{:S(2)}, u32[]{:S(2)}) %all-to-all-start.2) | async-done | bytes 1048608 | tf_op jit(solution)/shard_map/all_to_all | solution.py:553
  636.4 1.0 copy-done.6
  637.3 6.9 all-to-all-start.1
  644.3 3.1 fusion.9
  647.5 1.1 copy.65
  648.5 2.0 collective-permute-start.4
  650.6 5.0 collective-permute-done.5
  658.7 25.4 %all-to-all-done.1 = bf16[16,128,256]{2,1,0:T(8,128)(2,1)S(1)} async-done(((bf16[16,128,256]{2,1,0:T(8,128)(2,1)}), bf16[16,128,256]{2,1,0:T(8,128)(2,1)S(1)}, u32[]{:S(2)}, u32[]{:S(2)}) %all-to-all-start.1) | async-done | bytes 1048608 | tf_op jit(solution)/shard_map/all_to_all | solution.py:553
  684.2 2.8 convert_add_fusion.1
  687.0 1.8 convert_add_fusion.2
  688.9 20.0 %collective-permute-done.3 = bf16[128,4096]{1,0:T(8,128)(2,1)S(1)} collective-permute-done((bf16[128,4096]{1,0:T(8,128)(2,1)S(1)}, bf16[128,4096]{1,0:T(8,128)(2,1)S(1)}, u32[]{:S(2)}, u32[]{:S(2)}) %collective-permute-start.3) | collective-permute-done | bytes 1048608 | tf_op jit(solution)/shard_map/ppermute | solution.py:443
  709.2 2.7 multiply_reduce_fusion
  712.4 93.5 %reduce-scatter.5.cloned.1.call-done = bf16[1,256,2048]{2,1,0:T(8,128)(2,1)} async-done(((bf16[16,256,2048]{2,1,0:T(8,128)(2,1)}), bf16[1,256,2048]{2,1,0:T(8,128)(2,1)}) %reduce-scatter.5.cloned.1.call-update) | async-done | bytes 1048592 | tf_op jit(solution)/shard_map/reduce_scatter | solution.py:549
  806.0 1.7 fusion.6
  807.7 179.8 %reduce-scatter.3.cloned.1.call-done = bf16[1,256,2048]{2,1,0:T(8,128)(2,1)} async-done(((bf16[16,256,2048]{2,1,0:T(8,128)(2,1)}), bf16[1,256,2048]{2,1,0:T(8,128)(2,1)}) %reduce-scatter.3.cloned.1.call-update) | async-done | bytes 1048592 | tf_op jit(solution)/shard_map/reduce_scatter | solution.py:522
  987.5 3.8 fusion.5
  (131 shorter events, 13.4 us)
Async XLA Ops:
  7.2 190.1 %all-gather.7.cloned.1.call-start = ((), (), s32[]{:S(2)}) async-start(), calls=%async_computation.5 | async-start | bytes 17825792 | tf_op jit(solution)/shard_map/all_gather | solution.py:465
  32.5 2.7 copy-start.18
  32.5 3.4 copy-start.2
  35.2 304.5 %all-gather.9.cloned.1.call-start = ((), (), s32[]{:S(2)}) async-start(), calls=%async_computation.6 | async-start | bytes 17825792 | tf_op jit(solution)/shard_map/all_gather | solution.py:466
  41.2 4.0 copy-start.24
  41.2 87.3 %copy-start.35 = (bf16[256]{0:T(256)(128)(2,1)S(1)}, bf16[256]{0:T(256)(128)(2,1)}, u32[]{:S(2)}) copy-start(bf16[256]{0:T(256)(128)(2,1)} %param.19) | copy-start | bytes 1540
  41.2 87.9 %copy-start.16 = (bf16[4,256]{1,0:T(4,128)(2,1)S(1)}, bf16[4,256]{1,0:T(4,128)(2,1)}, u32[]{:S(2)}) copy-start(bf16[4,256]{1,0:T(4,128)(2,1)} %param.18) | copy-start | bytes 6148
  41.2 88.5 %copy-start.36 = (bf16[256]{0:T(256)(128)(2,1)S(1)}, bf16[256]{0:T(256)(128)(2,1)}, u32[]{:S(2)}) copy-start(bf16[256]{0:T(256)(128)(2,1)} %param.22) | copy-start | bytes 1540
  41.2 89.1 %copy-start.37 = (bf16[256]{0:T(256)(128)(2,1)S(1)}, bf16[256]{0:T(256)(128)(2,1)}, u32[]{:S(2)}) copy-start(bf16[256]{0:T(256)(128)(2,1)} %param.24) | copy-start | bytes 1540
  41.2 90.2 %copy-start.14 = (bf16[16,256]{1,0:T(8,128)(2,1)S(1)}, bf16[16,256]{1,0:T(8,128)(2,1)}, u32[]{:S(2)}) copy-start(bf16[16,256]{1,0:T(8,128)(2,1)} %param.23) | copy-start | bytes 24580
  41.3 163.1 %all-to-all-start = ((bf16[16,128,512]{2,1,0:T(8,128)(2,1)}), bf16[16,128,512]{2,1,0:T(8,128)(2,1)S(1)}, u32[]{:S(2)}, u32[]{:S(2)}) async-start(bf16[16,128,512]{2,1,0:T(8,128)(2,1)} %all_to_all.19), calls=%async_computation | async-start | bytes 4194304 | tf_op jit(solution)/shard_map/all_to_all | solution.py:468
  45.1 760.8 %reduce-scatter.5.cloned.1.call-start = ((), (), s32[]{:S(2)}) async-start(), calls=%async_computation.8 | async-start | bytes 17825792 | tf_op jit(solution)/shard_map/reduce_scatter | solution.py:549
  125.0 7.1 collective-permute-start.1
  198.5 5.9 collective-permute-start
  512.1 54.7 %copy-start.20 = (bf16[16,256]{1,0:T(8,128)(2,1)S(1)}, bf16[16,256]{1,0:T(8,128)(2,1)}, u32[]{:S(2)}) copy-start(bf16[16,256]{1,0:T(8,128)(2,1)} %get-tuple-element.40) | copy-start | bytes 24580
  512.1 55.3 %copy-start.13 = (bf16[256,160]{0,1:T(8,128)(2,1)S(1)}, bf16[256,160]{0,1:T(8,128)(2,1)}, u32[]{:S(2)}) copy-start(bf16[256,160]{0,1:T(8,128)(2,1)} %param.20) | copy-start | bytes 245764
  512.1 55.3 %copy-start.25 = (f32[2,8,1]{1,2,0:T(1,128)S(1)}, f32[2,8,1]{1,2,0:T(1,128)}, u32[]{:S(2)}) copy-start(f32[2,8,1]{1,2,0:T(1,128)} %get-tuple-element.67) | copy-start | bytes 196
  512.1 55.3 %copy-start.26 = (f32[2,8,1]{1,2,0:T(1,128)S(1)}, f32[2,8,1]{1,2,0:T(1,128)}, u32[]{:S(2)}) copy-start(f32[2,8,1]{1,2,0:T(1,128)} %get-tuple-element.68) | copy-start | bytes 196
  512.1 55.2 %copy-start.27 = (f32[2,8,1]{1,2,0:T(1,128)S(1)}, f32[2,8,1]{1,2,0:T(1,128)}, u32[]{:S(2)}) copy-start(f32[2,8,1]{1,2,0:T(1,128)} %get-tuple-element.69) | copy-start | bytes 196
  512.1 55.2 %copy-start.28 = (f32[1,256]{1,0:T(1,128)S(1)}, f32[1,256]{1,0:T(1,128)}, u32[]{:S(2)}) copy-start(f32[1,256]{1,0:T(1,128)} %get-tuple-element.72) | copy-start | bytes 3076
  512.1 55.2 %copy-start.29 = (f32[1,256]{1,0:T(1,128)S(1)}, f32[1,256]{1,0:T(1,128)}, u32[]{:S(2)}) copy-start(f32[1,256]{1,0:T(1,128)} %get-tuple-element.73) | copy-start | bytes 3076
  512.2 55.2 %copy-start.30 = (f32[1,256]{1,0:T(1,128)S(1)}, f32[1,256]{1,0:T(1,128)}, u32[]{:S(2)}) copy-start(f32[1,256]{1,0:T(1,128)} %get-tuple-element.74) | copy-start | bytes 3076
  512.2 55.2 %copy-start.31 = (f32[1,256]{1,0:T(1,128)S(1)}, f32[1,256]{1,0:T(1,128)}, u32[]{:S(2)}) copy-start(f32[1,256]{1,0:T(1,128)} %get-tuple-element.75) | copy-start | bytes 3076
  512.2 55.2 %copy-start.38 = (f32[256]{0:T(256)S(1)}, f32[256]{0:T(256)}, u32[]{:S(2)}) copy-start(f32[256]{0:T(256)} %convert_element_type.91) | copy-start | bytes 3076
  567.6 6.0 collective-permute-start.2
  604.7 382.8 %reduce-scatter.3.cloned.1.call-start = ((), (), s32[]{:S(2)}) async-start(), calls=%async_computation.7 | async-start | bytes 17825792 | tf_op jit(solution)/shard_map/reduce_scatter | solution.py:522
  605.3 8.1 copy-start.1
  608.1 28.2 %all-to-all-start.2 = ((bf16[16,128,256]{2,1,0:T(8,128)(2,1)}), bf16[16,128,256]{2,1,0:T(8,128)(2,1)S(1)}, u32[]{:S(2)}, u32[]{:S(2)}) async-start(bf16[16,128,256]{2,1,0:T(8,128)(2,1)} %bitcast.50), calls=%async_computation.4 | async-start | bytes 2097152 | tf_op jit(solution)/shard_map/all_to_all | solution.py:553
  613.4 2.4 copy-start.8
  614.5 69.7 %collective-permute-start.6 = (bf16[256,2048]{1,0:T(8,128)(2,1)}, bf16[256,2048]{1,0:T(8,128)(2,1)}, u32[]{:S(2)}, u32[]{:S(2)}) collective-permute-start(bf16[256,2048]{1,0:T(8,128)(2,1)} %convert_element_type.109), channel_id=1, source_target_pairs={{0,16},{16,0},{1,17},{17,1},{2,18},{18,2},{3,19},{19,3},{4,20},{20... | collective-permute-start | bytes 3145736 | tf_op jit(solution)/shard_map/ppermute | solution.py:443
  615.8 28.4 %copy-start.21 = (f32[8,256]{1,0:T(8,128)S(1)}, f32[8,256]{1,0:T(8,128)}, u32[]{:S(2)}) copy-start(f32[8,256]{1,0:T(8,128)} %get-tuple-element.47) | copy-start | bytes 24580
  615.8 28.4 %copy-start.22 = (f32[8,256]{1,0:T(8,128)S(1)}, f32[8,256]{1,0:T(8,128)}, u32[]{:S(2)}) copy-start(f32[8,256]{1,0:T(8,128)} %get-tuple-element.48) | copy-start | bytes 24580
  615.8 28.5 %copy-start.15 = (bf16[16,256]{1,0:T(8,128)(2,1)S(1)}, bf16[16,256]{1,0:T(8,128)(2,1)}, u32[]{:S(2)}) copy-start(bf16[16,256]{1,0:T(8,128)(2,1)} %param.23) | copy-start | bytes 24580
  615.8 28.5 %copy-start.17 = (f32[16,256]{1,0:T(8,128)S(1)}, f32[16,256]{1,0:T(8,128)}, u32[]{:S(2)}) copy-start(f32[16,256]{1,0:T(8,128)} %get-tuple-element.49) | copy-start | bytes 49156
  615.8 28.5 %copy-start.12 = (f32[128,256]{1,0:T(8,128)S(1)}, f32[128,256]{1,0:T(8,128)}, u32[]{:S(2)}) copy-start(f32[128,256]{1,0:T(8,128)} %get-tuple-element.50) | copy-start | bytes 393220
  637.3 46.7 %all-to-all-start.1 = ((bf16[16,128,256]{2,1,0:T(8,128)(2,1)}), bf16[16,128,256]{2,1,0:T(8,128)(2,1)S(1)}, u32[]{:S(2)}, u32[]{:S(2)}) async-start(bf16[16,128,256]{2,1,0:T(8,128)(2,1)} %bitcast.48), calls=%async_computation.3 | async-start | bytes 2097152 | tf_op jit(solution)/shard_map/all_to_all | solution.py:553
  644.3 3.2 copy-start.7
  647.4 8.1 collective-permute-start.5
  648.5 38.5 %collective-permute-start.4 = (bf16[128,4096]{1,0:T(8,128)(2,1)}, bf16[128,4096]{1,0:T(8,128)(2,1)}, u32[]{:S(2)}, u32[]{:S(2)}) collective-permute-start(bf16[128,4096]{1,0:T(8,128)(2,1)} %bitcast.63), channel_id=1, source_target_pairs={{0,16},{16,0},{1,17},{17,1},{2,18},{18,2},{3,19},{19,3},{4,20},{20... | collective-permute-start | bytes 3145736 | tf_op jit(solution)/shard_map/ppermute | solution.py:443
  684.2 24.7 %collective-permute-start.3 = (bf16[128,4096]{1,0:T(8,128)(2,1)S(1)}, bf16[128,4096]{1,0:T(8,128)(2,1)S(1)}, u32[]{:S(2)}, u32[]{:S(2)}) collective-permute-start(bf16[128,4096]{1,0:T(8,128)(2,1)S(1)} %bitcast.95), channel_id=1, source_target_pairs={{0,16},{16,0},{1,17},{17,1},{2,18},{18,2},{3,19},{19,3},{4,20},{20... | collective-permute-start | bytes 3145736 | tf_op jit(solution)/shard_map/ppermute | solution.py:443
  688.8 20.3 %copy-start.3 = (bf16[128,8192]{1,0:T(8,128)(2,1)S(1)}, bf16[128,8192]{1,0:T(8,128)(2,1)}, u32[]{:S(2)}) copy-start(bf16[128,8192]{1,0:T(8,128)(2,1)} %param.17) | copy-start | bytes 6291460
  709.1 2.8 copy-start.32
  709.2 96.8 %copy-start = (bf16[2,128,2048]{2,1,0:T(8,128)(2,1)S(1)}, bf16[2,128,2048]{2,1,0:T(8,128)(2,1)}, u32[]{:S(2)}) copy-start(bf16[2,128,2048]{2,1,0:T(8,128)(2,1)} %param.13) | copy-start | bytes 3145732
  709.2 96.8 %copy-start.11 = (f32[16,1,128]{2,1,0:T(1,128)S(1)}, f32[16,1,128]{2,1,0:T(1,128)}, u32[]{:S(2)}) copy-start(f32[16,1,128]{2,1,0:T(1,128)} %copy-done.10) | copy-start | bytes 24580
  711.9 275.6 %copy-start.4 = (bf16[2,128,2048]{2,1,0:T(8,128)(2,1)S(1)}, bf16[2,128,2048]{2,1,0:T(8,128)(2,1)}, u32[]{:S(2)}) copy-start(bf16[2,128,2048]{2,1,0:T(8,128)(2,1)} %param.15) | copy-start | bytes 3145732
  711.9 275.6 %copy-start.19 = (f32[2,128]{1,0:T(2,128)S(1)}, f32[2,128]{1,0:T(2,128)}, u32[]{:S(2)}) copy-start(f32[2,128]{1,0:T(2,128)} %copy-done.18) | copy-start | bytes 3076
  711.9 275.6 %copy-start.23 = (f32[2,128]{1,0:T(2,128)S(1)}, f32[2,128]{1,0:T(2,128)}, u32[]{:S(2)}) copy-start(f32[2,128]{1,0:T(2,128)} %get-tuple-element.76) | copy-start | bytes 3076
  806.0 181.6 %copy-start.5 = (bf16[1,256,2048]{2,1,0:T(8,128)(2,1)S(1)}, bf16[1,256,2048]{2,1,0:T(8,128)(2,1)}, u32[]{:S(2)}) copy-start(bf16[1,256,2048]{2,1,0:T(8,128)(2,1)} %reduce-scatter.5.cloned.1.call-done) | copy-start | bytes 3145732
  (6 other events, 7.6 us)
Sparse Core Ops, SparseCore 0:
  35.3 161.8 all-gather.6
  199.4 140.2 all-gather.8
  604.9 201.0 reduce-scatter.4
  809.9 177.5 reduce-scatter.2

commit v3 on v2

--- a/solution.py
+++ b/solution.py
@@ -208,6 +208,95 @@
         compiler_params=pltpu.CompilerParams(collective_id=collective_id, has_side_effects=True, vmem_limit_bytes=VMEM),
     )(part.reshape(nz, ny, nc, cols, w))
     return out.reshape(peers, w, 256)
+
+
+def scatter_kernel(part, out, own, rc, ry, rz, load, send, recv, *, dims, chunks):
+    nz, ny, _ = dims
+    me = lax.axis_index("shard")
+    c, y, z = me % 2, (me // 2) % ny, me // (2 * ny)
+    where = lambda a, b, d: (a * ny + b) * 2 + d
+    across = where(z, y, 1 - c)
+    ys = [lax.rem(y + k, ny) for k in range(1, ny)]
+    zs = [lax.rem(z + k, nz) for k in range(1, nz)]
+    greet([across] + [where(z, b, c) for b in ys] + [where(a, y, c) for a in zs])
+    size = part.shape[3] // chunks
+    rows = [pl.ds(q * size, size) for q in range(chunks)]
+    per = 1 + ny - 1 + nz - 1
+
+    def pair(q, k):
+        return send.at[q * per + k], recv.at[q * per + k]
+    loads, first, second, third = [], [], [None] * chunks, [None] * chunks
+    for q in range(chunks):
+        loads.append(pltpu.make_async_copy(part.at[:, :, c, rows[q]], own.at[:, :, rows[q]], load.at[q]))
+        first.append(remote(part.at[:, :, 1 - c, rows[q]], rc.at[:, :, rows[q]], *pair(q, 0), across))
+        loads[q].start()
+        first[q].start()
+
+    def over_core(q):
+        loads[q].wait()
+        first[q].wait()
+
+        def add(a, _):
+            i, j = a // ny, a % ny
+            own[i, j, rows[q]] = (own[i, j, rows[q]].astype(F32) + rc[i, j, rows[q]].astype(F32)).astype(BF16)
+            return 0
+        lax.fori_loop(0, nz * ny, add, 0)
+        second[q] = [remote(own.at[:, b, rows[q]], ry.at[k, :, rows[q]], *pair(q, 1 + k), where(z, b, c))
+                     for k, b in enumerate(ys)]
+        for copy in second[q]:
+            copy.start()
+
+    def over_y(q):
+        for copy in second[q]:
+            copy.wait()
+
+        def add(a, _):
+            total = own[a, y, rows[q]].astype(F32)
+            for k in range(ny - 1):
+                total = total + ry[k, a, rows[q]].astype(F32)
+            own[a, y, rows[q]] = total.astype(BF16)
+            return 0
+        lax.fori_loop(0, nz, add, 0)
+        third[q] = [remote(own.at[a, y, rows[q]], rz.at[k, rows[q]], *pair(q, ny + k), where(a, y, c))
+                    for k, a in enumerate(zs)]
+        for copy in third[q]:
+            copy.start()
+
+    def over_z(q):
+        for copy in third[q]:
+            copy.wait()
+        total = own[z, y, rows[q]].astype(F32)
+        for k in range(nz - 1):
+            total = total + rz[k, rows[q]].astype(F32)
+        out[rows[q]] = total
+
+    for s in range(chunks + 4):
+        if s < chunks:
+            over_core(s)
+        if 0 <= s - 2 < chunks:
+            over_y(s - 2)
+        if 0 <= s - 4 < chunks:
+            over_z(s - 4)
+
+
+def scatter(part, collective_id):
+    peers, w, d = part.shape
+    dims = lattice(peers)
+    nz, ny, nc = dims
+    chunks = w // 32
+    copies = chunks * (1 + ny - 1 + nz - 1)
+    return pl.pallas_call(
+        functools.partial(scatter_kernel, dims=dims, chunks=chunks),
+        out_shape=jax.ShapeDtypeStruct((w, d), F32),
+        in_specs=[pl.BlockSpec(memory_space=pl.ANY)],
+        out_specs=pl.BlockSpec(memory_space=pltpu.VMEM),
+        scratch_shapes=[pltpu.VMEM((nz, ny, w, d), BF16), pltpu.VMEM((nz, ny, w, d), BF16),
+                        pltpu.VMEM((ny - 1, nz, w, d), BF16), pltpu.VMEM((nz - 1, w, d), BF16),
+                        pltpu.SemaphoreType.DMA((chunks,)),
+                        pltpu.SemaphoreType.DMA((copies,)), pltpu.SemaphoreType.DMA((copies,))],
+        compiler_params=pltpu.CompilerParams(collective_id=collective_id, has_side_effects=True, vmem_limit_bytes=VMEM),
+        cost_estimate=pl.CostEstimate(flops=8 * 10 ** 10, bytes_accessed=2 * peers * w * d, transcendentals=0),
+    )(part.reshape(nz, ny, nc, w, d))
 
 
 def fill(low_ref, bcs_scr, bc_scr, n):
@@ -519,8 +608,8 @@
         [pltpu.VMEM((tl * n + n, e), F32), pltpu.VMEM((tl * n, e), F32), pltpu.VMEM((m, n, e), F32),
          pltpu.VMEM((w, 128), F32), pltpu.VMEM((w * n, 256), F32)] + [pltpu.VMEM((w, e), F32)] * 8, ins, flops=100 * 10 ** 9)
 
-    out_sum = lax.psum_scatter(part_out, "shard", scatter_dimension=0, tiled=True).reshape(m, tl, d)
-    layer_out = (u + w32(out_sum)).astype(BF16)
+    out_sum = scatter(part_out, 2).reshape(m, tl, d)
+    layer_out = (u + out_sum).astype(BF16)
 
     ddbc = allsum(part, functools.partial(spread_plain, n=n), 1)
     xpt = jnp.pad(x_proj.T, ((0, 256 - x_proj.shape[1]), (0, 0)))
@@ -546,7 +635,7 @@
         [block(outs[0], falling), whole(outs[1]), whole(outs[2])], outs,
         [pltpu.VMEM((taps - 1, m, EDGE, e), F32), pltpu.VMEM((w, e), F32)], ins, flops=2 * peers * w * d * 3 * e)
 
-    v = w32(lax.psum_scatter(v_part, "shard", scatter_dimension=0, tiled=True)).reshape(m, tl, d) * gain
+    v = scatter(v_part, 3).reshape(m, tl, d) * gain
     in_grad = w32(out_grad) + r * v - u * (r * r * r) * jnp.mean(v * u, axis=2, keepdims=True)
 
     def to_owner(g):

time: 999 us -> 927 us (0.928)
  waiting for transfers between devices: 448 us -> 135 us
  Pallas kernels: 347 us -> 585 us
    reduce_scatter x2 -> x0, waiting for transfers between devices: 273 us -> none  [the longest x1 180 us: on_device(): lax.psum_scatter(part_out, 'shard', scatter_dimension=0, tiled=True)]
    pallas_call x0 -> x2, Pallas kernels: none -> 238 us  [scatter(): pl.pallas_call(functools.partial(scatter_kernel, dims=dims, chunks=chunks...]
    all_to_all x2, waiting for transfers between devices: 44.9 us -> 0.01 us  [to_owner(): own = lax.all_to_all(g.astype(BF16), 'shard', 0, 0, tiled=True)]
    ppermute x4, waiting for transfers between devices: 25 us -> 36.2 us  [sum_rep(): other = lax.ppermute(low, 'rep', [(0, 1), (1, 0)])]
  transfers between devices with their start and end apart: 14 -> 12, of which waited for: 9 -> 4; matrix products, arithmetic and copies ran while one was open for 3% -> 4% of each run, Pallas kernels for 10% -> 45%
where the time goes in v3:
time: 927 us; the launch traced here: 925 us
  Pallas kernels  585 us (63%)
  waiting for transfers between devices  135 us (15%)
  blocking collectives  109 us (12%)
  starting transfers between devices  30.6 us (3%)
  other arithmetic  28.5 us (3%)
  local copies, waits for them, and re-layouts  19.9 us (2%)
  between operations  14.7 us (2%)
    pallas_call x2, Pallas kernels, scatter(): pl.pallas_call(functools.partial(scatter_kernel, dims=dims, chunks=chunks...  238 us
    pallas_call x4, Pallas kernels, call(): pl.pallas_call(kernel, grid=grid, in_specs=in_specs, out_specs=out_specs,...  218 us
    pallas_call x2, Pallas kernels, allsum(): pl.pallas_call(functools.partial(allsum_kernel, dims=dims, chunks=chunks,...  129 us
    all_gather x1, blocking collectives, on_device(): ids = lax.all_gather(segment_ids, 'shard')  79.8 us
    all_gather x1, waiting for transfers between devices, on_device(): nu_all = lax.all_gather(nu, 'shard')  64.2 us
    ppermute x4, waiting for transfers between devices, sum_rep(): other = lax.ppermute(low, 'rep', [(0, 1), (1, 0)])  36.2 us
    all_gather x1, waiting for transfers between devices, on_device(): dy_all = lax.all_gather(out_grad.reshape(w, d), 'shard')  34.1 us
    all_gather x1, blocking collectives, on_device(): gain = w32(lax.all_gather(norm_gain, 'shard', axis=0, tiled=True))  23.2 us
  transfers between devices with their start and end apart: 12, of which 4 were waited for; matrix products, arithmetic and copies ran while one was open for 4% of the time, Pallas kernels for 45%

profile of v3, /device:TPU:0, one launch (start us, length us, event | category | flops | bytes accessed | tf_op | source)
XLA Modules:
  0.0 925.1 jit_solution(10750723669616569923)
XLA Ops:
  7.2 23.2 %all-gather.2 = bf16[16,1,128]{2,1,0:T(2,128)(2,1)S(1)} all-gather(bf16[1,1,128]{2,1,0:T(2,128)(2,1)} %bitcast.135), channel_id=1, replica_groups=mesh['rep'=2,'shard'=16] {'shard'}, dimensions={0}, use_global_device_ids=true | all-gather | bytes 4352 | tf_op jit(solution)/shard_map/all_gather | solution.py:550
  30.4 1.5 fusion
  32.5 2.7 fusion.2
  35.2 0.7 all-gather.9.cloned.1.call-update
  36.5 2.0 copy.57
  38.6 2.6 all_to_all.19
  41.2 3.9 all-to-all-start
  45.1 79.8 %all-gather.3 = s32[16,2,128]{2,1,0:T(2,128)S(1)} all-gather(s32[1,2,128]{2,1,0:T(2,128)S(1)} %bitcast.124), channel_id=2, replica_groups=mesh['rep'=2,'shard'=16] {'shard'}, dimensions={0}, use_global_device_ids=true | all-gather | bytes 17408 | tf_op jit(solution)/shard_map/all_gather | solution.py:559
  124.9 3.6 collective-permute-start.1
  133.0 64.2 %all-gather.7.cloned.1.call-done.nu_ref = bf16[16,256,2048]{2,1,0:T(8,128)(2,1)} async-done(((bf16[1,256,2048]{2,1,0:T(8,128)(2,1)}), bf16[16,256,2048]{2,1,0:T(8,128)(2,1)}) %all-gather.7.cloned.1.call-update) | async-done | bytes 16777232 | tf_op jit(solution)/shard_map/all_gather | solution.py:554
  197.2 1.2 slice-done
  198.5 3.4 collective-permute-start
  202.4 1.9 copy.61
  204.4 1.3 copy-done.9
  205.7 22.0 %shard_map.220 = (bf16[16,256,512]{2,1,0:T(8,128)(2,1)}, bf16[16,256,256]{2,1,0:T(8,128)(2,1)}, f32[16,160,256]{2,1,0:T(8,128)}, bf16[16,256]{1,0:T(8,128)(2,1)}) custom-call(bf16[16,256,2048]{2,1,0:T(8,128)(2,1)} %all-gather.7.cloned.1.call-done.nu_ref, bf16[2048,512]{1,0:T(8,128)(2,1)} %bitcast.102, bf16[16,2048]{1,0:T(8,128)(2,1)} %copy-done.34, ...), custom_call_target="tpu_custom_call" | custom-call | flops 8589934592 | bytes 28079104 | tf_op jit(solution)/shard_map/pallas_call | solution.py:41
  227.7 76.8 %shard_map.221 = bf16[4,2,2,256,256]{4,3,2,1,0:T(8,128)(2,1)} custom-call(f32[4,2,2,160,256]{4,3,2,1,0:T(8,128)} %bitcast.98), custom_call_target="tpu_custom_call" | custom-call | tf_op jit(solution)/shard_map/pallas_call | solution.py:199
  304.5 1.0 slice.137
  305.5 34.1 %all-gather.9.cloned.1.call-done.dy_ref = bf16[16,256,2048]{2,1,0:T(8,128)(2,1)} async-done(((bf16[1,256,2048]{2,1,0:T(8,128)(2,1)}), bf16[16,256,2048]{2,1,0:T(8,128)(2,1)}) %all-gather.9.cloned.1.call-update) | async-done | bytes 16777232 | tf_op jit(solution)/shard_map/all_gather | solution.py:555
  339.7 47.4 %shard_map.222 = (f32[16,2,16,256]{3,2,1,0:T(8,128)}, f32[16,2,16,256]{3,2,1,0:T(8,128)}, f32[3,2,16,256]{3,2,1,0:T(8,128)}, f32[16,256,256]{2,1,0:T(8,128)}) custom-call(bf16[16,256,256]{2,1,0:T(8,128)(2,1)} %bitcast.108, bf16[16,256,512]{2,1,0:T(8,128)(2,1)} %get-tuple-element.33.xz_ref.prev_ref, bf16[16,256,256]{2,1,0:T(8,128)(2,1)} %get-tuple-element.34.xc_ref, ...), custom_call_target="tpu_custom_call" | custom-call | flops 40000000000 | bytes 31769600 | tf_op jit(solution)/shard_map/pallas_call | solution.py:41
  387.0 6.0 all-gather.1
  393.7 118.2 %shard_map.223 = (bf16[16,256,2048]{2,1,0:T(8,128)(2,1)}, bf16[16,256,256]{2,1,0:T(8,128)(2,1)}, f32[16,256,256]{2,1,0:T(8,128)}, f32[16,160,256]{2,1,0:T(8,128)...) custom-call(bf16[16,256,256]{2,1,0:T(8,128)(2,1)} %bitcast.109, ...), custom_call_target="tpu_custom_call" | custom-call | flops 99999997952 | bytes 78555136 | tf_op jit(solution)/shard_map/pallas_call | solution.py:41
  511.9 2.7 convert_element_type.100
  514.6 1.5 collective-permute-start.6
  516.3 51.7 %shard_map.225 = bf16[4,2,2,256,256]{4,3,2,1,0:T(8,128)(2,1)} custom-call(f32[4,2,2,160,256]{4,3,2,1,0:T(8,128)} %bitcast.97), custom_call_target="tpu_custom_call" | custom-call | tf_op jit(solution)/shard_map/pallas_call | solution.py:199
  568.0 0.9 slice.168
  568.9 1.0 slice.132
  570.7 1.3 collective-permute-start.2
  572.0 1.1 convert_element_type.93
  573.1 6.4 all-to-all-start.2
  579.5 118.9 %shard_map.224 = f32[256,2048]{1,0:T(8,128)} custom-call(bf16[4,2,2,256,2048]{4,3,2,1,0:T(8,128)(2,1)} %bitcast.136), custom_call_target="tpu_custom_call" | custom-call | flops 80000000000 | bytes 16777216 | tf_op jit(solution)/shard_map/pallas_call | solution.py:288
  699.1 30.7 %shard_map.226 = (bf16[16,256,2048]{2,1,0:T(8,128)(2,1)}, f32[2048,256]{1,0:T(8,128)}, f32[8,256]{1,0:T(8,128)}) custom-call(bf16[16,256,512]{2,1,0:T(8,128)(2,1)} %get-tuple-element.33.xz_ref.prev_ref, bf16[16,256,512]{2,1,0:T(8,128)(2,1)} %get-tuple-element.33.xz_ref.prev_ref, f32[16,256]{1,0:T(8,128)} %get-tuple-element.71.edge_ref, ...), custom_call_target="tpu_custom_call" | custom-call | flops 12884901888 | bytes 54866944 | tf_op jit(solution)/shard_map/pallas_call | solution.py:41
  729.8 0.7 constant_dynamic-update-slice_fusion.1
  730.5 2.5 fusion.7
  733.0 2.7 collective-permute-start.5
  735.8 1.1 convert_element_type.90
  736.8 5.9 all-to-all-start.1
  742.7 118.8 %shard_map.227 = f32[256,2048]{1,0:T(8,128)} custom-call(bf16[4,2,2,256,2048]{4,3,2,1,0:T(8,128)(2,1)} %bitcast.137), custom_call_target="tpu_custom_call" | custom-call | flops 80000000000 | bytes 16777216 | tf_op jit(solution)/shard_map/pallas_call | solution.py:288
  861.6 2.1 fusion.6
  864.0 2.5 fusion.5
  866.5 1.1 copy.65
  867.6 1.1 convert_add_fusion.4
  871.2 0.7 slice_bitcast_fusion
  871.9 1.9 collective-permute-start.3
  873.9 2.8 convert_add_fusion.1
  876.7 17.3 %collective-permute-done.4 = bf16[128,4096]{1,0:T(8,128)(2,1)} collective-permute-done((bf16[128,4096]{1,0:T(8,128)(2,1)}, bf16[128,4096]{1,0:T(8,128)(2,1)}, u32[]{:S(2)}, u32[]{:S(2)}) %collective-permute-start.4) | collective-permute-done | bytes 1048608 | tf_op jit(solution)/shard_map/ppermute | solution.py:532
  894.0 1.8 convert_add_fusion.2
  895.8 18.9 %collective-permute-done.3 = bf16[128,4096]{1,0:T(8,128)(2,1)S(1)} collective-permute-done((bf16[128,4096]{1,0:T(8,128)(2,1)S(1)}, bf16[128,4096]{1,0:T(8,128)(2,1)S(1)}, u32[]{:S(2)}, u32[]{:S(2)}) %collective-permute-start.3) | collective-permute-done | bytes 1048608 | tf_op jit(solution)/shard_map/ppermute | solution.py:532
  915.0 2.7 multiply_reduce_fusion
  (129 shorter events, 12.2 us)
Async XLA Ops:
  7.2 190.1 %all-gather.7.cloned.1.call-start = ((), (), s32[]{:S(2)}) async-start(), calls=%async_computation.3 | async-start | bytes 17825792 | tf_op jit(solution)/shard_map/all_gather | solution.py:554
  32.5 2.7 copy-start.20
  32.5 3.4 copy-start.2
  35.2 304.5 %all-gather.9.cloned.1.call-start = ((), (), s32[]{:S(2)}) async-start(), calls=%async_computation.4 | async-start | bytes 17825792 | tf_op jit(solution)/shard_map/all_gather | solution.py:555
  41.2 3.9 copy-start.25
  41.2 87.3 %copy-start.36 = (bf16[256]{0:T(256)(128)(2,1)S(1)}, bf16[256]{0:T(256)(128)(2,1)}, u32[]{:S(2)}) copy-start(bf16[256]{0:T(256)(128)(2,1)} %param.19) | copy-start | bytes 1540
  41.2 87.9 %copy-start.18 = (bf16[4,256]{1,0:T(4,128)(2,1)S(1)}, bf16[4,256]{1,0:T(4,128)(2,1)}, u32[]{:S(2)}) copy-start(bf16[4,256]{1,0:T(4,128)(2,1)} %param.18) | copy-start | bytes 6148
  41.2 88.5 %copy-start.37 = (bf16[256]{0:T(256)(128)(2,1)S(1)}, bf16[256]{0:T(256)(128)(2,1)}, u32[]{:S(2)}) copy-start(bf16[256]{0:T(256)(128)(2,1)} %param.22) | copy-start | bytes 1540
  41.2 89.1 %copy-start.38 = (bf16[256]{0:T(256)(128)(2,1)S(1)}, bf16[256]{0:T(256)(128)(2,1)}, u32[]{:S(2)}) copy-start(bf16[256]{0:T(256)(128)(2,1)} %param.24) | copy-start | bytes 1540
  41.2 89.6 %copy-start.14 = (bf16[256,160]{0,1:T(8,128)(2,1)S(1)}, bf16[256,160]{0,1:T(8,128)(2,1)}, u32[]{:S(2)}) copy-start(bf16[256,160]{0,1:T(8,128)(2,1)} %param.20) | copy-start | bytes 245764
  41.2 90.8 %copy-start.16 = (bf16[16,256]{1,0:T(8,128)(2,1)S(1)}, bf16[16,256]{1,0:T(8,128)(2,1)}, u32[]{:S(2)}) copy-start(bf16[16,256]{1,0:T(8,128)(2,1)} %param.23) | copy-start | bytes 24580
  41.2 163.1 %all-to-all-start = ((bf16[16,128,512]{2,1,0:T(8,128)(2,1)}), bf16[16,128,512]{2,1,0:T(8,128)(2,1)S(1)}, u32[]{:S(2)}, u32[]{:S(2)}) async-start(bf16[16,128,512]{2,1,0:T(8,128)(2,1)} %all_to_all.19), calls=%async_computation | async-start | bytes 4194304 | tf_op jit(solution)/shard_map/all_to_all | solution.py:557
  124.9 7.7 collective-permute-start.1
  198.5 5.9 collective-permute-start
  514.6 359.2 %collective-permute-start.6 = (bf16[256,2048]{1,0:T(8,128)(2,1)}, bf16[256,2048]{1,0:T(8,128)(2,1)}, u32[]{:S(2)}, u32[]{:S(2)}) collective-permute-start(bf16[256,2048]{1,0:T(8,128)(2,1)} %convert_element_type.100), channel_id=1, source_target_pairs={{0,16},{16,0},{1,17},{17,1},{2,18},{18,2},{3,19},{19,3},{4,20},{20... | collective-permute-start | bytes 3145736 | tf_op jit(solution)/shard_map/ppermute | solution.py:532
  516.2 53.7 %copy-start.22 = (bf16[16,256]{1,0:T(8,128)(2,1)S(1)}, bf16[16,256]{1,0:T(8,128)(2,1)}, u32[]{:S(2)}) copy-start(bf16[16,256]{1,0:T(8,128)(2,1)} %get-tuple-element.40) | copy-start | bytes 24580
  516.2 54.3 %copy-start.15 = (bf16[256,160]{0,1:T(8,128)(2,1)S(1)}, bf16[256,160]{0,1:T(8,128)(2,1)}, u32[]{:S(2)}) copy-start(bf16[256,160]{0,1:T(8,128)(2,1)} %param.20) | copy-start | bytes 245764
  516.2 54.3 %copy-start.26 = (f32[2,8,1]{1,2,0:T(1,128)S(1)}, f32[2,8,1]{1,2,0:T(1,128)}, u32[]{:S(2)}) copy-start(f32[2,8,1]{1,2,0:T(1,128)} %get-tuple-element.67) | copy-start | bytes 196
  516.2 54.3 %copy-start.27 = (f32[2,8,1]{1,2,0:T(1,128)S(1)}, f32[2,8,1]{1,2,0:T(1,128)}, u32[]{:S(2)}) copy-start(f32[2,8,1]{1,2,0:T(1,128)} %get-tuple-element.68) | copy-start | bytes 196
  516.2 54.3 %copy-start.28 = (f32[2,8,1]{1,2,0:T(1,128)S(1)}, f32[2,8,1]{1,2,0:T(1,128)}, u32[]{:S(2)}) copy-start(f32[2,8,1]{1,2,0:T(1,128)} %get-tuple-element.69) | copy-start | bytes 196
  516.2 54.3 %copy-start.29 = (f32[1,256]{1,0:T(1,128)S(1)}, f32[1,256]{1,0:T(1,128)}, u32[]{:S(2)}) copy-start(f32[1,256]{1,0:T(1,128)} %get-tuple-element.72) | copy-start | bytes 3076
  516.2 54.3 %copy-start.30 = (f32[1,256]{1,0:T(1,128)S(1)}, f32[1,256]{1,0:T(1,128)}, u32[]{:S(2)}) copy-start(f32[1,256]{1,0:T(1,128)} %get-tuple-element.73) | copy-start | bytes 3076
  516.2 54.3 %copy-start.31 = (f32[1,256]{1,0:T(1,128)S(1)}, f32[1,256]{1,0:T(1,128)}, u32[]{:S(2)}) copy-start(f32[1,256]{1,0:T(1,128)} %get-tuple-element.74) | copy-start | bytes 3076
  516.2 54.3 %copy-start.32 = (f32[1,256]{1,0:T(1,128)S(1)}, f32[1,256]{1,0:T(1,128)}, u32[]{:S(2)}) copy-start(f32[1,256]{1,0:T(1,128)} %get-tuple-element.75) | copy-start | bytes 3076
  516.2 54.3 %copy-start.39 = (f32[256]{0:T(256)S(1)}, f32[256]{0:T(256)}, u32[]{:S(2)}) copy-start(f32[256]{0:T(256)} %convert_element_type.84) | copy-start | bytes 3076
  516.2 55.8 %copy-start.7 = (f32[2048,256]{1,0:T(8,128)S(1)}, f32[2048,256]{1,0:T(8,128)}, u32[]{:S(2)}) copy-start(f32[2048,256]{1,0:T(8,128)} %get-tuple-element.46) | copy-start | bytes 6291460
  570.7 127.7 %collective-permute-start.2 = (f32[3,2,8,256]{3,2,1,0:T(8,128)S(1)}, f32[3,2,8,256]{3,2,1,0:T(8,128)S(1)}, u32[]{:S(2)}, u32[]{:S(2)}) collective-permute-start(f32[3,2,8,256]{3,2,1,0:T(8,128)S(1)} %pad_maximum_fusion.1), channel_id=1, source_target_pairs={{16,0},{17,1},{18,2},{19,3},{20,4},{21,5},{22,6},{23,7},{24,8},{25... | collective-permute-start | bytes 147464 | tf_op jit(solution)/shard_map/ppermute | solution.py:525
  573.1 163.7 %all-to-all-start.2 = ((bf16[16,128,256]{2,1,0:T(8,128)(2,1)}), bf16[16,128,256]{2,1,0:T(8,128)(2,1)S(1)}, u32[]{:S(2)}, u32[]{:S(2)}) async-start(bf16[16,128,256]{2,1,0:T(8,128)(2,1)} %bitcast.52), calls=%async_computation.2 | async-start | bytes 2097152 | tf_op jit(solution)/shard_map/all_to_all | solution.py:642
  579.5 118.9 %copy-start.23 = (f32[8,256]{1,0:T(8,128)S(1)}, f32[8,256]{1,0:T(8,128)}, u32[]{:S(2)}) copy-start(f32[8,256]{1,0:T(8,128)} %get-tuple-element.47) | copy-start | bytes 24580
  699.1 31.4 %copy-start.17 = (bf16[16,256]{1,0:T(8,128)(2,1)S(1)}, bf16[16,256]{1,0:T(8,128)(2,1)}, u32[]{:S(2)}) copy-start(bf16[16,256]{1,0:T(8,128)(2,1)} %param.23) | copy-start | bytes 24580
  699.1 31.4 %copy-start.19 = (f32[16,256]{1,0:T(8,128)S(1)}, f32[16,256]{1,0:T(8,128)}, u32[]{:S(2)}) copy-start(f32[16,256]{1,0:T(8,128)} %get-tuple-element.49) | copy-start | bytes 49156
  699.1 31.4 %copy-start.13 = (f32[128,256]{1,0:T(8,128)S(1)}, f32[128,256]{1,0:T(8,128)}, u32[]{:S(2)}) copy-start(f32[128,256]{1,0:T(8,128)} %get-tuple-element.50) | copy-start | bytes 393220
  699.1 31.4 %copy-start.6 = (bf16[4,2,2,256,256]{4,3,2,1,0:T(8,128)(2,1)S(1)}, bf16[4,2,2,256,256]{4,3,2,1,0:T(8,128)(2,1)}, u32[]{:S(2)}) copy-start(bf16[4,2,2,256,256]{4,3,2,1,0:T(8,128)(2,1)} %shard_map.225) | copy-start | bytes 6291460
  730.5 5.2 copy-start.8
  733.0 134.6 %collective-permute-start.5 = (bf16[416,256]{1,0:T(8,128)(2,1)S(1)}, bf16[416,256]{1,0:T(8,128)(2,1)}, u32[]{:S(2)}, u32[]{:S(2)}) collective-permute-start(bf16[416,256]{1,0:T(8,128)(2,1)S(1)} %fusion.7), channel_id=1, source_target_pairs={{0,16},{16,0},{1,17},{17,1},{2,18},{18,2},{3,19},{19,3},{4,20},{20... | collective-permute-start | bytes 638984 | tf_op jit(solution)/shard_map/ppermute | solution.py:532
  736.8 135.0 %all-to-all-start.1 = ((bf16[16,128,256]{2,1,0:T(8,128)(2,1)}), bf16[16,128,256]{2,1,0:T(8,128)(2,1)S(1)}, u32[]{:S(2)}, u32[]{:S(2)}) async-start(bf16[16,128,256]{2,1,0:T(8,128)(2,1)} %bitcast.50), calls=%async_computation.1 | async-start | bytes 2097152 | tf_op jit(solution)/shard_map/all_to_all | solution.py:642
  742.7 118.9 %copy-start = (bf16[2,128,2048]{2,1,0:T(8,128)(2,1)S(1)}, bf16[2,128,2048]{2,1,0:T(8,128)(2,1)}, u32[]{:S(2)}) copy-start(bf16[2,128,2048]{2,1,0:T(8,128)(2,1)} %param.13) | copy-start | bytes 3145732
  742.7 118.9 %copy-start.12 = (f32[16,1,128]{2,1,0:T(1,128)S(1)}, f32[16,1,128]{2,1,0:T(1,128)}, u32[]{:S(2)}) copy-start(f32[16,1,128]{2,1,0:T(1,128)} %copy-done.11) | copy-start | bytes 24580
  742.7 121.0 %copy-start.10 = (f32[256,2048]{1,0:T(8,128)S(1)}, f32[256,2048]{1,0:T(8,128)}, u32[]{:S(2)}) copy-start(f32[256,2048]{1,0:T(8,128)} %shard_map.224) | copy-start | bytes 6291460
  861.5 2.2 copy-start.4
  861.6 2.5 copy-start.5
  861.6 2.5 copy-start.21
  861.6 2.5 copy-start.24
  867.6 6.3 copy-start.1
  867.6 26.4 %collective-permute-start.4 = (bf16[128,4096]{1,0:T(8,128)(2,1)}, bf16[128,4096]{1,0:T(8,128)(2,1)}, u32[]{:S(2)}, u32[]{:S(2)}) collective-permute-start(bf16[128,4096]{1,0:T(8,128)(2,1)} %bitcast.63), channel_id=1, source_target_pairs={{0,16},{16,0},{1,17},{17,1},{2,18},{18,2},{3,19},{19,3},{4,20},{20... | collective-permute-start | bytes 3145736 | tf_op jit(solution)/shard_map/ppermute | solution.py:532
  871.9 42.8 %collective-permute-start.3 = (bf16[128,4096]{1,0:T(8,128)(2,1)S(1)}, bf16[128,4096]{1,0:T(8,128)(2,1)S(1)}, u32[]{:S(2)}, u32[]{:S(2)}) collective-permute-start(bf16[128,4096]{1,0:T(8,128)(2,1)S(1)} %bitcast.95), channel_id=1, source_target_pairs={{0,16},{16,0},{1,17},{17,1},{2,18},{18,2},{3,19},{19,3},{4,20},{20... | collective-permute-start | bytes 3145736 | tf_op jit(solution)/shard_map/ppermute | solution.py:532
  895.8 19.2 %copy-start.3 = (bf16[128,8192]{1,0:T(8,128)(2,1)S(1)}, bf16[128,8192]{1,0:T(8,128)(2,1)}, u32[]{:S(2)}) copy-start(bf16[128,8192]{1,0:T(8,128)(2,1)} %param.17) | copy-start | bytes 6291460
  915.0 2.7 copy-start.33
  (5 other events, 6.6 us)
Sparse Core Ops, SparseCore 0:
  35.3 161.8 all-gather.6
  199.4 140.2 all-gather.8

commit v4 on v3

--- a/solution.py
+++ b/solution.py
@@ -36,11 +36,11 @@
     return pl.ds(pl.multiple_of(start, unit), size)
 
 
-def call(kernel, grid, in_specs, out_specs, out_shape, scratch, args, flops=0):
+def call(kernel, grid, in_specs, out_specs, out_shape, scratch, args, flops=0, **params):
     size = sum(a.size * a.dtype.itemsize for a in args) + sum(s.size * s.dtype.itemsize for s in out_shape)
     return pl.pallas_call(
         kernel, grid=grid, in_specs=in_specs, out_specs=out_specs, out_shape=out_shape,
-        scratch_shapes=scratch, compiler_params=pltpu.CompilerParams(vmem_limit_bytes=VMEM),
+        scratch_shapes=scratch, compiler_params=pltpu.CompilerParams(vmem_limit_bytes=VMEM, **params),
         cost_estimate=pl.CostEstimate(flops=flops, bytes_accessed=size, transcendentals=0))(*args)
 
 
@@ -63,13 +63,21 @@
     return out
 
 
-def front(nu_ref, w_ref, halo_ref, mask_ref, cw_ref, cb_ref, xp_ref, xz_ref, xc_ref, part_ref, edge_ref, carry, *, m, e):
+def normalise(rows, gain):
+    u = rows.astype(F32)
+    return (u * lax.rsqrt(jnp.mean(u * u, axis=1, keepdims=True) + 1e-5) * gain).astype(BF16)
+
+
+def front(hid_ref, w_ref, halo_ref, mask_ref, cw_ref, cb_ref, xp_ref, gain_ref, xz_ref, xc_ref, part_ref, nu_ref, edge_ref,
+          carry, *, m, e):
     @pl.when(pl.program_id(0) == 0)
     def _():
-        edge = mm(halo_ref[...], w_ref[:, :e]).astype(BF16)
+        edge = mm(normalise(halo_ref[...], gain_ref[...]), w_ref[:, :e]).astype(BF16)
         edge_ref[...] = edge
         carry[...] = edge.astype(F32)
-    xz = mm(nu_ref[0], w_ref[...]).astype(BF16)
+    nu = normalise(hid_ref[0], gain_ref[...])
+    nu_ref[0] = nu
+    xz = mm(nu, w_ref[...]).astype(BF16)
     xz_ref[0] = xz
     rows = xz.shape[0] // m
     cw, cb = cw_ref[...], cb_ref[...]
@@ -208,6 +216,158 @@
         compiler_params=pltpu.CompilerParams(collective_id=collective_id, has_side_effects=True, vmem_limit_bytes=VMEM),
     )(part.reshape(nz, ny, nc, cols, w))
     return out.reshape(peers, w, 256)
+
+
+def gather_kernel(x, small, out, small_out, send, recv, s_send, s_recv, own_sem, *, dims, chunks):
+    nz, ny, _ = dims
+    me = lax.axis_index("shard")
+    c, y, z = me % 2, (me // 2) % ny, me // (2 * ny)
+    where = lambda a, b, d: (a * ny + b) * 2 + d
+    across = where(z, y, 1 - c)
+    ys = [lax.rem(y + k, ny) for k in range(1, ny)]
+    ys_from = [lax.rem(y + ny - k, ny) for k in range(1, ny)]
+    zs = [lax.rem(z + k, nz) for k in range(1, nz)]
+    greet([across] + [where(z, b, c) for b in ys] + [where(a, y, c) for a in zs])
+    size = x.shape[0] // chunks
+    rows = [pl.ds(q * size, size) for q in range(chunks)]
+
+    keep = pltpu.make_async_copy(small, small_out.at[z, y, c], own_sem.at[0])
+    keep.start()
+    whole_own = pltpu.make_async_copy(x, out.at[z, y, c], own_sem.at[1])
+    whole_own.start()
+
+    kinds = 2 * nz - 1
+    offset = [0] + [-1 - j for j in range(nz - 1)] + [1 + j for j in range(nz - 1)]
+
+    def valid(kind):
+        return (z + offset[kind] >= 0) & (z + offset[kind] < nz)
+
+    def sems(group, kind, q):
+        at_ = (group * kinds + kind) * chunks + q
+        return send.at[at_], recv.at[at_]
+
+    def hop(kind, q, up):
+        there = out.at[z + offset[kind], y, c, rows[q]]
+        src = x.at[rows[q]] if kind == 0 else there
+        j = -offset[kind] if up else offset[kind]
+        to_kind = 1 + j if up else nz + j
+        return remote(src, there, *sems(0, to_kind, q), where(z + 1 if up else z - 1, y, c))
+
+    def can_hop(kind, up):
+        return valid(kind) & ((z + 1 < nz) if up else (z >= 1))
+
+    def over_y(kind, q, k):
+        there = out.at[z + offset[kind], y, c, rows[q]]
+        src = x.at[rows[q]] if kind == 0 else there
+        return remote(src, there, *sems(1 + k, kind, q), where(z, ys[k], c))
+
+    def over_core(kind, q, k):
+        there = out.at[z + offset[kind], y if k == 0 else ys_from[k - 1], c, rows[q]]
+        src = x.at[rows[q]] if kind == 0 and k == 0 else there
+        return remote(src, there, *sems(ny + k, kind, q), across)
+
+    def landed(kind, q, b, d, group):
+        there = out.at[z + offset[kind], b, d, rows[q]]
+        return remote(there, there, *sems(group, kind, q), across)
+
+    def onward(kind, q):
+        if kind == 0:
+            ups = [True, False]
+        elif kind < nz:
+            ups = [True] if kind < nz - 1 else []
+        else:
+            ups = [False] if kind < kinds - 1 else []
+        for up in ups:
+            @pl.when(can_hop(kind, up))
+            def _(up=up):
+                hop(kind, q, up).start()
+        for k in range(ny - 1):
+            over_y(kind, q, k).start()
+        over_core(kind, q, 0).start()
+
+    tiny = []
+
+    def tiny_start(copies):
+        tiny.append(copies)
+        for copy in copies:
+            copy.start()
+
+    def tiny_wait():
+        for copy in tiny[-1]:
+            copy.wait()
+
+    tiny_start([remote(small, small_out.at[z, y, c], s_send.at[k], s_recv.at[k], where(a, y, c)) for k, a in enumerate(zs)])
+    for q in range(chunks):
+        onward(0, q)
+    tiny_wait()
+    keep.wait()
+    tiny_start([remote(small_out.at[:, y, c], small_out.at[:, y, c], s_send.at[nz - 1 + k], s_recv.at[nz - 1 + k], where(z, b, c))
+                for k, b in enumerate(ys)])
+
+    def from_y(kind, q):
+        @pl.when(valid(kind))
+        def _():
+            for k in range(1, ny):
+                landed(kind, q, ys_from[k - 1], c, k).wait_recv()
+                over_core(kind, q, k).start()
+
+    waves = [[0]] + [[1 + j, nz + j] for j in range(nz - 1)]
+    for number, wave in enumerate(waves):
+        for q in range(chunks):
+            for kind in wave:
+                if kind:
+                    @pl.when(valid(kind))
+                    def _(kind=kind, q=q):
+                        landed(kind, q, y, c, 0).wait_recv()
+                        onward(kind, q)
+        if number == 1:
+            tiny_wait()
+            last = small_out.at[:, :, c]
+            tiny_start([remote(last, last, s_send.at[nz + ny - 2], s_recv.at[nz + ny - 2], across)])
+        if number:
+            for q in range(chunks):
+                for kind in waves[number - 1]:
+                    from_y(kind, q)
+    for q in range(chunks):
+        for kind in waves[-1]:
+            from_y(kind, q)
+    tiny_wait()
+    for kind in range(kinds):
+        @pl.when(valid(kind))
+        def _(kind=kind):
+            for q in range(chunks):
+                for k in range(ny):
+                    landed(kind, q, y if k == 0 else ys_from[k - 1], 1 - c, ny + k).wait_recv()
+                    over_core(kind, q, k).wait_send()
+                for k in range(ny - 1):
+                    over_y(kind, q, k).wait_send()
+        for up in (True, False):
+            j = -offset[kind] if up else offset[kind]
+            if 0 <= j < nz - 1:
+                @pl.when(can_hop(kind, up))
+                def _(kind=kind, up=up):
+                    for q in range(chunks):
+                        hop(kind, q, up).wait_send()
+    whole_own.wait()
+
+
+def gather(x, small, collective_id, chunks=4):
+    w, d = x.shape
+    peers = lax.axis_size("shard")
+    dims = lattice(peers)
+    nz, ny, nc = dims
+    copies = 2 * ny * (2 * nz - 1) * chunks
+    out, tiles = pl.pallas_call(
+        functools.partial(gather_kernel, dims=dims, chunks=chunks),
+        out_shape=[jax.ShapeDtypeStruct((nz, ny, nc, w, d), x.dtype), jax.ShapeDtypeStruct((nz, ny, nc, 8, 128), F32)],
+        in_specs=[pl.BlockSpec(memory_space=pl.ANY), pl.BlockSpec(memory_space=pltpu.VMEM)],
+        out_specs=[pl.BlockSpec(memory_space=pl.ANY), pl.BlockSpec(memory_space=pltpu.VMEM)],
+        scratch_shapes=[pltpu.SemaphoreType.DMA((copies,)), pltpu.SemaphoreType.DMA((copies,)),
+                        pltpu.SemaphoreType.DMA((nz + ny,)), pltpu.SemaphoreType.DMA((nz + ny,)), pltpu.SemaphoreType.DMA((2,))],
+        compiler_params=pltpu.CompilerParams(collective_id=collective_id, has_side_effects=True, vmem_limit_bytes=VMEM),
+        cost_estimate=pl.CostEstimate(flops=8 * 10 ** 10, bytes_accessed=2 * peers * w * d, transcendentals=0),
+    )(x, small)
+    return out.reshape(peers, w, d), tiles.reshape(peers, 8, 128)
 
 
 def scatter_kernel(part, out, own, rc, ry, rz, load, send, recv, *, dims, chunks):
@@ -378,6 +538,7 @@
     b = pl.program_id(0)
     @pl.when(b == 0)
     def _():
+        greet([lax.axis_index("shard") + 1 - 2 * (lax.axis_index("shard") % 2)])
         q_scr[...] = qin_ref[...]
         for ref in (go_ref, gdt_ref, ga_ref, vec_ref, gz_ref):
             ref[...] = jnp.zeros_like(ref)
@@ -547,32 +708,35 @@
     rising = lambda i: i
     falling = lambda i: peers - 1 - i
 
-    gain = w32(lax.all_gather(norm_gain, "shard", axis=0, tiled=True))
+    own = jnp.pad(jnp.concatenate([w32(segment_ids), jnp.pad(w32(norm_gain)[None], ((0, 0), (0, 128 - dl)))], axis=0),
+                  ((0, 7 - m), (0, 0)))
+    w_split = in_proj.reshape(dl, 2, peers, e).transpose(2, 0, 1, 3).reshape(peers * dl, 2 * e)
+    own, w_split = lax.optimization_barrier((own, w_split))
+    w_cols = lax.all_to_all(w_split, "shard", 0, 0, tiled=True)
+    hid_all, tiles = gather(hidden_in.reshape(w, d), own, 4)
+    gain = tiles[:, m, :dl].reshape(1, d)
+    ids = tiles[:, :m, :tl].astype(jnp.int32)
+    later, hid_all = lax.optimization_barrier((out_grad, hid_all))
+    dy_all = lax.all_gather(later.reshape(w, d), "shard")
     u = w32(hidden_in)
     r = lax.rsqrt(jnp.mean(u * u, axis=2, keepdims=True) + 1e-5)
-    nu = (u * r * gain).astype(BF16).reshape(w, d)
-    nu_all = lax.all_gather(nu, "shard")
-    dy_all = lax.all_gather(out_grad.reshape(w, d), "shard")
-    w_split = in_proj.reshape(dl, 2, peers, e).transpose(2, 0, 1, 3).reshape(peers * dl, 2 * e)
-    w_cols = lax.all_to_all(w_split, "shard", 0, 0, tiled=True)
-
-    ids = lax.all_gather(segment_ids, "shard")
+
     row_ids = ids.transpose(1, 0, 2).reshape(m, t)
     before = jnp.where(rep > 0, shift_rep(row_ids[:, t - taps + 1:], 1), -1)
     ext = jnp.concatenate([before, row_ids], axis=1)
     same = jnp.stack([w32(ext[:, taps - 1 - k:taps - 1 - k + t] == row_ids) for k in range(1, taps)], axis=-1)
     mask = jnp.pad(same, ((0, 0), (0, 0), (0, 8 - same.shape[-1])))
     mask = mask.reshape(m, peers, tl, 8).transpose(1, 0, 2, 3).reshape(peers, w, 8)
-    halo = shift_rep(nu_all[peers - 1].reshape(m, tl, d)[:, tl - EDGE:].reshape(m * EDGE, d), 1)
+    halo = shift_rep(hid_all[peers - 1].reshape(m, tl, d)[:, tl - EDGE:].reshape(m * EDGE, d), 1)
 
     cw, cb = w32(conv_weight), w32(conv_bias)[None]
-    ins = [nu_all, w_cols, halo, mask, cw, cb, x_proj.T]
+    ins = [hid_all, w_cols, halo, mask, cw, cb, x_proj.T, gain]
     outs = [shp((peers, w, 2 * e), BF16), shp((peers, w, e), BF16), shp((peers, rank + 2 * n, w), F32),
-            shp((m * EDGE, e), BF16)]
-    xz, xc, part, edge = call(
+            shp((peers, w, d), BF16), shp((m * EDGE, e), BF16)]
+    xz, xc, part, nu_all, edge = call(
         functools.partial(front, m=m, e=e), (peers,),
-        [block(nu_all, rising)] + [whole(a) for a in ins[1:3]] + [block(mask, rising)] + [whole(a) for a in ins[4:]],
-        [block(a, rising) for a in outs[:3]] + [whole(outs[3])], outs,
+        [block(hid_all, rising)] + [whole(a) for a in ins[1:3]] + [block(mask, rising)] + [whole(a) for a in ins[4:]],
+        [block(a, rising) for a in outs[:4]] + [whole(outs[4])], outs,
         [pltpu.VMEM((m * EDGE, e), F32)], ins, flops=2 * peers * w * d * 2 * e)
 
     low = allsum(part, functools.partial(spread_low, n=n), 0)
@@ -606,7 +770,7 @@
         [block(a, falling) for a in ins[:9]] + [whole(a) for a in ins[9:]],
         [block(a, falling) for a in outs[:4]] + [whole(a) for a in outs[4:]], outs,
         [pltpu.VMEM((tl * n + n, e), F32), pltpu.VMEM((tl * n, e), F32), pltpu.VMEM((m, n, e), F32),
-         pltpu.VMEM((w, 128), F32), pltpu.VMEM((w * n, 256), F32)] + [pltpu.VMEM((w, e), F32)] * 8, ins, flops=100 * 10 ** 9)
+         pltpu.VMEM((w, 128), F32), pltpu.VMEM((w * n, 256), F32)] + [pltpu.VMEM((w, e), F32)] * 8, ins, flops=100 * 10 ** 9, collective_id=5, has_side_effects=True)
 
     out_sum = scatter(part_out, 2).reshape(m, tl, d)
     layer_out = (u + out_sum).astype(BF16)
@@ -635,6 +799,8 @@
         [block(outs[0], falling), whole(outs[1]), whole(outs[2])], outs,
         [pltpu.VMEM((taps - 1, m, EDGE, e), F32), pltpu.VMEM((w, e), F32)], ins, flops=2 * peers * w * d * 3 * e)
 
+    g_out = sum_rep(g_out)
+    v_part, g_out = lax.optimization_barrier((v_part, g_out))
     v = scatter(v_part, 3).reshape(m, tl, d) * gain
     in_grad = w32(out_grad) + r * v - u * (r * r * r) * jnp.mean(v * u, axis=2, keepdims=True)
 
@@ -649,7 +815,7 @@
     small = sum_rep(small)
     vec, vec2, g_a, g_dt, g_xp = (small[:8], small[8:16], small[16:16 + n], small[16 + n:16 + n + rank], small[16 + n + rank:])
     return (layer_out, in_grad, grad_gain, grad_in_proj, vec2[:taps], vec2[taps], g_xp[:rank + 2 * n].T, g_dt, vec[0],
-            g_a, vec[1], sum_rep(g_out))
+            g_a, vec[1], g_out)
 
 
 def solution(mesh):

time: 927 us -> 897 us (0.968)
  Pallas kernels: 585 us -> 700 us
  blocking collectives: 109 us -> 6.14 us
  waiting for transfers between devices: 135 us -> 94.2 us
    all_gather x2 -> x0, blocking collectives: 103 us -> none  [the longest x1 79.8 us: on_device(): ids = lax.all_gather(segment_ids, 'shard')]
    pallas_call x0 -> x1, Pallas kernels: none -> 103 us  [gather(): pl.pallas_call(functools.partial(gather_kernel, dims=dims, chunks=chunks)...]
    all_gather x2 -> x1, waiting for transfers between devices: 98.4 us -> 0.01 us  [on_device(): dy_all = lax.all_gather(later.reshape(w, d), 'shard')]
    all_to_all x1, waiting for transfers between devices: 0.01 us -> 57.6 us  [on_device(): w_cols = lax.all_to_all(w_split, 'shard', 0, 0, tiled=True)]
    pallas_call x2, Pallas kernels: 129 us -> 144 us  [allsum(): pl.pallas_call(functools.partial(allsum_kernel, dims=dims, chunks=chunks,...]
  transfers between devices with their start and end apart: 12 -> 11, of which waited for: 4 -> 3; matrix products, arithmetic and copies ran while one was open for 4% -> 4% of each run, Pallas kernels for 45% -> 42%
where the time goes in v4:
time: 897 us; the launch traced here: 895 us
  Pallas kernels  700 us (78%)
  waiting for transfers between devices  94.2 us (11%)
  starting transfers between devices  28.6 us (3%)
  local copies, waits for them, and re-layouts  27.9 us (3%)
  other arithmetic  20.4 us (2%)
  between operations  14.7 us (2%)
    pallas_call x2, Pallas kernels, scatter(): pl.pallas_call(functools.partial(scatter_kernel, dims=dims, chunks=chunks...  230 us
    pallas_call x4, Pallas kernels, call(): pl.pallas_call(kernel, grid=grid, in_specs=in_specs, out_specs=out_specs,...  224 us
    pallas_call x2, Pallas kernels, allsum(): pl.pallas_call(functools.partial(allsum_kernel, dims=dims, chunks=chunks,...  144 us
    pallas_call x1, Pallas kernels, gather(): pl.pallas_call(functools.partial(gather_kernel, dims=dims, chunks=chunks)...  103 us
    all_to_all x1, waiting for transfers between devices, on_device(): w_cols = lax.all_to_all(w_split, 'shard', 0, 0, tiled=True)  57.6 us
    ppermute x4, waiting for transfers between devices, sum_rep(): other = lax.ppermute(low, 'rep', [(0, 1), (1, 0)])  36.6 us
  transfers between devices with their start and end apart: 11, of which 3 were waited for; matrix products, arithmetic and copies ran while one was open for 4% of the time, Pallas kernels for 42%

profile of v4, /device:TPU:0, one launch (start us, length us, event | category | flops | bytes accessed | tf_op | source)
XLA Modules:
  0.0 894.6 jit_solution(7818784303715701207)
XLA Ops:
  7.2 2.2 copy.80
  9.4 3.9 copy.67
  13.3 2.2 copy.83
  16.1 102.5 %shard_map.220 = (bf16[4,2,2,256,2048]{4,3,2,1,0:T(8,128)(2,1)}, f32[4,2,2,8,128]{4,3,2,1,0:T(8,128)}) custom-call(bf16[256,2048]{1,0:T(8,128)(2,1)} %bitcast.109, f32[8,128]{1,0:T(8,128)} %select_maximum_fusion.small), custom_call_target="tpu_custom_call" | custom-call | flops 80000000000 | bytes 16777216 | tf_op jit(solution)/shard_map/pallas_call | solution.py:360
  118.7 2.5 copy.76
  121.2 3.7 all-to-all-start
  125.0 1.0 fusion.25
  126.0 3.4 collective-permute-start.1
  129.4 1.3 slice.127
  130.7 1.3 collective-permute-start
  134.3 0.7 pad.15.xpt_ref
  136.2 1.5 fusion.31
  138.6 1.9 copy.72
  140.5 57.6 %all-to-all-done = bf16[16,128,512]{2,1,0:T(8,128)(2,1)S(1)} async-done(((bf16[16,128,512]{2,1,0:T(8,128)(2,1)}), bf16[16,128,512]{2,1,0:T(8,128)(2,1)S(1)}, u32[]{:S(2)}, u32[]{:S(2)}) %all-to-all-start) | async-done | bytes 2097184 | tf_op jit(solution)/shard_map/all_to_all | solution.py:715
  198.1 1.3 copy-done.9
  199.4 27.4 %shard_map.221 = (bf16[16,256,512]{2,1,0:T(8,128)(2,1)}, bf16[16,256,256]{2,1,0:T(8,128)(2,1)}, f32[16,160,256]{2,1,0:T(8,128)}, bf16[16,256,2048]{2,1,0:T(8,128)(2,1)}, bf16[16,256]{1,0:T(8,128)(2,1)}) custom-call(bf16[16,256,2048]{2,1,0:T(8,128)(2,1)} %bitcast.138, bf16[2048,512]{1,0:T(8,128)(2,1)} %bitcast.118, bf16[16,2048]{1,0:T(8,128)(2,1)} %copy-done.28, ...), custom_call_target="tpu_custom_call" | custom-call | flops 8589934592 | bytes 44864512 | tf_op jit(solution)/shard_map/pallas_call | solution.py:41
  226.9 89.9 %shard_map.222 = bf16[4,2,2,256,256]{4,3,2,1,0:T(8,128)(2,1)} custom-call(f32[4,2,2,160,256]{4,3,2,1,0:T(8,128)} %bitcast.114), custom_call_target="tpu_custom_call" | custom-call | tf_op jit(solution)/shard_map/pallas_call | solution.py:207
  316.8 1.0 slice.145
  318.4 47.4 %shard_map.223 = (f32[16,2,16,256]{3,2,1,0:T(8,128)}, f32[16,2,16,256]{3,2,1,0:T(8,128)}, f32[3,2,16,256]{3,2,1,0:T(8,128)}, f32[16,256,256]{2,1,0:T(8,128)}) custom-call(bf16[16,256,256]{2,1,0:T(8,128)(2,1)} %bitcast.124, bf16[16,256,512]{2,1,0:T(8,128)(2,1)} %get-tuple-element.47.xz_ref.prev_ref, bf16[16,256,256]{2,1,0:T(8,128)(2,1)} %get-tuple-element.48.xc_ref, ...), custom_call_target="tpu_custom_call" | custom-call | flops 40000000000 | bytes 31769600 | tf_op jit(solution)/shard_map/pallas_call | solution.py:41
  365.7 6.1 all-gather
  371.9 0.6 fusion.9
  372.5 118.2 %shard_map.224 = (bf16[16,256,2048]{2,1,0:T(8,128)(2,1)}, bf16[16,256,256]{2,1,0:T(8,128)(2,1)}, f32[16,256,256]{2,1,0:T(8,128)}, f32[16,160,256]{2,1,0:T(8,128)...) custom-call(bf16[16,256,256]{2,1,0:T(8,128)(2,1)} %bitcast.125, ...), custom_call_target="tpu_custom_call" | custom-call | flops 99999997952 | bytes 78555136 | tf_op jit(solution)/shard_map/pallas_call | solution.py:41
  490.9 53.9 %shard_map.226 = bf16[4,2,2,256,256]{4,3,2,1,0:T(8,128)(2,1)} custom-call(f32[4,2,2,160,256]{4,3,2,1,0:T(8,128)} %bitcast.113), custom_call_target="tpu_custom_call" | custom-call | tf_op jit(solution)/shard_map/pallas_call | solution.py:207
  544.7 0.9 slice.177
  545.7 1.0 slice.140
  546.9 1.3 collective-permute-start.2
  548.2 1.1 convert_element_type.100
  549.3 6.8 all-to-all-start.2
  556.2 2.7 collective-permute-start.3
  559.6 30.6 %shard_map.227 = (bf16[16,256,2048]{2,1,0:T(8,128)(2,1)}, f32[2048,256]{1,0:T(8,128)}, f32[8,256]{1,0:T(8,128)}) custom-call(bf16[16,256,512]{2,1,0:T(8,128)(2,1)} %get-tuple-element.47.xz_ref.prev_ref, bf16[16,256,512]{2,1,0:T(8,128)(2,1)} %get-tuple-element.47.xz_ref.prev_ref, f32[16,256]{1,0:T(8,128)} %get-tuple-element.93.edge_ref, ...), custom_call_target="tpu_custom_call" | custom-call | flops 12884901888 | bytes 54866944 | tf_op jit(solution)/shard_map/pallas_call | solution.py:41
  590.2 0.7 constant_dynamic-update-slice_fusion.1
  591.0 2.3 fusion.5
  593.4 111.3 %shard_map.225 = f32[256,2048]{1,0:T(8,128)} custom-call(bf16[4,2,2,256,2048]{4,3,2,1,0:T(8,128)(2,1)} %bitcast.151), custom_call_target="tpu_custom_call" | custom-call | flops 80000000000 | bytes 16777216 | tf_op jit(solution)/shard_map/pallas_call | solution.py:448
  704.8 1.1 convert_element_type.97
  705.9 0.7 slice.194
  708.3 0.7 slice_bitcast_fusion
  709.0 1.6 convert_add_fusion.3
  710.6 6.4 all-to-all-start.1
  717.0 118.8 %shard_map.228 = f32[256,2048]{1,0:T(8,128)} custom-call(bf16[4,2,2,256,2048]{4,3,2,1,0:T(8,128)(2,1)} %bitcast.152), custom_call_target="tpu_custom_call" | custom-call | flops 80000000000 | bytes 16777216 | tf_op jit(solution)/shard_map/pallas_call | solution.py:448
  835.8 1.1 copy.79
  836.9 1.9 collective-permute-start.5
  839.4 1.4 copy.78
  840.8 0.9 collective-permute-start.4
  841.7 4.0 fusion.3
  845.8 17.5 %collective-permute-done.5 = bf16[128,4096]{1,0:T(8,128)(2,1)} collective-permute-done((bf16[128,4096]{1,0:T(8,128)(2,1)}, bf16[128,4096]{1,0:T(8,128)(2,1)}, u32[]{:S(2)}, u32[]{:S(2)}) %collective-permute-start.5) | collective-permute-done | bytes 1048608 | tf_op jit(solution)/shard_map/ppermute | solution.py:693
  863.3 1.8 convert_add_fusion.1
  865.1 19.1 %collective-permute-done.4 = bf16[128,4096]{1,0:T(8,128)(2,1)S(1)} collective-permute-done((bf16[128,4096]{1,0:T(8,128)(2,1)S(1)}, bf16[128,4096]{1,0:T(8,128)(2,1)S(1)}, u32[]{:S(2)}, u32[]{:S(2)}) %collective-permute-start.4) | collective-permute-done | bytes 1048608 | tf_op jit(solution)/shard_map/ppermute | solution.py:693
  884.5 2.7 multiply_reduce_fusion
  (118 shorter events, 10.0 us)
Async XLA Ops:
  7.2 311.2 %all-gather.3.cloned.1.call-start = ((), (), s32[]{:S(2)}) async-start(), calls=%async_computation.3 | async-start | bytes 17825792 | tf_op jit(solution)/shard_map/all_gather | solution.py:720
  13.3 2.2 copy-start.20
  13.3 2.2 copy-start.33
  121.2 76.9 %all-to-all-start = ((bf16[16,128,512]{2,1,0:T(8,128)(2,1)}), bf16[16,128,512]{2,1,0:T(8,128)(2,1)S(1)}, u32[]{:S(2)}, u32[]{:S(2)}) async-start(bf16[16,128,512]{2,1,0:T(8,128)(2,1)} %bitcast.4), calls=%async_computation | async-start | bytes 4194304 | tf_op jit(solution)/shard_map/all_to_all | solution.py:715
  124.9 7.1 copy-start.30
  124.9 7.7 copy-start.16
  124.9 8.3 copy-start.31
  125.0 8.8 copy-start.32
  125.0 9.4 %copy-start.11 = (bf16[256,160]{0,1:T(8,128)(2,1)S(1)}, bf16[256,160]{0,1:T(8,128)(2,1)}, u32[]{:S(2)}) copy-start(bf16[256,160]{0,1:T(8,128)(2,1)} %param.20) | copy-start | bytes 245764
  125.0 10.6 %copy-start.14 = (bf16[16,256]{1,0:T(8,128)(2,1)S(1)}, bf16[16,256]{1,0:T(8,128)(2,1)}, u32[]{:S(2)}) copy-start(bf16[16,256]{1,0:T(8,128)(2,1)} %param.23) | copy-start | bytes 24580
  126.0 11.6 %collective-permute-start.1 = (s32[2,3]{1,0:T(2,128)S(1)}, s32[2,3]{1,0:T(2,128)S(1)}, u32[]{:S(2)}, u32[]{:S(2)}) collective-permute-start(s32[2,3]{1,0:T(2,128)S(1)} %slice.165), channel_id=1, source_target_pairs={{0,16},{1,17},{2,18},{3,19},{4,20},{5,21},{6,22},{7,23},{8,24},{9,... | collective-permute-start | bytes 80 | tf_op jit(solution)/shard_map/ppermute | solution.py:686
  130.7 9.8 %collective-permute-start = (bf16[16,2048]{1,0:T(8,128)(2,1)S(1)}, bf16[16,2048]{1,0:T(8,128)(2,1)S(1)}, u32[]{:S(2)}, u32[]{:S(2)}) collective-permute-start(bf16[16,2048]{1,0:T(8,128)(2,1)S(1)} %slice_bitcast_fusion.1), channel_id=1, source_target_pairs={{0,16},{1,17},{2,18},{3,19},{4,20},{5,21},{6,22},{7,23},{8,24},{9,... | collective-permute-start | bytes 196616 | tf_op jit(solution)/shard_map/ppermute | solution.py:686
  140.5 57.6 %copy-start.28 = (bf16[16,2048]{1,0:T(8,128)(2,1)}, bf16[16,2048]{1,0:T(8,128)(2,1)S(1)}, u32[]{:S(2)}) copy-start(bf16[16,2048]{1,0:T(8,128)(2,1)S(1)} %collective-permute-done.halo_ref) | copy-start | bytes 196612
  198.1 1.3 copy-start.9
  226.9 90.9 %copy-start.18 = (bf16[16,256]{1,0:T(8,128)(2,1)S(1)}, bf16[16,256]{1,0:T(8,128)(2,1)}, u32[]{:S(2)}) copy-start(bf16[16,256]{1,0:T(8,128)(2,1)} %get-tuple-element.56) | copy-start | bytes 24580
  490.8 55.9 %copy-start.12 = (bf16[256,160]{0,1:T(8,128)(2,1)S(1)}, bf16[256,160]{0,1:T(8,128)(2,1)}, u32[]{:S(2)}) copy-start(bf16[256,160]{0,1:T(8,128)(2,1)} %param.20) | copy-start | bytes 245764
  490.8 55.9 %copy-start.21 = (f32[2,8,1]{1,2,0:T(1,128)S(1)}, f32[2,8,1]{1,2,0:T(1,128)}, u32[]{:S(2)}) copy-start(f32[2,8,1]{1,2,0:T(1,128)} %get-tuple-element.89) | copy-start | bytes 196
  490.8 55.9 %copy-start.22 = (f32[2,8,1]{1,2,0:T(1,128)S(1)}, f32[2,8,1]{1,2,0:T(1,128)}, u32[]{:S(2)}) copy-start(f32[2,8,1]{1,2,0:T(1,128)} %get-tuple-element.90) | copy-start | bytes 196
  490.8 55.9 %copy-start.23 = (f32[2,8,1]{1,2,0:T(1,128)S(1)}, f32[2,8,1]{1,2,0:T(1,128)}, u32[]{:S(2)}) copy-start(f32[2,8,1]{1,2,0:T(1,128)} %get-tuple-element.91) | copy-start | bytes 196
  490.8 55.9 %copy-start.24 = (f32[1,256]{1,0:T(1,128)S(1)}, f32[1,256]{1,0:T(1,128)}, u32[]{:S(2)}) copy-start(f32[1,256]{1,0:T(1,128)} %get-tuple-element.94) | copy-start | bytes 3076
  490.8 55.9 %copy-start.25 = (f32[1,256]{1,0:T(1,128)S(1)}, f32[1,256]{1,0:T(1,128)}, u32[]{:S(2)}) copy-start(f32[1,256]{1,0:T(1,128)} %get-tuple-element.95) | copy-start | bytes 3076
  490.8 55.9 %copy-start.26 = (f32[1,256]{1,0:T(1,128)S(1)}, f32[1,256]{1,0:T(1,128)}, u32[]{:S(2)}) copy-start(f32[1,256]{1,0:T(1,128)} %get-tuple-element.96) | copy-start | bytes 3076
  490.8 55.9 %copy-start.27 = (f32[1,256]{1,0:T(1,128)S(1)}, f32[1,256]{1,0:T(1,128)}, u32[]{:S(2)}) copy-start(f32[1,256]{1,0:T(1,128)} %get-tuple-element.97) | copy-start | bytes 3076
  490.8 55.9 %copy-start.35 = (f32[256]{0:T(256)S(1)}, f32[256]{0:T(256)}, u32[]{:S(2)}) copy-start(f32[256]{0:T(256)} %convert_element_type.88) | copy-start | bytes 3076
  490.8 57.3 %copy-start.19 = (f32[8,256]{1,0:T(8,128)S(1)}, f32[8,256]{1,0:T(8,128)}, u32[]{:S(2)}) copy-start(f32[8,256]{1,0:T(8,128)} %get-tuple-element.65) | copy-start | bytes 24580
  490.9 57.3 %copy-start.7 = (f32[2048,256]{1,0:T(8,128)S(1)}, f32[2048,256]{1,0:T(8,128)}, u32[]{:S(2)}) copy-start(f32[2048,256]{1,0:T(8,128)} %get-tuple-element.64) | copy-start | bytes 6291460
  546.9 12.1 %collective-permute-start.2 = (f32[3,2,8,256]{3,2,1,0:T(8,128)S(1)}, f32[3,2,8,256]{3,2,1,0:T(8,128)S(1)}, u32[]{:S(2)}, u32[]{:S(2)}) collective-permute-start(f32[3,2,8,256]{3,2,1,0:T(8,128)S(1)} %pad_maximum_fusion.1), channel_id=1, source_target_pairs={{16,0},{17,1},{18,2},{19,3},{20,4},{21,5},{22,6},{23,7},{24,8},{25... | collective-permute-start | bytes 147464 | tf_op jit(solution)/shard_map/ppermute | solution.py:686
  548.2 7.9 copy-start
  549.3 161.3 %all-to-all-start.2 = ((bf16[16,128,256]{2,1,0:T(8,128)(2,1)}), bf16[16,128,256]{2,1,0:T(8,128)(2,1)S(1)}, u32[]{:S(2)}, u32[]{:S(2)}) async-start(bf16[16,128,256]{2,1,0:T(8,128)(2,1)} %bitcast.55), calls=%async_computation.2 | async-start | bytes 2097152 | tf_op jit(solution)/shard_map/all_to_all | solution.py:808
  556.2 152.8 %collective-permute-start.3 = (bf16[256,2048]{1,0:T(8,128)(2,1)S(1)}, bf16[256,2048]{1,0:T(8,128)(2,1)S(1)}, u32[]{:S(2)}, u32[]{:S(2)}) collective-permute-start(bf16[256,2048]{1,0:T(8,128)(2,1)S(1)} %convert_element_type.94), channel_id=1, source_target_pairs={{0,16},{16,0},{1,17},{17,1},{2,18},{18,2},{3,19},{19,3},{4,20},{20... | collective-permute-start | bytes 3145736 | tf_op jit(solution)/shard_map/ppermute | solution.py:693
  559.0 0.6 copy-start.29
  559.6 31.4 %copy-start.15 = (bf16[16,256]{1,0:T(8,128)(2,1)S(1)}, bf16[16,256]{1,0:T(8,128)(2,1)}, u32[]{:S(2)}) copy-start(bf16[16,256]{1,0:T(8,128)(2,1)} %param.23) | copy-start | bytes 24580
  559.6 31.4 %copy-start.17 = (f32[16,256]{1,0:T(8,128)S(1)}, f32[16,256]{1,0:T(8,128)}, u32[]{:S(2)}) copy-start(f32[16,256]{1,0:T(8,128)} %get-tuple-element.67) | copy-start | bytes 49156
  559.6 31.4 %copy-start.10 = (f32[128,256]{1,0:T(8,128)S(1)}, f32[128,256]{1,0:T(8,128)}, u32[]{:S(2)}) copy-start(f32[128,256]{1,0:T(8,128)} %get-tuple-element.68) | copy-start | bytes 393220
  559.6 31.4 %copy-start.6 = (bf16[4,2,2,256,256]{4,3,2,1,0:T(8,128)(2,1)S(1)}, bf16[4,2,2,256,256]{4,3,2,1,0:T(8,128)(2,1)}, u32[]{:S(2)}) copy-start(bf16[4,2,2,256,256]{4,3,2,1,0:T(8,128)(2,1)} %shard_map.226) | copy-start | bytes 6291460
  593.3 112.5 %collective-permute-start.6 = (bf16[416,256]{1,0:T(8,128)(2,1)S(1)}, bf16[416,256]{1,0:T(8,128)(2,1)S(1)}, u32[]{:S(2)}, u32[]{:S(2)}) collective-permute-start(bf16[416,256]{1,0:T(8,128)(2,1)S(1)} %fusion.5), channel_id=1, source_target_pairs={{0,16},{16,0},{1,17},{17,1},{2,18},{18,2},{3,19},{19,3},{4,20},{20... | collective-permute-start | bytes 638984 | tf_op jit(solution)/shard_map/ppermute | solution.py:693
  593.4 111.3 %copy-start.8 = (f32[2048,256]{1,0:T(8,128)S(1)}, f32[2048,256]{1,0:T(8,128)}, u32[]{:S(2)}) copy-start(f32[2048,256]{1,0:T(8,128)} %get-tuple-element.63) | copy-start | bytes 6291460
  710.6 128.8 %all-to-all-start.1 = ((bf16[16,128,256]{2,1,0:T(8,128)(2,1)}), bf16[16,128,256]{2,1,0:T(8,128)(2,1)}, u32[]{:S(2)}, u32[]{:S(2)}) async-start(bf16[16,128,256]{2,1,0:T(8,128)(2,1)} %bitcast.53), calls=%async_computation.1 | async-start | bytes 2097152 | tf_op jit(solution)/shard_map/all_to_all | solution.py:808
  717.0 121.9 %copy-start.4 = (bf16[2,128,2048]{2,1,0:T(8,128)(2,1)S(1)}, bf16[2,128,2048]{2,1,0:T(8,128)(2,1)}, u32[]{:S(2)}) copy-start(bf16[2,128,2048]{2,1,0:T(8,128)(2,1)} %param.13) | copy-start | bytes 3145732
  835.8 3.0 copy-start.2
  835.8 3.0 copy-start.13
  836.9 26.4 %collective-permute-start.5 = (bf16[128,4096]{1,0:T(8,128)(2,1)}, bf16[128,4096]{1,0:T(8,128)(2,1)}, u32[]{:S(2)}, u32[]{:S(2)}) collective-permute-start(bf16[128,4096]{1,0:T(8,128)(2,1)} %bitcast.69), channel_id=1, source_target_pairs={{0,16},{16,0},{1,17},{17,1},{2,18},{18,2},{3,19},{19,3},{4,20},{20... | collective-permute-start | bytes 3145736 | tf_op jit(solution)/shard_map/ppermute | solution.py:693
  838.9 2.9 copy-start.3
  839.4 2.4 copy-start.5
  840.8 43.4 %collective-permute-start.4 = (bf16[128,4096]{1,0:T(8,128)(2,1)S(1)}, bf16[128,4096]{1,0:T(8,128)(2,1)S(1)}, u32[]{:S(2)}, u32[]{:S(2)}) collective-permute-start(bf16[128,4096]{1,0:T(8,128)(2,1)S(1)} %bitcast.111), channel_id=1, source_target_pairs={{0,16},{16,0},{1,17},{17,1},{2,18},{18,2},{3,19},{19,3},{4,20},{20... | collective-permute-start | bytes 3145736 | tf_op jit(solution)/shard_map/ppermute | solution.py:693
  865.1 19.3 %copy-start.1 = (bf16[128,8192]{1,0:T(8,128)(2,1)S(1)}, bf16[128,8192]{1,0:T(8,128)(2,1)}, u32[]{:S(2)}) copy-start(bf16[128,8192]{1,0:T(8,128)(2,1)} %param.17) | copy-start | bytes 6291460
  884.5 2.7 copy-start.34
Sparse Core Ops, SparseCore 0:
  118.8 193.8 all-gather.2

commit v5 on v4

--- a/solution.py
+++ b/solution.py
@@ -68,8 +68,9 @@
     return (u * lax.rsqrt(jnp.mean(u * u, axis=1, keepdims=True) + 1e-5) * gain).astype(BF16)
 
 
-def front(hid_ref, w_ref, halo_ref, mask_ref, cw_ref, cb_ref, xp_ref, gain_ref, xz_ref, xc_ref, part_ref, nu_ref, edge_ref,
-          carry, *, m, e):
+def front(hid_ref, w_ref, halo_ref, mask_ref, cw_ref, cb_ref, xp_ref, gain_ref, xz_ref, xc_ref, nu_ref, edge_ref,
+          *rest, m, e):
+    parts, carry = rest[:m], rest[m]
     @pl.when(pl.program_id(0) == 0)
     def _():
         edge = mm(normalise(halo_ref[...], gain_ref[...]), w_ref[:, :e]).astype(BF16)
@@ -86,8 +87,9 @@
         ext = jnp.concatenate([carry[i * EDGE:(i + 1) * EDGE], x], axis=0)
         carry[i * EDGE:(i + 1) * EDGE] = x[rows - EDGE:]
         conv = convolve(lags(ext, rows), mask_ref[0, i * rows:(i + 1) * rows], cw, cb)
-        xc_ref[0, i * rows:(i + 1) * rows] = (conv * jax.nn.sigmoid(conv)).astype(BF16)
-    part_ref[0] = nt(xp_ref[...], xc_ref[0])
+        xc = (conv * jax.nn.sigmoid(conv)).astype(BF16)
+        xc_ref[0, i * rows:(i + 1) * rows] = xc
+        parts[i][0] = nt(xp_ref[...], xc)
 
 
 def lattice(peers):
@@ -95,16 +97,20 @@
     return peers // (2 * y), y, 2
 
 
+def place(target):
+    return target if isinstance(target, dict) else {"shard": target}
+
+
 def greet(targets):
     barrier = pltpu.get_barrier_semaphore()
     for target in targets:
-        pl.semaphore_signal(barrier, inc=1, device_id={"shard": target}, device_id_type=pl.DeviceIdType.MESH)
+        pl.semaphore_signal(barrier, inc=1, device_id=place(target), device_id_type=pl.DeviceIdType.MESH)
     pl.semaphore_wait(barrier, len(targets))
 
 
 def remote(src, dst, send, recv, target):
     return pltpu.make_async_remote_copy(src_ref=src, dst_ref=dst, send_sem=send, recv_sem=recv,
-                                        device_id={"shard": target}, device_id_type=pl.DeviceIdType.MESH)
+                                        device_id=place(target), device_id_type=pl.DeviceIdType.MESH)
 
 
 def spread_low(total, n):
@@ -125,7 +131,9 @@
     return jnp.concatenate([total, jnp.zeros((256 - total.shape[0], total.shape[1]), F32)], axis=0).T.astype(BF16)
 
 
-def allsum_kernel(part, out, rc, ac, ry, ay, rz, send, recv, *, dims, chunks, finish):
+def allsum_kernel(*refs, dims, chunks, finish):
+    parts = refs[:chunks]
+    out, rc, ac, low, ry, rz, send, recv = refs[chunks:]
     nz, ny, _ = dims
     me = lax.axis_index("shard")
     c, y, z = me % 2, (me // 2) % ny, me // (2 * ny)
@@ -134,8 +142,7 @@
     ys = [lax.rem(y + k, ny) for k in range(1, ny)]
     zs = [lax.rem(z + k, nz) for k in range(1, nz)]
     greet([across] + [where(z, b, c) for b in ys] + [where(a, y, c) for a in zs])
-    width = part.shape[-1] // chunks
-    lanes = [pl.ds(q * width, width) for q in range(chunks)]
+    width = parts[0].shape[-1]
     rows = [pl.ds(q * width, width) for q in range(chunks)]
 
     def start(copies):
@@ -155,14 +162,16 @@
     first = []
     for q in range(chunks):
         (s, r), = sems(1)
-        first.append(start([remote(part.at[:, :, 1 - c, :, lanes[q]], rc.at[q], s, r, across)]))
+        first.append(start([remote(parts[q].at[:, :, 1 - c], rc.at[q], s, r, across)]))
     second = []
     for q in range(chunks):
         finish_all(first[q])
         for a in range(nz):
             for b in range(ny):
-                ac[q, a, b] = part[a, b, c, :, q * width:(q + 1) * width] + rc[q, a, b]
-        second.append(start([remote(ac.at[q, :, b], ry.at[q, k], *sem, where(z, b, c))
+                total = parts[q][a, b, c] + rc[q, a, b]
+                ac[q, a, b] = total
+                low[q, a, b] = total.astype(BF16)
+        second.append(start([remote(low.at[q, :, b], ry.at[q, k], *sem, where(z, b, c))
                              for k, (b, sem) in enumerate(zip(ys, sems(ny - 1)))]))
     third = []
     for q in range(chunks):
@@ -170,16 +179,17 @@
         for a in range(nz):
             got = ac[q, a, y]
             for k in range(ny - 1):
-                got = got + ry[q, k, a]
-            ay[q, a] = got
-        third.append(start([remote(ay.at[q, a], rz.at[q, k], *sem, where(a, y, c))
+                got = got + ry[q, k, a].astype(F32)
+            ac[q, a, y] = got
+            low[q, a, y] = got.astype(BF16)
+        third.append(start([remote(low.at[q, a, y], rz.at[q, k], *sem, where(a, y, c))
                             for k, (a, sem) in enumerate(zip(zs, sems(nz - 1)))]))
     fourth = []
     for q in range(chunks):
         finish_all(third[q])
-        got = ay[q, z]
+        got = ac[q, z, y]
         for k in range(nz - 1):
-            got = got + rz[q, k]
+            got = got + rz[q, k].astype(F32)
         out[z, y, c, q * width:(q + 1) * width] = finish(got)
         mine = out.at[z, y, c, rows[q]]
         fourth.append(start([remote(mine, mine, *sem, where(a, y, c)) for a, sem in zip(zs, sems(nz - 1))]))
@@ -198,27 +208,28 @@
         finish_all(last[q])
 
 
-def allsum(part, finish, collective_id):
-    peers, cols, w = part.shape
+def allsum(parts, finish, collective_id):
+    peers, cols, width = parts[0].shape
+    w = width * len(parts)
     dims = lattice(peers)
     nz, ny, nc = dims
-    chunks = w // 128
+    chunks = len(parts)
     copies = 2 * chunks * (1 + ny - 1 + nz - 1)
     out = pl.pallas_call(
         functools.partial(allsum_kernel, dims=dims, chunks=chunks, finish=finish),
         out_shape=jax.ShapeDtypeStruct((nz, ny, nc, w, 256), BF16),
-        in_specs=[pl.BlockSpec(memory_space=pltpu.VMEM)],
+        in_specs=[pl.BlockSpec(memory_space=pltpu.VMEM)] * chunks,
         out_specs=pl.BlockSpec(memory_space=pltpu.VMEM),
         scratch_shapes=[pltpu.VMEM((chunks, nz, ny, cols, 128), F32), pltpu.VMEM((chunks, nz, ny, cols, 128), F32),
-                        pltpu.VMEM((chunks, ny - 1, nz, cols, 128), F32), pltpu.VMEM((chunks, nz, cols, 128), F32),
-                        pltpu.VMEM((chunks, nz - 1, cols, 128), F32),
+                        pltpu.VMEM((chunks, nz, ny, cols, 128), BF16), pltpu.VMEM((chunks, ny - 1, nz, cols, 128), BF16),
+                        pltpu.VMEM((chunks, nz - 1, cols, 128), BF16),
                         pltpu.SemaphoreType.DMA((copies,)), pltpu.SemaphoreType.DMA((copies,))],
         compiler_params=pltpu.CompilerParams(collective_id=collective_id, has_side_effects=True, vmem_limit_bytes=VMEM),
-    )(part.reshape(nz, ny, nc, cols, w))
+    )(*[part.reshape(nz, ny, nc, cols, width) for part in parts])
     return out.reshape(peers, w, 256)
 
 
-def gather_kernel(x, small, out, small_out, send, recv, s_send, s_recv, own_sem, *, dims, chunks):
+def gather_kernel(x, small, wts, out, small_out, cols, send, recv, s_send, s_recv, w_send, w_recv, own_sem, *, dims, chunks):
     nz, ny, _ = dims
     me = lax.axis_index("shard")
     c, y, z = me % 2, (me // 2) % ny, me // (2 * ny)
@@ -227,7 +238,10 @@
     ys = [lax.rem(y + k, ny) for k in range(1, ny)]
     ys_from = [lax.rem(y + ny - k, ny) for k in range(1, ny)]
     zs = [lax.rem(z + k, nz) for k in range(1, nz)]
-    greet([across] + [where(z, b, c) for b in ys] + [where(a, y, c) for a in zs])
+    peers = nz * ny * 2
+    others = [lax.rem(me + k, peers) for k in range(1, peers)]
+    greet(others)
+    dl, e = wts.shape[0], wts.shape[1] // (2 * peers)
     size = x.shape[0] // chunks
     rows = [pl.ds(q * size, size) for q in range(chunks)]
 
@@ -235,6 +249,13 @@
     keep.start()
     whole_own = pltpu.make_async_copy(x, out.at[z, y, c], own_sem.at[1])
     whole_own.start()
+
+    def piece(half, src, dst):
+        return (wts.at[:, pl.ds(pl.multiple_of(half * peers * e + dst * e, 128), e)],
+                cols.at[pl.ds(pl.multiple_of(src * dl, dl), dl), pl.ds(half * e, e)])
+    kept = [pltpu.make_async_copy(*piece(half, me, me), own_sem.at[2 + half]) for half in range(2)]
+    sent = [remote(*piece(half, me, p), w_send.at[2 * k + half], w_recv.at[2 * k + half], p)
+            for k, p in enumerate(others) for half in range(2)]
 
     kinds = 2 * nz - 1
     offset = [0] + [-1 - j for j in range(nz - 1)] + [1 + j for j in range(nz - 1)]
@@ -299,6 +320,8 @@
     tiny_start([remote(small, small_out.at[z, y, c], s_send.at[k], s_recv.at[k], where(a, y, c)) for k, a in enumerate(zs)])
     for q in range(chunks):
         onward(0, q)
+    for copy in kept + sent:
+        copy.start()
     tiny_wait()
     keep.wait()
     tiny_start([remote(small_out.at[:, y, c], small_out.at[:, y, c], s_send.at[nz - 1 + k], s_recv.at[nz - 1 + k], where(z, b, c))
@@ -348,115 +371,208 @@
                 def _(kind=kind, up=up):
                     for q in range(chunks):
                         hop(kind, q, up).wait_send()
+    for copy in kept + sent:
+        copy.wait()
     whole_own.wait()
 
 
-def gather(x, small, collective_id, chunks=4):
+def gather(x, small, wts, collective_id, chunks=4):
     w, d = x.shape
     peers = lax.axis_size("shard")
     dims = lattice(peers)
     nz, ny, nc = dims
     copies = 2 * ny * (2 * nz - 1) * chunks
-    out, tiles = pl.pallas_call(
+    dl, e = wts.shape[0], wts.shape[1] // (2 * peers)
+    out, tiles, cols = pl.pallas_call(
         functools.partial(gather_kernel, dims=dims, chunks=chunks),
-        out_shape=[jax.ShapeDtypeStruct((nz, ny, nc, w, d), x.dtype), jax.ShapeDtypeStruct((nz, ny, nc, 8, 128), F32)],
-        in_specs=[pl.BlockSpec(memory_space=pl.ANY), pl.BlockSpec(memory_space=pltpu.VMEM)],
-        out_specs=[pl.BlockSpec(memory_space=pl.ANY), pl.BlockSpec(memory_space=pltpu.VMEM)],
+        out_shape=[jax.ShapeDtypeStruct((nz, ny, nc, w, d), x.dtype), jax.ShapeDtypeStruct((nz, ny, nc, 8, 128), F32),
+                   jax.ShapeDtypeStruct((peers * dl, 2 * e), BF16)],
+        in_specs=[pl.BlockSpec(memory_space=pl.ANY), pl.BlockSpec(memory_space=pltpu.VMEM), pl.BlockSpec(memory_space=pl.ANY)],
+        out_specs=[pl.BlockSpec(memory_space=pl.ANY), pl.BlockSpec(memory_space=pltpu.VMEM), pl.BlockSpec(memory_space=pl.ANY)],
         scratch_shapes=[pltpu.SemaphoreType.DMA((copies,)), pltpu.SemaphoreType.DMA((copies,)),
-                        pltpu.SemaphoreType.DMA((nz + ny,)), pltpu.SemaphoreType.DMA((nz + ny,)), pltpu.SemaphoreType.DMA((2,))],
+                        pltpu.SemaphoreType.DMA((nz + ny,)), pltpu.SemaphoreType.DMA((nz + ny,)),
+                        pltpu.SemaphoreType.DMA((2 * peers - 2,)), pltpu.SemaphoreType.DMA((2 * peers - 2,)),
+                        pltpu.SemaphoreType.DMA((4,))],
         compiler_params=pltpu.CompilerParams(collective_id=collective_id, has_side_effects=True, vmem_limit_bytes=VMEM),
         cost_estimate=pl.CostEstimate(flops=8 * 10 ** 10, bytes_accessed=2 * peers * w * d, transcendentals=0),
-    )(x, small)
-    return out.reshape(peers, w, d), tiles.reshape(peers, 8, 128)
-
-
-def scatter_kernel(part, out, own, rc, ry, rz, load, send, recv, *, dims, chunks):
+    )(x, small, wts)
+    return out.reshape(peers, w, d), tiles.reshape(peers, 8, 128), cols
+
+
+def scatter_steps(refs, dims, reps):
+    part, g, out, g_out, rc, own, ry, rz, rg, load, send, recv, g_load, g_send, g_recv = refs
     nz, ny, _ = dims
-    me = lax.axis_index("shard")
+    me, rep = lax.axis_index("shard"), lax.axis_index("rep")
     c, y, z = me % 2, (me // 2) % ny, me // (2 * ny)
     where = lambda a, b, d: (a * ny + b) * 2 + d
     across = where(z, y, 1 - c)
     ys = [lax.rem(y + k, ny) for k in range(1, ny)]
     zs = [lax.rem(z + k, nz) for k in range(1, nz)]
-    greet([across] + [where(z, b, c) for b in ys] + [where(a, y, c) for a in zs])
-    size = part.shape[3] // chunks
+    peers = nz * ny * 2
+    others = [lax.rem(me + k, peers) for k in range(1, peers)]
+    far = [{"rep": lax.rem(rep + k, reps)} for k in range(1, reps)]
+    slots, size = own.shape[0], own.shape[3]
+    chunks = part.shape[3] // size
     rows = [pl.ds(q * size, size) for q in range(chunks)]
-    per = 1 + ny - 1 + nz - 1
+    per = ny + nz - 1
 
     def pair(q, k):
         return send.at[q * per + k], recv.at[q * per + k]
-    loads, first, second, third = [], [], [None] * chunks, [None] * chunks
-    for q in range(chunks):
-        loads.append(pltpu.make_async_copy(part.at[:, :, c, rows[q]], own.at[:, :, rows[q]], load.at[q]))
-        first.append(remote(part.at[:, :, 1 - c, rows[q]], rc.at[:, :, rows[q]], *pair(q, 0), across))
-        loads[q].start()
-        first[q].start()
+
+    def loads(q):
+        return pltpu.make_async_copy(part.at[:, :, c, rows[q]], own.at[q % slots], load.at[q])
+
+    def first(q):
+        return remote(part.at[:, :, 1 - c, rows[q]], rc.at[:, :, rows[q]], *pair(q, 0), across)
+
+    def second(q):
+        return [remote(rc.at[:, b, rows[q]], ry.at[k, :, rows[q]], *pair(q, 1 + k), where(z, b, c))
+                for k, b in enumerate(ys)]
+
+    def third(q):
+        return [remote(rc.at[a, y, rows[q]], rz.at[k, rows[q]], *pair(q, ny + k), where(a, y, c))
+                for k, a in enumerate(zs)]
+
+    def handed():
+        dl = rg.shape[2]
+        spot = lambda p: g.at[pl.ds(pl.multiple_of(p * dl, dl), dl)]
+        return pltpu.make_async_copy(spot(me), rg.at[rep, me], g_load.at[0]), [
+            remote(spot(p), rg.at[rep, me], g_send.at[k], g_recv.at[k], p) for k, p in enumerate(others)]
+
+    def crossed():
+        return [remote(rg.at[rep], rg.at[rep], g_send.at[peers - 1 + k], g_recv.at[peers - 1 + k], p)
+                for k, p in enumerate(far)]
+
+    def start():
+        if g is None:
+            greet([across] + [where(z, b, c) for b in ys] + [where(a, y, c) for a in zs])
+        else:
+            greet(others + far)
+        for q in range(min(slots, chunks)):
+            loads(q).start()
+        for q in range(chunks):
+            first(q).start()
+        if g is not None:
+            kept, sent = handed()
+            for copy in [kept] + sent:
+                copy.start()
 
     def over_core(q):
-        loads[q].wait()
-        first[q].wait()
+        loads(q).wait()
+        first(q).wait()
 
         def add(a, _):
             i, j = a // ny, a % ny
-            own[i, j, rows[q]] = (own[i, j, rows[q]].astype(F32) + rc[i, j, rows[q]].astype(F32)).astype(BF16)
+            rc[i, j, rows[q]] = (own[q % slots, i, j].astype(F32) + rc[i, j, rows[q]].astype(F32)).astype(BF16)
             return 0
         lax.fori_loop(0, nz * ny, add, 0)
-        second[q] = [remote(own.at[:, b, rows[q]], ry.at[k, :, rows[q]], *pair(q, 1 + k), where(z, b, c))
-                     for k, b in enumerate(ys)]
-        for copy in second[q]:
+        if q + slots < chunks:
+            loads(q + slots).start()
+        for copy in second(q):
             copy.start()
 
     def over_y(q):
-        for copy in second[q]:
+        for copy in second(q):
             copy.wait()
 
         def add(a, _):
-            total = own[a, y, rows[q]].astype(F32)
+            total = rc[a, y, rows[q]].astype(F32)
             for k in range(ny - 1):
                 total = total + ry[k, a, rows[q]].astype(F32)
-            own[a, y, rows[q]] = total.astype(BF16)
+            rc[a, y, rows[q]] = total.astype(BF16)
             return 0
         lax.fori_loop(0, nz, add, 0)
-        third[q] = [remote(own.at[a, y, rows[q]], rz.at[k, rows[q]], *pair(q, ny + k), where(a, y, c))
-                    for k, a in enumerate(zs)]
-        for copy in third[q]:
+        for copy in third(q):
             copy.start()
 
     def over_z(q):
-        for copy in third[q]:
+        for copy in third(q):
             copy.wait()
-        total = own[z, y, rows[q]].astype(F32)
+        total = rc[z, y, rows[q]].astype(F32)
         for k in range(nz - 1):
             total = total + rz[k, rows[q]].astype(F32)
         out[rows[q]] = total
 
-    for s in range(chunks + 4):
+    def step(s):
         if s < chunks:
             over_core(s)
         if 0 <= s - 2 < chunks:
             over_y(s - 2)
         if 0 <= s - 4 < chunks:
             over_z(s - 4)
-
-
-def scatter(part, collective_id):
+        if s == chunks // 2 + 1 and g is not None:
+            kept, sent = handed()
+            for copy in [kept] + sent:
+                copy.wait()
+            for copy in crossed():
+                copy.start()
+
+    def finish():
+        if g is None:
+            return
+        for copy in crossed():
+            copy.wait()
+        e = rg.shape[3]
+        for p in range(peers):
+            total = rg[0, p].astype(F32)
+            for k in range(1, reps):
+                total = total + rg[k, p].astype(F32)
+            g_out[:, p * e:(p + 1) * e] = total
+    return start, [functools.partial(step, s) for s in range(chunks + 4)], finish
+
+
+def scatter_scratch(peers, w, d, size, g=None):
+    nz, ny, nc = lattice(peers)
+    chunks = w // size
+    dma = pltpu.SemaphoreType.DMA
+    copies = chunks * (ny + nz - 1)
+    out = [pltpu.VMEM((nz, ny, w, d), BF16), pltpu.VMEM((3, nz, ny, size, d), BF16),
+           pltpu.VMEM((ny - 1, nz, w, d), BF16), pltpu.VMEM((nz - 1, w, d), BF16)]
+    tail = [dma((chunks,)), dma((copies,)), dma((copies,))]
+    if g is None:
+        return out + tail
+    reps = lax.axis_size("rep")
+    count = peers + reps - 2
+    return (out + [pltpu.VMEM((reps, peers, g.shape[0] // peers, g.shape[1]), BF16)] + tail
+            + [dma((1,)), dma((count,)), dma((count,))])
+
+
+def scatter_kernel(part, g, out, g_out, rc, own, ry, rz, rg, load, send, recv, g_load, g_send, g_recv, *, dims, reps):
+    start, steps, finish = scatter_steps(
+        (part, g, out, g_out, rc, own, ry, rz, rg, load, send, recv, g_load, g_send, g_recv), dims, reps)
+    start()
+    for step in steps:
+        step()
+    finish()
+
+
+def scatter(part, g, collective_id, size=32):
     peers, w, d = part.shape
     dims = lattice(peers)
-    nz, ny, nc = dims
-    chunks = w // 32
-    copies = chunks * (1 + ny - 1 + nz - 1)
+    reps = lax.axis_size("rep")
+    dl, e = g.shape[0] // peers, g.shape[1]
     return pl.pallas_call(
-        functools.partial(scatter_kernel, dims=dims, chunks=chunks),
-        out_shape=jax.ShapeDtypeStruct((w, d), F32),
-        in_specs=[pl.BlockSpec(memory_space=pl.ANY)],
-        out_specs=pl.BlockSpec(memory_space=pltpu.VMEM),
-        scratch_shapes=[pltpu.VMEM((nz, ny, w, d), BF16), pltpu.VMEM((nz, ny, w, d), BF16),
-                        pltpu.VMEM((ny - 1, nz, w, d), BF16), pltpu.VMEM((nz - 1, w, d), BF16),
-                        pltpu.SemaphoreType.DMA((chunks,)),
-                        pltpu.SemaphoreType.DMA((copies,)), pltpu.SemaphoreType.DMA((copies,))],
+        functools.partial(scatter_kernel, dims=dims, reps=reps),
+        out_shape=[jax.ShapeDtypeStruct((w, d), F32), jax.ShapeDtypeStruct((dl, peers * e), F32)],
+        in_specs=[pl.BlockSpec(memory_space=pl.ANY)] * 2,
+        out_specs=[pl.BlockSpec(memory_space=pltpu.VMEM)] * 2,
+        scratch_shapes=scatter_scratch(peers, w, d, size, g),
         compiler_params=pltpu.CompilerParams(collective_id=collective_id, has_side_effects=True, vmem_limit_bytes=VMEM),
         cost_estimate=pl.CostEstimate(flops=8 * 10 ** 10, bytes_accessed=2 * peers * w * d, transcendentals=0),
-    )(part.reshape(nz, ny, nc, w, d))
+    )(part.reshape(dims + (w, d)), g)
+
+
+def beside(b, grid, start, steps, finish):
+    @pl.when(b == 0)
+    def _():
+        start()
+    for s, step in enumerate(steps):
+        @pl.when(b == (s * (grid - 1)) // len(steps) + 1)
+        def _(step=step):
+            step()
+    @pl.when(b == grid - 1)
+    def _():
+        finish()
 
 
 def fill(low_ref, bcs_scr, bc_scr, n):
@@ -531,14 +647,25 @@
         end_ref[2] = f_scr[...]
 
 
-def behind(low_ref, xz_ref, xc_ref, mask_ref, dy_ref, dg_ref, nu_ref, cks_ref, ckp_ref,
-           wo_ref, wdt_ref, dtb_ref, a2_ref, skip_ref, hin_ref, qin_ref,
-           out_ref, dz_ref, dxc_ref, part_ref, go_ref, gdt_ref, ga_ref, vec_ref, gz_ref,
-           h_scr, a_scr, q_scr, bcs_scr, bc_scr, pre_scr, st_scr, sd_scr, dx_scr, dy_scr, y_scr, da_scr, gb_scr, *, m, n, e):
+def behind(*refs, n, e, dims, reps, sending):
+    (low_ref, xz_ref, xc_ref, mask_ref, dy_ref, dg_ref, nu_ref, cks_ref, ckp_ref,
+     wo_ref, wdt_ref, dtb_ref, a2_ref, skip_ref, hin_ref, qin_ref) = refs[:16]
+    refs = refs[16:]
+    if sending:
+        before, refs = refs[0], refs[1:]
+    out_ref, dz_ref, dxc_ref, part_ref, go_ref, gdt_ref, ga_ref, vec_ref, gz_ref = refs[:9]
+    refs = refs[9:]
+    if sending:
+        summed, refs = refs[0], refs[1:]
+    (h_scr, a_scr, q_scr, bcs_scr, bc_scr, pre_scr, st_scr, sd_scr, dx_scr, dy_scr, y_scr, da_scr, gb_scr) = refs[:13]
     b = pl.program_id(0)
+    if sending:
+        rc, own, ry, rz, load, send, recv = refs[13:]
+        beside(b, dims[0] * dims[1] * dims[2], *scatter_steps(
+            (before, None, summed, None, rc, own, ry, rz, None, load, send, recv, None, None, None), dims, reps))
+    m = 1
     @pl.when(b == 0)
     def _():
-        greet([lax.axis_index("shard") + 1 - 2 * (lax.axis_index("shard") % 2)])
         q_scr[...] = qin_ref[...]
         for ref in (go_ref, gdt_ref, ga_ref, vec_ref, gz_ref):
             ref[...] = jnp.zeros_like(ref)
@@ -644,8 +771,14 @@
     return s * (1.0 + v * (1.0 - s))
 
 
-def back(xz_ref, prev_ref, edge_ref, mask_ref, dxc_ref, ddbc_ref, dz_ref, nu_ref, next_ref, w_ref, xpt_ref, cw_ref, cb_ref,
-         v_ref, gx_ref, vec_ref, carry, dx_scr, *, m, e):
+def back(*refs, m, e, dims, reps):
+    (xz_ref, prev_ref, edge_ref, mask_ref, ddbc_ref, nu_ref, next_ref, w_ref, xpt_ref, cw_ref, cb_ref) = refs[:11]
+    dxc_refs, dz_refs = refs[11:11 + m], refs[11 + m:11 + 2 * m]
+    before, gz_ref = refs[11 + 2 * m:13 + 2 * m]
+    v_ref, gxl_ref, vec_ref, summed, gz_out, gx_ref, carry, dx_scr = refs[13 + 2 * m:21 + 2 * m]
+    rc, own, ry, rz, rg, *sems = refs[21 + 2 * m:]
+    beside(pl.program_id(0), dims[0] * dims[1] * dims[2], *scatter_steps(
+        (before, gz_ref, summed, gz_out, rc, own, ry, rz, rg, *sems), dims, reps))
     b = pl.program_id(0)
     @pl.when(b == 0)
     def _():
@@ -655,7 +788,7 @@
     first = b == pl.num_programs(0) - 1
     rows = xz_ref.shape[1] // m
     cw, cb = cw_ref[...], cb_ref[...]
-    dxc_all = dxc_ref[0] + mm(ddbc_ref[0], xpt_ref[...])
+    dxc_all = mm(ddbc_ref[0], xpt_ref[...])
     for i in range(m):
         part = slice(i * rows, (i + 1) * rows)
         x = xz_ref[0, part, :e].astype(F32)
@@ -663,7 +796,7 @@
         before = jnp.where(first, edge_ref[i * EDGE:(i + 1) * EDGE], before)
         lag = lags(jnp.concatenate([before, x], axis=0), rows)
         same = mask_ref[0, part]
-        dconv = dxc_all[part] * dsilu(convolve(lag, same, cw, cb))
+        dconv = (dxc_refs[i][0] + dxc_all[part]) * dsilu(convolve(lag, same, cw, cb))
         vec_ref[4:5] += jnp.sum(dconv, axis=0, keepdims=True)
         vec_ref[3:4] += jnp.sum(dconv * x, axis=0, keepdims=True)
         dx = cw[3:4] * dconv
@@ -676,8 +809,12 @@
             carry[k - 1, i] = sent[:EDGE]
         dx_scr[part] = dx
     dx = dx_scr[...].astype(BF16)
-    v_ref[0] = nt(jnp.concatenate([dx, dz_ref[0]], axis=1), w_ref[...]).astype(BF16)
+    v_ref[0] = nt(jnp.concatenate([dx, jnp.concatenate([ref[0] for ref in dz_refs], axis=0)], axis=1), w_ref[...]).astype(BF16)
     gx_ref[...] += tn(nu_ref[0], dx)
+
+    @pl.when(first)
+    def _():
+        gxl_ref[...] = gx_ref[...].astype(BF16)
 
 
 def shift_rep(value, steps):
@@ -710,10 +847,7 @@
 
     own = jnp.pad(jnp.concatenate([w32(segment_ids), jnp.pad(w32(norm_gain)[None], ((0, 0), (0, 128 - dl)))], axis=0),
                   ((0, 7 - m), (0, 0)))
-    w_split = in_proj.reshape(dl, 2, peers, e).transpose(2, 0, 1, 3).reshape(peers * dl, 2 * e)
-    own, w_split = lax.optimization_barrier((own, w_split))
-    w_cols = lax.all_to_all(w_split, "shard", 0, 0, tiled=True)
-    hid_all, tiles = gather(hidden_in.reshape(w, d), own, 4)
+    hid_all, tiles, w_cols = gather(hidden_in.reshape(w, d), own, in_proj, 4)
     gain = tiles[:, m, :dl].reshape(1, d)
     ids = tiles[:, :m, :tl].astype(jnp.int32)
     later, hid_all = lax.optimization_barrier((out_grad, hid_all))
@@ -731,15 +865,15 @@
 
     cw, cb = w32(conv_weight), w32(conv_bias)[None]
     ins = [hid_all, w_cols, halo, mask, cw, cb, x_proj.T, gain]
-    outs = [shp((peers, w, 2 * e), BF16), shp((peers, w, e), BF16), shp((peers, rank + 2 * n, w), F32),
-            shp((peers, w, d), BF16), shp((m * EDGE, e), BF16)]
-    xz, xc, part, nu_all, edge = call(
+    outs = [shp((peers, w, 2 * e), BF16), shp((peers, w, e), BF16), shp((peers, w, d), BF16), shp((m * EDGE, e), BF16)]
+    outs += [shp((peers, rank + 2 * n, tl), F32)] * m
+    xz, xc, nu_all, edge, *parts = call(
         functools.partial(front, m=m, e=e), (peers,),
         [block(hid_all, rising)] + [whole(a) for a in ins[1:3]] + [block(mask, rising)] + [whole(a) for a in ins[4:]],
-        [block(a, rising) for a in outs[:4]] + [whole(outs[4])], outs,
+        [block(a, rising) for a in outs[:3]] + [whole(outs[3])] + [block(a, rising) for a in outs[4:]], outs,
         [pltpu.VMEM((m * EDGE, e), F32)], ins, flops=2 * peers * w * d * 2 * e)
 
-    low = allsum(part, functools.partial(spread_low, n=n), 0)
+    low = allsum(parts, functools.partial(spread_low, n=n), 0)
     a_mat = -jnp.exp(w32(a_log))
     a2 = a_mat * LOG2E
     dtb, skip = w32(dt_bias)[None], w32(d_skip)[None]
@@ -761,22 +895,41 @@
         h_in = jnp.where(k < rep, ends[k, 1] * h_in + ends[k, 0], h_in)
         q_in = jnp.where(o > rep, ends[o, 1] * q_in + ends[o, 2], q_in)
 
-    ins = [low, xz, xc, mask, dy_all, dg, nu_all, cks, ckp, out_proj, dt_weight, dtb, a2, skip, h_in, q_in]
-    outs = [shp((peers, w, d), BF16), shp((peers, w, e), BF16), shp((peers, w, e), F32),
-            shp((peers, rank + 2 * n, w), F32), shp((e, d), F32), shp((rank, e), F32), shp((n, e), F32), shp((8, e), F32),
-            shp((d, e), F32)]
-    part_out, dz, dxc, part, g_out, g_dt, g_a, vec, g_z = call(
-        functools.partial(behind, m=m, n=n, e=e), (peers,),
-        [block(a, falling) for a in ins[:9]] + [whole(a) for a in ins[9:]],
-        [block(a, falling) for a in outs[:4]] + [whole(a) for a in outs[4:]], outs,
-        [pltpu.VMEM((tl * n + n, e), F32), pltpu.VMEM((tl * n, e), F32), pltpu.VMEM((m, n, e), F32),
-         pltpu.VMEM((w, 128), F32), pltpu.VMEM((w * n, 256), F32)] + [pltpu.VMEM((w, e), F32)] * 8, ins, flops=100 * 10 ** 9, collective_id=5, has_side_effects=True)
-
-    out_sum = scatter(part_out, 2).reshape(m, tl, d)
-    layer_out = (u + out_sum).astype(BF16)
-
-    ddbc = allsum(part, functools.partial(spread_plain, n=n), 1)
+    dims = lattice(peers)
+    anywhere = pl.BlockSpec(memory_space=pl.ANY)
+    rows_done = []
+    for i in range(m):
+        def row(a, order, i=i):
+            shape = (1, tl) if a.ndim == 3 else (1, 1, a.shape[2])
+            return pl.BlockSpec(shape + a.shape[len(shape):], lambda b, r=a.ndim: (order(b), i) + (0,) * (r - 2))
+
+        def one(a, i=i):
+            return pl.BlockSpec((1,) + a.shape[1:], lambda b: (i, 0, 0))
+        ins = [low, xz, xc, mask, dy_all, dg, nu_all, cks, ckp, out_proj, dt_weight, dtb, a2, skip, h_in, q_in]
+        specs = [row(a, falling) for a in ins[:9]] + [whole(a) for a in ins[9:14]] + [one(a) for a in ins[14:]]
+        outs = [shp((peers, tl, d), BF16), shp((peers, tl, e), BF16), shp((peers, tl, e), F32),
+                shp((peers, rank + 2 * n, tl), F32), shp((e, d), F32), shp((rank, e), F32), shp((n, e), F32), shp((8, e), F32),
+                shp((d, e), F32)]
+        out_specs = [block(a, falling) for a in outs[:4]] + [whole(a) for a in outs[4:]]
+        scratch = [pltpu.VMEM((tl * n + n, e), F32), pltpu.VMEM((tl * n, e), F32), pltpu.VMEM((1, n, e), F32),
+                   pltpu.VMEM((tl, 128), F32), pltpu.VMEM((tl * n, 256), F32)] + [pltpu.VMEM((tl, e), F32)] * 8
+        params = {}
+        if i:
+            ins.append(rows_done[i - 1][0].reshape(dims + (tl, d)))
+            specs.append(anywhere)
+            outs.append(shp((tl, d), F32))
+            out_specs.append(whole(outs[-1]))
+            scratch += scatter_scratch(peers, tl, d, 16)
+            params = dict(collective_id=5 + i, has_side_effects=True)
+        rows_done.append(call(
+            functools.partial(behind, n=n, e=e, dims=dims, reps=reps, sending=bool(i)), (peers,), specs, out_specs, outs,
+            scratch, ins, flops=50 * 10 ** 9, **params))
+    g_out, g_dt, g_a, vec, g_z = (sum(done[k] for done in rows_done) for k in range(4, 9))
+    g_z = g_z.astype(BF16)
+
+    ddbc = allsum([done[3] for done in rows_done], functools.partial(spread_plain, n=n), 1)
     xpt = jnp.pad(x_proj.T, ((0, 256 - x_proj.shape[1]), (0, 0)))
+    dxc8 = jnp.stack([done[2][0, :EDGE] for done in rows_done])
 
     x8 = w32(xz[0].reshape(m, tl, 2 * e)[:, :EDGE, :e])
     ext8 = jnp.concatenate([w32(edge).reshape(m, EDGE, e), x8], axis=1)
@@ -784,31 +937,34 @@
     conv8 = cb + cw[3] * x8
     for k in range(1, taps):
         conv8 = conv8 + cw[3 - k] * ext8[:, EDGE - k:2 * EDGE - k] * same8[:, :, k - 1:k]
-    d8 = dxc[0].reshape(m, tl, e)[:, :EDGE] + mm(ddbc[0].reshape(m, tl, -1)[:, :EDGE].reshape(m * EDGE, -1), xpt).reshape(m, EDGE, e)
+    d8 = dxc8 + mm(ddbc[0].reshape(m, tl, -1)[:, :EDGE].reshape(m * EDGE, -1), xpt).reshape(m, EDGE, e)
     d8 = d8 * dsilu(conv8)
     sent = jnp.stack([cw[3 - k] * d8 * same8[:, :, k - 1:k] for k in range(1, taps)])
     follow = shift_rep(sent, -1)
 
-    ins = [xz, xz, w32(edge), mask, dxc, ddbc, dz, nu_all, follow, w_cols, xpt, cw, cb]
-    outs = [shp((peers, w, d), BF16), shp((d, e), F32), shp((8, e), F32)]
+    last = rows_done[-1][0].reshape(dims + (tl, d))
+    ins = [xz, xz, w32(edge), mask, ddbc, nu_all, follow, w_cols, xpt, cw, cb]
+    ins += [done[2] for done in rows_done] + [done[1] for done in rows_done] + [last, g_z]
+    outs = [shp((peers, w, d), BF16), shp((d, e), BF16), shp((8, e), F32), shp((tl, d), F32), shp((dl, peers * e), F32)]
     earlier = lambda i: jnp.maximum(peers - 2 - i, 0)
-    specs = [block(a, falling) for a in ins[:8]] + [whole(a) for a in ins[8:]]
+    specs = ([block(a, falling) for a in ins[:6]] + [whole(a) for a in ins[6:11]] + [block(a, falling) for a in ins[11:-2]]
+             + [anywhere] * 2)
     specs[1], specs[2] = block(xz, earlier), whole(ins[2])
-    v_part, g_x, vec2 = call(
-        functools.partial(back, m=m, e=e), (peers,), specs,
-        [block(outs[0], falling), whole(outs[1]), whole(outs[2])], outs,
-        [pltpu.VMEM((taps - 1, m, EDGE, e), F32), pltpu.VMEM((w, e), F32)], ins, flops=2 * peers * w * d * 3 * e)
+    v_part, g_x, vec2, last_sum, grad_z = call(
+        functools.partial(back, m=m, e=e, dims=dims, reps=reps), (peers,), specs,
+        [block(outs[0], falling)] + [whole(a) for a in outs[1:]], outs,
+        [pltpu.VMEM((d, e), F32), pltpu.VMEM((taps - 1, m, EDGE, e), F32), pltpu.VMEM((w, e), F32)]
+        + scatter_scratch(peers, tl, d, 16, g_z), ins, flops=2 * peers * w * d * 3 * e, collective_id=2, has_side_effects=True)
+    out_sum = jnp.stack([done[9] for done in rows_done[1:]] + [last_sum])
+    layer_out = (u + out_sum).astype(BF16)
 
     g_out = sum_rep(g_out)
     v_part, g_out = lax.optimization_barrier((v_part, g_out))
-    v = scatter(v_part, 3).reshape(m, tl, d) * gain
+    v, grad_x = scatter(v_part, g_x, 3)
+    v = v.reshape(m, tl, d) * gain
     in_grad = w32(out_grad) + r * v - u * (r * r * r) * jnp.mean(v * u, axis=2, keepdims=True)
 
-    def to_owner(g):
-        own = lax.all_to_all(g.astype(BF16), "shard", 0, 0, tiled=True)
-        own = own.reshape(peers, dl, e).transpose(1, 0, 2).reshape(dl, peers * e)
-        return sum_rep(own)
-    grad_in_proj = jnp.concatenate([to_owner(g_x), to_owner(g_z)], axis=1)
+    grad_in_proj = jnp.concatenate([grad_x, grad_z], axis=1)
     grad_gain = jnp.sum(grad_in_proj * w32(in_proj), axis=1) / w32(norm_gain)
 
     small = jnp.concatenate([vec, vec2, g_a * a_mat, g_dt, tn(xc.reshape(peers * w, e), ddbc.reshape(peers * w, -1)).T], axis=0)

time: 897 us -> 764 us (0.85)
  waiting for transfers between devices: 94.2 us -> 33.8 us
  Pallas kernels: 700 us -> 659 us
  starting transfers between devices: 28.6 us -> 10.3 us
    pallas_call x2 -> x1, Pallas kernels: 230 us -> 120 us  [scatter(): pl.pallas_call(functools.partial(scatter_kernel, dims=dims, reps=reps), o...]
    pallas_call x4 -> x5, Pallas kernels: 224 us -> 298 us  [call(): pl.pallas_call(kernel, grid=grid, in_specs=in_specs, out_specs=out_specs,...]
    all_to_all x3 -> x0, waiting for transfers between devices: 57.6 us -> none  [the longest x1 57.6 us: on_device(): w_cols = lax.all_to_all(w_split, 'shard', 0, 0, tiled=True)]
    ppermute x4 -> x2, waiting for transfers between devices: 36.6 us -> 5.09 us  [sum_rep(): other = lax.ppermute(low, 'rep', [(0, 1), (1, 0)])]
    pallas_call x2, Pallas kernels: 144 us -> 114 us  [allsum(): pl.pallas_call(functools.partial(allsum_kernel, dims=dims, chunks=chunks,...]
    all_gather x1, waiting for transfers between devices: 0.01 us -> 28.1 us  [on_device(): dy_all = lax.all_gather(later.reshape(w, d), 'shard')]
    pallas_call x1, Pallas kernels: 103 us -> 126 us  [gather(): pl.pallas_call(functools.partial(gather_kernel, dims=dims, chunks=chunks)...]
    all_to_all x3 -> x0, starting transfers between devices: 16.9 us -> none  [the longest x2 13.2 us: to_owner(): own = lax.all_to_all(g.astype(BF16), 'shard', 0, 0, tiled=True)]
  transfers between devices with their start and end apart: 11 -> 6, of which waited for: 3 -> 3; matrix products, arithmetic and copies ran while one was open for 4% -> 2% of each run, Pallas kernels for 42% -> 24%
where the time goes in v5:
time: 764 us; the launch traced here: 761 us
  Pallas kernels  659 us (86%)
  waiting for transfers between devices  33.8 us (4%)
  local copies, waits for them, and re-layouts  21.2 us (3%)
  other arithmetic  15.4 us (2%)
  between operations  14.6 us (2%)
  starting transfers between devices  10.3 us (1%)
    pallas_call x5, Pallas kernels, call(): pl.pallas_call(kernel, grid=grid, in_specs=in_specs, out_specs=out_specs,...  298 us
    pallas_call x1, Pallas kernels, gather(): pl.pallas_call(functools.partial(gather_kernel, dims=dims, chunks=chunks)...  126 us
    pallas_call x1, Pallas kernels, scatter(): pl.pallas_call(functools.partial(scatter_kernel, dims=dims, reps=reps), o...  120 us
    pallas_call x2, Pallas kernels, allsum(): pl.pallas_call(functools.partial(allsum_kernel, dims=dims, chunks=chunks,...  114 us
    all_gather x1, waiting for transfers between devices, on_device(): dy_all = lax.all_gather(later.reshape(w, d), 'shard')  28.1 us
  transfers between devices with their start and end apart: 6, of which 3 were waited for; matrix products, arithmetic and copies ran while one was open for 2% of the time, Pallas kernels for 24%

profile of v5, /device:TPU:0, one launch (start us, length us, event | category | flops | bytes accessed | tf_op | source)
XLA Modules:
  0.0 761.1 jit_solution(4456195962016216774)
XLA Ops:
  7.2 0.7 convert_element_type.69
  7.9 0.7 convert_bitcast_fusion.2
  8.6 0.6 select_maximum_fusion.small
  9.2 126.2 %shard_map.220 = (bf16[4,2,2,256,2048]{4,3,2,1,0:T(8,128)(2,1)}, f32[4,2,2,8,128]{4,3,2,1,0:T(8,128)}, bf16[2048,512]{1,0:T(8,128)(2,1)}) custom-call(bf16[256,2048]{1,0:T(8,128)(2,1)} %bitcast.87, f32[8,128]{1,0:T(8,128)} %select_maximum_fusion.small, bf16[128,8192]{1,0:T(8,128)(2,1)} %wts.1), custom_call_target="tpu_custom_call" | custom-call | flops 80000000000 | bytes 16777216 | tf_op jit(solution)/shard_map/pallas_call | solution.py:386
  135.5 0.9 fusion.26
  136.5 3.4 collective-permute-start.1
  139.9 1.4 slice.127
  141.3 1.3 collective-permute-start
  143.1 0.6 convert_element_type.72.cw_ref.refs_9_
  144.9 0.7 pad.15.refs_8_
  145.5 0.6 fusion.34
  146.1 0.6 fusion.27.a2_ref.refs_12_
  146.8 1.5 fusion.32
  148.6 0.6 fusion.33
  149.2 1.9 copy.48
  151.1 0.6 copy-done.33
  151.7 27.4 %shard_map.221 = (bf16[16,256,512]{2,1,0:T(8,128)(2,1)}, bf16[16,256,256]{2,1,0:T(8,128)(2,1)}, bf16[16,256,2048]{2,1,0:T(8,128)(2,1)}, bf16[16,256]{1,0:T(8,128...) custom-call(bf16[16,256,2048]{2,1,0:T(8,128)(2,1)} %bitcast.115, ...), custom_call_target="tpu_custom_call" | custom-call | flops 8589934592 | bytes 44864512 | tf_op jit(solution)/shard_map/pallas_call | solution.py:41
  179.1 1.0 slice.145
  180.1 69.9 %shard_map.222 = bf16[4,2,2,256,256]{4,3,2,1,0:T(8,128)(2,1)} custom-call(f32[4,2,2,160,128]{4,3,2,1,0:T(8,128)} %bitcast.101, f32[4,2,2,160,128]{4,3,2,1,0:T(8,128)} %bitcast.102), custom_call_target="tpu_custom_call" | custom-call | tf_op jit(solution)/shard_map/pallas_call | solution.py:218
  250.1 0.6 convert_bitcast_fusion.1
  250.7 28.1 %all-gather.3.cloned.1.call-done.dy_ref.refs_4_ = bf16[16,256,2048]{2,1,0:T(8,128)(2,1)} async-done(((bf16[1,256,2048]{2,1,0:T(8,128)(2,1)}), bf16[16,256,2048]{2,1,0:T(8,128)(2,1)}) %all-gather.3.cloned.1.call-update) | async-done | bytes 16777232 | tf_op jit(solution)/shard_map/all_gather | solution.py:854
  278.8 47.4 %shard_map.223 = (f32[16,2,16,256]{3,2,1,0:T(8,128)}, f32[16,2,16,256]{3,2,1,0:T(8,128)}, f32[3,2,16,256]{3,2,1,0:T(8,128)}, f32[16,256,256]{2,1,0:T(8,128)}) custom-call(bf16[16,256,256]{2,1,0:T(8,128)(2,1)} %bitcast.96, bf16[16,256,512]{2,1,0:T(8,128)(2,1)} %get-tuple-element.61.xz_ref.refs_1_.refs_0_, ...), custom_call_target="tpu_custom_call" | custom-call | flops 40000000000 | bytes 31769600 | tf_op jit(solution)/shard_map/pallas_call | solution.py:41
  326.2 6.0 all-gather
  332.2 0.6 fusion.10
  332.9 65.9 %shard_map.224 = (bf16[16,128,2048]{2,1,0:T(8,128)(2,1)}, bf16[16,128,256]{2,1,0:T(8,128)(2,1)}, f32[16,128,256]{2,1,0:T(8,128)}, f32[16,160,128]{2,1,0:T(8,128)...) custom-call(bf16[16,256,256]{2,1,0:T(8,128)(2,1)} %bitcast.97, ...), custom_call_target="tpu_custom_call" | custom-call | flops 49999998976 | bytes 65710080 | tf_op jit(solution)/shard_map/pallas_call | solution.py:41
  398.8 75.0 %shard_map.225 = (bf16[16,128,2048]{2,1,0:T(8,128)(2,1)}, bf16[16,128,256]{2,1,0:T(8,128)(2,1)}, f32[16,128,256]{2,1,0:T(8,128)}, f32[16,160,128]{2,1,0:T(8,128)...) custom-call(bf16[16,256,256]{2,1,0:T(8,128)(2,1)} %bitcast.98, ...), custom_call_target="tpu_custom_call" | custom-call | flops 49999998976 | bytes 75147264 | tf_op jit(solution)/shard_map/pallas_call | solution.py:41
  473.9 44.2 %shard_map.226 = bf16[4,2,2,256,256]{4,3,2,1,0:T(8,128)(2,1)} custom-call(f32[4,2,2,160,128]{4,3,2,1,0:T(8,128)} %bitcast.99, f32[4,2,2,160,128]{4,3,2,1,0:T(8,128)} %bitcast.100), custom_call_target="tpu_custom_call" | custom-call | tf_op jit(solution)/shard_map/pallas_call | solution.py:218
  518.1 0.9 slice.176
  519.0 0.7 slice.141
  519.7 0.7 slice.140
  520.7 1.5 collective-permute-start.2
  522.5 2.7 collective-permute-start.3
  525.3 1.2 add_convert_fusion.1.refs_16_
  527.1 0.6 copy-done.34
  527.8 82.6 %shard_map.227 = (bf16[16,256,2048]{2,1,0:T(8,128)(2,1)}, bf16[2048,256]{1,0:T(8,128)(2,1)}, f32[8,256]{1,0:T(8,128)}, f32[128,2048]{1,0:T(8,128)}, f32[128,4096]{1,0:T(8,128)}) custom-call(bf16[16,256,512]{2,1,0:T(8,128)(2,1)} %get-tuple-element.61.xz_ref.refs_1_.refs_0_, bf16[16,256,512]{2,1,0:T(8,128)(2,1)} %get-tuple-element.61.xz_ref.refs_1_.refs_0_, ...), custom_call_target="tpu_custom_call" | custom-call | flops 12884901888 | bytes 66401280 | tf_op jit(solution)/shard_map/pallas_call | solution.py:41
  610.4 0.7 constant_dynamic-update-slice_fusion.3
  611.2 0.8 fusion.5
  611.9 1.3 collective-permute-start.4
  613.2 5.1 collective-permute-done.4
  618.4 0.7 slice.193
  619.0 0.6 slice.195
  620.8 0.7 slice_bitcast_fusion
  621.5 1.7 convert_add_fusion.1
  623.2 120.2 %shard_map.228 = (f32[256,2048]{1,0:T(8,128)}, f32[128,4096]{1,0:T(8,128)}) custom-call(bf16[4,2,2,256,2048]{4,3,2,1,0:T(8,128)(2,1)} %bitcast.128, bf16[2048,256]{1,0:T(8,128)(2,1)} %get-tuple-element.86.g), custom_call_target="tpu_custom_call" | custom-call | flops 80000000000 | bytes 16777216 | tf_op jit(solution)/shard_map/pallas_call | solution.py:554
  743.4 1.9 constant_dynamic-update-slice_fusion.1
  745.8 1.4 copy-done.5
  747.8 1.6 copy-done
  751.7 2.5 fusion.3
  (112 shorter events, 7.9 us)
Async XLA Ops:
  7.2 271.6 %all-gather.3.cloned.1.call-start = ((), (), s32[]{:S(2)}) async-start(), calls=%async_computation | async-start | bytes 17825792 | tf_op jit(solution)/shard_map/all_gather | solution.py:854
  135.4 7.2 copy-start.35
  135.4 7.7 %copy-start.20 = (bf16[4,256]{1,0:T(4,128)(2,1)S(1)}, bf16[4,256]{1,0:T(4,128)(2,1)}, u32[]{:S(2)}) copy-start(bf16[4,256]{1,0:T(4,128)(2,1)} %param.18) | copy-start | bytes 6148
  135.4 8.3 %copy-start.36 = (bf16[256]{0:T(256)(128)(2,1)S(1)}, bf16[256]{0:T(256)(128)(2,1)}, u32[]{:S(2)}) copy-start(bf16[256]{0:T(256)(128)(2,1)} %param.22) | copy-start | bytes 1540
  135.4 8.9 %copy-start.37 = (bf16[256]{0:T(256)(128)(2,1)S(1)}, bf16[256]{0:T(256)(128)(2,1)}, u32[]{:S(2)}) copy-start(bf16[256]{0:T(256)(128)(2,1)} %param.24) | copy-start | bytes 1540
  135.5 9.4 %copy-start.15 = (bf16[256,160]{0,1:T(8,128)(2,1)S(1)}, bf16[256,160]{0,1:T(8,128)(2,1)}, u32[]{:S(2)}) copy-start(bf16[256,160]{0,1:T(8,128)(2,1)} %param.20) | copy-start | bytes 245764
  135.5 10.7 %copy-start.18 = (bf16[16,256]{1,0:T(8,128)(2,1)S(1)}, bf16[16,256]{1,0:T(8,128)(2,1)}, u32[]{:S(2)}) copy-start(bf16[16,256]{1,0:T(8,128)(2,1)} %param.23) | copy-start | bytes 24580
  136.5 11.8 %collective-permute-start.1 = (s32[2,3]{1,0:T(2,128)S(1)}, s32[2,3]{1,0:T(2,128)S(1)}, u32[]{:S(2)}, u32[]{:S(2)}) collective-permute-start(s32[2,3]{1,0:T(2,128)S(1)} %slice.165), channel_id=1, source_target_pairs={{0,16},{1,17},{2,18},{3,19},{4,20},{5,21},{6,22},{7,23},{8,24},{9,... | collective-permute-start | bytes 80 | tf_op jit(solution)/shard_map/ppermute | solution.py:823
  141.3 9.8 %collective-permute-start = (bf16[16,2048]{1,0:T(8,128)(2,1)S(1)}, bf16[16,2048]{1,0:T(8,128)(2,1)S(1)}, u32[]{:S(2)}, u32[]{:S(2)}) collective-permute-start(bf16[16,2048]{1,0:T(8,128)(2,1)S(1)} %slice_bitcast_fusion.1), channel_id=1, source_target_pairs={{0,16},{1,17},{2,18},{3,19},{4,20},{5,21},{6,22},{7,23},{8,24},{9,... | collective-permute-start | bytes 196616 | tf_op jit(solution)/shard_map/ppermute | solution.py:823
  151.1 0.6 copy-start.33
  180.1 69.9 %copy-start.23 = (bf16[16,256]{1,0:T(8,128)(2,1)S(1)}, bf16[16,256]{1,0:T(8,128)(2,1)}, u32[]{:S(2)}) copy-start(bf16[16,256]{1,0:T(8,128)(2,1)} %get-tuple-element.71) | copy-start | bytes 24580
  473.8 46.6 %copy-start.16 = (bf16[256,160]{0,1:T(8,128)(2,1)S(1)}, bf16[256,160]{0,1:T(8,128)(2,1)}, u32[]{:S(2)}) copy-start(bf16[256,160]{0,1:T(8,128)(2,1)} %param.20) | copy-start | bytes 245764
  473.8 46.6 %copy-start.26 = (f32[2,8,1]{1,2,0:T(1,128)S(1)}, f32[2,8,1]{1,2,0:T(1,128)}, u32[]{:S(2)}) copy-start(f32[2,8,1]{1,2,0:T(1,128)} %get-tuple-element.115) | copy-start | bytes 196
  473.8 46.6 %copy-start.27 = (f32[2,8,1]{1,2,0:T(1,128)S(1)}, f32[2,8,1]{1,2,0:T(1,128)}, u32[]{:S(2)}) copy-start(f32[2,8,1]{1,2,0:T(1,128)} %get-tuple-element.116) | copy-start | bytes 196
  473.8 46.6 %copy-start.28 = (f32[2,8,1]{1,2,0:T(1,128)S(1)}, f32[2,8,1]{1,2,0:T(1,128)}, u32[]{:S(2)}) copy-start(f32[2,8,1]{1,2,0:T(1,128)} %get-tuple-element.117) | copy-start | bytes 196
  473.8 46.6 %copy-start.29 = (f32[1,256]{1,0:T(1,128)S(1)}, f32[1,256]{1,0:T(1,128)}, u32[]{:S(2)}) copy-start(f32[1,256]{1,0:T(1,128)} %get-tuple-element.120) | copy-start | bytes 3076
  473.9 46.6 %copy-start.30 = (f32[1,256]{1,0:T(1,128)S(1)}, f32[1,256]{1,0:T(1,128)}, u32[]{:S(2)}) copy-start(f32[1,256]{1,0:T(1,128)} %get-tuple-element.121) | copy-start | bytes 3076
  473.9 46.6 %copy-start.31 = (f32[1,256]{1,0:T(1,128)S(1)}, f32[1,256]{1,0:T(1,128)}, u32[]{:S(2)}) copy-start(f32[1,256]{1,0:T(1,128)} %get-tuple-element.122) | copy-start | bytes 3076
  473.9 46.6 %copy-start.32 = (f32[1,256]{1,0:T(1,128)S(1)}, f32[1,256]{1,0:T(1,128)}, u32[]{:S(2)}) copy-start(f32[1,256]{1,0:T(1,128)} %get-tuple-element.123) | copy-start | bytes 3076
  473.9 46.6 %copy-start.40 = (f32[256]{0:T(256)S(1)}, f32[256]{0:T(256)}, u32[]{:S(2)}) copy-start(f32[256]{0:T(256)} %convert_element_type.73) | copy-start | bytes 3076
  473.9 48.3 %copy-start.8 = (f32[256,2048]{1,0:T(8,128)S(1)}, f32[256,2048]{1,0:T(8,128)}, u32[]{:S(2)}) copy-start(f32[256,2048]{1,0:T(8,128)} %get-tuple-element.83) | copy-start | bytes 6291460
  473.9 48.3 %copy-start.10 = (f32[256,2048]{1,0:T(8,128)S(1)}, f32[256,2048]{1,0:T(8,128)}, u32[]{:S(2)}) copy-start(f32[256,2048]{1,0:T(8,128)} %get-tuple-element.84) | copy-start | bytes 6291460
  520.7 6.5 collective-permute-start.2
  522.2 3.1 copy-start.6
  522.2 3.1 copy-start.9
  522.5 99.0 %collective-permute-start.3 = (bf16[256,2048]{1,0:T(8,128)(2,1)S(1)}, bf16[256,2048]{1,0:T(8,128)(2,1)S(1)}, u32[]{:S(2)}, u32[]{:S(2)}) collective-permute-start(bf16[256,2048]{1,0:T(8,128)(2,1)S(1)} %add_convert_fusion), channel_id=1, source_target_pairs={{0,16},{16,0},{1,17},{17,1},{2,18},{18,2},{3,19},{19,3},{4,20},{20... | collective-permute-start | bytes 3145736 | tf_op jit(solution)/shard_map/ppermute | solution.py:830
  525.3 1.2 copy-start.24
  525.3 1.2 copy-start.25
  527.1 0.6 copy-start.34
  527.7 83.4 %copy-start.19 = (bf16[16,256]{1,0:T(8,128)(2,1)S(1)}, bf16[16,256]{1,0:T(8,128)(2,1)}, u32[]{:S(2)}) copy-start(bf16[16,256]{1,0:T(8,128)(2,1)} %param.23) | copy-start | bytes 24580
  527.7 83.4 %copy-start.21 = (f32[16,256]{1,0:T(8,128)S(1)}, f32[16,256]{1,0:T(8,128)}, u32[]{:S(2)}) copy-start(f32[16,256]{1,0:T(8,128)} %get-tuple-element.93) | copy-start | bytes 49156
  527.7 83.4 %copy-start.22 = (f32[16,256]{1,0:T(8,128)S(1)}, f32[16,256]{1,0:T(8,128)}, u32[]{:S(2)}) copy-start(f32[16,256]{1,0:T(8,128)} %get-tuple-element.94) | copy-start | bytes 49156
  527.7 83.4 %copy-start.13 = (f32[128,256]{1,0:T(8,128)S(1)}, f32[128,256]{1,0:T(8,128)}, u32[]{:S(2)}) copy-start(f32[128,256]{1,0:T(8,128)} %get-tuple-element.95) | copy-start | bytes 393220
  527.7 83.4 %copy-start.14 = (f32[128,256]{1,0:T(8,128)S(1)}, f32[128,256]{1,0:T(8,128)}, u32[]{:S(2)}) copy-start(f32[128,256]{1,0:T(8,128)} %get-tuple-element.96) | copy-start | bytes 393220
  527.7 83.4 %copy-start.4 = (bf16[4,2,2,256,256]{4,3,2,1,0:T(8,128)(2,1)S(1)}, bf16[4,2,2,256,256]{4,3,2,1,0:T(8,128)(2,1)}, u32[]{:S(2)}) copy-start(bf16[4,2,2,256,256]{4,3,2,1,0:T(8,128)(2,1)} %shard_map.226) | copy-start | bytes 6291460
  527.8 83.4 %copy-start.39 = (bf16[16,256,256]{2,1,0:T(8,128)(2,1)S(1)}, bf16[16,256,256]{2,1,0:T(8,128)(2,1)}, u32[]{:S(2)}) copy-start(bf16[16,256,256]{2,1,0:T(8,128)(2,1)} %get-tuple-element.62.xc_ref.refs_2_) | copy-start | bytes 6291460
  611.9 6.4 collective-permute-start.4
  743.4 2.2 copy-start.7
  745.7 1.6 copy-start.5
  747.3 2.1 copy-start
  747.3 2.1 copy-start.38
  747.3 3.1 copy-start.1
  747.3 3.4 copy-start.3
  747.3 3.4 copy-start.17
  749.4 1.8 copy-start.2
  749.4 2.0 copy-start.11
  749.4 2.3 copy-start.12
Sparse Core Ops, SparseCore 0:
  135.6 143.1 all-gather.2

commit v6 on v5

--- a/solution.py
+++ b/solution.py
@@ -9,7 +9,7 @@
 F32, BF16 = jnp.float32, jnp.bfloat16
 LOG2E, LN2 = 1.4426950408889634, 0.6931471805599453
 EDGE = 8
-VMEM = 56 << 20
+VMEM = 60 << 20
 
 
 def nt(a, b):
@@ -240,7 +240,7 @@
     zs = [lax.rem(z + k, nz) for k in range(1, nz)]
     peers = nz * ny * 2
     others = [lax.rem(me + k, peers) for k in range(1, peers)]
-    greet(others)
+    greet(others + [{"rep": lax.axis_index("rep") + 1 - 2 * lax.rem(lax.axis_index("rep"), 2)}])
     dl, e = wts.shape[0], wts.shape[1] // (2 * peers)
     size = x.shape[0] // chunks
     rows = [pl.ds(q * size, size) for q in range(chunks)]
@@ -250,10 +250,15 @@
     whole_own = pltpu.make_async_copy(x, out.at[z, y, c], own_sem.at[1])
     whole_own.start()
 
+    rep = lax.axis_index("rep")
+    odd = lax.rem(rep, 2)
+    hl = dl // 2
+
     def piece(half, src, dst):
-        return (wts.at[:, pl.ds(pl.multiple_of(half * peers * e + dst * e, 128), e)],
-                cols.at[pl.ds(pl.multiple_of(src * dl, dl), dl), pl.ds(half * e, e)])
+        return (wts.at[pl.ds(pl.multiple_of(odd * hl, hl), hl), pl.ds(pl.multiple_of(half * peers * e + dst * e, 128), e)],
+                cols.at[src, odd, :, pl.ds(half * e, e)])
     kept = [pltpu.make_async_copy(*piece(half, me, me), own_sem.at[2 + half]) for half in range(2)]
+    swapped = remote(cols.at[:, odd], cols.at[:, odd], w_send.at[2 * peers - 2], w_recv.at[2 * peers - 2], {"rep": rep + 1 - 2 * odd})
     sent = [remote(*piece(half, me, p), w_send.at[2 * k + half], w_recv.at[2 * k + half], p)
             for k, p in enumerate(others) for half in range(2)]
 
@@ -343,6 +348,10 @@
                     def _(kind=kind, q=q):
                         landed(kind, q, y, c, 0).wait_recv()
                         onward(kind, q)
+        if number == 2:
+            for copy in kept + sent:
+                copy.wait()
+            swapped.start()
         if number == 1:
             tiny_wait()
             last = small_out.at[:, :, c]
@@ -371,8 +380,7 @@
                 def _(kind=kind, up=up):
                     for q in range(chunks):
                         hop(kind, q, up).wait_send()
-    for copy in kept + sent:
-        copy.wait()
+    swapped.wait()
     whole_own.wait()
 
 
@@ -386,21 +394,33 @@
     out, tiles, cols = pl.pallas_call(
         functools.partial(gather_kernel, dims=dims, chunks=chunks),
         out_shape=[jax.ShapeDtypeStruct((nz, ny, nc, w, d), x.dtype), jax.ShapeDtypeStruct((nz, ny, nc, 8, 128), F32),
-                   jax.ShapeDtypeStruct((peers * dl, 2 * e), BF16)],
+                   jax.ShapeDtypeStruct((peers, 2, dl // 2, 2 * e), BF16)],
         in_specs=[pl.BlockSpec(memory_space=pl.ANY), pl.BlockSpec(memory_space=pltpu.VMEM), pl.BlockSpec(memory_space=pl.ANY)],
         out_specs=[pl.BlockSpec(memory_space=pl.ANY), pl.BlockSpec(memory_space=pltpu.VMEM), pl.BlockSpec(memory_space=pl.ANY)],
         scratch_shapes=[pltpu.SemaphoreType.DMA((copies,)), pltpu.SemaphoreType.DMA((copies,)),
                         pltpu.SemaphoreType.DMA((nz + ny,)), pltpu.SemaphoreType.DMA((nz + ny,)),
-                        pltpu.SemaphoreType.DMA((2 * peers - 2,)), pltpu.SemaphoreType.DMA((2 * peers - 2,)),
+                        pltpu.SemaphoreType.DMA((2 * peers - 1,)), pltpu.SemaphoreType.DMA((2 * peers - 1,)),
                         pltpu.SemaphoreType.DMA((4,))],
         compiler_params=pltpu.CompilerParams(collective_id=collective_id, has_side_effects=True, vmem_limit_bytes=VMEM),
         cost_estimate=pl.CostEstimate(flops=8 * 10 ** 10, bytes_accessed=2 * peers * w * d, transcendentals=0),
     )(x, small, wts)
-    return out.reshape(peers, w, d), tiles.reshape(peers, 8, 128), cols
-
-
-def scatter_steps(refs, dims, reps):
-    part, g, out, g_out, rc, own, ry, rz, rg, load, send, recv, g_load, g_send, g_recv = refs
+    return out.reshape(peers, w, d), tiles.reshape(peers, 8, 128), cols.reshape(peers * dl, 2 * e)
+
+
+def meet(dims, reps):
+    nz, ny, _ = dims
+    me, rep = lax.axis_index("shard"), lax.axis_index("rep")
+    c, y, z = me % 2, (me // 2) % ny, me // (2 * ny)
+    if reps:
+        greet([lax.rem(me + k, nz * ny * 2) for k in range(1, nz * ny * 2)]
+              + [{"rep": lax.rem(rep + k, reps)} for k in range(1, reps)])
+    else:
+        greet([(z * ny + y) * 2 + 1 - c] + [(z * ny + lax.rem(y + k, ny)) * 2 + c for k in range(1, ny)]
+              + [(lax.rem(z + k, nz) * ny + y) * 2 + c for k in range(1, nz)])
+
+
+def scatter_steps(refs, dims, reps, lag_y=2, lag_z=4, sum_at=4, cross_at=9, first_col=0):
+    part, g, out, g_out, rc, own, ry, rz, ga, gs, rg, load, send, recv, g_load, a_send, a_recv, b_send, b_recv, c_send, c_recv = refs
     nz, ny, _ = dims
     me, rep = lax.axis_index("shard"), lax.axis_index("rep")
     c, y, z = me % 2, (me // 2) % ny, me // (2 * ny)
@@ -433,27 +453,82 @@
         return [remote(rc.at[a, y, rows[q]], rz.at[k, rows[q]], *pair(q, ny + k), where(a, y, c))
                 for k, a in enumerate(zs)]
 
-    def handed():
-        dl = rg.shape[2]
-        spot = lambda p: g.at[pl.ds(pl.multiple_of(p * dl, dl), dl)]
-        return pltpu.make_async_copy(spot(me), rg.at[rep, me], g_load.at[0]), [
-            remote(spot(p), rg.at[rep, me], g_send.at[k], g_recv.at[k], p) for k, p in enumerate(others)]
-
-    def crossed():
-        return [remote(rg.at[rep], rg.at[rep], g_send.at[peers - 1 + k], g_recv.at[peers - 1 + k], p)
-                for k, p in enumerate(far)]
+    groups = peers // reps
+    owner_here = lax.rem(me, reps) == rep
+
+    def shared():
+        return pltpu.make_async_copy(g.at[:, rep], ga.at[rep], g_load.at[0]), [
+            remote(g.at[:, lax.rem(rep + k, reps)], ga.at[rep], a_send.at[k - 1], a_recv.at[k - 1], far[k - 1])
+            for k in range(1, reps)]
+
+    def handed(k):
+        p = lax.rem(me // reps + k, groups)
+        return remote(gs.at[p], rg.at[me], b_send.at[k], b_recv.at[me], p * reps + rep)
+
+    def arrived(k):
+        src = lax.rem(me + k, peers)
+        return remote(gs.at[0], rg.at[src], b_send.at[0], b_recv.at[src], lax.rem(me + 1, peers))
+
+    def crossed(k):
+        return remote(rg, rg, c_send.at[k - 1], c_recv, far[k - 1])
+
+    def g_sum():
+        kept, sent = shared()
+        for copy in [kept] + sent:
+            copy.wait()
+
+        def add(p, _):
+            total = ga[0, p].astype(F32)
+            for k in range(1, reps):
+                total = total + ga[k, p].astype(F32)
+            gs[p] = total.astype(BF16)
+            return 0
+        lax.fori_loop(0, groups, add, 0)
+
+        @pl.when(owner_here)
+        def _():
+            rg[me] = gs[me // reps]
+
+        @pl.when(jnp.logical_not(owner_here))
+        def _():
+            handed(0).start()
+        for k in range(1, groups):
+            handed(k).start()
+
+    def g_cross():
+        @pl.when(owner_here)
+        def _():
+            for k in range(1, peers):
+                arrived(k).wait_recv()
+            for k in range(1, reps):
+                crossed(k).start()
+
+        @pl.when(jnp.logical_not(owner_here))
+        def _():
+            handed(0).wait_send()
+        for k in range(1, groups):
+            handed(k).wait_send()
+
+    def g_end():
+        @pl.when(owner_here)
+        def _():
+            for k in range(1, reps):
+                crossed(k).wait_send()
+
+        @pl.when(jnp.logical_not(owner_here))
+        def _():
+            crossed(1).wait_recv()
+        e = rg.shape[2]
+        for p in range(peers):
+            g_out[:, first_col + p * e:first_col + (p + 1) * e] = rg[p].astype(F32)
 
     def start():
-        if g is None:
-            greet([across] + [where(z, b, c) for b in ys] + [where(a, y, c) for a in zs])
-        else:
-            greet(others + far)
         for q in range(min(slots, chunks)):
             loads(q).start()
         for q in range(chunks):
             first(q).start()
         if g is not None:
-            kept, sent = handed()
+            kept, sent = shared()
             for copy in [kept] + sent:
                 copy.start()
 
@@ -496,29 +571,19 @@
     def step(s):
         if s < chunks:
             over_core(s)
-        if 0 <= s - 2 < chunks:
-            over_y(s - 2)
-        if 0 <= s - 4 < chunks:
-            over_z(s - 4)
-        if s == chunks // 2 + 1 and g is not None:
-            kept, sent = handed()
-            for copy in [kept] + sent:
-                copy.wait()
-            for copy in crossed():
-                copy.start()
+        if 0 <= s - lag_y < chunks:
+            over_y(s - lag_y)
+        if 0 <= s - lag_z < chunks:
+            over_z(s - lag_z)
+        if s == sum_at and g is not None:
+            g_sum()
+        if s == cross_at and g is not None:
+            g_cross()
 
     def finish():
-        if g is None:
-            return
-        for copy in crossed():
-            copy.wait()
-        e = rg.shape[3]
-        for p in range(peers):
-            total = rg[0, p].astype(F32)
-            for k in range(1, reps):
-                total = total + rg[k, p].astype(F32)
-            g_out[:, p * e:(p + 1) * e] = total
-    return start, [functools.partial(step, s) for s in range(chunks + 4)], finish
+        if g is not None:
+            g_end()
+    return start, [functools.partial(step, s) for s in range(chunks + lag_z)], finish
 
 
 def scatter_scratch(peers, w, d, size, g=None):
@@ -532,47 +597,112 @@
     if g is None:
         return out + tail
     reps = lax.axis_size("rep")
-    count = peers + reps - 2
-    return (out + [pltpu.VMEM((reps, peers, g.shape[0] // peers, g.shape[1]), BF16)] + tail
-            + [dma((1,)), dma((count,)), dma((count,))])
-
-
-def scatter_kernel(part, g, out, g_out, rc, own, ry, rz, rg, load, send, recv, g_load, g_send, g_recv, *, dims, reps):
-    start, steps, finish = scatter_steps(
-        (part, g, out, g_out, rc, own, ry, rz, rg, load, send, recv, g_load, g_send, g_recv), dims, reps)
-    start()
-    for step in steps:
-        step()
-    finish()
-
-
-def scatter(part, g, collective_id, size=32):
-    peers, w, d = part.shape
-    dims = lattice(peers)
-    reps = lax.axis_size("rep")
     dl, e = g.shape[0] // peers, g.shape[1]
-    return pl.pallas_call(
-        functools.partial(scatter_kernel, dims=dims, reps=reps),
-        out_shape=[jax.ShapeDtypeStruct((w, d), F32), jax.ShapeDtypeStruct((dl, peers * e), F32)],
-        in_specs=[pl.BlockSpec(memory_space=pl.ANY)] * 2,
-        out_specs=[pl.BlockSpec(memory_space=pltpu.VMEM)] * 2,
-        scratch_shapes=scatter_scratch(peers, w, d, size, g),
-        compiler_params=pltpu.CompilerParams(collective_id=collective_id, has_side_effects=True, vmem_limit_bytes=VMEM),
-        cost_estimate=pl.CostEstimate(flops=8 * 10 ** 10, bytes_accessed=2 * peers * w * d, transcendentals=0),
-    )(part.reshape(dims + (w, d)), g)
-
-
-def beside(b, grid, start, steps, finish):
+    return (out + [pltpu.VMEM((reps, peers // reps, dl, e), BF16), pltpu.VMEM((peers // reps, dl, e), BF16),
+                   pltpu.VMEM((peers, dl, e), BF16)] + tail
+            + [dma((1,)), dma((reps - 1,)), dma((reps - 1,)), dma((peers // reps,)), dma((peers,)), dma((reps - 1,)), dma])
+
+
+def allsum_steps(refs, dims, finish):
+    part, result, out, mine, rc, low, ry, rz, load, send, recv = refs
+    nz, ny, _ = dims
+    me = lax.axis_index("shard")
+    c, y, z = me % 2, (me // 2) % ny, me // (2 * ny)
+    where = lambda a, b, d: (a * ny + b) * 2 + d
+    across = where(z, y, 1 - c)
+    ys = [lax.rem(y + k, ny) for k in range(1, ny)]
+    zs = [lax.rem(z + k, nz) for k in range(1, nz)]
+    base = [0, 1, ny, ny + nz - 1, ny + 2 * nz - 2, 2 * ny + 2 * nz - 3]
+
+    def sem(stage, k):
+        return send.at[base[stage] + k], recv.at[base[stage] + k]
+
+    def copies(stage):
+        if stage == 0:
+            return [remote(part.at[:, :, 1 - c], rc, *sem(0, 0), across)]
+        if stage == 1:
+            return [remote(low.at[:, b], ry.at[k], *sem(1, k), where(z, b, c)) for k, b in enumerate(ys)]
+        if stage == 2:
+            return [remote(low.at[a, y], rz.at[k], *sem(2, k), where(a, y, c)) for k, a in enumerate(zs)]
+        if stage == 3:
+            held, targets = out.at[z, y, c], [where(a, y, c) for a in zs]
+        elif stage == 4:
+            held, targets = out.at[:, y, c], [where(z, b, c) for b in ys]
+        else:
+            held, targets = out.at[:, :, c], [across]
+        return [remote(held, held, *sem(stage, k), target) for k, target in enumerate(targets)]
+
+    def own():
+        return pltpu.make_async_copy(part.at[:, :, c], mine, load.at[0])
+
+    def start():
+        own().start()
+        for copy in copies(0):
+            copy.start()
+
+    def step(s):
+        if s == 0:
+            own().wait()
+        for copy in copies(s):
+            copy.wait()
+        if s == 0:
+            def add(a, _):
+                i, j = a // ny, a % ny
+                total = mine[i, j] + rc[i, j]
+                mine[i, j] = total
+                low[i, j] = total.astype(BF16)
+                return 0
+            lax.fori_loop(0, nz * ny, add, 0)
+        if s == 1:
+            for a in range(nz):
+                total = mine[a, y]
+                for k in range(ny - 1):
+                    total = total + ry[k, a].astype(F32)
+                mine[a, y] = total
+                low[a, y] = total.astype(BF16)
+        if s == 2:
+            total = mine[z, y]
+            for k in range(nz - 1):
+                total = total + rz[k].astype(F32)
+            out[z, y, c] = finish(total)
+        if s < 5:
+            for copy in copies(s + 1):
+                copy.start()
+
+    def end():
+        result[...] = out[...]
+    return start, [functools.partial(step, s) for s in range(6)], end
+
+
+def allsum_scratch(peers, cols, width):
+    nz, ny, nc = lattice(peers)
+    dma = pltpu.SemaphoreType.DMA
+    count = 2 * (1 + ny - 1 + nz - 1)
+    return [pltpu.VMEM((nz, ny, nc, width, 256), BF16), pltpu.VMEM((nz, ny, cols, width), F32),
+            pltpu.VMEM((nz, ny, cols, width), F32),
+            pltpu.VMEM((nz, ny, cols, width), BF16), pltpu.VMEM((ny - 1, nz, cols, width), BF16),
+            pltpu.VMEM((nz - 1, cols, width), BF16), dma((1,)), dma((count,)), dma((count,))]
+
+
+def beside(b, grid, dims, reps, transfers):
     @pl.when(b == 0)
     def _():
-        start()
-    for s, step in enumerate(steps):
-        @pl.when(b == (s * (grid - 1)) // len(steps) + 1)
-        def _(step=step):
-            step()
+        meet(dims, reps)
+        for start, _, _, _ in transfers:
+            start()
+    for _, steps, _, when in transfers:
+        for s, step in enumerate(steps):
+            @pl.when(b == (when[s] if when else (s * (grid - 1)) // len(steps) + 1))
+            def _(step=step):
+                step()
+
     @pl.when(b == grid - 1)
     def _():
-        finish()
+        for _, _, finish, _ in transfers:
+            finish()
+
+
+PACED = [1, 1, 1, 1, 2, 2, 2, 2, 3, 5, 6, 8, 9, 11, 13, 14, 15, 15]
 
 
 def fill(low_ref, bcs_scr, bc_scr, n):
@@ -648,26 +778,28 @@
 
 
 def behind(*refs, n, e, dims, reps, sending):
-    (low_ref, xz_ref, xc_ref, mask_ref, dy_ref, dg_ref, nu_ref, cks_ref, ckp_ref,
-     wo_ref, wdt_ref, dtb_ref, a2_ref, skip_ref, hin_ref, qin_ref) = refs[:16]
-    refs = refs[16:]
+    (low_ref, xz_ref, xc_ref, mask_ref, dg_ref, cks_ref, ckp_ref,
+     wo_ref, wdt_ref, dtb_ref, a2_ref, skip_ref, hin_ref, qin_ref) = refs[:14]
+    refs = refs[14:]
     if sending:
-        before, refs = refs[0], refs[1:]
-    out_ref, dz_ref, dxc_ref, part_ref, go_ref, gdt_ref, ga_ref, vec_ref, gz_ref = refs[:9]
-    refs = refs[9:]
+        before, adding, refs = refs[0], refs[1], refs[2:]
+    out_ref, dz_ref, dxc_ref, part_ref, gated_ref, gdt_ref, ga_ref, vec_ref = refs[:8]
+    refs = refs[8:]
     if sending:
-        summed, refs = refs[0], refs[1:]
+        summed, added, refs = refs[0], refs[1], refs[2:]
     (h_scr, a_scr, q_scr, bcs_scr, bc_scr, pre_scr, st_scr, sd_scr, dx_scr, dy_scr, y_scr, da_scr, gb_scr) = refs[:13]
     b = pl.program_id(0)
     if sending:
-        rc, own, ry, rz, load, send, recv = refs[13:]
-        beside(b, dims[0] * dims[1] * dims[2], *scatter_steps(
-            (before, None, summed, None, rc, own, ry, rz, None, load, send, recv, None, None, None), dims, reps))
+        rc, own, ry, rz, load, send, recv = refs[13:20]
+        beside(b, dims[0] * dims[1] * dims[2], dims, 0, [
+            allsum_steps((adding, added) + refs[20:], dims, functools.partial(spread_plain, n=n)) + (None,),
+            scatter_steps((before, None, summed, None, rc, own, ry, rz, None, None, None, load, send, recv) + (None,) * 7,
+                          dims, reps, 8, 10) + (PACED,)])
     m = 1
     @pl.when(b == 0)
     def _():
         q_scr[...] = qin_ref[...]
-        for ref in (go_ref, gdt_ref, ga_ref, vec_ref, gz_ref):
+        for ref in (gdt_ref, ga_ref, vec_ref):
             ref[...] = jnp.zeros_like(ref)
     fill(low_ref, bcs_scr, bc_scr, n)
     pre = mm(low_ref[0, :, :128], wdt_ref[...]) + dtb_ref[...]
@@ -751,10 +883,9 @@
     y = y_scr[...] + skip * xc
     gated = (y * (z * sz)).astype(BF16)
     out_ref[0] = mm(gated, wo_ref[...]).astype(BF16)
-    go_ref[...] += tn(gated, dy_ref[0])
+    gated_ref[0] = gated
     dz = (dg_ref[0] * y * (sz * (1.0 + z * (1.0 - sz)))).astype(BF16)
     dz_ref[0] = dz
-    gz_ref[...] += tn(nu_ref[0], dz)
     gb = gb_scr[...]
     dy_y = dy_scr[...]
     dxc_ref[0] = dy_y * skip + st_scr[...] * gb
@@ -766,55 +897,110 @@
     vec_ref[1:2] += jnp.sum(dy_y * xc, axis=0, keepdims=True)
 
 
+def back(*refs, e, n, dims, reps, role):
+    (xz_ref, prev_ref, edge_ref, mask_ref, ddbc_ref, nu_ref, next_ref, w_ref, xpt_ref, cw_ref, cb_ref, dxc_ref, dz_ref,
+     before, extra) = refs[:15]
+    b = pl.program_id(0)
+    peers = dims[0] * dims[1] * dims[2]
+    if role == "sum":
+        nu_all, dy_all, dz0, dz1, gated0, gated1 = refs[15:21]
+        v_ref, gx, vec_ref, summed, prod_z, prod_o, done, carry, acc_z, acc_o = refs[21:31]
+        refs = refs[31:]
+        rc, own, ry, rz, load, send, recv = refs[:7]
+        beside(b, peers, dims, 0, [
+            allsum_steps((extra, done) + refs[7:], dims, functools.partial(spread_plain, n=n)) + (None,),
+            scatter_steps((before, None, summed, None, rc, own, ry, rz, None, None, None, load, send, recv) + (None,) * 7,
+                          dims, reps) + (None,)])
+    else:
+        gx_before, v_out, vec_ref, summed, summed_own, g_done, carry, gx, gx_low, v_buf, v_sem, gx_sem = refs[15:27]
+        refs = refs[27:]
+        half = len(refs) // 2
+        earlier = scatter_steps((before, extra, summed, g_done) + refs[:half], dims, reps, 8, 10, 8, 15, peers * e)
+        latest = scatter_steps((v_out, gx_low, summed_own, g_done) + refs[half:], dims, reps, 8, 10, 4, 12)
+
+        @pl.when(b == 0)
+        def _():
+            meet(dims, reps)
+            earlier[0]()
+            copy = pltpu.make_async_copy(gx_before, gx, gx_sem.at[0])
+            copy.start()
+            copy.wait()
+        early = [1, 1, 1, 1, 2, 2, 2, 2, 7, 11, 14]
+        for k, when in enumerate(early):
+            @pl.when(b == when)
+            def _(k=k):
+                earlier[1][k]()
+
+    @pl.when(b == 0)
+    def _():
+        carry[...] = next_ref[...]
+        vec_ref[...] = jnp.zeros_like(vec_ref)
+        if role == "sum":
+            acc_z[...] = jnp.zeros_like(acc_z)
+            acc_o[...] = jnp.zeros_like(acc_o)
+            gx[...] = jnp.zeros_like(gx)
+    rows = xz_ref.shape[1]
+    cw, cb = cw_ref[...], cb_ref[...]
+    x = xz_ref[0, :, :e].astype(F32)
+    before_x = prev_ref[0, rows - 2 * EDGE:, :e].astype(F32)[EDGE:]
+    before_x = jnp.where(b == peers - 1, edge_ref[...], before_x)
+    lag = lags(jnp.concatenate([before_x, x], axis=0), rows)
+    same = mask_ref[0]
+    dconv = (dxc_ref[0] + mm(ddbc_ref[0], xpt_ref[...])) * dsilu(convolve(lag, same, cw, cb))
+    vec_ref[4:5] += jnp.sum(dconv, axis=0, keepdims=True)
+    vec_ref[3:4] += jnp.sum(dconv * x, axis=0, keepdims=True)
+    dx = cw[3:4] * dconv
+    for k in range(1, 4):
+        masked = dconv * same[:, k - 1:k]
+        vec_ref[3 - k:4 - k] += jnp.sum(masked * lag[k], axis=0, keepdims=True)
+        sent = cw[3 - k:4 - k] * masked
+        dx = dx + jnp.concatenate([sent, carry[k - 1]], axis=0)[k:k + rows]
+        carry[k - 1] = sent[:EDGE]
+    dx = dx.astype(BF16)
+    v = nt(jnp.concatenate([dx, dz_ref[0]], axis=1), w_ref[...]).astype(BF16)
+    gx[...] += tn(nu_ref[0], dx)
+    if role == "sum":
+        v_ref[0] = v
+        acc_z[...] += tn(nu_all[0], jnp.concatenate([dz0[0], dz1[0]], axis=0))
+        acc_o[...] += tn(jnp.concatenate([gated0[0], gated1[0]], axis=0), dy_all[0])
+
+        @pl.when(b == peers - 1)
+        def _():
+            prod_z[...] = acc_z[...].astype(BF16)
+            prod_o[...] = acc_o[...].astype(BF16)
+        return
+
+    slot, at_ = b % 2, peers - 1 - b
+
+    def write(slot):
+        return pltpu.make_async_copy(v_buf.at[slot], v_out.at[at_ // (2 * dims[1]), (at_ // 2) % dims[1], at_ % 2], v_sem.at[slot])
+
+    @pl.when(b >= 2)
+    def _():
+        write(slot).wait()
+    v_buf[slot] = v
+    write(slot).start()
+
+    @pl.when(b == peers - 1)
+    def _():
+        write(0).wait()
+        write(1).wait()
+        for p in range(peers // reps):
+            for k in range(reps):
+                first = (p * reps + k) * gx_low.shape[2]
+                gx_low[p, k] = gx[first:first + gx_low.shape[2]].astype(BF16)
+        latest[0]()
+        for k, step in enumerate(latest[1]):
+            if len(early) + k < len(earlier[1]):
+                earlier[1][len(early) + k]()
+            step()
+        earlier[2]()
+        latest[2]()
+
+
 def dsilu(v):
     s = jax.nn.sigmoid(v)
     return s * (1.0 + v * (1.0 - s))
-
-
-def back(*refs, m, e, dims, reps):
-    (xz_ref, prev_ref, edge_ref, mask_ref, ddbc_ref, nu_ref, next_ref, w_ref, xpt_ref, cw_ref, cb_ref) = refs[:11]
-    dxc_refs, dz_refs = refs[11:11 + m], refs[11 + m:11 + 2 * m]
-    before, gz_ref = refs[11 + 2 * m:13 + 2 * m]
-    v_ref, gxl_ref, vec_ref, summed, gz_out, gx_ref, carry, dx_scr = refs[13 + 2 * m:21 + 2 * m]
-    rc, own, ry, rz, rg, *sems = refs[21 + 2 * m:]
-    beside(pl.program_id(0), dims[0] * dims[1] * dims[2], *scatter_steps(
-        (before, gz_ref, summed, gz_out, rc, own, ry, rz, rg, *sems), dims, reps))
-    b = pl.program_id(0)
-    @pl.when(b == 0)
-    def _():
-        carry[...] = next_ref[...]
-        gx_ref[...] = jnp.zeros_like(gx_ref)
-        vec_ref[...] = jnp.zeros_like(vec_ref)
-    first = b == pl.num_programs(0) - 1
-    rows = xz_ref.shape[1] // m
-    cw, cb = cw_ref[...], cb_ref[...]
-    dxc_all = mm(ddbc_ref[0], xpt_ref[...])
-    for i in range(m):
-        part = slice(i * rows, (i + 1) * rows)
-        x = xz_ref[0, part, :e].astype(F32)
-        before = prev_ref[0, (i + 1) * rows - 2 * EDGE:(i + 1) * rows, :e].astype(F32)[EDGE:]
-        before = jnp.where(first, edge_ref[i * EDGE:(i + 1) * EDGE], before)
-        lag = lags(jnp.concatenate([before, x], axis=0), rows)
-        same = mask_ref[0, part]
-        dconv = (dxc_refs[i][0] + dxc_all[part]) * dsilu(convolve(lag, same, cw, cb))
-        vec_ref[4:5] += jnp.sum(dconv, axis=0, keepdims=True)
-        vec_ref[3:4] += jnp.sum(dconv * x, axis=0, keepdims=True)
-        dx = cw[3:4] * dconv
-        for k in range(1, 4):
-            masked = dconv * same[:, k - 1:k]
-            vec_ref[3 - k:4 - k] += jnp.sum(masked * lag[k], axis=0, keepdims=True)
-            sent = cw[3 - k:4 - k] * masked
-            ext = jnp.concatenate([sent, carry[k - 1, i]], axis=0)
-            dx = dx + ext[k:k + rows]
-            carry[k - 1, i] = sent[:EDGE]
-        dx_scr[part] = dx
-    dx = dx_scr[...].astype(BF16)
-    v_ref[0] = nt(jnp.concatenate([dx, jnp.concatenate([ref[0] for ref in dz_refs], axis=0)], axis=1), w_ref[...]).astype(BF16)
-    gx_ref[...] += tn(nu_ref[0], dx)
-
-    @pl.when(first)
-    def _():
-        gxl_ref[...] = gx_ref[...].astype(BF16)
 
 
 def shift_rep(value, steps):
@@ -845,22 +1031,23 @@
     rising = lambda i: i
     falling = lambda i: peers - 1 - i
 
-    own = jnp.pad(jnp.concatenate([w32(segment_ids), jnp.pad(w32(norm_gain)[None], ((0, 0), (0, 128 - dl)))], axis=0),
-                  ((0, 7 - m), (0, 0)))
+    span = peers * reps
+    before = lax.ppermute(segment_ids[:, tl - taps + 1:], ("rep", "shard"), [(k, k + 1) for k in range(span - 1)])
+    before = jnp.where((rep > 0) | (lax.axis_index("shard") > 0), before, -1)
+    ext = jnp.concatenate([before, segment_ids], axis=1)
+    same = [w32(ext[:, taps - 1 - k:taps - 1 - k + tl] == segment_ids) for k in range(1, taps)]
+    same = jnp.stack(same, axis=1).reshape(m * (taps - 1), tl)
+    own = jnp.concatenate([same, jnp.pad(w32(norm_gain)[None], ((0, 0), (0, tl - dl))),
+                           jnp.zeros((7 - m * (taps - 1), tl), F32)], axis=0)
     hid_all, tiles, w_cols = gather(hidden_in.reshape(w, d), own, in_proj, 4)
-    gain = tiles[:, m, :dl].reshape(1, d)
-    ids = tiles[:, :m, :tl].astype(jnp.int32)
+    gain = tiles[:, m * (taps - 1), :dl].reshape(1, d)
     later, hid_all = lax.optimization_barrier((out_grad, hid_all))
     dy_all = lax.all_gather(later.reshape(w, d), "shard")
     u = w32(hidden_in)
     r = lax.rsqrt(jnp.mean(u * u, axis=2, keepdims=True) + 1e-5)
 
-    row_ids = ids.transpose(1, 0, 2).reshape(m, t)
-    before = jnp.where(rep > 0, shift_rep(row_ids[:, t - taps + 1:], 1), -1)
-    ext = jnp.concatenate([before, row_ids], axis=1)
-    same = jnp.stack([w32(ext[:, taps - 1 - k:taps - 1 - k + t] == row_ids) for k in range(1, taps)], axis=-1)
-    mask = jnp.pad(same, ((0, 0), (0, 0), (0, 8 - same.shape[-1])))
-    mask = mask.reshape(m, peers, tl, 8).transpose(1, 0, 2, 3).reshape(peers, w, 8)
+    mask = tiles[:, :m * (taps - 1)].reshape(peers, m, taps - 1, tl).transpose(0, 1, 3, 2).reshape(peers, w, taps - 1)
+    mask = jnp.pad(mask, ((0, 0), (0, 0), (0, 9 - taps)))
     halo = shift_rep(hid_all[peers - 1].reshape(m, tl, d)[:, tl - EDGE:].reshape(m * EDGE, d), 1)
 
     cw, cb = w32(conv_weight), w32(conv_bias)[None]
@@ -905,73 +1092,88 @@
 
         def one(a, i=i):
             return pl.BlockSpec((1,) + a.shape[1:], lambda b: (i, 0, 0))
-        ins = [low, xz, xc, mask, dy_all, dg, nu_all, cks, ckp, out_proj, dt_weight, dtb, a2, skip, h_in, q_in]
-        specs = [row(a, falling) for a in ins[:9]] + [whole(a) for a in ins[9:14]] + [one(a) for a in ins[14:]]
+        ins = [low, xz, xc, mask, dg, cks, ckp, out_proj, dt_weight, dtb, a2, skip, h_in, q_in]
+        specs = [row(a, falling) for a in ins[:7]] + [whole(a) for a in ins[7:12]] + [one(a) for a in ins[12:]]
         outs = [shp((peers, tl, d), BF16), shp((peers, tl, e), BF16), shp((peers, tl, e), F32),
-                shp((peers, rank + 2 * n, tl), F32), shp((e, d), F32), shp((rank, e), F32), shp((n, e), F32), shp((8, e), F32),
-                shp((d, e), F32)]
-        out_specs = [block(a, falling) for a in outs[:4]] + [whole(a) for a in outs[4:]]
+                shp((peers, rank + 2 * n, tl), F32), shp((peers, tl, e), BF16), shp((rank, e), F32), shp((n, e), F32), shp((8, e), F32)]
+        out_specs = [block(a, falling) for a in outs[:5]] + [whole(a) for a in outs[5:]]
         scratch = [pltpu.VMEM((tl * n + n, e), F32), pltpu.VMEM((tl * n, e), F32), pltpu.VMEM((1, n, e), F32),
                    pltpu.VMEM((tl, 128), F32), pltpu.VMEM((tl * n, 256), F32)] + [pltpu.VMEM((tl, e), F32)] * 8
         params = {}
         if i:
-            ins.append(rows_done[i - 1][0].reshape(dims + (tl, d)))
-            specs.append(anywhere)
-            outs.append(shp((tl, d), F32))
-            out_specs.append(whole(outs[-1]))
-            scratch += scatter_scratch(peers, tl, d, 16)
+            ins += [rows_done[i - 1][0].reshape(dims + (tl, d)), rows_done[i - 1][3].reshape(dims + (rank + 2 * n, tl))]
+            specs += [anywhere] * 2
+            outs += [shp((tl, d), F32), shp(dims + (tl, 256), BF16)]
+            out_specs += [whole(a) for a in outs[-2:]]
+            scratch += scatter_scratch(peers, tl, d, 16) + allsum_scratch(peers, rank + 2 * n, tl)
             params = dict(collective_id=5 + i, has_side_effects=True)
         rows_done.append(call(
             functools.partial(behind, n=n, e=e, dims=dims, reps=reps, sending=bool(i)), (peers,), specs, out_specs, outs,
             scratch, ins, flops=50 * 10 ** 9, **params))
-    g_out, g_dt, g_a, vec, g_z = (sum(done[k] for done in rows_done) for k in range(4, 9))
-    g_z = g_z.astype(BF16)
-
-    ddbc = allsum([done[3] for done in rows_done], functools.partial(spread_plain, n=n), 1)
+    g_dt, g_a, vec = (sum(done[k] for done in rows_done) for k in range(5, 8))
+
     xpt = jnp.pad(x_proj.T, ((0, 256 - x_proj.shape[1]), (0, 0)))
-    dxc8 = jnp.stack([done[2][0, :EDGE] for done in rows_done])
-
-    x8 = w32(xz[0].reshape(m, tl, 2 * e)[:, :EDGE, :e])
-    ext8 = jnp.concatenate([w32(edge).reshape(m, EDGE, e), x8], axis=1)
-    same8 = mask[0].reshape(m, tl, 8)[:, :EDGE]
-    conv8 = cb + cw[3] * x8
-    for k in range(1, taps):
-        conv8 = conv8 + cw[3 - k] * ext8[:, EDGE - k:2 * EDGE - k] * same8[:, :, k - 1:k]
-    d8 = dxc8 + mm(ddbc[0].reshape(m, tl, -1)[:, :EDGE].reshape(m * EDGE, -1), xpt).reshape(m, EDGE, e)
-    d8 = d8 * dsilu(conv8)
-    sent = jnp.stack([cw[3 - k] * d8 * same8[:, :, k - 1:k] for k in range(1, taps)])
-    follow = shift_rep(sent, -1)
-
-    last = rows_done[-1][0].reshape(dims + (tl, d))
-    ins = [xz, xz, w32(edge), mask, ddbc, nu_all, follow, w_cols, xpt, cw, cb]
-    ins += [done[2] for done in rows_done] + [done[1] for done in rows_done] + [last, g_z]
-    outs = [shp((peers, w, d), BF16), shp((d, e), BF16), shp((8, e), F32), shp((tl, d), F32), shp((dl, peers * e), F32)]
-    earlier = lambda i: jnp.maximum(peers - 2 - i, 0)
-    specs = ([block(a, falling) for a in ins[:6]] + [whole(a) for a in ins[6:11]] + [block(a, falling) for a in ins[11:-2]]
-             + [anywhere] * 2)
-    specs[1], specs[2] = block(xz, earlier), whole(ins[2])
-    v_part, g_x, vec2, last_sum, grad_z = call(
-        functools.partial(back, m=m, e=e, dims=dims, reps=reps), (peers,), specs,
-        [block(outs[0], falling)] + [whole(a) for a in outs[1:]], outs,
-        [pltpu.VMEM((d, e), F32), pltpu.VMEM((taps - 1, m, EDGE, e), F32), pltpu.VMEM((w, e), F32)]
-        + scatter_scratch(peers, tl, d, 16, g_z), ins, flops=2 * peers * w * d * 3 * e, collective_id=2, has_side_effects=True)
-    out_sum = jnp.stack([done[9] for done in rows_done[1:]] + [last_sum])
-    layer_out = (u + out_sum).astype(BF16)
-
-    g_out = sum_rep(g_out)
-    v_part, g_out = lax.optimization_barrier((v_part, g_out))
-    v, grad_x = scatter(v_part, g_x, 3)
-    v = v.reshape(m, tl, d) * gain
+    xz_first = xz[0].reshape(m, tl, 2 * e)[:, :EDGE, :e]
+    edges = w32(edge).reshape(m, EDGE, e)
+    out_sums = [done[8] for done in rows_done[1:]]
+    ddbcs = [done[9].reshape(peers, tl, 256) for done in rows_done[1:]]
+    backs = []
+    for i in range(m):
+        ext8 = jnp.concatenate([edges[i], w32(xz_first[i])], axis=0)
+        same8 = mask[0, i * tl:i * tl + EDGE]
+        conv8 = cb + cw[3] * ext8[EDGE:]
+        for k in range(1, taps):
+            conv8 = conv8 + cw[3 - k] * ext8[EDGE - k:2 * EDGE - k] * same8[:, k - 1:k]
+        d8 = (rows_done[i][2][0, :EDGE] + mm(ddbcs[i][0, :EDGE], xpt)) * dsilu(conv8)
+        follow = shift_rep(jnp.stack([cw[3 - k] * d8 * same8[:, k - 1:k] for k in range(1, taps)]), -1)
+
+        def row(a, order, i=i):
+            return pl.BlockSpec((1, tl) + a.shape[2:], lambda b: (order(b), i, 0))
+        earlier = lambda b: jnp.maximum(peers - 2 - b, 0)
+        ins = [xz, xz, edges[i], mask, ddbcs[i], nu_all, follow, w_cols, xpt, cw, cb, rows_done[i][2], rows_done[i][1]]
+        specs = [row(xz, falling), row(xz, earlier), whole(ins[2]), row(mask, falling), block(ins[4], falling), row(nu_all, falling)]
+        specs += [whole(a) for a in ins[6:11]] + [block(a, falling) for a in ins[11:13]] + [anywhere] * 2
+        carry = pltpu.VMEM((taps - 1, EDGE, e), F32)
+        if i < m - 1:
+            ins += [rows_done[i + 1][0].reshape(dims + (tl, d)), rows_done[i + 1][3].reshape(dims + (rank + 2 * n, tl))]
+            more = [nu_all, dy_all] + [done[1] for done in rows_done] + [done[4] for done in rows_done]
+            ins += more
+            specs += [block(a, falling) for a in more]
+            outs = [shp((peers, tl, d), BF16), shp((d, e), F32), shp((8, e), F32), shp((tl, d), F32), shp((d, e), BF16),
+                    shp((e, d), BF16), shp(dims + (tl, 256), BF16)]
+            out_specs = [block(outs[0], falling)] + [whole(a) for a in outs[1:]]
+            scratch = [carry, pltpu.VMEM((d, e), F32), pltpu.VMEM((e, d), F32)]
+            scratch += scatter_scratch(peers, tl, d, 16) + allsum_scratch(peers, rank + 2 * n, tl)
+        else:
+            g_z = backs[i - 1][4]
+            ins += [backs[i - 1][0].reshape(dims + (tl, d)), g_z.reshape(peers // reps, reps, dl, e), backs[i - 1][1]]
+            specs += [anywhere]
+            outs = [shp(dims + (tl, d), BF16), shp((8, e), F32), shp((tl, d), F32), shp((tl, d), F32), shp((dl, 2 * peers * e), F32)]
+            out_specs = [anywhere] + [whole(a) for a in outs[1:]]
+            scratch = [carry, pltpu.VMEM((d, e), F32), pltpu.VMEM((peers // reps, reps, dl, e), BF16), pltpu.VMEM((2, tl, d), BF16),
+                       pltpu.SemaphoreType.DMA((2,)), pltpu.SemaphoreType.DMA((1,))] + scatter_scratch(peers, tl, d, 16, g_z) * 2
+        backs.append(call(
+            functools.partial(back, e=e, n=n, dims=dims, reps=reps, role="sum" if i < m - 1 else "owner"), (peers,), specs,
+            out_specs, outs, scratch, ins, flops=peers * w * d * 3 * e, collective_id=8 + i, has_side_effects=True))
+        if i < m - 1:
+            out_sums.append(backs[i][3])
+            ddbcs.append(backs[i][6].reshape(peers, tl, 256))
+    g_out, _ = lax.optimization_barrier((backs[0][5], follow))
+    vec2 = backs[0][2] + backs[1][1]
+    layer_out = (u + jnp.stack(out_sums)).astype(BF16)
+
+    v = jnp.stack([backs[1][2], backs[1][3]]) * gain
     in_grad = w32(out_grad) + r * v - u * (r * r * r) * jnp.mean(v * u, axis=2, keepdims=True)
 
-    grad_in_proj = jnp.concatenate([grad_x, grad_z], axis=1)
+    grad_in_proj = backs[1][4]
     grad_gain = jnp.sum(grad_in_proj * w32(in_proj), axis=1) / w32(norm_gain)
 
-    small = jnp.concatenate([vec, vec2, g_a * a_mat, g_dt, tn(xc.reshape(peers * w, e), ddbc.reshape(peers * w, -1)).T], axis=0)
-    small = sum_rep(small)
-    vec, vec2, g_a, g_dt, g_xp = (small[:8], small[8:16], small[16:16 + n], small[16 + n:16 + n + rank], small[16 + n + rank:])
+    g_xproj = sum(tn(xc.reshape(peers, m, tl, e)[:, i].reshape(peers * tl, e), ddbcs[i].reshape(peers * tl, 256)) for i in range(m))
+    small = jnp.concatenate([vec, g_a * a_mat, g_dt, g_xproj.T], axis=0)
+    small, vec2 = sum_rep(small), sum_rep(vec2)
+    vec, g_a, g_dt, g_xp = small[:8], small[8:8 + n], small[8 + n:8 + n + rank], small[8 + n + rank:]
     return (layer_out, in_grad, grad_gain, grad_in_proj, vec2[:taps], vec2[taps], g_xp[:rank + 2 * n].T, g_dt, vec[0],
-            g_a, vec[1], g_out)
+            g_a, vec[1], sum_rep(g_out))
 
 
 def solution(mesh):

time: 764 us -> 746 us (0.976)
  Pallas kernels: 659 us -> 638 us
    pallas_call x5 -> x6, Pallas kernels: 298 us -> 452 us  [call(): pl.pallas_call(kernel, grid=grid, in_specs=in_specs, out_specs=out_specs,...]
    pallas_call x1 -> x0, Pallas kernels: 120 us -> none  [scatter(): pl.pallas_call(functools.partial(scatter_kernel, dims=dims, reps=reps), o...]
    pallas_call x2 -> x1, Pallas kernels: 114 us -> 68.5 us  [allsum(): pl.pallas_call(functools.partial(allsum_kernel, dims=dims, chunks=chunks,...]
    pallas_call x1, Pallas kernels: 126 us -> 118 us  [gather(): pl.pallas_call(functools.partial(gather_kernel, dims=dims, chunks=chunks)...]
  transfers between devices with their start and end apart: 6 -> 8, of which waited for: 3 -> 3; matrix products, arithmetic and copies ran while one was open for 2% -> 4% of each run, Pallas kernels for 24% -> 33%
where the time goes in v6:
time: 746 us; the launch traced here: 744 us
  Pallas kernels  638 us (86%)
  waiting for transfers between devices  28.9 us (4%)
  local copies, waits for them, and re-layouts  21.2 us (3%)
  other arithmetic  18.2 us (2%)
  between operations  14.7 us (2%)
  starting transfers between devices  12.4 us (2%)
    pallas_call x6, Pallas kernels, call(): pl.pallas_call(kernel, grid=grid, in_specs=in_specs, out_specs=out_specs,...  452 us
    pallas_call x1, Pallas kernels, gather(): pl.pallas_call(functools.partial(gather_kernel, dims=dims, chunks=chunks)...  118 us
    pallas_call x1, Pallas kernels, allsum(): pl.pallas_call(functools.partial(allsum_kernel, dims=dims, chunks=chunks,...  68.5 us
    all_gather x1, waiting for transfers between devices, on_device(): dy_all = lax.all_gather(later.reshape(w, d), 'shard')  27.8 us
  transfers between devices with their start and end apart: 8, of which 3 were waited for; matrix products, arithmetic and copies ran while one was open for 4% of the time, Pallas kernels for 33%

profile of v6, /device:TPU:0, one launch (start us, length us, event | category | flops | bytes accessed | tf_op | source)
XLA Modules:
  0.0 744.3 jit_solution(13178593070966704042)
XLA Ops:
  7.2 0.8 slice.172
  8.0 2.3 collective-permute-start
  10.3 0.7 convert_bitcast_fusion
  11.1 0.9 compare_bitcast_fusion.2
  12.1 0.7 maximum_maximum_fusion.small
  12.8 117.6 %shard_map.220 = (bf16[4,2,2,256,2048]{4,3,2,1,0:T(8,128)(2,1)}, f32[4,2,2,8,128]{4,3,2,1,0:T(8,128)}, bf16[16,2,64,512]{3,2,1,0:T(8,128)(2,1)}) custom-call(bf16[256,2048]{1,0:T(8,128)(2,1)} %bitcast.129, f32[8,128]{1,0:T(8,128)} %maximum_maximum_fusion.small, bf16[128,8192]{1,0:T(8,128)(2,1)} %wts.1), custom_call_target="tpu_custom_call" | custom-call | flops 80000000000 | bytes 16777216 | tf_op jit(solution)/shard_map/pallas_call | solution.py:394
  132.7 0.7 pad.9.refs_8_
  133.9 0.6 fusion.14.a2_ref.refs_10_
  134.6 0.8 copy.35
  135.4 0.6 copy.33
  136.0 1.5 pad.8.mask_ref.refs_3_
  137.6 1.4 slice.176
  139.0 3.4 collective-permute-start.1
  142.5 0.8 slice_reduce_fusion.5
  143.2 1.5 fusion.45
  144.7 0.7 slice_reduce_fusion.2
  145.4 0.6 copy-done.40
  146.1 27.4 %shard_map.221 = (bf16[16,256,512]{2,1,0:T(8,128)(2,1)}, bf16[16,256,256]{2,1,0:T(8,128)(2,1)}, bf16[16,256,2048]{2,1,0:T(8,128)(2,1)}, bf16[16,256]{1,0:T(8,128...) custom-call(bf16[16,256,2048]{2,1,0:T(8,128)(2,1)} %bitcast.159, bf16[2048,512]{1,0:T(8,128)(2,1)} %bitcast.118, ...), custom_call_target="tpu_custom_call" | custom-call | flops 8589934592 | bytes 44864512 | tf_op jit(solution)/shard_map/pallas_call | solution.py:41
  173.5 1.0 slice.189
  174.5 68.5 %shard_map.222 = bf16[4,2,2,256,256]{4,3,2,1,0:T(8,128)(2,1)} custom-call(f32[4,2,2,160,128]{4,3,2,1,0:T(8,128)} %bitcast.140, f32[4,2,2,160,128]{4,3,2,1,0:T(8,128)} %bitcast.141), custom_call_target="tpu_custom_call" | custom-call | tf_op jit(solution)/shard_map/pallas_call | solution.py:218
  244.2 1.2 fusion.43
  245.4 27.8 %all-gather.3.cloned.1.call-done.dy_ref.refs_16_ = bf16[16,256,2048]{2,1,0:T(8,128)(2,1)} async-done(((bf16[1,256,2048]{2,1,0:T(8,128)(2,1)}), bf16[16,256,2048]{2,1,0:T(8,128)(2,1)}) %all-gather.3.cloned.1.call-update) | async-done | bytes 16777232 | tf_op jit(solution)/shard_map/all_gather | solution.py:1045
  273.2 47.4 %shard_map.223 = (f32[16,2,16,256]{3,2,1,0:T(8,128)}, f32[16,2,16,256]{3,2,1,0:T(8,128)}, f32[3,2,16,256]{3,2,1,0:T(8,128)}, f32[16,256,256]{2,1,0:T(8,128)}) custom-call(bf16[16,256,256]{2,1,0:T(8,128)(2,1)} %bitcast.137, bf16[16,256,512]{2,1,0:T(8,128)(2,1)} %get-tuple-element.63.xz_ref.refs_1_.refs_0_, ...), custom_call_target="tpu_custom_call" | custom-call | flops 40000000000 | bytes 31769600 | tf_op jit(solution)/shard_map/pallas_call | solution.py:41
  320.6 6.0 all-gather
  326.6 0.6 fusion.9
  327.2 59.3 %shard_map.224 = (bf16[16,128,2048]{2,1,0:T(8,128)(2,1)}, bf16[16,128,256]{2,1,0:T(8,128)(2,1)}, f32[16,128,256]{2,1,0:T(8,128)}, f32[16,160,128]{2,1,0:T(8,128)...) custom-call(bf16[16,256,256]{2,1,0:T(8,128)(2,1)} %bitcast.138, ...), custom_call_target="tpu_custom_call" | custom-call | flops 49999998976 | bytes 29009920 | tf_op jit(solution)/shard_map/pallas_call | solution.py:41
  386.6 87.3 %shard_map.225 = (bf16[16,128,2048]{2,1,0:T(8,128)(2,1)}, bf16[16,128,256]{2,1,0:T(8,128)(2,1)}, f32[16,128,256]{2,1,0:T(8,128)}, f32[16,160,128]{2,1,0:T(8,128)...) custom-call(bf16[16,256,256]{2,1,0:T(8,128)(2,1)} %bitcast.139, ...), custom_call_target="tpu_custom_call" | custom-call | flops 49999998976 | bytes 40806400 | tf_op jit(solution)/shard_map/pallas_call | solution.py:41
  474.1 0.8 multiply_bitcast_fusion.5
  474.9 1.3 collective-permute-start.2
  476.2 0.7 multiply_convert_fusion
  477.0 0.9 add_convert_fusion
  477.9 1.7 fusion.52
  479.6 1.0 collective-permute-done.2.refs_6_
  481.3 78.3 %shard_map.226 = (bf16[16,128,2048]{2,1,0:T(8,128)(2,1)}, f32[2048,256]{1,0:T(8,128)}, f32[8,256]{1,0:T(8,128)}, f32[128,2048]{1,0:T(8,128)}, bf16[2048,256]{1,0...) custom-call(bf16[16,256,512]{2,1,0:T(8,128)(2,1)} %get-tuple-element.63.xz_ref.refs_1_.refs_0_, ...), custom_call_target="tpu_custom_call" | custom-call | flops 6442450944 | bytes 93893632 | tf_op jit(solution)/shard_map/pallas_call | solution.py:41
  559.7 0.9 multiply_bitcast_fusion.2
  560.6 1.5 collective-permute-start.3
  562.2 1.7 fusion.5
  563.9 2.7 collective-permute-start.5
  567.2 151.9 %shard_map.227 = (bf16[4,2,2,128,2048]{4,3,2,1,0:T(8,128)(2,1)}, f32[8,256]{1,0:T(8,128)}, f32[128,2048]{1,0:T(8,128)}, f32[128,2048]{1,0:T(8,128)}, f32[128,8192]{1,0:T(8,128)}) custom-call(bf16[16,256,512]{2,1,0:T(8,128)(2,1)} %get-tuple-element.63.xz_ref.refs_1_.refs_0_, bf16[16,256,512]{2,1,0:T(8,128)(2,1)} %get-tuple-element.63.xz_ref.refs_1_.refs_0_, ...), custom_call_target="tpu_custom_call" | custom-call | flops 6442450944 | bytes 57979904 | tf_op jit(solution)/shard_map/pallas_call | solution.py:41
  719.1 0.7 add_convert_fusion.2
  719.8 1.0 collective-permute-start.4
  720.9 2.8 multiply_reduce_fusion
  725.6 2.4 fusion.3
  729.8 0.7 slice.254
  730.5 0.6 slice.256
  731.7 0.7 slice_bitcast_fusion
  732.3 3.1 convert_add_fusion.1
  735.4 2.0 copy.38
  (124 shorter events, 9.9 us)
Async XLA Ops:
  7.2 266.0 %all-gather.3.cloned.1.call-start = ((), (), s32[]{:S(2)}) async-start(), calls=%async_computation | async-start | bytes 17825792 | tf_op jit(solution)/shard_map/all_gather | solution.py:1045
  8.0 3.2 collective-permute-start
  12.7 117.6 %copy-start.41 = (bf16[256]{0:T(256)(128)(2,1)S(1)}, bf16[256]{0:T(256)(128)(2,1)}, u32[]{:S(2)}) copy-start(bf16[256]{0:T(256)(128)(2,1)} %param.19) | copy-start | bytes 1540
  12.7 118.2 %copy-start.22 = (bf16[4,256]{1,0:T(4,128)(2,1)S(1)}, bf16[4,256]{1,0:T(4,128)(2,1)}, u32[]{:S(2)}) copy-start(bf16[4,256]{1,0:T(4,128)(2,1)} %param.18) | copy-start | bytes 6148
  12.7 118.8 %copy-start.42 = (bf16[256]{0:T(256)(128)(2,1)S(1)}, bf16[256]{0:T(256)(128)(2,1)}, u32[]{:S(2)}) copy-start(bf16[256]{0:T(256)(128)(2,1)} %param.22) | copy-start | bytes 1540
  12.7 119.4 %copy-start.43 = (bf16[256]{0:T(256)(128)(2,1)S(1)}, bf16[256]{0:T(256)(128)(2,1)}, u32[]{:S(2)}) copy-start(bf16[256]{0:T(256)(128)(2,1)} %param.24) | copy-start | bytes 1540
  12.7 119.9 %copy-start.12 = (bf16[256,160]{0,1:T(8,128)(2,1)S(1)}, bf16[256,160]{0,1:T(8,128)(2,1)}, u32[]{:S(2)}) copy-start(bf16[256,160]{0,1:T(8,128)(2,1)} %param.20) | copy-start | bytes 245764
  12.8 121.2 %copy-start.17 = (bf16[16,256]{1,0:T(8,128)(2,1)S(1)}, bf16[16,256]{1,0:T(8,128)(2,1)}, u32[]{:S(2)}) copy-start(bf16[16,256]{1,0:T(8,128)(2,1)} %param.23) | copy-start | bytes 24580
  139.0 6.4 collective-permute-start.1
  174.5 69.1 %copy-start.19 = (bf16[16,256]{1,0:T(8,128)(2,1)S(1)}, bf16[16,256]{1,0:T(8,128)(2,1)}, u32[]{:S(2)}) copy-start(bf16[16,256]{1,0:T(8,128)(2,1)} %get-tuple-element.73) | copy-start | bytes 24580
  174.5 69.7 %copy-start.7 = (bf16[16,256,256]{2,1,0:T(8,128)(2,1)S(1)}, bf16[16,256,256]{2,1,0:T(8,128)(2,1)}, u32[]{:S(2)}) copy-start(bf16[16,256,256]{2,1,0:T(8,128)(2,1)} %get-tuple-element.64.xc_ref.refs_2_) | copy-start | bytes 6291460
  244.2 229.8 %copy-start.16 = (f32[8,256]{1,0:T(8,128)}, f32[8,256]{1,0:T(8,128)S(1)}, u32[]{:S(2)}) copy-start(f32[8,256]{1,0:T(8,128)S(1)} %get-tuple-element.128.refs_2_) | copy-start | bytes 24580
  386.5 87.5 %copy-start.13 = (bf16[256,160]{0,1:T(8,128)(2,1)S(1)}, bf16[256,160]{0,1:T(8,128)(2,1)}, u32[]{:S(2)}) copy-start(bf16[256,160]{0,1:T(8,128)(2,1)} %param.20) | copy-start | bytes 245764
  386.5 87.5 %copy-start.28 = (f32[256]{0:T(256)S(1)}, f32[256]{0:T(256)}, u32[]{:S(2)}) copy-start(f32[256]{0:T(256)} %convert_element_type.74) | copy-start | bytes 3076
  386.5 87.5 %copy-start.30 = (f32[1,256]{1,0:T(1,128)S(1)}, f32[1,256]{1,0:T(1,128)}, u32[]{:S(2)}) copy-start(f32[1,256]{1,0:T(1,128)} %get-tuple-element.132) | copy-start | bytes 3076
  386.5 87.5 %copy-start.31 = (f32[1,256]{1,0:T(1,128)S(1)}, f32[1,256]{1,0:T(1,128)}, u32[]{:S(2)}) copy-start(f32[1,256]{1,0:T(1,128)} %get-tuple-element.133) | copy-start | bytes 3076
  386.5 87.5 %copy-start.32 = (f32[1,256]{1,0:T(1,128)S(1)}, f32[1,256]{1,0:T(1,128)}, u32[]{:S(2)}) copy-start(f32[1,256]{1,0:T(1,128)} %get-tuple-element.134) | copy-start | bytes 3076
  386.5 87.5 %copy-start.33 = (f32[1,256]{1,0:T(1,128)S(1)}, f32[1,256]{1,0:T(1,128)}, u32[]{:S(2)}) copy-start(f32[1,256]{1,0:T(1,128)} %get-tuple-element.135) | copy-start | bytes 3076
  386.5 87.5 %copy-start.37 = (f32[8]{0:T(128)S(1)}, f32[8]{0:T(128)}, u32[]{:S(2)}) copy-start(f32[8]{0:T(128)} %get-tuple-element.107) | copy-start | bytes 100
  386.6 87.5 %copy-start.38 = (f32[8]{0:T(128)S(1)}, f32[8]{0:T(128)}, u32[]{:S(2)}) copy-start(f32[8]{0:T(128)} %get-tuple-element.108) | copy-start | bytes 100
  386.6 87.5 %copy-start.39 = (f32[8]{0:T(128)S(1)}, f32[8]{0:T(128)}, u32[]{:S(2)}) copy-start(f32[8]{0:T(128)} %get-tuple-element.109) | copy-start | bytes 100
  386.6 89.6 %copy-start.18 = (bf16[16,256]{1,0:T(8,128)(2,1)S(1)}, bf16[16,256]{1,0:T(8,128)(2,1)}, u32[]{:S(2)}) copy-start(bf16[16,256]{1,0:T(8,128)(2,1)} %param.23) | copy-start | bytes 24580
  386.6 89.6 %copy-start.23 = (f32[16,256]{1,0:T(8,128)S(1)}, f32[16,256]{1,0:T(8,128)}, u32[]{:S(2)}) copy-start(f32[16,256]{1,0:T(8,128)} %get-tuple-element.96) | copy-start | bytes 49156
  386.6 90.4 %copy-start.11 = (f32[128,256]{1,0:T(8,128)S(1)}, f32[128,256]{1,0:T(8,128)}, u32[]{:S(2)}) copy-start(f32[128,256]{1,0:T(8,128)} %get-tuple-element.98) | copy-start | bytes 393220
  473.9 5.7 copy-start.26
  474.0 5.7 copy-start.27
  474.9 5.7 collective-permute-start.2
  481.2 78.4 %copy-start.15 = (f32[8,256]{1,0:T(8,128)S(1)}, f32[8,256]{1,0:T(8,128)}, u32[]{:S(2)}) copy-start(f32[8,256]{1,0:T(8,128)} %get-tuple-element.127.refs_2_) | copy-start | bytes 24580
  481.2 78.4 %copy-start.24 = (f32[8,256]{1,0:T(8,128)S(1)}, f32[8,256]{1,0:T(8,128)}, u32[]{:S(2)}) copy-start(f32[8,256]{1,0:T(8,128)} %get-tuple-element.118) | copy-start | bytes 24580
  481.3 78.4 %copy-start.29 = (f32[256]{0:T(256)S(1)}, f32[256]{0:T(256)}, u32[]{:S(2)}) copy-start(f32[256]{0:T(256)} %convert_element_type.74) | copy-start | bytes 3076
  481.3 78.4 %copy-start.34 = (f32[8]{0:T(128)S(1)}, f32[8]{0:T(128)}, u32[]{:S(2)}) copy-start(f32[8]{0:T(128)} %get-tuple-element.104) | copy-start | bytes 100
  481.3 78.4 %copy-start.35 = (f32[8]{0:T(128)S(1)}, f32[8]{0:T(128)}, u32[]{:S(2)}) copy-start(f32[8]{0:T(128)} %get-tuple-element.105) | copy-start | bytes 100
  481.3 78.4 %copy-start.36 = (f32[8]{0:T(128)S(1)}, f32[8]{0:T(128)}, u32[]{:S(2)}) copy-start(f32[8]{0:T(128)} %get-tuple-element.106) | copy-start | bytes 100
  481.3 80.9 %copy-start.5 = (bf16[16,1,128,256]{3,2,1,0:T(8,128)(2,1)S(1)}, bf16[16,1,128,256]{3,2,1,0:T(8,128)(2,1)}, u32[]{:S(2)}) copy-start(bf16[16,1,128,256]{3,2,1,0:T(8,128)(2,1)} %get-tuple-element.110) | copy-start | bytes 3145732
  559.6 7.0 copy-start.10
  560.6 6.0 collective-permute-start.3
  563.9 165.9 %collective-permute-start.5 = (bf16[408,256]{1,0:T(8,128)(2,1)S(1)}, bf16[408,256]{1,0:T(8,128)(2,1)S(1)}, u32[]{:S(2)}, u32[]{:S(2)}) collective-permute-start(bf16[408,256]{1,0:T(8,128)(2,1)S(1)} %pad_maximum_fusion), channel_id=1, source_target_pairs={{0,16},{16,0},{1,17},{17,1},{2,18},{18,2},{3,19},{19,3},{4,20},{20... | collective-permute-start | bytes 626696 | tf_op jit(solution)/shard_map/ppermute | solution.py:1016
  566.6 165.7 %collective-permute-start.6 = (bf16[256,2048]{1,0:T(8,128)(2,1)S(1)}, bf16[256,2048]{1,0:T(8,128)(2,1)}, u32[]{:S(2)}, u32[]{:S(2)}) collective-permute-start(bf16[256,2048]{1,0:T(8,128)(2,1)S(1)} %copy-done.10), channel_id=1, source_target_pairs={{0,16},{16,0},{1,17},{17,1},{2,18},{18,2},{3,19},{19,3},{4,20},{20... | collective-permute-start | bytes 3145736 | tf_op jit(solution)/shard_map/ppermute | solution.py:1016
  567.2 151.9 %copy-start.25 = (f32[8,256]{1,0:T(8,128)S(1)}, f32[8,256]{1,0:T(8,128)}, u32[]{:S(2)}) copy-start(f32[8,256]{1,0:T(8,128)} %get-tuple-element.92) | copy-start | bytes 24580
  567.2 153.7 %copy-start.6 = (bf16[128,8192]{1,0:T(8,128)(2,1)S(1)}, bf16[128,8192]{1,0:T(8,128)(2,1)}, u32[]{:S(2)}) copy-start(bf16[128,8192]{1,0:T(8,128)(2,1)} %wts.1) | copy-start | bytes 6291460
  719.8 8.8 %collective-permute-start.4 = (bf16[8,256]{1,0:T(8,128)(2,1)S(1)}, bf16[8,256]{1,0:T(8,128)(2,1)S(1)}, u32[]{:S(2)}, u32[]{:S(2)}) collective-permute-start(bf16[8,256]{1,0:T(8,128)(2,1)S(1)} %add_convert_fusion.2), channel_id=1, source_target_pairs={{0,16},{16,0},{1,17},{17,1},{2,18},{18,2},{3,19},{19,3},{4,20},{20... | collective-permute-start | bytes 12296 | tf_op jit(solution)/shard_map/ppermute | solution.py:1016
  720.9 2.9 copy-start.2
  720.9 2.9 copy-start.3
  720.9 3.1 copy-start.4
  720.9 3.1 copy-start.14
  723.7 1.9 copy-start.9
  725.6 2.4 copy-start.44
  732.3 3.1 copy-start
  (5 other events, 4.7 us)
Sparse Core Ops, SparseCore 0:
  130.5 142.6 all-gather.2

commit v7 on v6

--- a/solution.py
+++ b/solution.py
@@ -903,9 +903,9 @@
     b = pl.program_id(0)
     peers = dims[0] * dims[1] * dims[2]
     if role == "sum":
-        nu_all, dy_all, dz0, dz1, gated0, gated1 = refs[15:21]
-        v_ref, gx, vec_ref, summed, prod_z, prod_o, done, carry, acc_z, acc_o = refs[21:31]
-        refs = refs[31:]
+        nu_all, dy0, dy1, dz0, dz1, gated0, gated1 = refs[15:22]
+        v_ref, gx, vec_ref, summed, prod_z, prod_o, done, carry, acc_z, acc_o = refs[22:32]
+        refs = refs[32:]
         rc, own, ry, rz, load, send, recv = refs[:7]
         beside(b, peers, dims, 0, [
             allsum_steps((extra, done) + refs[7:], dims, functools.partial(spread_plain, n=n)) + (None,),
@@ -962,7 +962,7 @@
     if role == "sum":
         v_ref[0] = v
         acc_z[...] += tn(nu_all[0], jnp.concatenate([dz0[0], dz1[0]], axis=0))
-        acc_o[...] += tn(jnp.concatenate([gated0[0], gated1[0]], axis=0), dy_all[0])
+        acc_o[...] += tn(jnp.concatenate([gated0[0], gated1[0]], axis=0), jnp.concatenate([dy0[0], dy1[0]], axis=0))
 
         @pl.when(b == peers - 1)
         def _():
@@ -1042,7 +1042,7 @@
     hid_all, tiles, w_cols = gather(hidden_in.reshape(w, d), own, in_proj, 4)
     gain = tiles[:, m * (taps - 1), :dl].reshape(1, d)
     later, hid_all = lax.optimization_barrier((out_grad, hid_all))
-    dy_all = lax.all_gather(later.reshape(w, d), "shard")
+    dy_rows = [lax.all_gather(later[i], "shard") for i in range(m)]
     u = w32(hidden_in)
     r = lax.rsqrt(jnp.mean(u * u, axis=2, keepdims=True) + 1e-5)
 
@@ -1065,23 +1065,6 @@
     a2 = a_mat * LOG2E
     dtb, skip = w32(dt_bias)[None], w32(d_skip)[None]
 
-    ins = [low, xz, xc, mask, dy_all, out_proj, dt_weight, dtb, a2]
-    outs = [shp((peers, m, n, e), F32)] * 2 + [shp((3, m, n, e), F32), shp((peers, w, e), F32)]
-    cks, ckp, end, dg = call(
-        functools.partial(ahead, m=m, n=n, e=e), (peers,),
-        [block(a, rising) for a in ins[:5]] + [whole(a) for a in ins[5:]],
-        [block(outs[0], rising), block(outs[1], rising), whole(outs[2]), block(outs[3], rising)], outs,
-        [pltpu.VMEM((m, n, e), F32)] * 3 + [pltpu.VMEM((w, e), F32)] * 3 + [pltpu.VMEM((w, 128), F32), pltpu.VMEM((w * n, 256), F32)],
-        ins, flops=40 * 10 ** 9)
-
-    ends = lax.all_gather(end, "rep")
-    h_in = jnp.zeros((m, n, e), F32)
-    q_in = jnp.zeros((m, n, e), F32)
-    for k in range(reps - 1):
-        o = reps - 1 - k
-        h_in = jnp.where(k < rep, ends[k, 1] * h_in + ends[k, 0], h_in)
-        q_in = jnp.where(o > rep, ends[o, 1] * q_in + ends[o, 2], q_in)
-
     dims = lattice(peers)
     anywhere = pl.BlockSpec(memory_space=pl.ANY)
     rows_done = []
@@ -1090,10 +1073,25 @@
             shape = (1, tl) if a.ndim == 3 else (1, 1, a.shape[2])
             return pl.BlockSpec(shape + a.shape[len(shape):], lambda b, r=a.ndim: (order(b), i) + (0,) * (r - 2))
 
-        def one(a, i=i):
-            return pl.BlockSpec((1,) + a.shape[1:], lambda b: (i, 0, 0))
+        if i:
+            low, _ = lax.optimization_barrier((low, rows_done[i - 1][7]))
+        ins = [low, xz, xc, mask, dy_rows[i], out_proj, dt_weight, dtb, a2]
+        outs = [shp((peers, 1, n, e), F32)] * 2 + [shp((3, 1, n, e), F32), shp((peers, tl, e), F32)]
+        cks, ckp, end, dg = call(
+            functools.partial(ahead, m=1, n=n, e=e), (peers,),
+            [row(a, rising) for a in ins[:4]] + [block(ins[4], rising)] + [whole(a) for a in ins[5:]],
+            [block(outs[0], rising), block(outs[1], rising), whole(outs[2]), block(outs[3], rising)], outs,
+            [pltpu.VMEM((1, n, e), F32)] * 3 + [pltpu.VMEM((tl, e), F32)] * 3
+            + [pltpu.VMEM((tl, 128), F32), pltpu.VMEM((tl * n, 256), F32)], ins, flops=20 * 10 ** 9)
+        ends = lax.all_gather(end, "rep")
+        h_in = jnp.zeros((1, n, e), F32)
+        q_in = jnp.zeros((1, n, e), F32)
+        for k in range(reps - 1):
+            o = reps - 1 - k
+            h_in = jnp.where(k < rep, ends[k, 1] * h_in + ends[k, 0], h_in)
+            q_in = jnp.where(o > rep, ends[o, 1] * q_in + ends[o, 2], q_in)
         ins = [low, xz, xc, mask, dg, cks, ckp, out_proj, dt_weight, dtb, a2, skip, h_in, q_in]
-        specs = [row(a, falling) for a in ins[:7]] + [whole(a) for a in ins[7:12]] + [one(a) for a in ins[12:]]
+        specs = [row(a, falling) for a in ins[:4]] + [block(a, falling) for a in ins[4:7]] + [whole(a) for a in ins[7:]]
         outs = [shp((peers, tl, d), BF16), shp((peers, tl, e), BF16), shp((peers, tl, e), F32),
                 shp((peers, rank + 2 * n, tl), F32), shp((peers, tl, e), BF16), shp((rank, e), F32), shp((n, e), F32), shp((8, e), F32)]
         out_specs = [block(a, falling) for a in outs[:5]] + [whole(a) for a in outs[5:]]
@@ -1136,7 +1134,7 @@
         carry = pltpu.VMEM((taps - 1, EDGE, e), F32)
         if i < m - 1:
             ins += [rows_done[i + 1][0].reshape(dims + (tl, d)), rows_done[i + 1][3].reshape(dims + (rank + 2 * n, tl))]
-            more = [nu_all, dy_all] + [done[1] for done in rows_done] + [done[4] for done in rows_done]
+            more = [nu_all] + dy_rows + [done[1] for done in rows_done] + [done[4] for done in rows_done]
             ins += more
             specs += [block(a, falling) for a in more]
             outs = [shp((peers, tl, d), BF16), shp((d, e), F32), shp((8, e), F32), shp((tl, d), F32), shp((d, e), BF16),

time: 746 us -> 721 us (0.966)
  waiting for transfers between devices: 28.9 us -> 1.81 us
    all_gather x1 -> x2, waiting for transfers between devices: 27.8 us -> 0.02 us  [on_device(): dy_rows = [lax.all_gather(later[i], 'shard') for i in range(m)]]
    pallas_call x1, Pallas kernels: 68.5 us -> 59.1 us  [allsum(): pl.pallas_call(functools.partial(allsum_kernel, dims=dims, chunks=chunks,...]
    pallas_call x6 -> x7, Pallas kernels: 452 us -> 459 us  [call(): pl.pallas_call(kernel, grid=grid, in_specs=in_specs, out_specs=out_specs,...]
  transfers between devices with their start and end apart: 8 -> 9, of which waited for: 3 -> 2; matrix products, arithmetic and copies ran while one was open for 4% -> 4% of each run, Pallas kernels for 33% -> 45%
where the time goes in v7:
time: 721 us; the launch traced here: 719 us
  Pallas kernels  636 us (88%)
  local copies, waits for them, and re-layouts  20.5 us (3%)
  other arithmetic  18.9 us (3%)
  between operations  14.7 us (2%)
  starting transfers between devices  12.3 us (2%)
  blocking collectives  10.2 us (1%)
    pallas_call x7, Pallas kernels, call(): pl.pallas_call(kernel, grid=grid, in_specs=in_specs, out_specs=out_specs,...  459 us
    pallas_call x1, Pallas kernels, gather(): pl.pallas_call(functools.partial(gather_kernel, dims=dims, chunks=chunks)...  118 us
    pallas_call x1, Pallas kernels, allsum(): pl.pallas_call(functools.partial(allsum_kernel, dims=dims, chunks=chunks,...  59.1 us
  transfers between devices with their start and end apart: 9, of which 2 were waited for; matrix products, arithmetic and copies ran while one was open for 4% of the time, Pallas kernels for 45%

profile of v7, /device:TPU:0, one launch (start us, length us, event | category | flops | bytes accessed | tf_op | source)
XLA Modules:
  0.0 719.3 jit_solution(4562707889205194183)
XLA Ops:
  7.2 0.8 slice.190
  8.0 2.3 collective-permute-start
  10.3 0.7 convert_bitcast_fusion
  11.1 0.9 compare_bitcast_fusion.2
  12.1 0.7 maximum_maximum_fusion.small
  12.7 117.6 %shard_map.220 = (bf16[4,2,2,256,2048]{4,3,2,1,0:T(8,128)(2,1)}, f32[4,2,2,8,128]{4,3,2,1,0:T(8,128)}, bf16[16,2,64,512]{3,2,1,0:T(8,128)(2,1)}) custom-call(bf16[256,2048]{1,0:T(8,128)(2,1)} %bitcast.132, f32[8,128]{1,0:T(8,128)} %maximum_maximum_fusion.small, bf16[128,8192]{1,0:T(8,128)(2,1)} %wts.1), custom_call_target="tpu_custom_call" | custom-call | flops 80000000000 | bytes 16777216 | tf_op jit(solution)/shard_map/pallas_call | solution.py:394
  130.4 1.1 fusion.48
  131.6 0.7 all-gather.7.cloned.1.call-update
  134.6 0.7 pad.9.refs_8_
  135.9 0.6 fusion.18.a2_ref.refs_10_
  136.5 0.6 copy.33
  137.1 1.5 pad.8.mask_ref.refs_3_
  138.7 1.4 slice.194
  140.1 3.4 collective-permute-start.1
  143.5 0.8 slice_reduce_fusion.5
  144.9 0.7 slice_reduce_fusion.2
  145.6 0.6 copy-done.42
  146.2 27.5 %shard_map.221 = (bf16[16,256,512]{2,1,0:T(8,128)(2,1)}, bf16[16,256,256]{2,1,0:T(8,128)(2,1)}, bf16[16,256,2048]{2,1,0:T(8,128)(2,1)}, bf16[16,256]{1,0:T(8,128...) custom-call(bf16[16,256,2048]{2,1,0:T(8,128)(2,1)} %bitcast.164, bf16[2048,512]{1,0:T(8,128)(2,1)} %bitcast.122, ...), custom_call_target="tpu_custom_call" | custom-call | flops 8589934592 | bytes 44864512 | tf_op jit(solution)/shard_map/pallas_call | solution.py:41
  173.8 1.0 slice.213
  174.7 59.1 %shard_map.222 = bf16[4,2,2,256,256]{4,3,2,1,0:T(8,128)(2,1)} custom-call(f32[4,2,2,160,128]{4,3,2,1,0:T(8,128)} %bitcast.144, f32[4,2,2,160,128]{4,3,2,1,0:T(8,128)} %bitcast.145), custom_call_target="tpu_custom_call" | custom-call | tf_op jit(solution)/shard_map/pallas_call | solution.py:218
  235.0 1.2 fusion.47
  236.2 26.6 %shard_map.223 = (f32[16,1,16,256]{3,2,1,0:T(8,128)}, f32[16,1,16,256]{3,2,1,0:T(8,128)}, f32[3,1,16,256]{3,2,1,0:T(8,128)}, f32[16,128,256]{2,1,0:T(8,128)}) custom-call(bf16[16,256,256]{2,1,0:T(8,128)(2,1)} %bitcast.140, bf16[16,256,512]{2,1,0:T(8,128)(2,1)} %get-tuple-element.68.xz_ref.refs_1_.refs_0_, ...), custom_call_target="tpu_custom_call" | custom-call | flops 20000000000 | bytes 20710400 | tf_op jit(solution)/shard_map/pallas_call | solution.py:41
  262.9 5.0 all-gather
  267.9 0.6 fusion.15
  268.5 59.3 %shard_map.224 = (bf16[16,128,2048]{2,1,0:T(8,128)(2,1)}, bf16[16,128,256]{2,1,0:T(8,128)(2,1)}, f32[16,128,256]{2,1,0:T(8,128)}, f32[16,160,128]{2,1,0:T(8,128)...) custom-call(bf16[16,256,256]{2,1,0:T(8,128)(2,1)} %bitcast.141, ...), custom_call_target="tpu_custom_call" | custom-call | flops 49999998976 | bytes 26355712 | tf_op jit(solution)/shard_map/pallas_call | solution.py:41
  327.8 26.7 %shard_map.225 = (f32[16,1,16,256]{3,2,1,0:T(8,128)}, f32[16,1,16,256]{3,2,1,0:T(8,128)}, f32[3,1,16,256]{3,2,1,0:T(8,128)}, f32[16,128,256]{2,1,0:T(8,128)}) custom-call(bf16[16,256,256]{2,1,0:T(8,128)(2,1)} %bitcast.142, bf16[16,256,512]{2,1,0:T(8,128)(2,1)} %get-tuple-element.68.xz_ref.refs_1_.refs_0_, ...), custom_call_target="tpu_custom_call" | custom-call | flops 20000000000 | bytes 20710400 | tf_op jit(solution)/shard_map/pallas_call | solution.py:41
  354.5 5.2 all-gather.1
  360.4 88.4 %shard_map.226 = (bf16[16,128,2048]{2,1,0:T(8,128)(2,1)}, bf16[16,128,256]{2,1,0:T(8,128)(2,1)}, f32[16,128,256]{2,1,0:T(8,128)}, f32[16,160,128]{2,1,0:T(8,128)...) custom-call(bf16[16,256,256]{2,1,0:T(8,128)(2,1)} %bitcast.143, ...), custom_call_target="tpu_custom_call" | custom-call | flops 49999998976 | bytes 38152192 | tf_op jit(solution)/shard_map/pallas_call | solution.py:41
  448.9 0.8 multiply_bitcast_fusion.5
  449.7 1.3 collective-permute-start.2
  451.1 0.7 multiply_convert_fusion
  451.8 0.9 add_convert_fusion
  452.7 1.7 fusion.57
  454.5 1.0 collective-permute-done.2.refs_6_
  456.1 79.6 %shard_map.227 = (bf16[16,128,2048]{2,1,0:T(8,128)(2,1)}, f32[2048,256]{1,0:T(8,128)}, f32[8,256]{1,0:T(8,128)}, f32[128,2048]{1,0:T(8,128)}, bf16[2048,256]{1,0...) custom-call(bf16[16,256,512]{2,1,0:T(8,128)(2,1)} %get-tuple-element.68.xz_ref.refs_1_.refs_0_, ...), custom_call_target="tpu_custom_call" | custom-call | flops 6442450944 | bytes 93893632 | tf_op jit(solution)/shard_map/pallas_call | solution.py:41
  535.8 0.9 multiply_bitcast_fusion.2
  536.7 1.5 collective-permute-start.3
  538.2 1.7 fusion.5
  540.0 2.7 collective-permute-start.5
  543.3 151.0 %shard_map.228 = (bf16[4,2,2,128,2048]{4,3,2,1,0:T(8,128)(2,1)}, f32[8,256]{1,0:T(8,128)}, f32[128,2048]{1,0:T(8,128)}, f32[128,2048]{1,0:T(8,128)}, f32[128,8192]{1,0:T(8,128)}) custom-call(bf16[16,256,512]{2,1,0:T(8,128)(2,1)} %get-tuple-element.68.xz_ref.refs_1_.refs_0_, bf16[16,256,512]{2,1,0:T(8,128)(2,1)} %get-tuple-element.68.xz_ref.refs_1_.refs_0_, ...), custom_call_target="tpu_custom_call" | custom-call | flops 6442450944 | bytes 57979904 | tf_op jit(solution)/shard_map/pallas_call | solution.py:41
  694.3 0.7 add_convert_fusion.2
  695.0 0.9 collective-permute-start.4
  695.9 2.8 multiply_reduce_fusion
  700.7 2.4 fusion.3
  704.9 0.7 slice.282
  706.7 0.7 slice_bitcast_fusion
  707.4 3.1 convert_add_fusion.1
  710.4 2.0 copy.38
  (135 shorter events, 11.8 us)
Async XLA Ops:
  7.2 229.0 %all-gather.5.cloned.1.call-start = ((), (), s32[]{:S(2)}) async-start(), calls=%async_computation | async-start | bytes 8912896 | tf_op jit(solution)/shard_map/all_gather | solution.py:1045
  8.0 3.2 collective-permute-start
  12.7 117.7 %copy-start.1 = (bf16[2,128,2048]{2,1,0:T(8,128)(2,1)S(1)}, bf16[2,128,2048]{2,1,0:T(8,128)(2,1)}, u32[]{:S(2)}) copy-start(bf16[2,128,2048]{2,1,0:T(8,128)(2,1)} %param.15) | copy-start | bytes 3145732
  130.3 2.5 copy-start.24
  130.3 3.1 copy-start.44
  130.4 3.7 copy-start.45
  130.4 4.2 copy-start.14
  130.4 5.5 copy-start.19
  130.4 6.1 copy-start.13
  131.5 196.3 %all-gather.7.cloned.1.call-start = ((), (), s32[]{:S(2)}) async-start(), calls=%async_computation.1 | async-start | bytes 8912896 | tf_op jit(solution)/shard_map/all_gather | solution.py:1045
  140.1 5.5 collective-permute-start.1
  174.7 59.7 %copy-start.21 = (bf16[16,256]{1,0:T(8,128)(2,1)S(1)}, bf16[16,256]{1,0:T(8,128)(2,1)}, u32[]{:S(2)}) copy-start(bf16[16,256]{1,0:T(8,128)(2,1)} %get-tuple-element.84) | copy-start | bytes 24580
  174.7 60.3 %copy-start.8 = (bf16[16,256,256]{2,1,0:T(8,128)(2,1)S(1)}, bf16[16,256,256]{2,1,0:T(8,128)(2,1)}, u32[]{:S(2)}) copy-start(bf16[16,256,256]{2,1,0:T(8,128)(2,1)} %get-tuple-element.69.xc_ref.refs_2_) | copy-start | bytes 6291460
  235.0 213.8 %copy-start.18 = (f32[8,256]{1,0:T(8,128)}, f32[8,256]{1,0:T(8,128)S(1)}, u32[]{:S(2)}) copy-start(f32[8,256]{1,0:T(8,128)S(1)} %get-tuple-element.142.refs_2_) | copy-start | bytes 24580
  360.3 88.5 %copy-start.15 = (bf16[256,160]{0,1:T(8,128)(2,1)S(1)}, bf16[256,160]{0,1:T(8,128)(2,1)}, u32[]{:S(2)}) copy-start(bf16[256,160]{0,1:T(8,128)(2,1)} %param.20) | copy-start | bytes 245764
  360.3 88.5 %copy-start.30 = (f32[256]{0:T(256)S(1)}, f32[256]{0:T(256)}, u32[]{:S(2)}) copy-start(f32[256]{0:T(256)} %convert_element_type.74) | copy-start | bytes 3076
  360.3 88.5 %copy-start.32 = (f32[1,256]{1,0:T(1,128)S(1)}, f32[1,256]{1,0:T(1,128)}, u32[]{:S(2)}) copy-start(f32[1,256]{1,0:T(1,128)} %get-tuple-element.146) | copy-start | bytes 3076
  360.3 88.6 %copy-start.33 = (f32[1,256]{1,0:T(1,128)S(1)}, f32[1,256]{1,0:T(1,128)}, u32[]{:S(2)}) copy-start(f32[1,256]{1,0:T(1,128)} %get-tuple-element.147) | copy-start | bytes 3076
  360.3 88.6 %copy-start.34 = (f32[1,256]{1,0:T(1,128)S(1)}, f32[1,256]{1,0:T(1,128)}, u32[]{:S(2)}) copy-start(f32[1,256]{1,0:T(1,128)} %get-tuple-element.148) | copy-start | bytes 3076
  360.3 88.6 %copy-start.35 = (f32[1,256]{1,0:T(1,128)S(1)}, f32[1,256]{1,0:T(1,128)}, u32[]{:S(2)}) copy-start(f32[1,256]{1,0:T(1,128)} %get-tuple-element.149) | copy-start | bytes 3076
  360.3 88.6 %copy-start.39 = (f32[8]{0:T(128)S(1)}, f32[8]{0:T(128)}, u32[]{:S(2)}) copy-start(f32[8]{0:T(128)} %get-tuple-element.117) | copy-start | bytes 100
  360.3 88.6 %copy-start.40 = (f32[8]{0:T(128)S(1)}, f32[8]{0:T(128)}, u32[]{:S(2)}) copy-start(f32[8]{0:T(128)} %get-tuple-element.118) | copy-start | bytes 100
  360.3 88.6 %copy-start.41 = (f32[8]{0:T(128)S(1)}, f32[8]{0:T(128)}, u32[]{:S(2)}) copy-start(f32[8]{0:T(128)} %get-tuple-element.119) | copy-start | bytes 100
  360.3 90.7 %copy-start.20 = (bf16[16,256]{1,0:T(8,128)(2,1)S(1)}, bf16[16,256]{1,0:T(8,128)(2,1)}, u32[]{:S(2)}) copy-start(bf16[16,256]{1,0:T(8,128)(2,1)} %param.23) | copy-start | bytes 24580
  360.3 90.7 %copy-start.25 = (f32[16,256]{1,0:T(8,128)S(1)}, f32[16,256]{1,0:T(8,128)}, u32[]{:S(2)}) copy-start(f32[16,256]{1,0:T(8,128)} %get-tuple-element.106) | copy-start | bytes 49156
  360.4 91.4 %copy-start.12 = (f32[128,256]{1,0:T(8,128)S(1)}, f32[128,256]{1,0:T(8,128)}, u32[]{:S(2)}) copy-start(f32[128,256]{1,0:T(8,128)} %get-tuple-element.108) | copy-start | bytes 393220
  448.8 5.7 copy-start.27
  448.8 5.7 copy-start.29
  449.7 5.7 collective-permute-start.2
  456.1 79.7 %copy-start.17 = (f32[8,256]{1,0:T(8,128)S(1)}, f32[8,256]{1,0:T(8,128)}, u32[]{:S(2)}) copy-start(f32[8,256]{1,0:T(8,128)} %get-tuple-element.141.refs_2_) | copy-start | bytes 24580
  456.1 79.7 %copy-start.26 = (f32[8,256]{1,0:T(8,128)S(1)}, f32[8,256]{1,0:T(8,128)}, u32[]{:S(2)}) copy-start(f32[8,256]{1,0:T(8,128)} %get-tuple-element.130) | copy-start | bytes 24580
  456.1 79.7 %copy-start.31 = (f32[256]{0:T(256)S(1)}, f32[256]{0:T(256)}, u32[]{:S(2)}) copy-start(f32[256]{0:T(256)} %convert_element_type.74) | copy-start | bytes 3076
  456.1 79.7 %copy-start.36 = (f32[8]{0:T(128)S(1)}, f32[8]{0:T(128)}, u32[]{:S(2)}) copy-start(f32[8]{0:T(128)} %get-tuple-element.114) | copy-start | bytes 100
  456.1 79.7 %copy-start.37 = (f32[8]{0:T(128)S(1)}, f32[8]{0:T(128)}, u32[]{:S(2)}) copy-start(f32[8]{0:T(128)} %get-tuple-element.115) | copy-start | bytes 100
  456.1 79.7 %copy-start.38 = (f32[8]{0:T(128)S(1)}, f32[8]{0:T(128)}, u32[]{:S(2)}) copy-start(f32[8]{0:T(128)} %get-tuple-element.116) | copy-start | bytes 100
  456.1 82.1 %copy-start.6 = (bf16[16,1,128,256]{3,2,1,0:T(8,128)(2,1)S(1)}, bf16[16,1,128,256]{3,2,1,0:T(8,128)(2,1)}, u32[]{:S(2)}) copy-start(bf16[16,1,128,256]{3,2,1,0:T(8,128)(2,1)} %get-tuple-element.120) | copy-start | bytes 3145732
  535.7 7.0 copy-start.11
  536.7 6.0 collective-permute-start.3
  540.0 164.8 %collective-permute-start.5 = (bf16[408,256]{1,0:T(8,128)(2,1)S(1)}, bf16[408,256]{1,0:T(8,128)(2,1)S(1)}, u32[]{:S(2)}, u32[]{:S(2)}) collective-permute-start(bf16[408,256]{1,0:T(8,128)(2,1)S(1)} %pad_maximum_fusion), channel_id=1, source_target_pairs={{0,16},{16,0},{1,17},{17,1},{2,18},{18,2},{3,19},{19,3},{4,20},{20... | collective-permute-start | bytes 626696 | tf_op jit(solution)/shard_map/ppermute | solution.py:1016
  542.7 164.7 %collective-permute-start.6 = (bf16[256,2048]{1,0:T(8,128)(2,1)S(1)}, bf16[256,2048]{1,0:T(8,128)(2,1)}, u32[]{:S(2)}, u32[]{:S(2)}) collective-permute-start(bf16[256,2048]{1,0:T(8,128)(2,1)S(1)} %copy-done.11), channel_id=1, source_target_pairs={{0,16},{16,0},{1,17},{17,1},{2,18},{18,2},{3,19},{19,3},{4,20},{20... | collective-permute-start | bytes 3145736 | tf_op jit(solution)/shard_map/ppermute | solution.py:1016
  543.3 151.0 %copy-start.28 = (f32[8,256]{1,0:T(8,128)S(1)}, f32[8,256]{1,0:T(8,128)}, u32[]{:S(2)}) copy-start(f32[8,256]{1,0:T(8,128)} %get-tuple-element.103) | copy-start | bytes 24580
  543.3 152.6 %copy-start.7 = (bf16[128,8192]{1,0:T(8,128)(2,1)S(1)}, bf16[128,8192]{1,0:T(8,128)(2,1)}, u32[]{:S(2)}) copy-start(bf16[128,8192]{1,0:T(8,128)(2,1)} %wts.1) | copy-start | bytes 6291460
  695.0 8.6 %collective-permute-start.4 = (bf16[8,256]{1,0:T(8,128)(2,1)S(1)}, bf16[8,256]{1,0:T(8,128)(2,1)S(1)}, u32[]{:S(2)}, u32[]{:S(2)}) collective-permute-start(bf16[8,256]{1,0:T(8,128)(2,1)S(1)} %add_convert_fusion.2), channel_id=1, source_target_pairs={{0,16},{16,0},{1,17},{17,1},{2,18},{18,2},{3,19},{19,3},{4,20},{20... | collective-permute-start | bytes 12296 | tf_op jit(solution)/shard_map/ppermute | solution.py:1016
  695.9 2.9 copy-start.3
  695.9 2.9 copy-start.4
  695.9 3.1 copy-start.5
  695.9 3.1 copy-start.16
  707.4 3.1 copy-start
  (8 other events, 11.0 us)
Sparse Core Ops, SparseCore 0:
  131.6 94.7 all-gather.4
  228.6 72.6 all-gather.6

commit v8 on v7

--- a/solution.py
+++ b/solution.py
@@ -730,8 +730,19 @@
     return vals[0]
 
 
-def ahead(low_ref, xz_ref, xc_ref, mask_ref, dy_ref, wo_ref, wdt_ref, dtb_ref, a2_ref,
-          cks_ref, ckp_ref, end_ref, dg_ref, s_scr, p_scr, f_scr, sd_scr, dx_scr, dy_scr, bcs_scr, bc_scr, *, m, n, e):
+def ahead(*refs, m, n, e, dims, sending):
+    (low_ref, xz_ref, xc_ref, mask_ref, dy_ref, wo_ref, wdt_ref, dtb_ref, a2_ref) = refs[:9]
+    refs = refs[9:]
+    if sending:
+        adding, refs = refs[0], refs[1:]
+    cks_ref, ckp_ref, end_ref, dg_ref = refs[:4]
+    refs = refs[4:]
+    if sending:
+        added, refs = refs[0], refs[1:]
+    s_scr, p_scr, f_scr, sd_scr, dx_scr, dy_scr, bcs_scr, bc_scr = refs[:8]
+    if sending:
+        beside(pl.program_id(0), dims[0] * dims[1] * dims[2], dims, 0,
+               [allsum_steps((adding, added) + refs[8:], dims, functools.partial(spread_plain, n=n)) + (None,)])
     b = pl.program_id(0)
     @pl.when(b == 0)
     def _():
@@ -782,17 +793,16 @@
      wo_ref, wdt_ref, dtb_ref, a2_ref, skip_ref, hin_ref, qin_ref) = refs[:14]
     refs = refs[14:]
     if sending:
-        before, adding, refs = refs[0], refs[1], refs[2:]
+        before, refs = refs[0], refs[1:]
     out_ref, dz_ref, dxc_ref, part_ref, gated_ref, gdt_ref, ga_ref, vec_ref = refs[:8]
     refs = refs[8:]
     if sending:
-        summed, added, refs = refs[0], refs[1], refs[2:]
+        summed, refs = refs[0], refs[1:]
     (h_scr, a_scr, q_scr, bcs_scr, bc_scr, pre_scr, st_scr, sd_scr, dx_scr, dy_scr, y_scr, da_scr, gb_scr) = refs[:13]
     b = pl.program_id(0)
     if sending:
         rc, own, ry, rz, load, send, recv = refs[13:20]
         beside(b, dims[0] * dims[1] * dims[2], dims, 0, [
-            allsum_steps((adding, added) + refs[20:], dims, functools.partial(spread_plain, n=n)) + (None,),
             scatter_steps((before, None, summed, None, rc, own, ry, rz, None, None, None, load, send, recv) + (None,) * 7,
                           dims, reps, 8, 10) + (PACED,)])
     m = 1
@@ -912,8 +922,9 @@
             scatter_steps((before, None, summed, None, rc, own, ry, rz, None, None, None, load, send, recv) + (None,) * 7,
                           dims, reps) + (None,)])
     else:
-        gx_before, v_out, vec_ref, summed, summed_own, g_done, carry, gx, gx_low, v_buf, v_sem, gx_sem = refs[15:27]
-        refs = refs[27:]
+        gx_before, go_part, v_out, vec_ref, summed, summed_own, g_done, go_done = refs[15:23]
+        carry, gx, gx_low, v_buf, go_all, v_sem, gx_sem, go_send, go_recv = refs[23:32]
+        refs = refs[32:]
         half = len(refs) // 2
         earlier = scatter_steps((before, extra, summed, g_done) + refs[:half], dims, reps, 8, 10, 8, 15, peers * e)
         latest = scatter_steps((v_out, gx_low, summed_own, g_done) + refs[half:], dims, reps, 8, 10, 4, 12)
@@ -990,11 +1001,24 @@
                 first = (p * reps + k) * gx_low.shape[2]
                 gx_low[p, k] = gx[first:first + gx_low.shape[2]].astype(BF16)
         latest[0]()
+        rep = lax.axis_index("rep")
+        kept = pltpu.make_async_copy(go_part, go_all.at[rep], gx_sem.at[0])
+        swaps = [remote(go_part, go_all.at[rep], go_send.at[k - 1], go_recv.at[k - 1], {"rep": lax.rem(rep + k, reps)})
+                 for k in range(1, reps)]
         for k, step in enumerate(latest[1]):
+            if k == 6:
+                for copy in [kept] + swaps:
+                    copy.start()
             if len(early) + k < len(earlier[1]):
                 earlier[1][len(early) + k]()
             step()
         earlier[2]()
+        for copy in [kept] + swaps:
+            copy.wait()
+        total = go_all[0].astype(F32)
+        for k in range(1, reps):
+            total = total + go_all[k].astype(F32)
+        go_done[...] = total
         latest[2]()
 
 
@@ -1067,7 +1091,7 @@
 
     dims = lattice(peers)
     anywhere = pl.BlockSpec(memory_space=pl.ANY)
-    rows_done = []
+    rows_done, ddbcs = [], []
     for i in range(m):
         def row(a, order, i=i):
             shape = (1, tl) if a.ndim == 3 else (1, 1, a.shape[2])
@@ -1077,12 +1101,22 @@
             low, _ = lax.optimization_barrier((low, rows_done[i - 1][7]))
         ins = [low, xz, xc, mask, dy_rows[i], out_proj, dt_weight, dtb, a2]
         outs = [shp((peers, 1, n, e), F32)] * 2 + [shp((3, 1, n, e), F32), shp((peers, tl, e), F32)]
-        cks, ckp, end, dg = call(
-            functools.partial(ahead, m=1, n=n, e=e), (peers,),
-            [row(a, rising) for a in ins[:4]] + [block(ins[4], rising)] + [whole(a) for a in ins[5:]],
-            [block(outs[0], rising), block(outs[1], rising), whole(outs[2]), block(outs[3], rising)], outs,
-            [pltpu.VMEM((1, n, e), F32)] * 3 + [pltpu.VMEM((tl, e), F32)] * 3
-            + [pltpu.VMEM((tl, 128), F32), pltpu.VMEM((tl * n, 256), F32)], ins, flops=20 * 10 ** 9)
+        specs = [row(a, rising) for a in ins[:4]] + [block(ins[4], rising)] + [whole(a) for a in ins[5:]]
+        out_specs = [block(outs[0], rising), block(outs[1], rising), whole(outs[2]), block(outs[3], rising)]
+        scratch = ([pltpu.VMEM((1, n, e), F32)] * 3 + [pltpu.VMEM((tl, e), F32)] * 3
+                   + [pltpu.VMEM((tl, 128), F32), pltpu.VMEM((tl * n, 256), F32)])
+        params = {}
+        if i:
+            ins.append(rows_done[i - 1][3].reshape(dims + (rank + 2 * n, tl)))
+            specs.append(anywhere)
+            outs.append(shp(dims + (tl, 256), BF16))
+            out_specs.append(whole(outs[-1]))
+            scratch += allsum_scratch(peers, rank + 2 * n, tl)
+            params = dict(collective_id=11 + i, has_side_effects=True)
+        cks, ckp, end, dg, *sums = call(
+            functools.partial(ahead, m=1, n=n, e=e, dims=dims, sending=bool(i)), (peers,), specs, out_specs, outs, scratch,
+            ins, flops=20 * 10 ** 9, **params)
+        ddbcs += [a.reshape(peers, tl, 256) for a in sums]
         ends = lax.all_gather(end, "rep")
         h_in = jnp.zeros((1, n, e), F32)
         q_in = jnp.zeros((1, n, e), F32)
@@ -1099,11 +1133,11 @@
                    pltpu.VMEM((tl, 128), F32), pltpu.VMEM((tl * n, 256), F32)] + [pltpu.VMEM((tl, e), F32)] * 8
         params = {}
         if i:
-            ins += [rows_done[i - 1][0].reshape(dims + (tl, d)), rows_done[i - 1][3].reshape(dims + (rank + 2 * n, tl))]
-            specs += [anywhere] * 2
-            outs += [shp((tl, d), F32), shp(dims + (tl, 256), BF16)]
-            out_specs += [whole(a) for a in outs[-2:]]
-            scratch += scatter_scratch(peers, tl, d, 16) + allsum_scratch(peers, rank + 2 * n, tl)
+            ins.append(rows_done[i - 1][0].reshape(dims + (tl, d)))
+            specs.append(anywhere)
+            outs.append(shp((tl, d), F32))
+            out_specs.append(whole(outs[-1]))
+            scratch += scatter_scratch(peers, tl, d, 16)
             params = dict(collective_id=5 + i, has_side_effects=True)
         rows_done.append(call(
             functools.partial(behind, n=n, e=e, dims=dims, reps=reps, sending=bool(i)), (peers,), specs, out_specs, outs,
@@ -1114,7 +1148,6 @@
     xz_first = xz[0].reshape(m, tl, 2 * e)[:, :EDGE, :e]
     edges = w32(edge).reshape(m, EDGE, e)
     out_sums = [done[8] for done in rows_done[1:]]
-    ddbcs = [done[9].reshape(peers, tl, 256) for done in rows_done[1:]]
     backs = []
     for i in range(m):
         ext8 = jnp.concatenate([edges[i], w32(xz_first[i])], axis=0)
@@ -1144,19 +1177,20 @@
             scratch += scatter_scratch(peers, tl, d, 16) + allsum_scratch(peers, rank + 2 * n, tl)
         else:
             g_z = backs[i - 1][4]
-            ins += [backs[i - 1][0].reshape(dims + (tl, d)), g_z.reshape(peers // reps, reps, dl, e), backs[i - 1][1]]
-            specs += [anywhere]
-            outs = [shp(dims + (tl, d), BF16), shp((8, e), F32), shp((tl, d), F32), shp((tl, d), F32), shp((dl, 2 * peers * e), F32)]
+            ins += [backs[i - 1][0].reshape(dims + (tl, d)), g_z.reshape(peers // reps, reps, dl, e), backs[i - 1][1], backs[i - 1][5]]
+            specs += [anywhere] * 2
+            outs = [shp(dims + (tl, d), BF16), shp((8, e), F32), shp((tl, d), F32), shp((tl, d), F32), shp((dl, 2 * peers * e), F32),
+                    shp((e, d), F32)]
             out_specs = [anywhere] + [whole(a) for a in outs[1:]]
             scratch = [carry, pltpu.VMEM((d, e), F32), pltpu.VMEM((peers // reps, reps, dl, e), BF16), pltpu.VMEM((2, tl, d), BF16),
-                       pltpu.SemaphoreType.DMA((2,)), pltpu.SemaphoreType.DMA((1,))] + scatter_scratch(peers, tl, d, 16, g_z) * 2
+                       pltpu.VMEM((reps, e, d), BF16), pltpu.SemaphoreType.DMA((2,)), pltpu.SemaphoreType.DMA((1,)),
+                       pltpu.SemaphoreType.DMA((reps - 1,)), pltpu.SemaphoreType.DMA((reps - 1,))] + scatter_scratch(peers, tl, d, 16, g_z) * 2
         backs.append(call(
             functools.partial(back, e=e, n=n, dims=dims, reps=reps, role="sum" if i < m - 1 else "owner"), (peers,), specs,
             out_specs, outs, scratch, ins, flops=peers * w * d * 3 * e, collective_id=8 + i, has_side_effects=True))
         if i < m - 1:
             out_sums.append(backs[i][3])
             ddbcs.append(backs[i][6].reshape(peers, tl, 256))
-    g_out, _ = lax.optimization_barrier((backs[0][5], follow))
     vec2 = backs[0][2] + backs[1][1]
     layer_out = (u + jnp.stack(out_sums)).astype(BF16)
 
@@ -1171,7 +1205,7 @@
     small, vec2 = sum_rep(small), sum_rep(vec2)
     vec, g_a, g_dt, g_xp = small[:8], small[8:8 + n], small[8 + n:8 + n + rank], small[8 + n + rank:]
     return (layer_out, in_grad, grad_gain, grad_in_proj, vec2[:taps], vec2[taps], g_xp[:rank + 2 * n].T, g_dt, vec[0],
-            g_a, vec[1], sum_rep(g_out))
+            g_a, vec[1], backs[1][5])
 
 
 def solution(mesh):

time: 721 us -> 707 us (0.981)
  Pallas kernels: 636 us -> 625 us
    pallas_call x7, Pallas kernels: 459 us -> 448 us  [call(): pl.pallas_call(kernel, grid=grid, in_specs=in_specs, out_specs=out_specs,...]
  transfers between devices with their start and end apart: 9 -> 8, of which waited for: 2 -> 1; matrix products, arithmetic and copies ran while one was open for 4% -> 4% of each run, Pallas kernels for 45% -> 55%
where the time goes in v8:
time: 707 us; the launch traced here: 706 us
  Pallas kernels  625 us (88%)
  local copies, waits for them, and re-layouts  21.6 us (3%)
  other arithmetic  15.9 us (2%)
  between operations  14.7 us (2%)
  starting transfers between devices  11.4 us (2%)
  blocking collectives  10.8 us (2%)
    pallas_call x7, Pallas kernels, call(): pl.pallas_call(kernel, grid=grid, in_specs=in_specs, out_specs=out_specs,...  448 us
    pallas_call x1, Pallas kernels, gather(): pl.pallas_call(functools.partial(gather_kernel, dims=dims, chunks=chunks)...  118 us
    pallas_call x1, Pallas kernels, allsum(): pl.pallas_call(functools.partial(allsum_kernel, dims=dims, chunks=chunks,...  59.3 us
  transfers between devices with their start and end apart: 8, of which 1 were waited for; matrix products, arithmetic and copies ran while one was open for 4% of the time, Pallas kernels for 55%

profile of v8, /device:TPU:0, one launch (start us, length us, event | category | flops | bytes accessed | tf_op | source)
XLA Modules:
  0.0 705.5 jit_solution(15683426107120515894)
XLA Ops:
  7.2 0.8 slice.190
  8.0 2.3 collective-permute-start
  10.3 0.7 convert_bitcast_fusion
  11.1 0.9 compare_bitcast_fusion.2
  12.1 0.7 maximum_maximum_fusion.small
  12.7 117.6 %shard_map.220 = (bf16[4,2,2,256,2048]{4,3,2,1,0:T(8,128)(2,1)}, f32[4,2,2,8,128]{4,3,2,1,0:T(8,128)}, bf16[16,2,64,512]{3,2,1,0:T(8,128)(2,1)}) custom-call(bf16[256,2048]{1,0:T(8,128)(2,1)} %bitcast.132, f32[8,128]{1,0:T(8,128)} %maximum_maximum_fusion.small, bf16[128,8192]{1,0:T(8,128)(2,1)} %wts.1), custom_call_target="tpu_custom_call" | custom-call | flops 80000000000 | bytes 16777216 | tf_op jit(solution)/shard_map/pallas_call | solution.py:394
  130.4 1.1 fusion.48
  131.5 0.7 all-gather.7.cloned.1.call-update
  134.6 0.7 pad.9.refs_8_
  135.2 0.6 fusion.18.refs_8_.refs_10_
  135.9 1.3 slice.194
  137.2 3.4 collective-permute-start.1
  140.6 0.6 copy.33
  141.2 1.5 pad.8.mask_ref.refs_3_
  142.8 0.8 slice_reduce_fusion.2
  143.6 0.6 fusion.50
  144.4 0.6 copy-done.35
  145.0 27.5 %shard_map.221 = (bf16[16,256,512]{2,1,0:T(8,128)(2,1)}, bf16[16,256,256]{2,1,0:T(8,128)(2,1)}, bf16[16,256,2048]{2,1,0:T(8,128)(2,1)}, bf16[16,256]{1,0:T(8,128...) custom-call(bf16[16,256,2048]{2,1,0:T(8,128)(2,1)} %bitcast.164, bf16[2048,512]{1,0:T(8,128)(2,1)} %bitcast.122, ...), custom_call_target="tpu_custom_call" | custom-call | flops 8589934592 | bytes 44864512 | tf_op jit(solution)/shard_map/pallas_call | solution.py:41
  172.5 1.0 slice.213
  173.5 59.3 %shard_map.222 = bf16[4,2,2,256,256]{4,3,2,1,0:T(8,128)(2,1)} custom-call(f32[4,2,2,160,128]{4,3,2,1,0:T(8,128)} %bitcast.144, f32[4,2,2,160,128]{4,3,2,1,0:T(8,128)} %bitcast.145), custom_call_target="tpu_custom_call" | custom-call | tf_op jit(solution)/shard_map/pallas_call | solution.py:218
  234.1 1.1 fusion.47
  235.2 26.7 %shard_map.223 = (f32[16,1,16,256]{3,2,1,0:T(8,128)}, f32[16,1,16,256]{3,2,1,0:T(8,128)}, f32[3,1,16,256]{3,2,1,0:T(8,128)}, f32[16,128,256]{2,1,0:T(8,128)}) custom-call(bf16[16,256,256]{2,1,0:T(8,128)(2,1)} %bitcast.140, bf16[16,256,512]{2,1,0:T(8,128)(2,1)} %get-tuple-element.68.refs_1_.refs_0_, bf16[16,256,256]{2,1,0:T(8,128)(2,1)} %get-tuple-element.69.refs_2_, ...), custom_call_target="tpu_custom_call" | custom-call | flops 20000000000 | bytes 20710400 | tf_op jit(solution)/shard_map/pallas_call | solution.py:41
  261.9 5.0 all-gather
  266.9 0.6 fusion.15
  267.5 59.3 %shard_map.224 = (bf16[16,128,2048]{2,1,0:T(8,128)(2,1)}, bf16[16,128,256]{2,1,0:T(8,128)(2,1)}, f32[16,128,256]{2,1,0:T(8,128)}, f32[16,160,128]{2,1,0:T(8,128)...) custom-call(bf16[16,256,256]{2,1,0:T(8,128)(2,1)} %bitcast.141, ...), custom_call_target="tpu_custom_call" | custom-call | flops 49999998976 | bytes 26355712 | tf_op jit(solution)/shard_map/pallas_call | solution.py:41
  326.8 40.8 %shard_map.225 = (f32[16,1,16,256]{3,2,1,0:T(8,128)}, f32[16,1,16,256]{3,2,1,0:T(8,128)}, f32[3,1,16,256]{3,2,1,0:T(8,128)}, f32[16,128,256]{2,1,0:T(8,128)}, bf16[4,2,2,128,256]{4,3,2,1,0:T(8,128)(2,1)}) custom-call(bf16[16,256,256]{2,1,0:T(8,128)(2,1)} %bitcast.142, bf16[16,256,512]{2,1,0:T(8,128)(2,1)} %get-tuple-element.68.refs_1_.refs_0_, ...), custom_call_target="tpu_custom_call" | custom-call | flops 20000000000 | bytes 23069696 | tf_op jit(solution)/shard_map/pallas_call | solution.py:41
  367.6 0.8 multiply_bitcast_fusion.5
  368.5 1.3 collective-permute-start.2
  369.8 5.8 all-gather.1
  375.6 0.6 fusion.11
  376.2 1.7 fusion.57
  377.9 72.7 %shard_map.226 = (bf16[16,128,2048]{2,1,0:T(8,128)(2,1)}, bf16[16,128,256]{2,1,0:T(8,128)(2,1)}, f32[16,128,256]{2,1,0:T(8,128)}, f32[16,160,128]{2,1,0:T(8,128)...) custom-call(bf16[16,256,256]{2,1,0:T(8,128)(2,1)} %bitcast.143, ...), custom_call_target="tpu_custom_call" | custom-call | flops 49999998976 | bytes 35792896 | tf_op jit(solution)/shard_map/pallas_call | solution.py:41
  450.7 0.9 add_convert_fusion
  451.6 0.7 multiply_convert_fusion
  452.4 0.7 add_convert_fusion.1
  453.7 77.9 %shard_map.227 = (bf16[16,128,2048]{2,1,0:T(8,128)(2,1)}, f32[2048,256]{1,0:T(8,128)}, f32[8,256]{1,0:T(8,128)}, f32[128,2048]{1,0:T(8,128)}, bf16[2048,256]{1,0...) custom-call(bf16[16,256,512]{2,1,0:T(8,128)(2,1)} %get-tuple-element.68.refs_1_.refs_0_, ...), custom_call_target="tpu_custom_call" | custom-call | flops 6442450944 | bytes 93893632 | tf_op jit(solution)/shard_map/pallas_call | solution.py:41
  531.7 0.8 multiply_bitcast_fusion.2
  532.6 1.5 collective-permute-start.3
  534.1 1.7 fusion.5
  535.8 2.7 collective-permute-start.5
  539.2 143.5 %shard_map.228 = (bf16[4,2,2,128,2048]{4,3,2,1,0:T(8,128)(2,1)}, f32[8,256]{1,0:T(8,128)}, f32[128,2048]{1,0:T(8,128)}, f32[128,2048]{1,0:T(8,128)}, f32[128,8192]{1,0:T(8,128)}, /*index=5*/f32[256,2048]{1,0:T(8,128)}) custom-call(bf16[16,256,512]{2,1,0:T(8,128)(2,1)} %get-tuple-element.68.refs_1_.refs_0_, ...), custom_call_target="tpu_custom_call" | custom-call | flops 6442450944 | bytes 61125632 | tf_op jit(solution)/shard_map/pallas_call | solution.py:41
  682.7 2.9 multiply_reduce_fusion
  687.5 2.5 fusion.3
  692.9 0.7 slice.282
  693.6 0.7 slice_bitcast_fusion
  694.3 2.1 copy.39
  696.4 1.0 copy-done.9
  697.4 1.3 copy.40
  (119 shorter events, 10.1 us)
Async XLA Ops:
  7.2 228.0 %all-gather.5.cloned.1.call-start = ((), (), s32[]{:S(2)}) async-start(), calls=%async_computation | async-start | bytes 8912896 | tf_op jit(solution)/shard_map/all_gather | solution.py:1069
  8.0 3.2 collective-permute-start
  12.7 117.7 %copy-start.1 = (bf16[2,128,2048]{2,1,0:T(8,128)(2,1)S(1)}, bf16[2,128,2048]{2,1,0:T(8,128)(2,1)}, u32[]{:S(2)}) copy-start(bf16[2,128,2048]{2,1,0:T(8,128)(2,1)} %param.15) | copy-start | bytes 3145732
  130.3 2.0 copy-start.36
  130.3 2.5 copy-start.37
  130.3 3.1 copy-start.38
  130.3 3.6 copy-start.24
  130.3 4.2 copy-start.14
  130.4 4.9 copy-start.19
  130.4 5.5 copy-start.13
  131.5 195.3 %all-gather.7.cloned.1.call-start = ((), (), s32[]{:S(2)}) async-start(), calls=%async_computation.1 | async-start | bytes 8912896 | tf_op jit(solution)/shard_map/all_gather | solution.py:1069
  137.2 7.2 %collective-permute-start.1 = (bf16[16,2048]{1,0:T(8,128)(2,1)S(1)}, bf16[16,2048]{1,0:T(8,128)(2,1)S(1)}, u32[]{:S(2)}, u32[]{:S(2)}) collective-permute-start(bf16[16,2048]{1,0:T(8,128)(2,1)S(1)} %slice_bitcast_fusion.1), channel_id=1, source_target_pairs={{0,16},{1,17},{2,18},{3,19},{4,20},{5,21},{6,22},{7,23},{8,24},{9,... | collective-permute-start | bytes 196616 | tf_op jit(solution)/shard_map/ppermute | solution.py:1033
  144.4 0.6 copy-start.35
  173.5 59.4 %copy-start.21 = (bf16[16,256]{1,0:T(8,128)(2,1)S(1)}, bf16[16,256]{1,0:T(8,128)(2,1)}, u32[]{:S(2)}) copy-start(bf16[16,256]{1,0:T(8,128)(2,1)} %get-tuple-element.84) | copy-start | bytes 24580
  173.5 60.6 %copy-start.8 = (bf16[16,256,256]{2,1,0:T(8,128)(2,1)S(1)}, bf16[16,256,256]{2,1,0:T(8,128)(2,1)}, u32[]{:S(2)}) copy-start(bf16[16,256,256]{2,1,0:T(8,128)(2,1)} %get-tuple-element.69.refs_2_) | copy-start | bytes 6291460
  233.5 134.1 %copy-start.18 = (f32[8,256]{1,0:T(8,128)}, f32[8,256]{1,0:T(8,128)S(1)}, u32[]{:S(2)}) copy-start(f32[8,256]{1,0:T(8,128)S(1)} %get-tuple-element.142.refs_2_) | copy-start | bytes 24580
  326.8 40.8 %copy-start.15 = (bf16[256,160]{0,1:T(8,128)(2,1)S(1)}, bf16[256,160]{0,1:T(8,128)(2,1)}, u32[]{:S(2)}) copy-start(bf16[256,160]{0,1:T(8,128)(2,1)} %param.20) | copy-start | bytes 245764
  326.8 40.8 %copy-start.30 = (f32[256]{0:T(256)S(1)}, f32[256]{0:T(256)}, u32[]{:S(2)}) copy-start(f32[256]{0:T(256)} %convert_element_type.68) | copy-start | bytes 3076
  368.5 84.6 %collective-permute-start.2 = (f32[3,8,256]{2,1,0:T(8,128)S(1)}, f32[3,8,256]{2,1,0:T(8,128)S(1)}, u32[]{:S(2)}, u32[]{:S(2)}) collective-permute-start(f32[3,8,256]{2,1,0:T(8,128)S(1)} %pad_maximum_fusion.1), channel_id=1, source_target_pairs={{16,0},{17,1},{18,2},{19,3},{20,4},{21,5},{22,6},{23,7},{24,8},{25... | collective-permute-start | bytes 73736 | tf_op jit(solution)/shard_map/ppermute | solution.py:1033
  377.9 72.8 %copy-start.12 = (f32[128,256]{1,0:T(8,128)S(1)}, f32[128,256]{1,0:T(8,128)}, u32[]{:S(2)}) copy-start(f32[128,256]{1,0:T(8,128)} %get-tuple-element.109) | copy-start | bytes 393220
  377.9 73.7 %copy-start.20 = (bf16[16,256]{1,0:T(8,128)(2,1)S(1)}, bf16[16,256]{1,0:T(8,128)(2,1)}, u32[]{:S(2)}) copy-start(bf16[16,256]{1,0:T(8,128)(2,1)} %param.23) | copy-start | bytes 24580
  377.9 73.7 %copy-start.25 = (f32[16,256]{1,0:T(8,128)S(1)}, f32[16,256]{1,0:T(8,128)}, u32[]{:S(2)}) copy-start(f32[16,256]{1,0:T(8,128)} %get-tuple-element.107) | copy-start | bytes 49156
  377.9 74.4 %copy-start.27 = (f32[8,256]{1,0:T(8,128)S(1)}, f32[8,256]{1,0:T(8,128)}, u32[]{:S(2)}) copy-start(f32[8,256]{1,0:T(8,128)} %get-tuple-element.75) | copy-start | bytes 24580
  453.1 0.6 copy-start.22
  453.7 78.0 %copy-start.17 = (f32[8,256]{1,0:T(8,128)S(1)}, f32[8,256]{1,0:T(8,128)}, u32[]{:S(2)}) copy-start(f32[8,256]{1,0:T(8,128)} %get-tuple-element.141.refs_2_) | copy-start | bytes 24580
  453.7 78.0 %copy-start.26 = (f32[8,256]{1,0:T(8,128)S(1)}, f32[8,256]{1,0:T(8,128)}, u32[]{:S(2)}) copy-start(f32[8,256]{1,0:T(8,128)} %get-tuple-element.130) | copy-start | bytes 24580
  453.7 78.0 %copy-start.31 = (f32[256]{0:T(256)S(1)}, f32[256]{0:T(256)}, u32[]{:S(2)}) copy-start(f32[256]{0:T(256)} %convert_element_type.68) | copy-start | bytes 3076
  453.7 78.0 %copy-start.32 = (f32[8]{0:T(128)S(1)}, f32[8]{0:T(128)}, u32[]{:S(2)}) copy-start(f32[8]{0:T(128)} %get-tuple-element.114) | copy-start | bytes 100
  453.7 78.0 %copy-start.33 = (f32[8]{0:T(128)S(1)}, f32[8]{0:T(128)}, u32[]{:S(2)}) copy-start(f32[8]{0:T(128)} %get-tuple-element.115) | copy-start | bytes 100
  453.7 78.0 %copy-start.34 = (f32[8]{0:T(128)S(1)}, f32[8]{0:T(128)}, u32[]{:S(2)}) copy-start(f32[8]{0:T(128)} %get-tuple-element.116) | copy-start | bytes 100
  453.7 80.4 %copy-start.6 = (bf16[16,1,128,256]{3,2,1,0:T(8,128)(2,1)S(1)}, bf16[16,1,128,256]{3,2,1,0:T(8,128)(2,1)}, u32[]{:S(2)}) copy-start(bf16[16,1,128,256]{3,2,1,0:T(8,128)(2,1)} %get-tuple-element.120) | copy-start | bytes 3145732
  532.6 6.0 collective-permute-start.3
  535.8 155.9 %collective-permute-start.5 = (bf16[408,256]{1,0:T(8,128)(2,1)S(1)}, bf16[408,256]{1,0:T(8,128)(2,1)S(1)}, u32[]{:S(2)}, u32[]{:S(2)}) collective-permute-start(bf16[408,256]{1,0:T(8,128)(2,1)S(1)} %pad_maximum_fusion), channel_id=1, source_target_pairs={{0,16},{16,0},{1,17},{17,1},{2,18},{18,2},{3,19},{19,3},{4,20},{20... | collective-permute-start | bytes 626696 | tf_op jit(solution)/shard_map/ppermute | solution.py:1040
  538.5 0.6 copy-start.23
  539.2 143.5 %copy-start.7 = (bf16[128,8192]{1,0:T(8,128)(2,1)S(1)}, bf16[128,8192]{1,0:T(8,128)(2,1)}, u32[]{:S(2)}) copy-start(bf16[128,8192]{1,0:T(8,128)(2,1)} %wts.1) | copy-start | bytes 6291460
  682.7 3.0 copy-start.28
  682.7 3.0 copy-start.29
  682.7 3.1 copy-start.3
  682.7 3.1 copy-start.4
  682.7 3.1 copy-start.5
  682.7 3.1 copy-start.16
  685.6 1.3 copy-start.2
  685.7 1.6 copy-start.10
  685.7 1.9 copy-start.11
  685.7 4.8 collective-permute-start.4
  687.5 2.5 copy-start.39
  687.5 6.7 copy-start
  694.3 3.1 copy-start.9
Sparse Core Ops, SparseCore 0:
  131.6 93.5 all-gather.4
  227.4 74.0 all-gather.6

commit v9 on v8

--- a/solution.py
+++ b/solution.py
@@ -742,7 +742,7 @@
     s_scr, p_scr, f_scr, sd_scr, dx_scr, dy_scr, bcs_scr, bc_scr = refs[:8]
     if sending:
         beside(pl.program_id(0), dims[0] * dims[1] * dims[2], dims, 0,
-               [allsum_steps((adding, added) + refs[8:], dims, functools.partial(spread_plain, n=n)) + (None,)])
+               [allsum_steps((adding, added) + refs[8:], dims, functools.partial(spread_plain, n=n)) + ([1, 4, 7, 10, 13, 15],)])
     b = pl.program_id(0)
     @pl.when(b == 0)
     def _():

time: 707 us -> 704 us (level)
  no operation moved by 1% of the time
where the time goes in v9:
time: 704 us; the launch traced here: 702 us
  Pallas kernels  621 us (88%)
  local copies, waits for them, and re-layouts  20.5 us (3%)
  other arithmetic  15.9 us (2%)
  between operations  14.7 us (2%)
  starting transfers between devices  13.1 us (2%)
  blocking collectives  10.8 us (2%)
    pallas_call x7, Pallas kernels, call(): pl.pallas_call(kernel, grid=grid, in_specs=in_specs, out_specs=out_specs,...  444 us
    pallas_call x1, Pallas kernels, gather(): pl.pallas_call(functools.partial(gather_kernel, dims=dims, chunks=chunks)...  118 us
    pallas_call x1, Pallas kernels, allsum(): pl.pallas_call(functools.partial(allsum_kernel, dims=dims, chunks=chunks,...  59.3 us
  transfers between devices with their start and end apart: 8, of which 1 were waited for; matrix products, arithmetic and copies ran while one was open for 4% of the time, Pallas kernels for 55%

profile of v9, /device:TPU:0, one launch (start us, length us, event | category | flops | bytes accessed | tf_op | source)
XLA Modules:
  0.0 702.1 jit_solution(2439463539093331022)
XLA Ops:
  7.2 0.8 slice.190
  8.0 2.3 collective-permute-start
  10.3 0.7 convert_bitcast_fusion
  11.1 0.9 compare_bitcast_fusion.2
  12.1 0.7 maximum_maximum_fusion.small
  12.7 117.6 %shard_map.220 = (bf16[4,2,2,256,2048]{4,3,2,1,0:T(8,128)(2,1)}, f32[4,2,2,8,128]{4,3,2,1,0:T(8,128)}, bf16[16,2,64,512]{3,2,1,0:T(8,128)(2,1)}) custom-call(bf16[256,2048]{1,0:T(8,128)(2,1)} %bitcast.132, f32[8,128]{1,0:T(8,128)} %maximum_maximum_fusion.small, bf16[128,8192]{1,0:T(8,128)(2,1)} %wts.1), custom_call_target="tpu_custom_call" | custom-call | flops 80000000000 | bytes 16777216 | tf_op jit(solution)/shard_map/pallas_call | solution.py:394
  130.4 1.1 fusion.48
  131.5 0.7 all-gather.7.cloned.1.call-update
  134.6 0.7 pad.9.refs_8_
  135.2 0.6 fusion.18.refs_8_.refs_10_
  135.9 1.3 slice.194
  137.2 3.4 collective-permute-start.1
  140.6 0.6 copy.33
  141.2 1.5 pad.8.mask_ref.refs_3_
  142.8 0.8 slice_reduce_fusion.2
  143.6 0.6 fusion.50
  144.4 0.6 copy-done.35
  145.0 27.5 %shard_map.221 = (bf16[16,256,512]{2,1,0:T(8,128)(2,1)}, bf16[16,256,256]{2,1,0:T(8,128)(2,1)}, bf16[16,256,2048]{2,1,0:T(8,128)(2,1)}, bf16[16,256]{1,0:T(8,128...) custom-call(bf16[16,256,2048]{2,1,0:T(8,128)(2,1)} %bitcast.164, bf16[2048,512]{1,0:T(8,128)(2,1)} %bitcast.122, ...), custom_call_target="tpu_custom_call" | custom-call | flops 8589934592 | bytes 44864512 | tf_op jit(solution)/shard_map/pallas_call | solution.py:41
  172.5 1.0 slice.213
  173.5 59.3 %shard_map.222 = bf16[4,2,2,256,256]{4,3,2,1,0:T(8,128)(2,1)} custom-call(f32[4,2,2,160,128]{4,3,2,1,0:T(8,128)} %bitcast.144, f32[4,2,2,160,128]{4,3,2,1,0:T(8,128)} %bitcast.145), custom_call_target="tpu_custom_call" | custom-call | tf_op jit(solution)/shard_map/pallas_call | solution.py:218
  234.1 1.1 fusion.47
  235.2 26.7 %shard_map.223 = (f32[16,1,16,256]{3,2,1,0:T(8,128)}, f32[16,1,16,256]{3,2,1,0:T(8,128)}, f32[3,1,16,256]{3,2,1,0:T(8,128)}, f32[16,128,256]{2,1,0:T(8,128)}) custom-call(bf16[16,256,256]{2,1,0:T(8,128)(2,1)} %bitcast.140, bf16[16,256,512]{2,1,0:T(8,128)(2,1)} %get-tuple-element.68.refs_1_.refs_0_, bf16[16,256,256]{2,1,0:T(8,128)(2,1)} %get-tuple-element.69.refs_2_, ...), custom_call_target="tpu_custom_call" | custom-call | flops 20000000000 | bytes 20710400 | tf_op jit(solution)/shard_map/pallas_call | solution.py:41
  261.9 5.0 all-gather
  267.5 59.3 %shard_map.224 = (bf16[16,128,2048]{2,1,0:T(8,128)(2,1)}, bf16[16,128,256]{2,1,0:T(8,128)(2,1)}, f32[16,128,256]{2,1,0:T(8,128)}, f32[16,160,128]{2,1,0:T(8,128)...) custom-call(bf16[16,256,256]{2,1,0:T(8,128)(2,1)} %bitcast.141, ...), custom_call_target="tpu_custom_call" | custom-call | flops 49999998976 | bytes 26355712 | tf_op jit(solution)/shard_map/pallas_call | solution.py:41
  326.8 37.4 %shard_map.225 = (f32[16,1,16,256]{3,2,1,0:T(8,128)}, f32[16,1,16,256]{3,2,1,0:T(8,128)}, f32[3,1,16,256]{3,2,1,0:T(8,128)}, f32[16,128,256]{2,1,0:T(8,128)}, bf16[4,2,2,128,256]{4,3,2,1,0:T(8,128)(2,1)}) custom-call(bf16[16,256,256]{2,1,0:T(8,128)(2,1)} %bitcast.142, bf16[16,256,512]{2,1,0:T(8,128)(2,1)} %get-tuple-element.68.refs_1_.refs_0_, ...), custom_call_target="tpu_custom_call" | custom-call | flops 20000000000 | bytes 23069696 | tf_op jit(solution)/shard_map/pallas_call | solution.py:41
  364.3 0.8 multiply_bitcast_fusion.5
  365.1 1.3 collective-permute-start.2
  366.4 5.8 all-gather.1
  372.3 0.6 fusion.11
  372.9 1.7 fusion.57
  374.6 72.8 %shard_map.226 = (bf16[16,128,2048]{2,1,0:T(8,128)(2,1)}, bf16[16,128,256]{2,1,0:T(8,128)(2,1)}, f32[16,128,256]{2,1,0:T(8,128)}, f32[16,160,128]{2,1,0:T(8,128)...) custom-call(bf16[16,256,256]{2,1,0:T(8,128)(2,1)} %bitcast.143, ...), custom_call_target="tpu_custom_call" | custom-call | flops 49999998976 | bytes 35792896 | tf_op jit(solution)/shard_map/pallas_call | solution.py:41
  447.4 0.9 add_convert_fusion
  448.3 0.7 multiply_convert_fusion
  449.1 0.7 add_convert_fusion.1
  450.4 79.1 %shard_map.227 = (bf16[16,128,2048]{2,1,0:T(8,128)(2,1)}, f32[2048,256]{1,0:T(8,128)}, f32[8,256]{1,0:T(8,128)}, f32[128,2048]{1,0:T(8,128)}, bf16[2048,256]{1,0...) custom-call(bf16[16,256,512]{2,1,0:T(8,128)(2,1)} %get-tuple-element.68.refs_1_.refs_0_, ...), custom_call_target="tpu_custom_call" | custom-call | flops 6442450944 | bytes 93893632 | tf_op jit(solution)/shard_map/pallas_call | solution.py:41
  529.6 0.8 multiply_bitcast_fusion.2
  530.5 1.5 collective-permute-start.3
  532.0 1.7 fusion.5
  533.8 2.7 collective-permute-start.5
  537.1 141.6 %shard_map.228 = (bf16[4,2,2,128,2048]{4,3,2,1,0:T(8,128)(2,1)}, f32[8,256]{1,0:T(8,128)}, f32[128,2048]{1,0:T(8,128)}, f32[128,2048]{1,0:T(8,128)}, f32[128,8192]{1,0:T(8,128)}, /*index=5*/f32[256,2048]{1,0:T(8,128)}) custom-call(bf16[16,256,512]{2,1,0:T(8,128)(2,1)} %get-tuple-element.68.refs_1_.refs_0_, ...), custom_call_target="tpu_custom_call" | custom-call | flops 6442450944 | bytes 61125632 | tf_op jit(solution)/shard_map/pallas_call | solution.py:41
  678.7 2.9 multiply_reduce_fusion
  681.7 1.7 collective-permute-start.4
  684.2 2.5 fusion.3
  689.5 0.7 slice.282
  690.2 0.7 slice_bitcast_fusion
  690.9 2.1 copy.39
  693.0 1.0 copy-done.9
  694.0 1.3 copy.40
  (119 shorter events, 9.5 us)
Async XLA Ops:
  7.2 228.0 %all-gather.5.cloned.1.call-start = ((), (), s32[]{:S(2)}) async-start(), calls=%async_computation | async-start | bytes 8912896 | tf_op jit(solution)/shard_map/all_gather | solution.py:1069
  8.0 3.2 collective-permute-start
  12.7 117.7 %copy-start.1 = (bf16[2,128,2048]{2,1,0:T(8,128)(2,1)S(1)}, bf16[2,128,2048]{2,1,0:T(8,128)(2,1)}, u32[]{:S(2)}) copy-start(bf16[2,128,2048]{2,1,0:T(8,128)(2,1)} %param.15) | copy-start | bytes 3145732
  130.3 2.0 copy-start.36
  130.3 2.5 copy-start.37
  130.3 3.1 copy-start.38
  130.3 3.6 copy-start.24
  130.3 4.2 copy-start.14
  130.4 4.9 copy-start.19
  130.4 5.5 copy-start.13
  131.5 195.3 %all-gather.7.cloned.1.call-start = ((), (), s32[]{:S(2)}) async-start(), calls=%async_computation.1 | async-start | bytes 8912896 | tf_op jit(solution)/shard_map/all_gather | solution.py:1069
  137.2 7.2 %collective-permute-start.1 = (bf16[16,2048]{1,0:T(8,128)(2,1)S(1)}, bf16[16,2048]{1,0:T(8,128)(2,1)S(1)}, u32[]{:S(2)}, u32[]{:S(2)}) collective-permute-start(bf16[16,2048]{1,0:T(8,128)(2,1)S(1)} %slice_bitcast_fusion.1), channel_id=1, source_target_pairs={{0,16},{1,17},{2,18},{3,19},{4,20},{5,21},{6,22},{7,23},{8,24},{9,... | collective-permute-start | bytes 196616 | tf_op jit(solution)/shard_map/ppermute | solution.py:1033
  144.4 0.6 copy-start.35
  173.5 59.4 %copy-start.21 = (bf16[16,256]{1,0:T(8,128)(2,1)S(1)}, bf16[16,256]{1,0:T(8,128)(2,1)}, u32[]{:S(2)}) copy-start(bf16[16,256]{1,0:T(8,128)(2,1)} %get-tuple-element.84) | copy-start | bytes 24580
  173.5 60.6 %copy-start.8 = (bf16[16,256,256]{2,1,0:T(8,128)(2,1)S(1)}, bf16[16,256,256]{2,1,0:T(8,128)(2,1)}, u32[]{:S(2)}) copy-start(bf16[16,256,256]{2,1,0:T(8,128)(2,1)} %get-tuple-element.69.refs_2_) | copy-start | bytes 6291460
  233.5 130.8 %copy-start.18 = (f32[8,256]{1,0:T(8,128)}, f32[8,256]{1,0:T(8,128)S(1)}, u32[]{:S(2)}) copy-start(f32[8,256]{1,0:T(8,128)S(1)} %get-tuple-element.142.refs_2_) | copy-start | bytes 24580
  326.8 37.5 %copy-start.15 = (bf16[256,160]{0,1:T(8,128)(2,1)S(1)}, bf16[256,160]{0,1:T(8,128)(2,1)}, u32[]{:S(2)}) copy-start(bf16[256,160]{0,1:T(8,128)(2,1)} %param.20) | copy-start | bytes 245764
  326.8 37.5 %copy-start.30 = (f32[256]{0:T(256)S(1)}, f32[256]{0:T(256)}, u32[]{:S(2)}) copy-start(f32[256]{0:T(256)} %convert_element_type.68) | copy-start | bytes 3076
  365.1 84.6 %collective-permute-start.2 = (f32[3,8,256]{2,1,0:T(8,128)S(1)}, f32[3,8,256]{2,1,0:T(8,128)S(1)}, u32[]{:S(2)}, u32[]{:S(2)}) collective-permute-start(f32[3,8,256]{2,1,0:T(8,128)S(1)} %pad_maximum_fusion.1), channel_id=1, source_target_pairs={{16,0},{17,1},{18,2},{19,3},{20,4},{21,5},{22,6},{23,7},{24,8},{25... | collective-permute-start | bytes 73736 | tf_op jit(solution)/shard_map/ppermute | solution.py:1033
  374.6 72.8 %copy-start.12 = (f32[128,256]{1,0:T(8,128)S(1)}, f32[128,256]{1,0:T(8,128)}, u32[]{:S(2)}) copy-start(f32[128,256]{1,0:T(8,128)} %get-tuple-element.109) | copy-start | bytes 393220
  374.6 73.7 %copy-start.20 = (bf16[16,256]{1,0:T(8,128)(2,1)S(1)}, bf16[16,256]{1,0:T(8,128)(2,1)}, u32[]{:S(2)}) copy-start(bf16[16,256]{1,0:T(8,128)(2,1)} %param.23) | copy-start | bytes 24580
  374.6 73.7 %copy-start.25 = (f32[16,256]{1,0:T(8,128)S(1)}, f32[16,256]{1,0:T(8,128)}, u32[]{:S(2)}) copy-start(f32[16,256]{1,0:T(8,128)} %get-tuple-element.107) | copy-start | bytes 49156
  374.6 74.5 %copy-start.27 = (f32[8,256]{1,0:T(8,128)S(1)}, f32[8,256]{1,0:T(8,128)}, u32[]{:S(2)}) copy-start(f32[8,256]{1,0:T(8,128)} %get-tuple-element.75) | copy-start | bytes 24580
  449.8 0.6 copy-start.22
  450.4 79.2 %copy-start.17 = (f32[8,256]{1,0:T(8,128)S(1)}, f32[8,256]{1,0:T(8,128)}, u32[]{:S(2)}) copy-start(f32[8,256]{1,0:T(8,128)} %get-tuple-element.141.refs_2_) | copy-start | bytes 24580
  450.4 79.2 %copy-start.26 = (f32[8,256]{1,0:T(8,128)S(1)}, f32[8,256]{1,0:T(8,128)}, u32[]{:S(2)}) copy-start(f32[8,256]{1,0:T(8,128)} %get-tuple-element.130) | copy-start | bytes 24580
  450.4 79.2 %copy-start.31 = (f32[256]{0:T(256)S(1)}, f32[256]{0:T(256)}, u32[]{:S(2)}) copy-start(f32[256]{0:T(256)} %convert_element_type.68) | copy-start | bytes 3076
  450.4 79.2 %copy-start.32 = (f32[8]{0:T(128)S(1)}, f32[8]{0:T(128)}, u32[]{:S(2)}) copy-start(f32[8]{0:T(128)} %get-tuple-element.114) | copy-start | bytes 100
  450.4 79.2 %copy-start.33 = (f32[8]{0:T(128)S(1)}, f32[8]{0:T(128)}, u32[]{:S(2)}) copy-start(f32[8]{0:T(128)} %get-tuple-element.115) | copy-start | bytes 100
  450.4 79.2 %copy-start.34 = (f32[8]{0:T(128)S(1)}, f32[8]{0:T(128)}, u32[]{:S(2)}) copy-start(f32[8]{0:T(128)} %get-tuple-element.116) | copy-start | bytes 100
  450.4 81.6 %copy-start.6 = (bf16[16,1,128,256]{3,2,1,0:T(8,128)(2,1)S(1)}, bf16[16,1,128,256]{3,2,1,0:T(8,128)(2,1)}, u32[]{:S(2)}) copy-start(bf16[16,1,128,256]{3,2,1,0:T(8,128)(2,1)} %get-tuple-element.120) | copy-start | bytes 3145732
  530.5 6.0 collective-permute-start.3
  533.8 154.5 %collective-permute-start.5 = (bf16[408,256]{1,0:T(8,128)(2,1)S(1)}, bf16[408,256]{1,0:T(8,128)(2,1)S(1)}, u32[]{:S(2)}, u32[]{:S(2)}) collective-permute-start(bf16[408,256]{1,0:T(8,128)(2,1)S(1)} %pad_maximum_fusion), channel_id=1, source_target_pairs={{0,16},{16,0},{1,17},{17,1},{2,18},{18,2},{3,19},{19,3},{4,20},{20... | collective-permute-start | bytes 626696 | tf_op jit(solution)/shard_map/ppermute | solution.py:1040
  536.5 0.6 copy-start.23
  537.1 141.6 %copy-start.7 = (bf16[128,8192]{1,0:T(8,128)(2,1)S(1)}, bf16[128,8192]{1,0:T(8,128)(2,1)}, u32[]{:S(2)}) copy-start(bf16[128,8192]{1,0:T(8,128)(2,1)} %wts.1) | copy-start | bytes 6291460
  678.7 3.0 copy-start.28
  678.7 3.0 copy-start.29
  678.7 4.8 copy-start.3
  678.7 4.8 copy-start.4
  678.7 4.8 copy-start.5
  678.7 4.8 copy-start.16
  681.7 2.4 copy-start.2
  681.7 2.4 copy-start.10
  681.7 2.4 copy-start.11
  681.7 5.4 collective-permute-start.4
  684.1 2.5 copy-start.39
  684.1 6.7 copy-start
  690.9 3.1 copy-start.9
Sparse Core Ops, SparseCore 0:
  131.6 93.5 all-gather.4
  227.4 74.0 all-gather.6
